TPU v7x, 128 devices: a whole 4x4x4 slice. The times are simulated.
128 devices in a mesh: gx: 8 (over x, z_hi), gy: 4 (over y), gz: 4 (over z_lo, core).
Axes of the slice: x: 4, y: 4, z: 4 (z_hi: 2, z_lo: 2; z = z_hi * 2 + z_lo), core: 2. Of those that a mesh axis runs over, the one named last changes fastest.
Arguments:
- pre_act: bfloat16 [2048, 24576], P('gx', ('gy', 'gz')), may hold values from -6 to 6
- grad_out: bfloat16 [2048, 6144], P(('gx', 'gy'), 'gz'), may hold values from -0.3125 to 0.3125
- weight: bfloat16 [3072, 8, 6144], P('gy', 'gx', 'gz'), may hold values from -6 to 6
Outputs:
- pre_grad: bfloat16 [2048, 24576], P('gx', ('gy', 'gz'))
- weight_grad: bfloat16 [3072, 8, 6144], P('gy', 'gx', 'gz')
All inputs are finite; a program needn't handle non-finite values.
Results may differ from a plain program's by a relative error of at most 0.02.
Values may be sent and summed in bfloat16 or wider, within the bound.
No kernel may reach another device: no remote copies, remote signals or barrier semaphores. Data moves between devices by JAX's collectives and lax.ppermute only.
A program may use at most 128 MiB of HBM per device.

v0:
```python
import functools

import jax
import jax.numpy as jnp
from jax import lax
from jax.experimental import pallas as pl
from jax.experimental.pallas import tpu as pltpu
from jax.sharding import PartitionSpec as P

tanh_scale = 0.7978845608028654
cubic_coef = 0.044715
bf16 = jnp.bfloat16
f32 = jnp.float32
MIB = 1024 * 1024
VMEM = pl.BlockSpec(memory_space=pltpu.VMEM)
SMEM = pl.BlockSpec(memory_space=pltpu.SMEM)
ANY = pl.BlockSpec(memory_space=pl.ANY)


def send(v, axis, count, to):
    return lax.ppermute(v, axis, [(i, to(i)) for i in range(count)])


def send_x(v, d):
    return send(v, "gx", 8, lambda i: ((i // 2 + d) % 4) * 2 + i % 2)


def send_y(v, d):
    return send(v, "gy", 4, lambda i: (i + d) % 4)


def swap_z_hi(v):
    return send(v, "gx", 8, lambda i: i ^ 1)


def swap_z_lo(v):
    return send(v, "gz", 4, lambda i: i ^ 2)


def swap_core(v):
    return send(v, "gz", 4, lambda i: i ^ 1)


def call(body, out_shape, in_specs, cost, out_specs=None, scratch=(), limit=56):
    if out_specs is None:
        out_specs = [VMEM] * len(out_shape)
    flops, moved = cost
    return pl.pallas_call(
        body,
        out_shape=[jax.ShapeDtypeStruct(*s) for s in out_shape],
        in_specs=in_specs,
        out_specs=out_specs,
        scratch_shapes=list(scratch),
        compiler_params=pltpu.CompilerParams(vmem_limit_bytes=limit * MIB),
        cost_estimate=pl.CostEstimate(flops=flops, bytes_accessed=moved, transcendentals=0),
    )


def one_hot(at, rows):
    q = lax.broadcasted_iota(jnp.int32, (rows, 256), 0)
    u = lax.broadcasted_iota(jnp.int32, (rows, 256), 1)
    i, r = q // 32, q % 32
    s = ((at[0] - i // 2) & 3) * 2 + ((at[1] + i) & 1)
    return jnp.where(u == r * 8 + s, 1.0, 0.0).astype(bf16)


def token_rows(y, half, k):
    return pl.ds(pl.multiple_of(((y - k) & 3) * 64 + half * 32, 32), 32)


def pack_body(at, pre, *outs):
    slope, parts = outs[0], outs[1:]
    pick = one_hot(at, 256)
    for j in range(pre.shape[1] // 256):
        cols = slice(256 * j, 256 * j + 256)
        u = jnp.concatenate([pre[token_rows(at[2], h, k), cols] for h in range(2) for k in range(4)], 0)
        u = u.astype(f32)
        t = jnp.tanh(tanh_scale * (u + cubic_coef * u * u * u))
        slope[:, cols] = 0.5 * (1.0 + t) + 0.5 * u * (1.0 - t * t) * tanh_scale * (
            1.0 + 3.0 * cubic_coef * u * u
        )
        hidden = (0.5 * u * (1.0 + t)).astype(bf16)
        turned = lax.dot_general(pick, hidden, (((1,), (1,)), ((), ())), preferred_element_type=f32)
        turned = turned.astype(bf16)
        for i in range(8):
            parts[i][32 * j : 32 * j + 32, :] = turned[32 * i : 32 * i + 32, :]


def grad_copies(pieces, held, sems):
    a4, a1, a3, a2p, a2m, b4, b1, b3, b2p, b2m = pieces
    lower, todo = pl.ds(0, 128), []
    for k, src in ((0, a4), (1, a1), (3, a3)):
        todo.append((src, held.at[k, :, lower, :]))
    todo.append((a2p, held.at[2, pl.ds(0, 1), lower, :]))
    todo.append((a2m, held.at[2, pl.ds(1, 1), lower, :]))
    for k, src in ((0, b4), (1, b1), (3, b3)):
        todo.append((src, held.at[:, :, pl.ds(128 + 32 * k, 32), :]))
    todo.append((b2p, held.at[pl.ds(0, 2), :, pl.ds(192, 32), :]))
    todo.append((b2m, held.at[pl.ds(2, 2), :, pl.ds(192, 32), :]))
    return [pltpu.make_async_copy(s, d, sems.at[n]) for n, (s, d) in enumerate(todo)]


def input_body(at, w, *refs):
    pieces, (mine, theirs, held, sems) = refs[:10], refs[10:]
    copies = grad_copies(pieces, held, sems)
    for c in copies:
        c.start()
    for c in copies:
        c.wait()
    rows = w.shape[0] // 4
    ws = []
    for core, out in ((0, mine), (1, theirs)):
        for lo in range(2):
            block = ((at[3] + lo) & 1) * 2 + ((at[4] + core) & 1)
            ws.append(w[pl.ds(pl.multiple_of(block * rows, 64), rows), :])
    turned = jnp.concatenate(ws, 0)

    @pl.loop(0, 8)
    def _(d):
        k, z = d // 2, d % 2
        part = lax.dot_general(
            turned, held[k, z], (((1,), (1,)), ((), ())), preferred_element_type=f32
        ).astype(bf16)
        for lo in range(2):
            mine[lo, z, k] = part[lo * rows : lo * rows + rows]
            theirs[lo, z, k] = part[(lo + 2) * rows : (lo + 3) * rows]


def core_sum_body(mine, other, *outs):
    for lo in range(2):
        for z in range(2):
            for k in range(4):
                total = mine[lo, z, k].astype(f32) + other[lo, z, k].astype(f32)
                outs[lo * 2 + z][k] = total.astype(bf16)


def z_sum_body(r00, r01, r10, r11, *outs):
    for k in range(4):
        outs[k][0] = (r00[k].astype(f32) + r10[k].astype(f32)).astype(bf16)
        outs[k][1] = (r01[k].astype(f32) + r11[k].astype(f32)).astype(bf16)


def finish_body(at, slope, p0, p1, p2, p3, out):
    pick = one_hot(at, 256)
    for j in range(out.shape[1] // 256):
        cols = slice(256 * j, 256 * j + 256)
        v = jnp.concatenate([p[z, 32 * j : 32 * j + 32, :] for p in (p0, p1, p2, p3) for z in range(2)], 0)
        total = lax.dot_general(v, pick, (((0,), (0,)), ((), ())), preferred_element_type=f32)
        result = (total * slope[:, cols]).astype(bf16)
        for h in range(2):
            for k in range(4):
                n = (h * 4 + k) * 32
                out[token_rows(at[2], h, k), cols] = result[n : n + 32, :]


def weight_body(at, *refs):
    hidden, pieces, (out, held, sems) = refs[:4], refs[4:14], refs[14:]
    copies = grad_copies(pieces, held, sems)
    for c in copies:
        c.start()
    for c in copies:
        c.wait()
    rows = out.shape[0] // 4
    lhs = jnp.concatenate(
        [jnp.concatenate([h[d] for d in range(8)], 1) for h in hidden], 0
    )

    @pl.loop(0, out.shape[1] // 256)
    def _(j):
        cols = pl.ds(pl.multiple_of(j * 256, 256), 256)
        grads = held[:, :, :, cols].reshape(2048, 256)
        total = lax.dot_general(lhs, grads, (((1,), (0,)), ((), ())), preferred_element_type=f32)
        total = total.astype(bf16)
        for n, (lo, core) in enumerate(((0, 0), (1, 0), (0, 1), (1, 1))):
            block = ((at[3] + lo) & 1) * 2 + ((at[4] + core) & 1)
            out[pl.ds(pl.multiple_of(block * rows, 64), rows), cols] = total[n * rows : n * rows + rows]


def gather_grad(grad_out):
    half = grad_out.shape[0] // 2
    other = swap_z_hi(grad_out)
    a = jnp.stack([grad_out[:half], other[:half]])
    b = jnp.stack([grad_out[half:], other[half:]])
    a4 = jnp.stack([a] + [send_y(a, k) for k in (1, 2, 3)], 1)
    b4 = jnp.stack([b] + [send_x(b, k) for k in (1, 2, 3)], 0)
    a1, a3 = send_x(a4, 1), send_x(a4, 3)
    b1, b3 = send_y(b4, 1), send_y(b4, 3)
    a2p, a2m = send_x(a1[:1], 1), send_x(a3[1:], 3)
    b2p, b2m = send_y(b1[:2], 1), send_y(b3[2:], 3)
    a = [v.reshape(-1, 4 * half, v.shape[-1]) for v in (a4, a1, a3, a2p, a2m)]
    return a + [b4, b1, b3, b2p, b2m]


def per_device(pre_act, grad_out, weight):
    tokens, columns = pre_act.shape
    rows, features = columns // 8, grad_out.shape[1]
    gx, y, gz = lax.axis_index("gx"), lax.axis_index("gy"), lax.axis_index("gz")
    at = jnp.stack([gx // 2, gx % 2, y, gz // 2, gz % 2]).astype(jnp.int32)
    w = weight.reshape(4 * rows, features)
    block = (rows, tokens)
    grad_scratch = [pltpu.VMEM((4, 2, tokens, features), bf16), pltpu.SemaphoreType.DMA((10,))]
    product = 2 * 4 * rows * 8 * tokens * features

    slope, *parts = call(
        pack_body,
        [((tokens, columns), f32)] + [(block, bf16)] * 8,
        [SMEM, VMEM],
        (2 * tokens * 256 * columns, 8 * tokens * columns),
    )(at, pre_act)

    pieces = gather_grad(grad_out)

    got = [None] * 8
    for k in range(4):
        for z in range(2):
            to = lambda i, k=k, z=z: ((i // 2 - k) % 4) * 2 + (i % 2 ^ z)
            moved = parts[2 * k + z] if k == z == 0 else send(parts[2 * k + z], "gx", 8, to)
            got[2 * ((4 - k) % 4) + z] = moved
    own = jnp.stack(got)
    far = swap_z_lo(own)
    hidden = [own, far, swap_core(own), swap_core(far)]

    shape = ((2, 2, 4) + block, bf16)
    mine, theirs = call(
        input_body,
        [shape, shape],
        [SMEM, VMEM] + [ANY] * 10,
        (product, 2 * (6 * rows * features + 2048 * features)),
        scratch=grad_scratch,
    )(at, w, *pieces)
    other = swap_core(theirs)
    size = 2 * 4 * rows * tokens
    r00, r01, r10, r11 = call(
        core_sum_body, [((4,) + block, bf16)] * 4, [VMEM] * 2, (4 * size, 12 * size)
    )(mine, other)
    q01, q10 = swap_z_hi(r01), swap_z_lo(r10)
    q11 = send(r11, ("gx", "gz"), 32, lambda i: i ^ 6)
    sums = call(z_sum_body, [((2,) + block, bf16)] * 4, [VMEM] * 4, (2 * size, 6 * size))(
        r00, q01, q10, q11
    )
    back = [sums[0]] + [send_x(sums[4 - k], k) for k in (1, 2, 3)]
    (pre_grad,) = call(
        finish_body,
        [((tokens, columns), bf16)],
        [SMEM] + [VMEM] * 5,
        (2 * tokens * 256 * columns, 8 * tokens * columns),
    )(at, slope, *back)
    (weight_grad,) = call(
        weight_body,
        [((4 * rows, features), bf16)],
        [SMEM] + [VMEM] * 4 + [ANY] * 10,
        (product, 2 * (8 * rows * features + 2048 * features)),
        scratch=grad_scratch,
    )(at, *hidden, *pieces)
    return pre_grad, weight_grad.reshape(weight.shape)


def solution(mesh):
    placed = (P("gx", ("gy", "gz")), P(("gx", "gy"), "gz"), P("gy", "gx", "gz"))
    return jax.shard_map(
        per_device,
        mesh=mesh,
        in_specs=placed,
        out_specs=(P("gx", ("gy", "gz")), P("gy", "gx", "gz")),
        check_vma=False,
    )
```

profile of v0, /device:TPU:0, one launch (start us, length us, event | category | flops | bytes accessed | tf_op | source)
XLA Modules:
  0.0 159.5 jit_solution(6599443911277645240)
XLA Ops:
  0.6 4.0 %collective-permute-start = (bf16[64,1536]{1,0:T(8,128)(2,1)}, bf16[64,1536]{1,0:T(8,128)(2,1)S(1)}, u32[]{:S(2)}, u32[]{:S(2)}) collective-permute-start(bf16[64,1536]{1,0:T(8,128)(2,1)} %param.4), channel_id=1, source_target_pairs={{0,16},{16,0},{32,48},{48,32},{64,80},{80,64},{96,112},{112,96},{1... | collective-permute-start | bytes 589832 | tf_op jit(solution)/shard_map/ppermute | solution.py:21
  4.7 0.7 stack.98.at
  5.3 3.7 %shard_map.50 = (f32[256,1536]{1,0:T(8,128)}, bf16[192,256]{1,0:T(8,128)(2,1)}, bf16[192,256]{1,0:T(8,128)(2,1)}, bf16[192,256]{1,0:T(8,128)(2,1)}, bf16[192,256...) custom-call(s32[5]{0:T(128)} %stack.98.at, ...), custom_call_target="tpu_custom_call" | custom-call | flops 201326592 | bytes 3145728 | tf_op jit(solution)/shard_map/pallas_call | solution.py:204
  9.1 1.0 slice_bitcast_fusion.2
  10.1 3.3 %collective-permute-start.2 = (bf16[2,32,1536]{2,1,0:T(8,128)(2,1)S(1)}, bf16[2,32,1536]{2,1,0:T(8,128)(2,1)S(1)}, u32[]{:S(2)}, u32[]{:S(2)}) collective-permute-start(bf16[2,32,1536]{2,1,0:T(8,128)(2,1)S(1)} %get-tuple-element.47), channel_id=1, source_target_pairs={{0,8},{4,12},{8,0},{12,4},{1,9},{5,13},{9,1},{13,5},{2,10},{6,14},... | collective-permute-start | bytes 589832 | tf_op jit(solution)/shard_map/ppermute | solution.py:21
  13.4 0.7 collective-permute-start.1
  14.1 2.6 %collective-permute-start.3 = (bf16[2,32,1536]{2,1,0:T(8,128)(2,1)S(1)}, bf16[2,32,1536]{2,1,0:T(8,128)(2,1)S(1)}, u32[]{:S(2)}, u32[]{:S(2)}) collective-permute-start(bf16[2,32,1536]{2,1,0:T(8,128)(2,1)S(1)} %get-tuple-element.47), channel_id=1, source_target_pairs={{0,12},{4,0},{8,4},{12,8},{1,13},{5,1},{9,5},{13,9},{2,14},{6,2},{... | collective-permute-start | bytes 589832 | tf_op jit(solution)/shard_map/ppermute | solution.py:21
  16.7 3.1 %collective-permute-start.9 = (bf16[2,32,1536]{2,1,0:T(8,128)(2,1)S(1)}, bf16[2,32,1536]{2,1,0:T(8,128)(2,1)S(1)}, u32[]{:S(2)}, u32[]{:S(2)}) collective-permute-start(bf16[2,32,1536]{2,1,0:T(8,128)(2,1)S(1)} %get-tuple-element.41), channel_id=1, source_target_pairs={{0,64},{16,80},{32,96},{48,112},{64,0},{80,16},{96,32},{112,48},{1... | collective-permute-start | bytes 589832 | tf_op jit(solution)/shard_map/ppermute | solution.py:21
  19.8 1.3 collective-permute-start.8
  21.0 1.3 collective-permute-done.1
  22.3 2.8 %collective-permute-start.10 = (bf16[2,32,1536]{2,1,0:T(8,128)(2,1)S(1)}, bf16[2,32,1536]{2,1,0:T(8,128)(2,1)S(1)}, u32[]{:S(2)}, u32[]{:S(2)}) collective-permute-start(bf16[2,32,1536]{2,1,0:T(8,128)(2,1)S(1)} %get-tuple-element.41), channel_id=1, source_target_pairs={{0,96},{16,112},{32,0},{48,16},{64,32},{80,48},{96,64},{112,80},{1... | collective-permute-start | bytes 589832 | tf_op jit(solution)/shard_map/ppermute | solution.py:21
  25.1 0.1 pad_maximum_fusion
  25.2 0.9 collective-permute-start.5
  26.1 1.2 collective-permute-start.4
  27.3 1.0 collective-permute-done.8
  28.3 2.1 %collective-permute-done.10 = bf16[2,32,1536]{2,1,0:T(8,128)(2,1)S(1)} collective-permute-done((bf16[2,32,1536]{2,1,0:T(8,128)(2,1)S(1)}, bf16[2,32,1536]{2,1,0:T(8,128)(2,1)S(1)}, u32[]{:S(2)}, u32[]{:S(2)}) %collective-permute-start.10) | collective-permute-done | bytes 196640 | tf_op jit(solution)/shard_map/ppermute | solution.py:21
  30.4 0.1 pad_maximum_fusion.1.refs_5_.refs_9_
  30.5 1.4 collective-permute-start.12
  31.9 0.7 collective-permute-start.11
  32.6 1.3 collective-permute-start.23
  33.9 13.6 %collective-permute-done.23 = bf16[192,256]{1,0:T(8,128)(2,1)S(1)} collective-permute-done((bf16[192,256]{1,0:T(8,128)(2,1)S(1)}, bf16[192,256]{1,0:T(8,128)(2,1)S(1)}, u32[]{:S(2)}, u32[]{:S(2)}) %collective-permute-start.23) | collective-permute-done | bytes 98336 | tf_op jit(solution)/shard_map/ppermute | solution.py:21
  47.6 3.6 %collective-permute-start.24 = (bf16[192,256]{1,0:T(8,128)(2,1)S(1)}, bf16[192,256]{1,0:T(8,128)(2,1)S(1)}, u32[]{:S(2)}, u32[]{:S(2)}) collective-permute-start(bf16[192,256]{1,0:T(8,128)(2,1)S(1)} %copy-done.23), channel_id=1, source_target_pairs={{0,48},{16,32},{32,80},{48,64},{64,112},{80,96},{96,16},{112,0},{1... | collective-permute-start | bytes 294920 | tf_op jit(solution)/shard_map/ppermute | solution.py:21
  51.2 4.6 %collective-permute-done.24 = bf16[192,256]{1,0:T(8,128)(2,1)S(1)} collective-permute-done((bf16[192,256]{1,0:T(8,128)(2,1)S(1)}, bf16[192,256]{1,0:T(8,128)(2,1)S(1)}, u32[]{:S(2)}, u32[]{:S(2)}) %collective-permute-start.24) | collective-permute-done | bytes 98336 | tf_op jit(solution)/shard_map/ppermute | solution.py:21
  55.8 1.0 collective-permute-start.25
  56.8 5.2 %collective-permute-start.26 = (bf16[192,256]{1,0:T(8,128)(2,1)S(1)}, bf16[192,256]{1,0:T(8,128)(2,1)S(1)}, u32[]{:S(2)}, u32[]{:S(2)}) collective-permute-start(bf16[192,256]{1,0:T(8,128)(2,1)S(1)} %copy-done.21), channel_id=1, source_target_pairs={{0,80},{16,64},{32,112},{48,96},{64,16},{80,0},{96,48},{112,32},{1... | collective-permute-start | bytes 294920 | tf_op jit(solution)/shard_map/ppermute | solution.py:21
  62.0 0.1 collective-permute-start.7
  62.1 2.1 %collective-permute-start.6 = (bf16[1,4,32,1536]{3,2,0,1:T(8,128)(2,1)S(1)}, bf16[1,4,32,1536]{3,2,0,1:T(8,128)(2,1)S(1)}, u32[]{:S(2)}, u32[]{:S(2)}) collective-permute-start(bf16[1,4,32,1536]{3,2,0,1:T(8,128)(2,1)S(1)} %slice.33), channel_id=1, source_target_pairs={{0,32},{16,48},{32,64},{48,80},{64,96},{80,112},{96,0},{112,16},{1... | collective-permute-start | bytes 1179656 | tf_op jit(solution)/shard_map/ppermute | solution.py:21
  64.3 2.4 %collective-permute-start.14 = (bf16[2,2,32,1536]{3,2,1,0:T(8,128)(2,1)S(1)}, bf16[2,2,32,1536]{3,2,1,0:T(8,128)(2,1)S(1)}, u32[]{:S(2)}, u32[]{:S(2)}) collective-permute-start(bf16[2,2,32,1536]{3,2,1,0:T(8,128)(2,1)S(1)} %slice.37), channel_id=1, source_target_pairs={{0,12},{4,0},{8,4},{12,8},{1,13},{5,1},{9,5},{13,9},{2,14},{6,2},{... | collective-permute-start | bytes 1179656 | tf_op jit(solution)/shard_map/ppermute | solution.py:21
  66.7 0.1 collective-permute-start.13
  66.8 0.9 collective-permute-done.26
  67.7 0.4 collective-permute-start.27
  68.1 0.9 copy.5
  69.0 0.9 copy.7
  70.0 1.0 copy.6
  70.9 0.6 collective-permute-done.7
  71.5 3.6 %collective-permute-start.28 = (bf16[192,256]{1,0:T(8,128)(2,1)S(1)}, bf16[192,256]{1,0:T(8,128)(2,1)S(1)}, u32[]{:S(2)}, u32[]{:S(2)}) collective-permute-start(bf16[192,256]{1,0:T(8,128)(2,1)S(1)} %copy-done.19), channel_id=1, source_target_pairs={{0,112},{16,96},{32,16},{48,0},{64,48},{80,32},{96,80},{112,64},{1... | collective-permute-start | bytes 294920 | tf_op jit(solution)/shard_map/ppermute | solution.py:21
  75.1 0.6 collective-permute-done.13.refs_8_.refs_12_
  75.7 0.1 copy-done.16
  75.8 0.1 copy-done.17
  76.0 0.5 copy-done.18
  76.5 12.7 %shard_map.51 = (bf16[2,2,4,192,256]{4,3,2,1,0:T(8,128)(2,1)}, bf16[2,2,4,192,256]{4,3,2,1,0:T(8,128)(2,1)}) custom-call(s32[5]{0:T(128)} %stack.98.at, bf16[768,1536]{1,0:T(8,128)(2,1)} %bitcast.58, bf16[2,128,1536]{2,1,0:T(8,128)(2,1)} %bitcast.46, bf16[2,128,1536]{2,1,0:T(8,128)(2,1)} %bitcast.50, bf16[2,128,1536]{2,1,0:T(8,128)(2,1)} %bitcast.48, ...), custom_call_target="tpu_custom_call" | custom-call | flops 4831838208 | bytes 9830400 | tf_op jit(solution)/shard_map/pallas_call | solution.py:224
  89.2 0.1 collective-permute-start.15
  89.4 1.1 collective-permute-start.29
  90.5 0.2 collective-permute-start.30
  90.7 18.7 %collective-permute-done.29.refs_1_ = bf16[8,192,256]{2,1,0:T(8,128)(2,1)S(1)} collective-permute-done((bf16[8,192,256]{2,1,0:T(8,128)(2,1)S(1)}, bf16[8,192,256]{2,1,0:T(8,128)(2,1)S(1)}, u32[]{:S(2)}, u32[]{:S(2)}) %collective-permute-start.29) | collective-permute-done | bytes 786464 | tf_op jit(solution)/shard_map/ppermute | solution.py:21
  109.4 1.2 copy-done
  110.6 3.1 %shard_map.52 = (bf16[4,192,256]{2,1,0:T(8,128)(2,1)}, bf16[4,192,256]{2,1,0:T(8,128)(2,1)}, bf16[4,192,256]{2,1,0:T(8,128)(2,1)}, bf16[4,192,256]{2,1,0:T(8,128)(2,1)}) custom-call(bf16[2,2,4,192,256]{4,3,2,1,0:T(8,128)(2,1)} %get-tuple-element.22.mine, bf16[2,2,4,192,256]{4,3,2,1,0:T(8,128)(2,1)} %copy-done), custom_call_target="tpu_custom_call" | custom-call | flops 1572864 | bytes 4718592 | tf_op jit(solution)/shard_map/pallas_call | solution.py:233
  113.7 1.2 collective-permute-start.16
  114.9 1.0 collective-permute-start.17
  115.9 1.9 %collective-permute-start.18 = (bf16[4,192,256]{2,1,0:T(8,128)(2,1)}, bf16[4,192,256]{2,1,0:T(8,128)(2,1)S(1)}, u32[]{:S(2)}, u32[]{:S(2)}) collective-permute-start(bf16[4,192,256]{2,1,0:T(8,128)(2,1)} %get-tuple-element.27), channel_id=1, source_target_pairs={{0,18},{1,19},{2,16},{3,17},{16,2},{17,3},{18,0},{19,1},{32,50},{3... | collective-permute-start | bytes 1179656 | tf_op jit(solution)/shard_map/ppermute | solution.py:21
  117.8 9.6 %collective-permute-done.16.r01 = bf16[4,192,256]{2,1,0:T(8,128)(2,1)S(1)} collective-permute-done((bf16[4,192,256]{2,1,0:T(8,128)(2,1)}, bf16[4,192,256]{2,1,0:T(8,128)(2,1)S(1)}, u32[]{:S(2)}, u32[]{:S(2)}) %collective-permute-start.16) | collective-permute-done | bytes 393248 | tf_op jit(solution)/shard_map/ppermute | solution.py:21
  127.4 6.7 %collective-permute-done.17.r10 = bf16[4,192,256]{2,1,0:T(8,128)(2,1)S(1)} collective-permute-done((bf16[4,192,256]{2,1,0:T(8,128)(2,1)}, bf16[4,192,256]{2,1,0:T(8,128)(2,1)S(1)}, u32[]{:S(2)}, u32[]{:S(2)}) %collective-permute-start.17) | collective-permute-done | bytes 393248 | tf_op jit(solution)/shard_map/ppermute | solution.py:21
  134.1 1.3 collective-permute-done.18.r11
  135.4 0.8 copy-done.4
  136.1 2.3 %shard_map.53 = (bf16[2,192,256]{2,1,0:T(8,128)(2,1)}, bf16[2,192,256]{2,1,0:T(8,128)(2,1)}, bf16[2,192,256]{2,1,0:T(8,128)(2,1)}, bf16[2,192,256]{2,1,0:T(8,128)(2,1)}) custom-call(bf16[4,192,256]{2,1,0:T(8,128)(2,1)} %get-tuple-element.24.r00, bf16[4,192,256]{2,1,0:T(8,128)(2,1)} %copy-done.2, bf16[4,192,256]{2,1,0:T(8,128)(2,1)} %copy-done.3, ...), custom_call_target="tpu_custom_call" | custom-call | flops 786432 | bytes 2359296 | tf_op jit(solution)/shard_map/pallas_call | solution.py:238
  138.5 2.6 %collective-permute-start.20 = (bf16[2,192,256]{2,1,0:T(8,128)(2,1)}, bf16[2,192,256]{2,1,0:T(8,128)(2,1)S(1)}, u32[]{:S(2)}, u32[]{:S(2)}) collective-permute-start(bf16[2,192,256]{2,1,0:T(8,128)(2,1)} %get-tuple-element.30), channel_id=1, source_target_pairs={{0,64},{16,80},{32,96},{48,112},{64,0},{80,16},{96,32},{112,48},{1... | collective-permute-start | bytes 589832 | tf_op jit(solution)/shard_map/ppermute | solution.py:21
  141.1 0.5 collective-permute-start.21
  141.7 0.9 copy-done.13
  142.5 0.9 copy-done.14
  143.4 12.2 %shard_map.55 = bf16[768,1536]{1,0:T(8,128)(2,1)} custom-call(s32[5]{0:T(128)} %stack.98.at, bf16[8,192,256]{2,1,0:T(8,128)(2,1)} %copy-done.11, bf16[8,192,256]{2,1,0:T(8,128)(2,1)} %copy-done.12, bf16[8,192,256]{2,1,0:T(8,128)(2,1)} %copy-done.13, bf16[8,192,256]{2,1,0:T(8,128)(2,1)} %copy-done.14, bf16[2,128,1536]{2,1,0:T(8,128)(2,1)} %bitcast.47, ...), custom_call_target="tpu_custom_call" | custom-call | flops 4831838208 | bytes 11010048 | tf_op jit(solution)/shard_map/pallas_call | solution.py:248
  155.7 0.6 copy-done.7
  156.3 0.1 copy-done.8
  156.4 0.1 copy-done.9
  156.5 3.0 %shard_map.54 = bf16[256,1536]{1,0:T(8,128)(2,1)} custom-call(s32[5]{0:T(128)} %stack.98.at, f32[256,1536]{1,0:T(8,128)} %get-tuple-element.21.slope, bf16[2,192,256]{2,1,0:T(8,128)(2,1)} %get-tuple-element.28.p0, bf16[2,192,256]{2,1,0:T(8,128)(2,1)} %copy-done.7, bf16[2,192,256]{2,1,0:T(8,128)(2,1)} %copy-done.8, bf16[2,192,256]{2,1,0:T(8,128)(2,1)} %copy-done.9), custom_call_target="tpu_custom_call" | custom-call | flops 201326592 | bytes 3145728 | tf_op jit(solution)/shard_map/pallas_call | solution.py:242
  (78 shorter events, 0.5 us)
Async XLA Ops:
  0.6 9.4 %collective-permute-start = (bf16[64,1536]{1,0:T(8,128)(2,1)}, bf16[64,1536]{1,0:T(8,128)(2,1)S(1)}, u32[]{:S(2)}, u32[]{:S(2)}) collective-permute-start(bf16[64,1536]{1,0:T(8,128)(2,1)} %param.4), channel_id=1, source_target_pairs={{0,16},{16,0},{32,48},{48,32},{64,80},{80,64},{96,112},{112,96},{1... | collective-permute-start | bytes 589832 | tf_op jit(solution)/shard_map/ppermute | solution.py:21
  9.1 23.6 %collective-permute-start.22 = (bf16[192,256]{1,0:T(8,128)(2,1)}, bf16[192,256]{1,0:T(8,128)(2,1)S(1)}, u32[]{:S(2)}, u32[]{:S(2)}) collective-permute-start(bf16[192,256]{1,0:T(8,128)(2,1)} %get-tuple-element.33), channel_id=1, source_target_pairs={{0,16},{16,0},{32,48},{48,32},{64,80},{80,64},{96,112},{112,96},{1... | collective-permute-start | bytes 294920 | tf_op jit(solution)/shard_map/ppermute | solution.py:21
  10.1 9.6 %collective-permute-start.2 = (bf16[2,32,1536]{2,1,0:T(8,128)(2,1)S(1)}, bf16[2,32,1536]{2,1,0:T(8,128)(2,1)S(1)}, u32[]{:S(2)}, u32[]{:S(2)}) collective-permute-start(bf16[2,32,1536]{2,1,0:T(8,128)(2,1)S(1)} %get-tuple-element.47), channel_id=1, source_target_pairs={{0,8},{4,12},{8,0},{12,4},{1,9},{5,13},{9,1},{13,5},{2,10},{6,14},... | collective-permute-start | bytes 589832 | tf_op jit(solution)/shard_map/ppermute | solution.py:21
  13.4 8.9 %collective-permute-start.1 = (bf16[2,32,1536]{2,1,0:T(8,128)(2,1)S(1)}, bf16[2,32,1536]{2,1,0:T(8,128)(2,1)S(1)}, u32[]{:S(2)}, u32[]{:S(2)}) collective-permute-start(bf16[2,32,1536]{2,1,0:T(8,128)(2,1)S(1)} %get-tuple-element.47), channel_id=1, source_target_pairs={{0,4},{4,8},{8,12},{12,0},{1,5},{5,9},{9,13},{13,1},{2,6},{6,10},{... | collective-permute-start | bytes 589832 | tf_op jit(solution)/shard_map/ppermute | solution.py:21
  14.1 11.0 %collective-permute-start.3 = (bf16[2,32,1536]{2,1,0:T(8,128)(2,1)S(1)}, bf16[2,32,1536]{2,1,0:T(8,128)(2,1)S(1)}, u32[]{:S(2)}, u32[]{:S(2)}) collective-permute-start(bf16[2,32,1536]{2,1,0:T(8,128)(2,1)S(1)} %get-tuple-element.47), channel_id=1, source_target_pairs={{0,12},{4,0},{8,4},{12,8},{1,13},{5,1},{9,5},{13,9},{2,14},{6,2},{... | collective-permute-start | bytes 589832 | tf_op jit(solution)/shard_map/ppermute | solution.py:21
  16.7 9.4 %collective-permute-start.9 = (bf16[2,32,1536]{2,1,0:T(8,128)(2,1)S(1)}, bf16[2,32,1536]{2,1,0:T(8,128)(2,1)S(1)}, u32[]{:S(2)}, u32[]{:S(2)}) collective-permute-start(bf16[2,32,1536]{2,1,0:T(8,128)(2,1)S(1)} %get-tuple-element.41), channel_id=1, source_target_pairs={{0,64},{16,80},{32,96},{48,112},{64,0},{80,16},{96,32},{112,48},{1... | collective-permute-start | bytes 589832 | tf_op jit(solution)/shard_map/ppermute | solution.py:21
  19.8 8.5 %collective-permute-start.8 = (bf16[2,32,1536]{2,1,0:T(8,128)(2,1)S(1)}, bf16[2,32,1536]{2,1,0:T(8,128)(2,1)S(1)}, u32[]{:S(2)}, u32[]{:S(2)}) collective-permute-start(bf16[2,32,1536]{2,1,0:T(8,128)(2,1)S(1)} %get-tuple-element.41), channel_id=1, source_target_pairs={{0,32},{16,48},{32,64},{48,80},{64,96},{80,112},{96,0},{112,16},{1... | collective-permute-start | bytes 589832 | tf_op jit(solution)/shard_map/ppermute | solution.py:21
  22.3 8.1 %collective-permute-start.10 = (bf16[2,32,1536]{2,1,0:T(8,128)(2,1)S(1)}, bf16[2,32,1536]{2,1,0:T(8,128)(2,1)S(1)}, u32[]{:S(2)}, u32[]{:S(2)}) collective-permute-start(bf16[2,32,1536]{2,1,0:T(8,128)(2,1)S(1)} %get-tuple-element.41), channel_id=1, source_target_pairs={{0,96},{16,112},{32,0},{48,16},{64,32},{80,48},{96,64},{112,80},{1... | collective-permute-start | bytes 589832 | tf_op jit(solution)/shard_map/ppermute | solution.py:21
  25.1 7.6 %copy-start.10 = (bf16[192,256]{1,0:T(8,128)(2,1)S(1)}, bf16[192,256]{1,0:T(8,128)(2,1)}, u32[]{:S(2)}) copy-start(bf16[192,256]{1,0:T(8,128)(2,1)} %get-tuple-element.32) | copy-start | bytes 294916
  25.1 7.6 %copy-start.24 = (bf16[192,256]{1,0:T(8,128)(2,1)S(1)}, bf16[192,256]{1,0:T(8,128)(2,1)}, u32[]{:S(2)}) copy-start(bf16[192,256]{1,0:T(8,128)(2,1)} %get-tuple-element.34) | copy-start | bytes 294916
  25.1 22.5 %copy-start.23 = (bf16[192,256]{1,0:T(8,128)(2,1)S(1)}, bf16[192,256]{1,0:T(8,128)(2,1)}, u32[]{:S(2)}) copy-start(bf16[192,256]{1,0:T(8,128)(2,1)} %get-tuple-element.35) | copy-start | bytes 294916
  25.1 30.7 %copy-start.22 = (bf16[192,256]{1,0:T(8,128)(2,1)S(1)}, bf16[192,256]{1,0:T(8,128)(2,1)}, u32[]{:S(2)}) copy-start(bf16[192,256]{1,0:T(8,128)(2,1)} %get-tuple-element.36) | copy-start | bytes 294916
  25.2 31.6 %copy-start.21 = (bf16[192,256]{1,0:T(8,128)(2,1)S(1)}, bf16[192,256]{1,0:T(8,128)(2,1)}, u32[]{:S(2)}) copy-start(bf16[192,256]{1,0:T(8,128)(2,1)} %get-tuple-element.37) | copy-start | bytes 294916
  25.2 31.6 %collective-permute-start.5 = (bf16[2,4,32,1536]{3,2,0,1:T(8,128)(2,1)S(1)}, bf16[2,4,32,1536]{3,2,0,1:T(8,128)(2,1)S(1)}, u32[]{:S(2)}, u32[]{:S(2)}) collective-permute-start(bf16[2,4,32,1536]{3,2,0,1:T(8,128)(2,1)S(1)} %pad_maximum_fusion), channel_id=1, source_target_pairs={{0,96},{16,112},{32,0},{48,16},{64,32},{80,48},{96,64},{112,80},{1... | collective-permute-start | bytes 2359304 | tf_op jit(solution)/shard_map/ppermute | solution.py:21
  26.1 35.9 %collective-permute-start.4 = (bf16[2,4,32,1536]{3,2,0,1:T(8,128)(2,1)S(1)}, bf16[2,4,32,1536]{3,2,0,1:T(8,128)(2,1)S(1)}, u32[]{:S(2)}, u32[]{:S(2)}) collective-permute-start(bf16[2,4,32,1536]{3,2,0,1:T(8,128)(2,1)S(1)} %pad_maximum_fusion), channel_id=1, source_target_pairs={{0,32},{16,48},{32,64},{48,80},{64,96},{80,112},{96,0},{112,16},{1... | collective-permute-start | bytes 2359304 | tf_op jit(solution)/shard_map/ppermute | solution.py:21
  30.5 33.7 %copy-start.1 = (bf16[4,2,32,1536]{3,2,1,0:T(8,128)(2,1)}, bf16[4,2,32,1536]{3,2,1,0:T(8,128)(2,1)S(1)}, u32[]{:S(2)}) copy-start(bf16[4,2,32,1536]{3,2,1,0:T(8,128)(2,1)S(1)} %pad_maximum_fusion.1.refs_5_.refs_9_) | copy-start | bytes 2359300
  30.5 31.6 %collective-permute-start.12 = (bf16[4,2,32,1536]{3,2,1,0:T(8,128)(2,1)S(1)}, bf16[4,2,32,1536]{3,2,1,0:T(8,128)(2,1)S(1)}, u32[]{:S(2)}, u32[]{:S(2)}) collective-permute-start(bf16[4,2,32,1536]{3,2,1,0:T(8,128)(2,1)S(1)} %pad_maximum_fusion.1.refs_5_.refs_9_), channel_id=1, source_target_pairs={{0,12},{4,0},{8,4},{12,8},{1,13},{5,1},{9,5},{13,9},{2,14},{6,2},{... | collective-permute-start | bytes 2359304 | tf_op jit(solution)/shard_map/ppermute | solution.py:21
  31.9 32.3 %collective-permute-start.11 = (bf16[4,2,32,1536]{3,2,1,0:T(8,128)(2,1)S(1)}, bf16[4,2,32,1536]{3,2,1,0:T(8,128)(2,1)S(1)}, u32[]{:S(2)}, u32[]{:S(2)}) collective-permute-start(bf16[4,2,32,1536]{3,2,1,0:T(8,128)(2,1)S(1)} %pad_maximum_fusion.1.refs_5_.refs_9_), channel_id=1, source_target_pairs={{0,4},{4,8},{8,12},{12,0},{1,5},{5,9},{9,13},{13,1},{2,6},{6,10},{... | collective-permute-start | bytes 2359304 | tf_op jit(solution)/shard_map/ppermute | solution.py:21
  32.6 14.9 %collective-permute-start.23 = (bf16[192,256]{1,0:T(8,128)(2,1)S(1)}, bf16[192,256]{1,0:T(8,128)(2,1)S(1)}, u32[]{:S(2)}, u32[]{:S(2)}) collective-permute-start(bf16[192,256]{1,0:T(8,128)(2,1)S(1)} %copy-done.24), channel_id=1, source_target_pairs={{0,32},{16,48},{32,64},{48,80},{64,96},{80,112},{96,0},{112,16},{1... | collective-permute-start | bytes 294920 | tf_op jit(solution)/shard_map/ppermute | solution.py:21
  47.6 8.2 %collective-permute-start.24 = (bf16[192,256]{1,0:T(8,128)(2,1)S(1)}, bf16[192,256]{1,0:T(8,128)(2,1)S(1)}, u32[]{:S(2)}, u32[]{:S(2)}) collective-permute-start(bf16[192,256]{1,0:T(8,128)(2,1)S(1)} %copy-done.23), channel_id=1, source_target_pairs={{0,48},{16,32},{32,80},{48,64},{64,112},{80,96},{96,16},{112,0},{1... | collective-permute-start | bytes 294920 | tf_op jit(solution)/shard_map/ppermute | solution.py:21
  55.8 10.9 %collective-permute-start.25 = (bf16[192,256]{1,0:T(8,128)(2,1)S(1)}, bf16[192,256]{1,0:T(8,128)(2,1)S(1)}, u32[]{:S(2)}, u32[]{:S(2)}) collective-permute-start(bf16[192,256]{1,0:T(8,128)(2,1)S(1)} %copy-done.22), channel_id=1, source_target_pairs={{0,64},{16,80},{32,96},{48,112},{64,0},{80,16},{96,32},{112,48},{1... | collective-permute-start | bytes 294920 | tf_op jit(solution)/shard_map/ppermute | solution.py:21
  56.8 10.9 %copy-start.20 = (bf16[192,256]{1,0:T(8,128)(2,1)S(1)}, bf16[192,256]{1,0:T(8,128)(2,1)}, u32[]{:S(2)}) copy-start(bf16[192,256]{1,0:T(8,128)(2,1)} %get-tuple-element.38) | copy-start | bytes 294916
  56.8 10.9 %collective-permute-start.26 = (bf16[192,256]{1,0:T(8,128)(2,1)S(1)}, bf16[192,256]{1,0:T(8,128)(2,1)S(1)}, u32[]{:S(2)}, u32[]{:S(2)}) collective-permute-start(bf16[192,256]{1,0:T(8,128)(2,1)S(1)} %copy-done.21), channel_id=1, source_target_pairs={{0,80},{16,64},{32,112},{48,96},{64,16},{80,0},{96,48},{112,32},{1... | collective-permute-start | bytes 294920 | tf_op jit(solution)/shard_map/ppermute | solution.py:21
  62.0 9.5 %collective-permute-start.7 = (bf16[1,4,32,1536]{3,2,0,1:T(8,128)(2,1)S(1)}, bf16[1,4,32,1536]{3,2,0,1:T(8,128)(2,1)S(1)}, u32[]{:S(2)}, u32[]{:S(2)}) collective-permute-start(bf16[1,4,32,1536]{3,2,0,1:T(8,128)(2,1)S(1)} %slice.34), channel_id=1, source_target_pairs={{0,96},{16,112},{32,0},{48,16},{64,32},{80,48},{96,64},{112,80},{1... | collective-permute-start | bytes 1179656 | tf_op jit(solution)/shard_map/ppermute | solution.py:21
  62.1 6.9 %copy-start.5 = (bf16[4,2,32,1536]{3,2,1,0:T(8,128)(2,1)}, bf16[4,2,32,1536]{3,2,1,0:T(8,128)(2,1)S(1)}, u32[]{:S(2)}) copy-start(bf16[4,2,32,1536]{3,2,1,0:T(8,128)(2,1)S(1)} %collective-permute-done.12.refs_7_.refs_11_) | copy-start | bytes 2359300
  62.1 12.9 %collective-permute-start.6 = (bf16[1,4,32,1536]{3,2,0,1:T(8,128)(2,1)S(1)}, bf16[1,4,32,1536]{3,2,0,1:T(8,128)(2,1)S(1)}, u32[]{:S(2)}, u32[]{:S(2)}) collective-permute-start(bf16[1,4,32,1536]{3,2,0,1:T(8,128)(2,1)S(1)} %slice.33), channel_id=1, source_target_pairs={{0,32},{16,48},{32,64},{48,80},{64,96},{80,112},{96,0},{112,16},{1... | collective-permute-start | bytes 1179656 | tf_op jit(solution)/shard_map/ppermute | solution.py:21
  64.3 5.7 %copy-start.6 = (bf16[4,2,32,1536]{3,2,1,0:T(8,128)(2,1)}, bf16[4,2,32,1536]{3,2,1,0:T(8,128)(2,1)S(1)}, u32[]{:S(2)}) copy-start(bf16[4,2,32,1536]{3,2,1,0:T(8,128)(2,1)S(1)} %collective-permute-done.11.refs_6_.refs_10_) | copy-start | bytes 2359300
  64.3 10.8 %collective-permute-start.14 = (bf16[2,2,32,1536]{3,2,1,0:T(8,128)(2,1)S(1)}, bf16[2,2,32,1536]{3,2,1,0:T(8,128)(2,1)S(1)}, u32[]{:S(2)}, u32[]{:S(2)}) collective-permute-start(bf16[2,2,32,1536]{3,2,1,0:T(8,128)(2,1)S(1)} %slice.37), channel_id=1, source_target_pairs={{0,12},{4,0},{8,4},{12,8},{1,13},{5,1},{9,5},{13,9},{2,14},{6,2},{... | collective-permute-start | bytes 1179656 | tf_op jit(solution)/shard_map/ppermute | solution.py:21
  66.7 9.1 %collective-permute-start.13 = (bf16[2,2,32,1536]{3,2,1,0:T(8,128)(2,1)S(1)}, bf16[2,2,32,1536]{3,2,1,0:T(8,128)(2,1)S(1)}, u32[]{:S(2)}, u32[]{:S(2)}) collective-permute-start(bf16[2,2,32,1536]{3,2,1,0:T(8,128)(2,1)S(1)} %slice.36), channel_id=1, source_target_pairs={{0,4},{4,8},{8,12},{12,0},{1,5},{5,9},{9,13},{13,1},{2,6},{6,10},{... | collective-permute-start | bytes 1179656 | tf_op jit(solution)/shard_map/ppermute | solution.py:21
  67.7 21.7 %collective-permute-start.27 = (bf16[192,256]{1,0:T(8,128)(2,1)S(1)}, bf16[192,256]{1,0:T(8,128)(2,1)S(1)}, u32[]{:S(2)}, u32[]{:S(2)}) collective-permute-start(bf16[192,256]{1,0:T(8,128)(2,1)S(1)} %copy-done.20), channel_id=1, source_target_pairs={{0,96},{16,112},{32,0},{48,16},{64,32},{80,48},{96,64},{112,80},{1... | collective-permute-start | bytes 294920 | tf_op jit(solution)/shard_map/ppermute | solution.py:21
  69.0 2.5 %copy-start.19 = (bf16[192,256]{1,0:T(8,128)(2,1)S(1)}, bf16[192,256]{1,0:T(8,128)(2,1)}, u32[]{:S(2)}) copy-start(bf16[192,256]{1,0:T(8,128)(2,1)} %get-tuple-element.39) | copy-start | bytes 294916
  71.5 4.2 %copy-start.15 = (bf16[1,4,32,1536]{3,2,0,1:T(8,128)(2,1)}, bf16[1,4,32,1536]{3,2,0,1:T(8,128)(2,1)S(1)}, u32[]{:S(2)}) copy-start(bf16[1,4,32,1536]{3,2,0,1:T(8,128)(2,1)S(1)} %collective-permute-done.7) | copy-start | bytes 1179652
  71.5 17.8 %collective-permute-start.28 = (bf16[192,256]{1,0:T(8,128)(2,1)S(1)}, bf16[192,256]{1,0:T(8,128)(2,1)S(1)}, u32[]{:S(2)}, u32[]{:S(2)}) collective-permute-start(bf16[192,256]{1,0:T(8,128)(2,1)S(1)} %copy-done.19), channel_id=1, source_target_pairs={{0,112},{16,96},{32,16},{48,0},{64,48},{80,32},{96,80},{112,64},{1... | collective-permute-start | bytes 294920 | tf_op jit(solution)/shard_map/ppermute | solution.py:21
  75.1 0.7 copy-start.16
  75.1 0.9 copy-start.17
  75.7 0.8 copy-start.18
  89.2 20.2 %collective-permute-start.15 = (bf16[2,2,4,192,256]{4,3,2,1,0:T(8,128)(2,1)}, bf16[2,2,4,192,256]{4,3,2,1,0:T(8,128)(2,1)S(1)}, u32[]{:S(2)}, u32[]{:S(2)}) collective-permute-start(bf16[2,2,4,192,256]{4,3,2,1,0:T(8,128)(2,1)} %get-tuple-element.23), channel_id=1, source_target_pairs={{0,1},{1,0},{2,3},{3,2},{4,5},{5,4},{6,7},{7,6},{8,9},{9,8},{10,11... | collective-permute-start | bytes 4718600 | tf_op jit(solution)/shard_map/ppermute | solution.py:21
  89.4 52.3 %copy-start.11 = (bf16[8,192,256]{2,1,0:T(8,128)(2,1)}, bf16[8,192,256]{2,1,0:T(8,128)(2,1)S(1)}, u32[]{:S(2)}) copy-start(bf16[8,192,256]{2,1,0:T(8,128)(2,1)S(1)} %bitcast_dynamic-update-slice_fusion.refs_0_) | copy-start | bytes 2359300
  89.4 20.0 %collective-permute-start.29 = (bf16[8,192,256]{2,1,0:T(8,128)(2,1)S(1)}, bf16[8,192,256]{2,1,0:T(8,128)(2,1)S(1)}, u32[]{:S(2)}, u32[]{:S(2)}) collective-permute-start(bf16[8,192,256]{2,1,0:T(8,128)(2,1)S(1)} %bitcast_dynamic-update-slice_fusion.refs_0_), channel_id=1, source_target_pairs={{0,2},{1,3},{2,0},{3,1},{4,6},{5,7},{6,4},{7,5},{8,10},{9,11},{10,... | collective-permute-start | bytes 2359304 | tf_op jit(solution)/shard_map/ppermute | solution.py:21
  90.5 51.2 %collective-permute-start.30 = (bf16[8,192,256]{2,1,0:T(8,128)(2,1)S(1)}, bf16[8,192,256]{2,1,0:T(8,128)(2,1)S(1)}, u32[]{:S(2)}, u32[]{:S(2)}) collective-permute-start(bf16[8,192,256]{2,1,0:T(8,128)(2,1)S(1)} %bitcast_dynamic-update-slice_fusion.refs_0_), channel_id=1, source_target_pairs={{0,1},{1,0},{2,3},{3,2},{4,5},{5,4},{6,7},{7,6},{8,9},{9,8},{10,11... | collective-permute-start | bytes 2359304 | tf_op jit(solution)/shard_map/ppermute | solution.py:21
  109.4 32.3 %copy-start.12 = (bf16[8,192,256]{2,1,0:T(8,128)(2,1)}, bf16[8,192,256]{2,1,0:T(8,128)(2,1)S(1)}, u32[]{:S(2)}) copy-start(bf16[8,192,256]{2,1,0:T(8,128)(2,1)S(1)} %collective-permute-done.29.refs_1_) | copy-start | bytes 2359300
  109.4 32.3 %collective-permute-start.31 = (bf16[8,192,256]{2,1,0:T(8,128)(2,1)S(1)}, bf16[8,192,256]{2,1,0:T(8,128)(2,1)S(1)}, u32[]{:S(2)}, u32[]{:S(2)}) collective-permute-start(bf16[8,192,256]{2,1,0:T(8,128)(2,1)S(1)} %collective-permute-done.29.refs_1_), channel_id=1, source_target_pairs={{0,1},{1,0},{2,3},{3,2},{4,5},{5,4},{6,7},{7,6},{8,9},{9,8},{10,11... | collective-permute-start | bytes 2359304 | tf_op jit(solution)/shard_map/ppermute | solution.py:21
  109.4 1.2 copy-start
  113.7 13.7 %collective-permute-start.16 = (bf16[4,192,256]{2,1,0:T(8,128)(2,1)}, bf16[4,192,256]{2,1,0:T(8,128)(2,1)S(1)}, u32[]{:S(2)}, u32[]{:S(2)}) collective-permute-start(bf16[4,192,256]{2,1,0:T(8,128)(2,1)} %get-tuple-element.25), channel_id=1, source_target_pairs={{0,16},{16,0},{32,48},{48,32},{64,80},{80,64},{96,112},{112,96},{1... | collective-permute-start | bytes 1179656 | tf_op jit(solution)/shard_map/ppermute | solution.py:21
  114.9 19.2 %collective-permute-start.17 = (bf16[4,192,256]{2,1,0:T(8,128)(2,1)}, bf16[4,192,256]{2,1,0:T(8,128)(2,1)S(1)}, u32[]{:S(2)}, u32[]{:S(2)}) collective-permute-start(bf16[4,192,256]{2,1,0:T(8,128)(2,1)} %get-tuple-element.26), channel_id=1, source_target_pairs={{0,2},{1,3},{2,0},{3,1},{4,6},{5,7},{6,4},{7,5},{8,10},{9,11},{10,... | collective-permute-start | bytes 1179656 | tf_op jit(solution)/shard_map/ppermute | solution.py:21
  115.9 19.4 %collective-permute-start.18 = (bf16[4,192,256]{2,1,0:T(8,128)(2,1)}, bf16[4,192,256]{2,1,0:T(8,128)(2,1)S(1)}, u32[]{:S(2)}, u32[]{:S(2)}) collective-permute-start(bf16[4,192,256]{2,1,0:T(8,128)(2,1)} %get-tuple-element.27), channel_id=1, source_target_pairs={{0,18},{1,19},{2,16},{3,17},{16,2},{17,3},{18,0},{19,1},{32,50},{3... | collective-permute-start | bytes 1179656 | tf_op jit(solution)/shard_map/ppermute | solution.py:21
  127.4 8.0 %copy-start.2 = (bf16[4,192,256]{2,1,0:T(8,128)(2,1)}, bf16[4,192,256]{2,1,0:T(8,128)(2,1)S(1)}, u32[]{:S(2)}) copy-start(bf16[4,192,256]{2,1,0:T(8,128)(2,1)S(1)} %collective-permute-done.16.r01) | copy-start | bytes 1179652
  134.1 1.3 copy-start.3
  135.4 0.8 copy-start.4
  138.4 17.2 %collective-permute-start.19 = (bf16[2,192,256]{2,1,0:T(8,128)(2,1)}, bf16[2,192,256]{2,1,0:T(8,128)(2,1)S(1)}, u32[]{:S(2)}, u32[]{:S(2)}) collective-permute-start(bf16[2,192,256]{2,1,0:T(8,128)(2,1)} %get-tuple-element.29), channel_id=1, source_target_pairs={{0,32},{16,48},{32,64},{48,80},{64,96},{80,112},{96,0},{112,16},{1... | collective-permute-start | bytes 589832 | tf_op jit(solution)/shard_map/ppermute | solution.py:21
  138.5 17.2 %collective-permute-start.20 = (bf16[2,192,256]{2,1,0:T(8,128)(2,1)}, bf16[2,192,256]{2,1,0:T(8,128)(2,1)S(1)}, u32[]{:S(2)}, u32[]{:S(2)}) collective-permute-start(bf16[2,192,256]{2,1,0:T(8,128)(2,1)} %get-tuple-element.30), channel_id=1, source_target_pairs={{0,64},{16,80},{32,96},{48,112},{64,0},{80,16},{96,32},{112,48},{1... | collective-permute-start | bytes 589832 | tf_op jit(solution)/shard_map/ppermute | solution.py:21
  141.1 14.6 %collective-permute-start.21 = (bf16[2,192,256]{2,1,0:T(8,128)(2,1)}, bf16[2,192,256]{2,1,0:T(8,128)(2,1)S(1)}, u32[]{:S(2)}, u32[]{:S(2)}) collective-permute-start(bf16[2,192,256]{2,1,0:T(8,128)(2,1)} %get-tuple-element.31), channel_id=1, source_target_pairs={{0,96},{16,112},{32,0},{48,16},{64,32},{80,48},{96,64},{112,80},{1... | collective-permute-start | bytes 589832 | tf_op jit(solution)/shard_map/ppermute | solution.py:21
  141.7 0.9 copy-start.13
  142.5 0.9 copy-start.14
  155.7 0.7 copy-start.7
  155.7 0.7 copy-start.8
  155.7 0.8 copy-start.9
where the time goes:
time: 160 us; the launch traced here: 159 us
  waiting for transfers between devices  61 us (38%)
  starting transfers between devices  50.2 us (31%)
  Pallas kernels  37 us (23%)
  local copies, waits for them, and re-layouts  9.93 us (6%)
    ppermute x32, waiting for transfers between devices, send(): return lax.ppermute(v, axis, [(i, to(i)) for i in range(count)])  61 us
    ppermute x32, starting transfers between devices, send(): return lax.ppermute(v, axis, [(i, to(i)) for i in range(count)])  50.2 us
    pallas_call x1, Pallas kernels, per_device(): call(input_body, [shape, shape], [SMEM, VMEM] + [ANY] * 10, (product, 2 *...  12.7 us
    pallas_call x1, Pallas kernels, per_device(): call(weight_body, [((4 * rows, features), bf16)], [SMEM] + [VMEM] * 4 + [...  12.2 us
    unnamed x57, local copies, waits for them, and re-layouts  5.36 us
    pallas_call x1, Pallas kernels, per_device(): call(pack_body, [((tokens, columns), f32)] + [(block, bf16)] * 8, [SMEM,...  3.72 us
  transfers between devices with their start and end apart: 32, of which 12 were waited for; matrix products, arithmetic and copies ran while one was open for 3% of the time, Pallas kernels for 21%

commit v1 on v0

v1 whole, which is shorter than its diff:
```python
import functools

import jax
import jax.numpy as jnp
from jax import lax
from jax.experimental import pallas as pl
from jax.experimental.pallas import tpu as pltpu
from jax.sharding import PartitionSpec as P

tanh_scale = 0.7978845608028654
cubic_coef = 0.044715
bf16 = jnp.bfloat16
f32 = jnp.float32
MIB = 1024 * 1024
VMEM = pl.BlockSpec(memory_space=pltpu.VMEM)
SMEM = pl.BlockSpec(memory_space=pltpu.SMEM)
ANY = pl.BlockSpec(memory_space=pl.ANY)


def send(v, axis, count, to):
    return lax.ppermute(v, axis, [(i, to(i)) for i in range(count)])


def send_x(v, d):
    return send(v, "gx", 8, lambda i: ((i // 2 + d) % 4) * 2 + i % 2)


def send_y(v, d):
    return send(v, "gy", 4, lambda i: (i + d) % 4)


def swap_z_hi(v):
    return send(v, "gx", 8, lambda i: i ^ 1)


def swap_z_lo(v):
    return send(v, "gz", 4, lambda i: i ^ 2)


def swap_core(v):
    return send(v, "gz", 4, lambda i: i ^ 1)


def send_by_core(v, d, first):
    pairs = []
    for i in range(128):
        x, z_hi, y, z_lo, core = i // 32, i // 16 % 2, i // 4 % 4, i // 2 % 2, i % 2
        if (core == 0) == first:
            y = (y + d) % 4
        else:
            x = (x + d) % 4
        pairs.append((i, (((x * 2 + z_hi) * 4 + y) * 2 + z_lo) * 2 + core))
    return lax.ppermute(v, ("gx", "gy", "gz"), pairs)


def call(body, out_shape, in_specs, cost, out_specs=None, scratch=(), limit=56):
    if out_specs is None:
        out_specs = [VMEM] * len(out_shape)
    flops, moved = cost
    return pl.pallas_call(
        body,
        out_shape=[jax.ShapeDtypeStruct(*s) for s in out_shape],
        in_specs=in_specs,
        out_specs=out_specs,
        scratch_shapes=list(scratch),
        compiler_params=pltpu.CompilerParams(vmem_limit_bytes=limit * MIB),
        cost_estimate=pl.CostEstimate(flops=flops, bytes_accessed=moved, transcendentals=0),
    )


def one_hot(at, rows):
    q = lax.broadcasted_iota(jnp.int32, (rows, 256), 0)
    u = lax.broadcasted_iota(jnp.int32, (rows, 256), 1)
    i, r = q // 32, q % 32
    s = ((at[0] - i // 2) & 3) * 2 + ((at[1] + i) & 1)
    return jnp.where(u == r * 8 + s, 1.0, 0.0).astype(bf16)


def token_rows(y, k):
    return pl.ds(pl.multiple_of(((y - k) & 3) * 64, 64), 64)


def pack_body(at, pre, *outs):
    slope, parts = outs[0], outs[1:]
    pick = one_hot(at, 256)
    for j in range(pre.shape[1] // 256):
        cols = slice(256 * j, 256 * j + 256)
        u = jnp.concatenate([pre[token_rows(at[2], k), cols] for k in range(4)], 0)
        u = u.astype(f32)
        t = jnp.tanh(tanh_scale * (u + cubic_coef * u * u * u))
        slope[:, cols] = 0.5 * (1.0 + t) + 0.5 * u * (1.0 - t * t) * tanh_scale * (
            1.0 + 3.0 * cubic_coef * u * u
        )
        hidden = (0.5 * u * (1.0 + t)).astype(bf16)
        turned = lax.dot_general(pick, hidden, (((1,), (1,)), ((), ())), preferred_element_type=f32)
        turned = turned.astype(bf16)
        for i in range(8):
            parts[i // 2][i % 2, 32 * j : 32 * j + 32, :] = turned[32 * i : 32 * i + 32, :]


def load_grads(at, pieces, held, sems):
    p0, p1, p3, p2p, p2m = pieces
    todo = [(p0, 0, 0), (p0, 0, 1), (p1, 1, 0), (p1, 1, 1), (p3, 3, 0), (p3, 3, 1), (p2p, 2, 0), (p2m, 2, 1)]

    def copies(core):
        made = []
        for n, (src, k, z) in enumerate(todo):
            src = src.at[z if src.shape[0] == 2 else 0]
            dst = held.at[k, z] if core == 0 else held.at[:, z, k]
            made.append(pltpu.make_async_copy(src, dst, sems.at[n]))
        return made

    for core in range(2):

        @pl.when(at[4] == core)
        def _():
            for c in copies(core):
                c.start()
            for c in copies(core):
                c.wait()


def input_body(at, w, *refs):
    pieces, (mine, theirs, held, sems) = refs[:5], refs[5:]
    load_grads(at, pieces, held, sems)
    rows = w.shape[0] // 4
    ws = []
    for core, out in ((0, mine), (1, theirs)):
        for lo in range(2):
            block = ((at[3] + lo) & 1) * 2 + ((at[4] + core) & 1)
            ws.append(w[pl.ds(pl.multiple_of(block * rows, 64), rows), :])
    turned = jnp.concatenate(ws, 0)

    @pl.loop(0, 8)
    def _(d):
        k, z = d // 2, d % 2
        part = lax.dot_general(
            turned, held[k, z].reshape(256, -1), (((1,), (1,)), ((), ())), preferred_element_type=f32
        ).astype(bf16)
        for lo in range(2):
            mine[lo, z, k] = part[lo * rows : lo * rows + rows]
            theirs[lo, z, k] = part[(lo + 2) * rows : (lo + 3) * rows]


def core_sum_body(mine, other, *outs):
    for lo in range(2):
        for z in range(2):
            for k in range(4):
                total = mine[lo, z, k].astype(f32) + other[lo, z, k].astype(f32)
                outs[lo * 2 + z][k] = total.astype(bf16)


def z_sum_body(r00, r01, r10, r11, *outs):
    for k in range(4):
        outs[k][0] = (r00[k].astype(f32) + r10[k].astype(f32)).astype(bf16)
        outs[k][1] = (r01[k].astype(f32) + r11[k].astype(f32)).astype(bf16)


def finish_body(at, slope, p0, p1, p2, p3, out):
    pick = one_hot(at, 256)
    for j in range(out.shape[1] // 256):
        cols = slice(256 * j, 256 * j + 256)
        v = jnp.concatenate([p[z, 32 * j : 32 * j + 32, :] for p in (p0, p1, p2, p3) for z in range(2)], 0)
        total = lax.dot_general(v, pick, (((0,), (0,)), ((), ())), preferred_element_type=f32)
        result = (total * slope[:, cols]).astype(bf16)
        for k in range(4):
            out[token_rows(at[2], k), cols] = result[64 * k : 64 * k + 64, :]


def weight_body(at, *refs):
    hidden, pieces, (out, held, sems) = refs[:4], refs[4:9], refs[9:]
    load_grads(at, pieces, held, sems)
    rows = out.shape[0] // 4
    lhs = jnp.concatenate(
        [jnp.concatenate([h[z, k] for k in range(4) for z in range(2)], 1) for h in hidden], 0
    )

    @pl.loop(0, out.shape[1] // 256)
    def _(j):
        cols = pl.ds(pl.multiple_of(j * 256, 256), 256)
        grads = held[:, :, :, :, cols].reshape(2048, 256)
        total = lax.dot_general(lhs, grads, (((1,), (0,)), ((), ())), preferred_element_type=f32)
        total = total.astype(bf16)
        for n, (lo, core) in enumerate(((0, 0), (1, 0), (0, 1), (1, 1))):
            block = ((at[3] + lo) & 1) * 2 + ((at[4] + core) & 1)
            out[pl.ds(pl.multiple_of(block * rows, 64), rows), cols] = total[n * rows : n * rows + rows]


def gather_grad(grad_out, first):
    other, first = lax.optimization_barrier((swap_z_hi(grad_out), first))
    both = jnp.stack([grad_out, other])
    p0 = jnp.stack([both] + [send_by_core(both, k, True) for k in (1, 2, 3)], 1)
    p1, p3 = send_by_core(p0, 1, False), send_by_core(p0, 3, False)
    return (p0, p1, p3, send_by_core(p1[:1], 1, False), send_by_core(p3[1:], 3, False)), first


def per_device(pre_act, grad_out, weight):
    tokens, columns = pre_act.shape
    rows, features = columns // 8, grad_out.shape[1]
    gx, y, gz = lax.axis_index("gx"), lax.axis_index("gy"), lax.axis_index("gz")
    at = jnp.stack([gx // 2, gx % 2, y, gz // 2, gz % 2]).astype(jnp.int32)
    w = weight.reshape(4 * rows, features)
    block = (rows, tokens)
    grad_scratch = [pltpu.VMEM((4, 2, 4, tokens // 4, features), bf16), pltpu.SemaphoreType.DMA((8,))]
    product = 2 * 4 * rows * 8 * tokens * features

    slope, *parts = call(
        pack_body,
        [((tokens, columns), f32)] + [((2,) + block, bf16)] * 4,
        [SMEM, VMEM],
        (2 * tokens * 256 * columns, 8 * tokens * columns),
    )(at, pre_act)

    pieces, parts = gather_grad(grad_out, parts)

    by_x = [parts[0]] + [send_x(parts[4 - k], k) for k in (1, 2, 3)]
    by_x, _ = lax.optimization_barrier((by_x, pieces[0]))
    own = jnp.stack([p[0] for p in by_x])
    own = jnp.stack([own, swap_z_hi(jnp.stack([p[1] for p in by_x]))])
    own, _ = lax.optimization_barrier((own, pieces[1]))
    far = swap_z_lo(own)

    shape = ((2, 2, 4) + block, bf16)
    mine, theirs = call(
        input_body,
        [shape, shape],
        [SMEM, VMEM] + [ANY] * 5,
        (product, 2 * (6 * rows * features + 2048 * features)),
        scratch=grad_scratch,
    )(at, w, *pieces)
    other = swap_core(theirs)
    size = 2 * 4 * rows * tokens
    r00, r01, r10, r11 = call(
        core_sum_body, [((4,) + block, bf16)] * 4, [VMEM] * 2, (4 * size, 12 * size)
    )(mine, other)
    q01, q10 = swap_z_hi(r01), swap_z_lo(r10)
    q11 = send(r11, ("gx", "gz"), 32, lambda i: i ^ 6)
    own, far, _ = lax.optimization_barrier((own, far, r00))
    hidden = [own, far, swap_core(own), swap_core(far)]
    (weight_grad,) = call(
        weight_body,
        [((4 * rows, features), bf16)],
        [SMEM] + [VMEM] * 4 + [ANY] * 5,
        (product, 2 * (8 * rows * features + 2048 * features)),
        scratch=grad_scratch,
    )(at, *hidden, *pieces)
    q01, q10, q11, weight_grad = lax.optimization_barrier((q01, q10, q11, weight_grad))
    sums = call(z_sum_body, [((2,) + block, bf16)] * 4, [VMEM] * 4, (2 * size, 6 * size))(
        r00, q01, q10, q11
    )
    back = [sums[0]] + [send_x(sums[4 - k], k) for k in (1, 2, 3)]
    (pre_grad,) = call(
        finish_body,
        [((tokens, columns), bf16)],
        [SMEM] + [VMEM] * 5,
        (2 * tokens * 256 * columns, 8 * tokens * columns),
    )(at, slope, *back)
    return pre_grad, weight_grad.reshape(weight.shape)


def solution(mesh):
    placed = (P("gx", ("gy", "gz")), P(("gx", "gy"), "gz"), P("gy", "gx", "gz"))
    return jax.shard_map(
        per_device,
        mesh=mesh,
        in_specs=placed,
        out_specs=(P("gx", ("gy", "gz")), P("gy", "gx", "gz")),
        check_vma=False,
    )
```

time: 160 us -> 158 us (0.988)
  starting transfers between devices: 50.2 us -> 34.5 us
  waiting for transfers between devices: 61 us -> 76.3 us
  local copies, waits for them, and re-layouts: 9.93 us -> 7.2 us
    ppermute x32 -> x15, starting transfers between devices: 50.2 us -> 21.4 us  [send(): return lax.ppermute(v, axis, [(i, to(i)) for i in range(count)])]
    ppermute x0 -> x7, waiting for transfers between devices: none -> 25.3 us  [send_by_core(): return lax.ppermute(v, ('gx', 'gy', 'gz'), pairs)]
    ppermute x0 -> x7, starting transfers between devices: none -> 13.2 us  [send_by_core(): return lax.ppermute(v, ('gx', 'gy', 'gz'), pairs)]
    ppermute x32 -> x15, waiting for transfers between devices: 61 us -> 51 us  [send(): return lax.ppermute(v, axis, [(i, to(i)) for i in range(count)])]
    another operation x4 -> x0, local copies, waits for them, and re-layouts: 1.91 us -> none  [the longest x2 0.97 us: gather_grad(): b = jnp.stack([grad_out[half:], other[half:]])]
    ppermute x2 -> x0, local copies, waits for them, and re-layouts: 1.9 us -> none  [send(): return lax.ppermute(v, axis, [(i, to(i)) for i in range(count)])]
    unnamed x57 -> x40, local copies, waits for them, and re-layouts: 5.36 us -> 6.37 us
  transfers between devices with their start and end apart: 32 -> 22, of which waited for: 12 -> 12; matrix products, arithmetic and copies ran while one was open for 3% -> 1% of each run, Pallas kernels for 21% -> 12%
where the time goes in v1:
time: 158 us; the launch traced here: 157 us
  waiting for transfers between devices  76.3 us (48%)
  Pallas kernels  37.1 us (23%)
  starting transfers between devices  34.5 us (22%)
  local copies, waits for them, and re-layouts  7.2 us (5%)
    ppermute x15, waiting for transfers between devices, send(): return lax.ppermute(v, axis, [(i, to(i)) for i in range(count)])  51 us
    ppermute x7, waiting for transfers between devices, send_by_core(): return lax.ppermute(v, ('gx', 'gy', 'gz'), pairs)  25.3 us
    ppermute x15, starting transfers between devices, send(): return lax.ppermute(v, axis, [(i, to(i)) for i in range(count)])  21.4 us
    ppermute x7, starting transfers between devices, send_by_core(): return lax.ppermute(v, ('gx', 'gy', 'gz'), pairs)  13.2 us
    pallas_call x1, Pallas kernels, per_device(): call(input_body, [shape, shape], [SMEM, VMEM] + [ANY] * 5, (product, 2 *...  12.8 us
    pallas_call x1, Pallas kernels, per_device(): call(weight_body, [((4 * rows, features), bf16)], [SMEM] + [VMEM] * 4 + [...  12.2 us
    unnamed x40, local copies, waits for them, and re-layouts  6.37 us
    pallas_call x1, Pallas kernels, per_device(): call(pack_body, [((tokens, columns), f32)] + [((2,) + block, bf16)] * 4,...  3.72 us
  transfers between devices with their start and end apart: 22, of which 12 were waited for; matrix products, arithmetic and copies ran while one was open for 1% of the time, Pallas kernels for 12%

profile of v1, /device:TPU:0, one launch (start us, length us, event | category | flops | bytes accessed | tf_op | source)
XLA Modules:
  0.0 157.5 jit_solution(5974195096839322261)
XLA Ops:
  0.6 4.0 %collective-permute-start = (bf16[64,1536]{1,0:T(8,128)(2,1)}, bf16[64,1536]{1,0:T(8,128)(2,1)S(1)}, u32[]{:S(2)}, u32[]{:S(2)}) collective-permute-start(bf16[64,1536]{1,0:T(8,128)(2,1)} %param.4), channel_id=1, source_target_pairs={{0,16},{16,0},{32,48},{48,32},{64,80},{80,64},{96,112},{112,96},{1... | collective-permute-start | bytes 589832 | tf_op jit(solution)/shard_map/ppermute | solution.py:21
  4.7 0.7 stack.62.at
  5.3 3.7 %shard_map.50 = (f32[256,1536]{1,0:T(8,128)}, bf16[2,192,256]{2,1,0:T(8,128)(2,1)}, bf16[2,192,256]{2,1,0:T(8,128)(2,1)}, bf16[2,192,256]{2,1,0:T(8,128)(2,1)}, bf16[2,192,256]{2,1,0:T(8,128)(2,1)}) custom-call(s32[5]{0:T(128)} %stack.62.at, bf16[256,1536]{1,0:T(8,128)(2,1)} %pre.1), custom_call_target="tpu_custom_call" | custom-call | flops 201326592 | bytes 3145728 | tf_op jit(solution)/shard_map/pallas_call | solution.py:207
  9.1 0.7 collective-permute-done
  9.8 1.0 fusion
  10.8 3.3 %collective-permute-start.2 = (bf16[2,64,1536]{2,1,0:T(8,128)(2,1)S(1)}, bf16[2,64,1536]{2,1,0:T(8,128)(2,1)S(1)}, u32[]{:S(2)}, u32[]{:S(2)}) collective-permute-start(bf16[2,64,1536]{2,1,0:T(8,128)(2,1)S(1)} %get-tuple-element.65), channel_id=1, source_target_pairs={{0,8},{1,65},{2,10},{3,67},{4,12},{5,69},{6,14},{7,71},{8,0},{9,73... | collective-permute-start | bytes 1179656 | tf_op jit(solution)/shard_map/ppermute | solution.py:53
  14.0 0.7 collective-permute-start.1
  14.7 2.6 %collective-permute-start.3 = (bf16[2,64,1536]{2,1,0:T(8,128)(2,1)S(1)}, bf16[2,64,1536]{2,1,0:T(8,128)(2,1)S(1)}, u32[]{:S(2)}, u32[]{:S(2)}) collective-permute-start(bf16[2,64,1536]{2,1,0:T(8,128)(2,1)S(1)} %get-tuple-element.65), channel_id=1, source_target_pairs={{0,12},{1,97},{2,14},{3,99},{4,0},{5,101},{6,2},{7,103},{8,4},{9,1... | collective-permute-start | bytes 1179656 | tf_op jit(solution)/shard_map/ppermute | solution.py:53
  17.3 3.0 %collective-permute-done.2 = bf16[2,64,1536]{2,1,0:T(8,128)(2,1)S(1)} collective-permute-done((bf16[2,64,1536]{2,1,0:T(8,128)(2,1)S(1)}, bf16[2,64,1536]{2,1,0:T(8,128)(2,1)S(1)}, u32[]{:S(2)}, u32[]{:S(2)}) %collective-permute-start.2) | collective-permute-done | bytes 393248 | tf_op jit(solution)/shard_map/ppermute | solution.py:53
  20.2 4.1 %collective-permute-done.1 = bf16[2,64,1536]{2,1,0:T(8,128)(2,1)S(1)} collective-permute-done((bf16[2,64,1536]{2,1,0:T(8,128)(2,1)S(1)}, bf16[2,64,1536]{2,1,0:T(8,128)(2,1)S(1)}, u32[]{:S(2)}, u32[]{:S(2)}) %collective-permute-start.1) | collective-permute-done | bytes 393248 | tf_op jit(solution)/shard_map/ppermute | solution.py:53
  24.3 0.3 collective-permute-done.3
  24.7 0.2 pad_maximum_fusion.refs_0_.refs_4_
  24.9 0.0 copy-start.17
  24.9 0.0 copy-start.8
  24.9 2.8 %collective-permute-start.5 = (bf16[2,4,64,1536]{3,2,1,0:T(8,128)(2,1)S(1)}, bf16[2,4,64,1536]{3,2,1,0:T(8,128)(2,1)S(1)}, u32[]{:S(2)}, u32[]{:S(2)}) collective-permute-start(bf16[2,4,64,1536]{3,2,1,0:T(8,128)(2,1)S(1)} %pad_maximum_fusion.refs_0_.refs_4_), channel_id=1, source_target_pairs={{0,96},{1,13},{2,98},{3,15},{4,100},{5,1},{6,102},{7,3},{8,104},{9... | collective-permute-start | bytes 4718600 | tf_op jit(solution)/shard_map/ppermute | solution.py:53
  27.8 0.0 collective-permute-start.4
  27.8 17.9 %collective-permute-done.5.refs_2_.refs_6_ = bf16[2,4,64,1536]{3,2,1,0:T(8,128)(2,1)S(1)} collective-permute-done((bf16[2,4,64,1536]{3,2,1,0:T(8,128)(2,1)S(1)}, bf16[2,4,64,1536]{3,2,1,0:T(8,128)(2,1)S(1)}, u32[]{:S(2)}, u32[]{:S(2)}) %collective-permute-start.5) | collective-permute-done | bytes 1572896 | tf_op jit(solution)/shard_map/ppermute | solution.py:53
  45.7 0.1 slice.41
  45.8 3.8 %collective-permute-start.7 = (bf16[1,4,64,1536]{3,2,1,0:T(8,128)(2,1)S(1)}, bf16[1,4,64,1536]{3,2,1,0:T(8,128)(2,1)S(1)}, u32[]{:S(2)}, u32[]{:S(2)}) collective-permute-start(bf16[1,4,64,1536]{3,2,1,0:T(8,128)(2,1)S(1)} %slice.41), channel_id=1, source_target_pairs={{0,96},{1,13},{2,98},{3,15},{4,100},{5,1},{6,102},{7,3},{8,104},{9... | collective-permute-start | bytes 2359304 | tf_op jit(solution)/shard_map/ppermute | solution.py:53
  49.5 0.0 collective-permute-done.4.refs_1_.refs_5_
  49.5 0.1 slice.40
  49.6 0.1 collective-permute-start.6
  49.7 0.1 collective-permute-start.12
  49.8 4.6 %collective-permute-start.13 = (bf16[2,192,256]{2,1,0:T(8,128)(2,1)S(1)}, bf16[2,192,256]{2,1,0:T(8,128)(2,1)S(1)}, u32[]{:S(2)}, u32[]{:S(2)}) collective-permute-start(bf16[2,192,256]{2,1,0:T(8,128)(2,1)S(1)} %copy-done.18), channel_id=1, source_target_pairs={{0,64},{16,80},{32,96},{48,112},{64,0},{80,16},{96,32},{112,48},{1... | collective-permute-start | bytes 589832 | tf_op jit(solution)/shard_map/ppermute | solution.py:21
  54.4 0.3 collective-permute-start.14
  54.7 14.4 %collective-permute-done.12 = bf16[2,192,256]{2,1,0:T(8,128)(2,1)S(1)} collective-permute-done((bf16[2,192,256]{2,1,0:T(8,128)(2,1)S(1)}, bf16[2,192,256]{2,1,0:T(8,128)(2,1)S(1)}, u32[]{:S(2)}, u32[]{:S(2)}) %collective-permute-start.12) | collective-permute-done | bytes 196640 | tf_op jit(solution)/shard_map/ppermute | solution.py:21
  69.0 0.0 collective-permute-done.13
  69.1 0.0 collective-permute-done.7.refs_4_.refs_8_
  69.1 0.0 collective-permute-done.6.refs_3_.refs_7_
  69.1 0.0 copy-start.13
  69.1 0.9 copy-done.12
  70.1 0.2 copy-done.13
  70.2 12.8 %shard_map.51 = (bf16[2,2,4,192,256]{4,3,2,1,0:T(8,128)(2,1)}, bf16[2,2,4,192,256]{4,3,2,1,0:T(8,128)(2,1)}) custom-call(s32[5]{0:T(128)} %stack.62.at, bf16[768,1536]{1,0:T(8,128)(2,1)} %bitcast.29, bf16[2,4,64,1536]{3,2,1,0:T(8,128)(2,1)} %copy-done, bf16[2,4,64,1536]{3,2,1,0:T(8,128)(2,1)} %copy-done.4, bf16[2,4,64,1536]{3,2,1,0:T(8,128)(2,1)} %copy-done.3, ...), custom_call_target="tpu_custom_call" | custom-call | flops 4831838208 | bytes 9830400 | tf_op jit(solution)/shard_map/pallas_call | solution.py:224
  83.0 0.1 collective-permute-start.8
  83.2 0.1 pad_maximum_fusion.3
  83.2 3.0 %collective-permute-start.15 = (bf16[4,192,256]{2,1,0:T(8,128)(2,1)S(1)}, bf16[4,192,256]{2,1,0:T(8,128)(2,1)S(1)}, u32[]{:S(2)}, u32[]{:S(2)}) collective-permute-start(bf16[4,192,256]{2,1,0:T(8,128)(2,1)S(1)} %pad_maximum_fusion.3), channel_id=1, source_target_pairs={{0,16},{16,0},{32,48},{48,32},{64,80},{80,64},{96,112},{112,96},{1... | collective-permute-start | bytes 1179656 | tf_op jit(solution)/shard_map/ppermute | solution.py:21
  86.2 0.1 maximum_bitcast_fusion
  86.3 10.1 %collective-permute-done.15 = bf16[4,192,256]{2,1,0:T(8,128)(2,1)S(1)} collective-permute-done((bf16[4,192,256]{2,1,0:T(8,128)(2,1)S(1)}, bf16[4,192,256]{2,1,0:T(8,128)(2,1)S(1)}, u32[]{:S(2)}, u32[]{:S(2)}) %collective-permute-start.15) | collective-permute-done | bytes 393248 | tf_op jit(solution)/shard_map/ppermute | solution.py:21
  96.3 0.1 pad_maximum_fusion.1.refs_0_
  96.4 1.0 collective-permute-start.16
  97.4 0.0 collective-permute-done.8.other
  97.4 1.2 copy-done.1
  98.6 3.1 %shard_map.52 = (bf16[4,192,256]{2,1,0:T(8,128)(2,1)}, bf16[4,192,256]{2,1,0:T(8,128)(2,1)}, bf16[4,192,256]{2,1,0:T(8,128)(2,1)}, bf16[4,192,256]{2,1,0:T(8,128)(2,1)}) custom-call(bf16[2,2,4,192,256]{4,3,2,1,0:T(8,128)(2,1)} %get-tuple-element.39.mine, bf16[2,2,4,192,256]{4,3,2,1,0:T(8,128)(2,1)} %copy-done.1), custom_call_target="tpu_custom_call" | custom-call | flops 1572864 | bytes 4718592 | tf_op jit(solution)/shard_map/pallas_call | solution.py:233
  101.7 13.9 %collective-permute-done.16.refs_1_ = bf16[2,4,192,256]{3,2,1,0:T(8,128)(2,1)S(1)} collective-permute-done((bf16[2,4,192,256]{3,2,1,0:T(8,128)(2,1)S(1)}, bf16[2,4,192,256]{3,2,1,0:T(8,128)(2,1)S(1)}, u32[]{:S(2)}, u32[]{:S(2)}) %collective-permute-start.16) | collective-permute-done | bytes 786464 | tf_op jit(solution)/shard_map/ppermute | solution.py:21
  115.6 0.0 collective-permute-start.17
  115.6 0.5 collective-permute-start.18
  116.2 2.9 %collective-permute-start.9 = (bf16[4,192,256]{2,1,0:T(8,128)(2,1)}, bf16[4,192,256]{2,1,0:T(8,128)(2,1)S(1)}, u32[]{:S(2)}, u32[]{:S(2)}) collective-permute-start(bf16[4,192,256]{2,1,0:T(8,128)(2,1)} %get-tuple-element.42), channel_id=1, source_target_pairs={{0,16},{16,0},{32,48},{48,32},{64,80},{80,64},{96,112},{112,96},{1... | collective-permute-start | bytes 1179656 | tf_op jit(solution)/shard_map/ppermute | solution.py:21
  119.1 1.0 collective-permute-start.10
  120.1 0.1 collective-permute-start.11
  120.3 0.9 copy-done.15
  121.2 0.9 copy-done.16
  122.1 12.2 %shard_map.53 = bf16[768,1536]{1,0:T(8,128)(2,1)} custom-call(s32[5]{0:T(128)} %stack.62.at, bf16[2,4,192,256]{3,2,1,0:T(8,128)(2,1)} %copy-done.2, bf16[2,4,192,256]{3,2,1,0:T(8,128)(2,1)} %copy-done.14, bf16[2,4,192,256]{3,2,1,0:T(8,128)(2,1)} %copy-done.15, bf16[2,4,192,256]{3,2,1,0:T(8,128)(2,1)} %copy-done.16, bf16[2,4,64,1536]{3,2,1,0:T(8,128)(2,1)} %copy-done, ...), custom_call_target="tpu_custom_call" | custom-call | flops 4831838208 | bytes 11010048 | tf_op jit(solution)/shard_map/pallas_call | solution.py:240
  134.3 0.0 copy-start.5
  134.4 3.4 %collective-permute-done.10.r10 = bf16[4,192,256]{2,1,0:T(8,128)(2,1)S(1)} collective-permute-done((bf16[4,192,256]{2,1,0:T(8,128)(2,1)}, bf16[4,192,256]{2,1,0:T(8,128)(2,1)S(1)}, u32[]{:S(2)}, u32[]{:S(2)}) %collective-permute-start.10) | collective-permute-done | bytes 393248 | tf_op jit(solution)/shard_map/ppermute | solution.py:21
  137.8 0.7 copy-done.6
  138.5 0.8 copy-done.7
  139.3 2.3 %shard_map.54 = (bf16[2,192,256]{2,1,0:T(8,128)(2,1)}, bf16[2,192,256]{2,1,0:T(8,128)(2,1)}, bf16[2,192,256]{2,1,0:T(8,128)(2,1)}, bf16[2,192,256]{2,1,0:T(8,128)(2,1)}) custom-call(bf16[4,192,256]{2,1,0:T(8,128)(2,1)} %get-tuple-element.41.r00, bf16[4,192,256]{2,1,0:T(8,128)(2,1)} %copy-done.5, bf16[4,192,256]{2,1,0:T(8,128)(2,1)} %copy-done.6, ...), custom_call_target="tpu_custom_call" | custom-call | flops 786432 | bytes 2359296 | tf_op jit(solution)/shard_map/pallas_call | solution.py:248
  141.6 3.7 %collective-permute-start.20 = (bf16[2,192,256]{2,1,0:T(8,128)(2,1)}, bf16[2,192,256]{2,1,0:T(8,128)(2,1)S(1)}, u32[]{:S(2)}, u32[]{:S(2)}) collective-permute-start(bf16[2,192,256]{2,1,0:T(8,128)(2,1)} %get-tuple-element.61), channel_id=1, source_target_pairs={{0,64},{16,80},{32,96},{48,112},{64,0},{80,16},{96,32},{112,48},{1... | collective-permute-start | bytes 589832 | tf_op jit(solution)/shard_map/ppermute | solution.py:21
  145.3 5.1 %collective-permute-done.19.p1 = bf16[2,192,256]{2,1,0:T(8,128)(2,1)S(1)} collective-permute-done((bf16[2,192,256]{2,1,0:T(8,128)(2,1)}, bf16[2,192,256]{2,1,0:T(8,128)(2,1)S(1)}, u32[]{:S(2)}, u32[]{:S(2)}) %collective-permute-start.19) | collective-permute-done | bytes 196640 | tf_op jit(solution)/shard_map/ppermute | solution.py:21
  150.4 3.2 %collective-permute-done.20.p2 = bf16[2,192,256]{2,1,0:T(8,128)(2,1)S(1)} collective-permute-done((bf16[2,192,256]{2,1,0:T(8,128)(2,1)}, bf16[2,192,256]{2,1,0:T(8,128)(2,1)S(1)}, u32[]{:S(2)}, u32[]{:S(2)}) %collective-permute-start.20) | collective-permute-done | bytes 196640 | tf_op jit(solution)/shard_map/ppermute | solution.py:21
  153.6 0.2 collective-permute-done.21.p3
  153.8 0.5 copy-done.10
  154.3 0.2 copy-done.11
  154.5 3.0 %shard_map.55 = bf16[256,1536]{1,0:T(8,128)(2,1)} custom-call(s32[5]{0:T(128)} %stack.62.at, f32[256,1536]{1,0:T(8,128)} %get-tuple-element.33.slope, bf16[2,192,256]{2,1,0:T(8,128)(2,1)} %get-tuple-element.59.p0, bf16[2,192,256]{2,1,0:T(8,128)(2,1)} %copy-done.9, bf16[2,192,256]{2,1,0:T(8,128)(2,1)} %copy-done.10, bf16[2,192,256]{2,1,0:T(8,128)(2,1)} %copy-done.11), custom_call_target="tpu_custom_call" | custom-call | flops 201326592 | bytes 3145728 | tf_op jit(solution)/shard_map/pallas_call | solution.py:252
  (36 shorter events, 0.1 us)
Async XLA Ops:
  0.6 9.2 %collective-permute-start = (bf16[64,1536]{1,0:T(8,128)(2,1)}, bf16[64,1536]{1,0:T(8,128)(2,1)S(1)}, u32[]{:S(2)}, u32[]{:S(2)}) collective-permute-start(bf16[64,1536]{1,0:T(8,128)(2,1)} %param.4), channel_id=1, source_target_pairs={{0,16},{16,0},{32,48},{48,32},{64,80},{80,64},{96,112},{112,96},{1... | collective-permute-start | bytes 589832 | tf_op jit(solution)/shard_map/ppermute | solution.py:21
  10.8 9.5 %collective-permute-start.2 = (bf16[2,64,1536]{2,1,0:T(8,128)(2,1)S(1)}, bf16[2,64,1536]{2,1,0:T(8,128)(2,1)S(1)}, u32[]{:S(2)}, u32[]{:S(2)}) collective-permute-start(bf16[2,64,1536]{2,1,0:T(8,128)(2,1)S(1)} %get-tuple-element.65), channel_id=1, source_target_pairs={{0,8},{1,65},{2,10},{3,67},{4,12},{5,69},{6,14},{7,71},{8,0},{9,73... | collective-permute-start | bytes 1179656 | tf_op jit(solution)/shard_map/ppermute | solution.py:53
  14.0 10.3 %collective-permute-start.1 = (bf16[2,64,1536]{2,1,0:T(8,128)(2,1)S(1)}, bf16[2,64,1536]{2,1,0:T(8,128)(2,1)S(1)}, u32[]{:S(2)}, u32[]{:S(2)}) collective-permute-start(bf16[2,64,1536]{2,1,0:T(8,128)(2,1)S(1)} %get-tuple-element.65), channel_id=1, source_target_pairs={{0,4},{1,33},{2,6},{3,35},{4,8},{5,37},{6,10},{7,39},{8,12},{9,41}... | collective-permute-start | bytes 1179656 | tf_op jit(solution)/shard_map/ppermute | solution.py:53
  14.7 10.0 %collective-permute-start.3 = (bf16[2,64,1536]{2,1,0:T(8,128)(2,1)S(1)}, bf16[2,64,1536]{2,1,0:T(8,128)(2,1)S(1)}, u32[]{:S(2)}, u32[]{:S(2)}) collective-permute-start(bf16[2,64,1536]{2,1,0:T(8,128)(2,1)S(1)} %get-tuple-element.65), channel_id=1, source_target_pairs={{0,12},{1,97},{2,14},{3,99},{4,0},{5,101},{6,2},{7,103},{8,4},{9,1... | collective-permute-start | bytes 1179656 | tf_op jit(solution)/shard_map/ppermute | solution.py:53
  24.9 24.7 %copy-start = (bf16[2,4,64,1536]{3,2,1,0:T(8,128)(2,1)}, bf16[2,4,64,1536]{3,2,1,0:T(8,128)(2,1)S(1)}, u32[]{:S(2)}) copy-start(bf16[2,4,64,1536]{3,2,1,0:T(8,128)(2,1)S(1)} %pad_maximum_fusion.refs_0_.refs_4_) | copy-start | bytes 4718596
  24.9 24.8 %copy-start.19 = (bf16[2,192,256]{2,1,0:T(8,128)(2,1)S(1)}, bf16[2,192,256]{2,1,0:T(8,128)(2,1)}, u32[]{:S(2)}) copy-start(bf16[2,192,256]{2,1,0:T(8,128)(2,1)} %get-tuple-element.46) | copy-start | bytes 589828
  24.9 24.9 %copy-start.18 = (bf16[2,192,256]{2,1,0:T(8,128)(2,1)S(1)}, bf16[2,192,256]{2,1,0:T(8,128)(2,1)}, u32[]{:S(2)}) copy-start(bf16[2,192,256]{2,1,0:T(8,128)(2,1)} %get-tuple-element.47) | copy-start | bytes 589828
  24.9 29.5 %copy-start.17 = (bf16[2,192,256]{2,1,0:T(8,128)(2,1)S(1)}, bf16[2,192,256]{2,1,0:T(8,128)(2,1)}, u32[]{:S(2)}) copy-start(bf16[2,192,256]{2,1,0:T(8,128)(2,1)} %get-tuple-element.48) | copy-start | bytes 589828
  24.9 44.1 %copy-start.8 = (bf16[2,192,256]{2,1,0:T(8,128)(2,1)S(1)}, bf16[2,192,256]{2,1,0:T(8,128)(2,1)}, u32[]{:S(2)}) copy-start(bf16[2,192,256]{2,1,0:T(8,128)(2,1)} %get-tuple-element.49) | copy-start | bytes 589828
  24.9 20.8 %collective-permute-start.5 = (bf16[2,4,64,1536]{3,2,1,0:T(8,128)(2,1)S(1)}, bf16[2,4,64,1536]{3,2,1,0:T(8,128)(2,1)S(1)}, u32[]{:S(2)}, u32[]{:S(2)}) collective-permute-start(bf16[2,4,64,1536]{3,2,1,0:T(8,128)(2,1)S(1)} %pad_maximum_fusion.refs_0_.refs_4_), channel_id=1, source_target_pairs={{0,96},{1,13},{2,98},{3,15},{4,100},{5,1},{6,102},{7,3},{8,104},{9... | collective-permute-start | bytes 4718600 | tf_op jit(solution)/shard_map/ppermute | solution.py:53
  27.8 21.8 %collective-permute-start.4 = (bf16[2,4,64,1536]{3,2,1,0:T(8,128)(2,1)S(1)}, bf16[2,4,64,1536]{3,2,1,0:T(8,128)(2,1)S(1)}, u32[]{:S(2)}, u32[]{:S(2)}) collective-permute-start(bf16[2,4,64,1536]{3,2,1,0:T(8,128)(2,1)S(1)} %pad_maximum_fusion.refs_0_.refs_4_), channel_id=1, source_target_pairs={{0,32},{1,5},{2,34},{3,7},{4,36},{5,9},{6,38},{7,11},{8,40},{9,13}... | collective-permute-start | bytes 4718600 | tf_op jit(solution)/shard_map/ppermute | solution.py:53
  45.7 3.9 %copy-start.3 = (bf16[2,4,64,1536]{3,2,1,0:T(8,128)(2,1)}, bf16[2,4,64,1536]{3,2,1,0:T(8,128)(2,1)S(1)}, u32[]{:S(2)}) copy-start(bf16[2,4,64,1536]{3,2,1,0:T(8,128)(2,1)S(1)} %collective-permute-done.5.refs_2_.refs_6_) | copy-start | bytes 4718596
  45.8 23.3 %collective-permute-start.7 = (bf16[1,4,64,1536]{3,2,1,0:T(8,128)(2,1)S(1)}, bf16[1,4,64,1536]{3,2,1,0:T(8,128)(2,1)S(1)}, u32[]{:S(2)}, u32[]{:S(2)}) collective-permute-start(bf16[1,4,64,1536]{3,2,1,0:T(8,128)(2,1)S(1)} %slice.41), channel_id=1, source_target_pairs={{0,96},{1,13},{2,98},{3,15},{4,100},{5,1},{6,102},{7,3},{8,104},{9... | collective-permute-start | bytes 2359304 | tf_op jit(solution)/shard_map/ppermute | solution.py:53
  49.5 19.6 %copy-start.4 = (bf16[2,4,64,1536]{3,2,1,0:T(8,128)(2,1)}, bf16[2,4,64,1536]{3,2,1,0:T(8,128)(2,1)S(1)}, u32[]{:S(2)}) copy-start(bf16[2,4,64,1536]{3,2,1,0:T(8,128)(2,1)S(1)} %collective-permute-done.4.refs_1_.refs_5_) | copy-start | bytes 4718596
  49.6 19.5 %collective-permute-start.6 = (bf16[1,4,64,1536]{3,2,1,0:T(8,128)(2,1)S(1)}, bf16[1,4,64,1536]{3,2,1,0:T(8,128)(2,1)S(1)}, u32[]{:S(2)}, u32[]{:S(2)}) collective-permute-start(bf16[1,4,64,1536]{3,2,1,0:T(8,128)(2,1)S(1)} %slice.40), channel_id=1, source_target_pairs={{0,32},{1,5},{2,34},{3,7},{4,36},{5,9},{6,38},{7,11},{8,40},{9,13}... | collective-permute-start | bytes 2359304 | tf_op jit(solution)/shard_map/ppermute | solution.py:53
  49.7 19.3 %collective-permute-start.12 = (bf16[2,192,256]{2,1,0:T(8,128)(2,1)S(1)}, bf16[2,192,256]{2,1,0:T(8,128)(2,1)S(1)}, u32[]{:S(2)}, u32[]{:S(2)}) collective-permute-start(bf16[2,192,256]{2,1,0:T(8,128)(2,1)S(1)} %copy-done.19), channel_id=1, source_target_pairs={{0,32},{16,48},{32,64},{48,80},{64,96},{80,112},{96,0},{112,16},{1... | collective-permute-start | bytes 589832 | tf_op jit(solution)/shard_map/ppermute | solution.py:21
  49.8 19.2 %collective-permute-start.13 = (bf16[2,192,256]{2,1,0:T(8,128)(2,1)S(1)}, bf16[2,192,256]{2,1,0:T(8,128)(2,1)S(1)}, u32[]{:S(2)}, u32[]{:S(2)}) collective-permute-start(bf16[2,192,256]{2,1,0:T(8,128)(2,1)S(1)} %copy-done.18), channel_id=1, source_target_pairs={{0,64},{16,80},{32,96},{48,112},{64,0},{80,16},{96,32},{112,48},{1... | collective-permute-start | bytes 589832 | tf_op jit(solution)/shard_map/ppermute | solution.py:21
  54.4 14.6 %collective-permute-start.14 = (bf16[2,192,256]{2,1,0:T(8,128)(2,1)S(1)}, bf16[2,192,256]{2,1,0:T(8,128)(2,1)S(1)}, u32[]{:S(2)}, u32[]{:S(2)}) collective-permute-start(bf16[2,192,256]{2,1,0:T(8,128)(2,1)S(1)} %copy-done.17), channel_id=1, source_target_pairs={{0,96},{16,112},{32,0},{48,16},{64,32},{80,48},{96,64},{112,80},{1... | collective-permute-start | bytes 589832 | tf_op jit(solution)/shard_map/ppermute | solution.py:21
  69.1 1.0 copy-start.12
  69.1 1.1 copy-start.13
  83.0 14.4 %collective-permute-start.8 = (bf16[2,2,4,192,256]{4,3,2,1,0:T(8,128)(2,1)}, bf16[2,2,4,192,256]{4,3,2,1,0:T(8,128)(2,1)S(1)}, u32[]{:S(2)}, u32[]{:S(2)}) collective-permute-start(bf16[2,2,4,192,256]{4,3,2,1,0:T(8,128)(2,1)} %get-tuple-element.40), channel_id=1, source_target_pairs={{0,1},{1,0},{2,3},{3,2},{4,5},{5,4},{6,7},{7,6},{8,9},{9,8},{10,11... | collective-permute-start | bytes 4718600 | tf_op jit(solution)/shard_map/ppermute | solution.py:21
  83.2 13.1 %collective-permute-start.15 = (bf16[4,192,256]{2,1,0:T(8,128)(2,1)S(1)}, bf16[4,192,256]{2,1,0:T(8,128)(2,1)S(1)}, u32[]{:S(2)}, u32[]{:S(2)}) collective-permute-start(bf16[4,192,256]{2,1,0:T(8,128)(2,1)S(1)} %pad_maximum_fusion.3), channel_id=1, source_target_pairs={{0,16},{16,0},{32,48},{48,32},{64,80},{80,64},{96,112},{112,96},{1... | collective-permute-start | bytes 1179656 | tf_op jit(solution)/shard_map/ppermute | solution.py:21
  96.4 23.9 %copy-start.2 = (bf16[2,4,192,256]{3,2,1,0:T(8,128)(2,1)}, bf16[2,4,192,256]{3,2,1,0:T(8,128)(2,1)S(1)}, u32[]{:S(2)}) copy-start(bf16[2,4,192,256]{3,2,1,0:T(8,128)(2,1)S(1)} %pad_maximum_fusion.1.refs_0_) | copy-start | bytes 2359300
  96.4 19.2 %collective-permute-start.16 = (bf16[2,4,192,256]{3,2,1,0:T(8,128)(2,1)S(1)}, bf16[2,4,192,256]{3,2,1,0:T(8,128)(2,1)S(1)}, u32[]{:S(2)}, u32[]{:S(2)}) collective-permute-start(bf16[2,4,192,256]{3,2,1,0:T(8,128)(2,1)S(1)} %pad_maximum_fusion.1.refs_0_), channel_id=1, source_target_pairs={{0,2},{1,3},{2,0},{3,1},{4,6},{5,7},{6,4},{7,5},{8,10},{9,11},{10,... | collective-permute-start | bytes 2359304 | tf_op jit(solution)/shard_map/ppermute | solution.py:21
  97.4 1.2 copy-start.1
  115.6 4.6 %copy-start.14 = (bf16[2,4,192,256]{3,2,1,0:T(8,128)(2,1)}, bf16[2,4,192,256]{3,2,1,0:T(8,128)(2,1)S(1)}, u32[]{:S(2)}) copy-start(bf16[2,4,192,256]{3,2,1,0:T(8,128)(2,1)S(1)} %collective-permute-done.16.refs_1_) | copy-start | bytes 2359300
  115.6 4.6 %collective-permute-start.17 = (bf16[2,4,192,256]{3,2,1,0:T(8,128)(2,1)S(1)}, bf16[2,4,192,256]{3,2,1,0:T(8,128)(2,1)S(1)}, u32[]{:S(2)}, u32[]{:S(2)}) collective-permute-start(bf16[2,4,192,256]{3,2,1,0:T(8,128)(2,1)S(1)} %pad_maximum_fusion.1.refs_0_), channel_id=1, source_target_pairs={{0,1},{1,0},{2,3},{3,2},{4,5},{5,4},{6,7},{7,6},{8,9},{9,8},{10,11... | collective-permute-start | bytes 2359304 | tf_op jit(solution)/shard_map/ppermute | solution.py:21
  115.6 4.6 %collective-permute-start.18 = (bf16[2,4,192,256]{3,2,1,0:T(8,128)(2,1)S(1)}, bf16[2,4,192,256]{3,2,1,0:T(8,128)(2,1)S(1)}, u32[]{:S(2)}, u32[]{:S(2)}) collective-permute-start(bf16[2,4,192,256]{3,2,1,0:T(8,128)(2,1)S(1)} %collective-permute-done.16.refs_1_), channel_id=1, source_target_pairs={{0,1},{1,0},{2,3},{3,2},{4,5},{5,4},{6,7},{7,6},{8,9},{9,8},{10,11... | collective-permute-start | bytes 2359304 | tf_op jit(solution)/shard_map/ppermute | solution.py:21
  116.2 18.2 %collective-permute-start.9 = (bf16[4,192,256]{2,1,0:T(8,128)(2,1)}, bf16[4,192,256]{2,1,0:T(8,128)(2,1)S(1)}, u32[]{:S(2)}, u32[]{:S(2)}) collective-permute-start(bf16[4,192,256]{2,1,0:T(8,128)(2,1)} %get-tuple-element.42), channel_id=1, source_target_pairs={{0,16},{16,0},{32,48},{48,32},{64,80},{80,64},{96,112},{112,96},{1... | collective-permute-start | bytes 1179656 | tf_op jit(solution)/shard_map/ppermute | solution.py:21
  119.1 18.7 %collective-permute-start.10 = (bf16[4,192,256]{2,1,0:T(8,128)(2,1)}, bf16[4,192,256]{2,1,0:T(8,128)(2,1)S(1)}, u32[]{:S(2)}, u32[]{:S(2)}) collective-permute-start(bf16[4,192,256]{2,1,0:T(8,128)(2,1)} %get-tuple-element.43), channel_id=1, source_target_pairs={{0,2},{1,3},{2,0},{3,1},{4,6},{5,7},{6,4},{7,5},{8,10},{9,11},{10,... | collective-permute-start | bytes 1179656 | tf_op jit(solution)/shard_map/ppermute | solution.py:21
  120.1 17.7 %collective-permute-start.11 = (bf16[4,192,256]{2,1,0:T(8,128)(2,1)}, bf16[4,192,256]{2,1,0:T(8,128)(2,1)S(1)}, u32[]{:S(2)}, u32[]{:S(2)}) collective-permute-start(bf16[4,192,256]{2,1,0:T(8,128)(2,1)} %get-tuple-element.44), channel_id=1, source_target_pairs={{0,18},{1,19},{2,16},{3,17},{16,2},{17,3},{18,0},{19,1},{32,50},{3... | collective-permute-start | bytes 1179656 | tf_op jit(solution)/shard_map/ppermute | solution.py:21
  120.3 1.0 copy-start.15
  121.2 0.9 copy-start.16
  134.3 3.4 %copy-start.5 = (bf16[4,192,256]{2,1,0:T(8,128)(2,1)}, bf16[4,192,256]{2,1,0:T(8,128)(2,1)S(1)}, u32[]{:S(2)}) copy-start(bf16[4,192,256]{2,1,0:T(8,128)(2,1)S(1)} %collective-permute-done.9.r01) | copy-start | bytes 1179652
  137.8 0.7 copy-start.6
  138.5 0.8 copy-start.7
  141.6 8.8 %collective-permute-start.19 = (bf16[2,192,256]{2,1,0:T(8,128)(2,1)}, bf16[2,192,256]{2,1,0:T(8,128)(2,1)S(1)}, u32[]{:S(2)}, u32[]{:S(2)}) collective-permute-start(bf16[2,192,256]{2,1,0:T(8,128)(2,1)} %get-tuple-element.60), channel_id=1, source_target_pairs={{0,32},{16,48},{32,64},{48,80},{64,96},{80,112},{96,0},{112,16},{1... | collective-permute-start | bytes 589832 | tf_op jit(solution)/shard_map/ppermute | solution.py:21
  141.6 12.0 %collective-permute-start.20 = (bf16[2,192,256]{2,1,0:T(8,128)(2,1)}, bf16[2,192,256]{2,1,0:T(8,128)(2,1)S(1)}, u32[]{:S(2)}, u32[]{:S(2)}) collective-permute-start(bf16[2,192,256]{2,1,0:T(8,128)(2,1)} %get-tuple-element.61), channel_id=1, source_target_pairs={{0,64},{16,80},{32,96},{48,112},{64,0},{80,16},{96,32},{112,48},{1... | collective-permute-start | bytes 589832 | tf_op jit(solution)/shard_map/ppermute | solution.py:21
  145.3 8.5 %collective-permute-start.21 = (bf16[2,192,256]{2,1,0:T(8,128)(2,1)}, bf16[2,192,256]{2,1,0:T(8,128)(2,1)S(1)}, u32[]{:S(2)}, u32[]{:S(2)}) collective-permute-start(bf16[2,192,256]{2,1,0:T(8,128)(2,1)} %get-tuple-element.62), channel_id=1, source_target_pairs={{0,96},{16,112},{32,0},{48,16},{64,32},{80,48},{96,64},{112,80},{1... | collective-permute-start | bytes 589832 | tf_op jit(solution)/shard_map/ppermute | solution.py:21
  150.4 3.4 %copy-start.9 = (bf16[2,192,256]{2,1,0:T(8,128)(2,1)}, bf16[2,192,256]{2,1,0:T(8,128)(2,1)S(1)}, u32[]{:S(2)}) copy-start(bf16[2,192,256]{2,1,0:T(8,128)(2,1)S(1)} %collective-permute-done.19.p1) | copy-start | bytes 589828
  153.6 0.7 copy-start.10
  153.8 0.7 copy-start.11

commit v2 on v1

--- a/solution.py
+++ b/solution.py
@@ -95,7 +95,7 @@
         turned = lax.dot_general(pick, hidden, (((1,), (1,)), ((), ())), preferred_element_type=f32)
         turned = turned.astype(bf16)
         for i in range(8):
-            parts[i // 2][i % 2, 32 * j : 32 * j + 32, :] = turned[32 * i : 32 * i + 32, :]
+            parts[i][32 * j : 32 * j + 32, :] = turned[32 * i : 32 * i + 32, :]
 
 
 def load_grads(at, pieces, held, sems):
@@ -120,34 +120,49 @@
                 c.wait()
 
 
-def input_body(at, w, *refs):
-    pieces, (mine, theirs, held, sems) = refs[:5], refs[5:]
-    load_grads(at, pieces, held, sems)
+def input_body(count, at, w, *refs):
+    pieces, (mine, theirs, held, sems) = refs[:count], refs[count:]
+    blocks = [(n, z) for n, p in enumerate(pieces) for z in range(p.shape[0])]
+    copies = [
+        pltpu.make_async_copy(pieces[n].at[z], held.at[i], sems.at[i]) for i, (n, z) in enumerate(blocks)
+    ]
+    for c in copies:
+        c.start()
     rows = w.shape[0] // 4
-    ws = []
-    for core, out in ((0, mine), (1, theirs)):
-        for lo in range(2):
-            block = ((at[3] + lo) & 1) * 2 + ((at[4] + core) & 1)
-            ws.append(w[pl.ds(pl.multiple_of(block * rows, 64), rows), :])
-    turned = jnp.concatenate(ws, 0)
-
-    @pl.loop(0, 8)
-    def _(d):
-        k, z = d // 2, d % 2
+    for i, c in enumerate(copies):
+        c.wait()
         part = lax.dot_general(
-            turned, held[k, z].reshape(256, -1), (((1,), (1,)), ((), ())), preferred_element_type=f32
+            w[...], held[i].reshape(256, -1), (((1,), (1,)), ((), ())), preferred_element_type=f32
         ).astype(bf16)
-        for lo in range(2):
-            mine[lo, z, k] = part[lo * rows : lo * rows + rows]
-            theirs[lo, z, k] = part[(lo + 2) * rows : (lo + 3) * rows]
-
-
-def core_sum_body(mine, other, *outs):
-    for lo in range(2):
-        for z in range(2):
-            for k in range(4):
-                total = mine[lo, z, k].astype(f32) + other[lo, z, k].astype(f32)
-                outs[lo * 2 + z][k] = total.astype(bf16)
+        for core in range(2):
+
+            @pl.when(at[4] == core)
+            def _():
+                for n in range(4):
+                    out = mine if n % 2 == core else theirs
+                    out[i, at[3] ^ (n // 2)] = part[n * rows : n * rows + rows]
+
+
+def core_sum_body(at, mine, mine2, other, other2, *outs):
+    def block(early, late, k, z, lo):
+        if k == 2:
+            return late[z, lo]
+        return early[2 * (k - k // 3) + z, lo]
+
+    for core in range(2):
+
+        @pl.when(at[4] == core)
+        def _():
+            by_x, by_y = (mine, mine2), (other, other2)
+            if core:
+                by_x, by_y = by_y, by_x
+            for lo in range(2):
+                for z in range(2):
+                    y = [block(*by_y, k, z, lo) for k in range(4)]
+                    for k in range(4):
+                        turned = jnp.concatenate([v[:, 64 * k : 64 * k + 64] for v in y], 1)
+                        total = block(*by_x, k, z, lo).astype(f32) + turned.astype(f32)
+                        outs[lo * 2 + z][k] = total.astype(bf16)
 
 
 def z_sum_body(r00, r01, r10, r11, *outs):
@@ -186,14 +201,6 @@
             out[pl.ds(pl.multiple_of(block * rows, 64), rows), cols] = total[n * rows : n * rows + rows]
 
 
-def gather_grad(grad_out, first):
-    other, first = lax.optimization_barrier((swap_z_hi(grad_out), first))
-    both = jnp.stack([grad_out, other])
-    p0 = jnp.stack([both] + [send_by_core(both, k, True) for k in (1, 2, 3)], 1)
-    p1, p3 = send_by_core(p0, 1, False), send_by_core(p0, 3, False)
-    return (p0, p1, p3, send_by_core(p1[:1], 1, False), send_by_core(p3[1:], 3, False)), first
-
-
 def per_device(pre_act, grad_out, weight):
     tokens, columns = pre_act.shape
     rows, features = columns // 8, grad_out.shape[1]
@@ -206,33 +213,49 @@
 
     slope, *parts = call(
         pack_body,
-        [((tokens, columns), f32)] + [((2,) + block, bf16)] * 4,
+        [((tokens, columns), f32)] + [(block, bf16)] * 8,
         [SMEM, VMEM],
         (2 * tokens * 256 * columns, 8 * tokens * columns),
     )(at, pre_act)
 
-    pieces, parts = gather_grad(grad_out, parts)
-
-    by_x = [parts[0]] + [send_x(parts[4 - k], k) for k in (1, 2, 3)]
-    by_x, _ = lax.optimization_barrier((by_x, pieces[0]))
-    own = jnp.stack([p[0] for p in by_x])
-    own = jnp.stack([own, swap_z_hi(jnp.stack([p[1] for p in by_x]))])
-    own, _ = lax.optimization_barrier((own, pieces[1]))
+    other, parts = lax.optimization_barrier((swap_z_hi(grad_out), parts))
+    both = jnp.stack([grad_out, other])
+    p0 = jnp.stack([both] + [send_by_core(both, k, True) for k in (1, 2, 3)], 1)
+    p0, parts = lax.optimization_barrier((p0, parts))
+    p1, p3 = send_by_core(p0, 1, False), send_by_core(p0, 3, False)
+
+    got = [None] * 8
+    for k in range(4):
+        for z in range(2):
+            to = lambda i, k=k, z=z: ((i // 2 - k) % 4) * 2 + (i % 2 ^ z)
+            moved = parts[2 * k + z] if k == z == 0 else send(parts[2 * k + z], "gx", 8, to)
+            got[4 * z + (4 - k) % 4] = moved
+    p1, p3, got = lax.optimization_barrier((p1, p3, got))
+    p2p, p2m = send_by_core(p1[:1], 1, False), send_by_core(p3[1:], 3, False)
+    pieces = p0, p1, p3, p2p, p2m
+    own = jnp.stack(got).reshape((2, 4) + block)
     far = swap_z_lo(own)
 
-    shape = ((2, 2, 4) + block, bf16)
-    mine, theirs = call(
-        input_body,
-        [shape, shape],
-        [SMEM, VMEM] + [ANY] * 5,
-        (product, 2 * (6 * rows * features + 2048 * features)),
-        scratch=grad_scratch,
-    )(at, w, *pieces)
-    other = swap_core(theirs)
+    def input_part(*given):
+        count = sum(p.shape[0] for p in given)
+        return call(
+            functools.partial(input_body, len(given)),
+            [((count, 2) + block, bf16)] * 2,
+            [SMEM, VMEM] + [ANY] * len(given),
+            (product * count // 8, 2 * (4 * rows * features + count * (4 * rows + features) * tokens)),
+            scratch=[
+                pltpu.VMEM((count, 4, tokens // 4, features), bf16),
+                pltpu.SemaphoreType.DMA((count,)),
+            ],
+        )(at, w, *given)
+
+    mine, theirs = input_part(p0, p1, p3)
+    other, p2p, p2m = lax.optimization_barrier((swap_core(theirs), p2p, p2m))
+    mine2, theirs2 = input_part(p2p, p2m)
     size = 2 * 4 * rows * tokens
     r00, r01, r10, r11 = call(
-        core_sum_body, [((4,) + block, bf16)] * 4, [VMEM] * 2, (4 * size, 12 * size)
-    )(mine, other)
+        core_sum_body, [((4,) + block, bf16)] * 4, [SMEM] + [VMEM] * 4, (4 * size, 12 * size)
+    )(at, mine, mine2, other, swap_core(theirs2))
     q01, q10 = swap_z_hi(r01), swap_z_lo(r10)
     q11 = send(r11, ("gx", "gz"), 32, lambda i: i ^ 6)
     own, far, _ = lax.optimization_barrier((own, far, r00))

time: 158 us -> 147 us (0.930)
  waiting for transfers between devices: 76.3 us -> 53.4 us
  Pallas kernels: 37.1 us -> 44.5 us
  starting transfers between devices: 34.5 us -> 40.8 us
    ppermute x7, waiting for transfers between devices: 25.3 us -> 7.41 us  [send_by_core(): return lax.ppermute(v, ('gx', 'gy', 'gz'), pairs)]
    pallas_call x3 -> x4, Pallas kernels: 19.6 us -> 27.1 us  [the longest x2 19.8 us: input_part(): call(functools.partial(input_body, len(given)), [((count, 2) + block, bf1...]
    ppermute x15 -> x19, starting transfers between devices: 21.4 us -> 28.4 us  [send(): return lax.ppermute(v, axis, [(i, to(i)) for i in range(count)])]
    ppermute x15 -> x19, waiting for transfers between devices: 51 us -> 46 us  [send(): return lax.ppermute(v, axis, [(i, to(i)) for i in range(count)])]
    unnamed x40 -> x55, local copies, waits for them, and re-layouts: 6.37 us -> 5.51 us
  transfers between devices with their start and end apart: 22 -> 26, of which waited for: 12 -> 14; matrix products, arithmetic and copies ran while one was open for 1% -> 0% of each run, Pallas kernels for 12% -> 27%
where the time goes in v2:
time: 147 us
  waiting for transfers between devices  53.4 us (36%)
  Pallas kernels  44.5 us (30%)
  starting transfers between devices  40.8 us (28%)
  local copies, waits for them, and re-layouts  6.26 us (4%)
    ppermute x19, waiting for transfers between devices, send(): return lax.ppermute(v, axis, [(i, to(i)) for i in range(count)])  46 us
    ppermute x19, starting transfers between devices, send(): return lax.ppermute(v, axis, [(i, to(i)) for i in range(count)])  28.4 us
    pallas_call x2, Pallas kernels, input_part(): call(functools.partial(input_body, len(given)), [((count, 2) + block, bf1...  19.8 us
    ppermute x7, starting transfers between devices, send_by_core(): return lax.ppermute(v, ('gx', 'gy', 'gz'), pairs)  12.4 us
    pallas_call x1, Pallas kernels, per_device(): call(weight_body, [((4 * rows, features), bf16)], [SMEM] + [VMEM] * 4 + [...  12.2 us
    ppermute x7, waiting for transfers between devices, send_by_core(): return lax.ppermute(v, ('gx', 'gy', 'gz'), pairs)  7.41 us
    unnamed x55, local copies, waits for them, and re-layouts  5.51 us
    pallas_call x1, Pallas kernels, per_device(): call(pack_body, [((tokens, columns), f32)] + [(block, bf16)] * 8, [SMEM,...  3.72 us
  transfers between devices with their start and end apart: 26, of which 14 were waited for; matrix products, arithmetic and copies ran while one was open for 0% of the time, Pallas kernels for 27%

profile of v2, /device:TPU:0, one launch (start us, length us, event | category | flops | bytes accessed | tf_op | source)
XLA Modules:
  0.0 147.1 jit_solution(4916501267271440836)
XLA Ops:
  0.6 4.0 %collective-permute-start = (bf16[64,1536]{1,0:T(8,128)(2,1)}, bf16[64,1536]{1,0:T(8,128)(2,1)S(1)}, u32[]{:S(2)}, u32[]{:S(2)}) collective-permute-start(bf16[64,1536]{1,0:T(8,128)(2,1)} %param.4), channel_id=1, source_target_pairs={{0,16},{16,0},{32,48},{48,32},{64,80},{80,64},{96,112},{112,96},{1... | collective-permute-start | bytes 589832 | tf_op jit(solution)/shard_map/ppermute | solution.py:21
  4.7 0.6 stack.74.at
  5.3 3.7 %shard_map.50 = (f32[256,1536]{1,0:T(8,128)}, bf16[192,256]{1,0:T(8,128)(2,1)}, bf16[192,256]{1,0:T(8,128)(2,1)}, bf16[192,256]{1,0:T(8,128)(2,1)}, bf16[192,256...) custom-call(s32[5]{0:T(128)} %stack.74.at, ...), custom_call_target="tpu_custom_call" | custom-call | flops 201326592 | bytes 3145728 | tf_op jit(solution)/shard_map/pallas_call | solution.py:214
  9.0 0.8 collective-permute-done
  9.8 1.0 fusion
  10.8 3.3 %collective-permute-start.2 = (bf16[2,64,1536]{2,1,0:T(8,128)(2,1)S(1)}, bf16[2,64,1536]{2,1,0:T(8,128)(2,1)S(1)}, u32[]{:S(2)}, u32[]{:S(2)}) collective-permute-start(bf16[2,64,1536]{2,1,0:T(8,128)(2,1)S(1)} %get-tuple-element.119), channel_id=1, source_target_pairs={{0,8},{1,65},{2,10},{3,67},{4,12},{5,69},{6,14},{7,71},{8,0},{9,73... | collective-permute-start | bytes 1179656 | tf_op jit(solution)/shard_map/ppermute | solution.py:53
  14.0 0.7 collective-permute-start.1
  14.7 2.6 %collective-permute-start.3 = (bf16[2,64,1536]{2,1,0:T(8,128)(2,1)S(1)}, bf16[2,64,1536]{2,1,0:T(8,128)(2,1)S(1)}, u32[]{:S(2)}, u32[]{:S(2)}) collective-permute-start(bf16[2,64,1536]{2,1,0:T(8,128)(2,1)S(1)} %get-tuple-element.119), channel_id=1, source_target_pairs={{0,12},{1,97},{2,14},{3,99},{4,0},{5,101},{6,2},{7,103},{8,4},{9,1... | collective-permute-start | bytes 1179656 | tf_op jit(solution)/shard_map/ppermute | solution.py:53
  17.3 3.0 %collective-permute-done.2 = bf16[2,64,1536]{2,1,0:T(8,128)(2,1)S(1)} collective-permute-done((bf16[2,64,1536]{2,1,0:T(8,128)(2,1)S(1)}, bf16[2,64,1536]{2,1,0:T(8,128)(2,1)S(1)}, u32[]{:S(2)}, u32[]{:S(2)}) %collective-permute-start.2) | collective-permute-done | bytes 393248 | tf_op jit(solution)/shard_map/ppermute | solution.py:53
  20.2 4.1 %collective-permute-done.1 = bf16[2,64,1536]{2,1,0:T(8,128)(2,1)S(1)} collective-permute-done((bf16[2,64,1536]{2,1,0:T(8,128)(2,1)S(1)}, bf16[2,64,1536]{2,1,0:T(8,128)(2,1)S(1)}, u32[]{:S(2)}, u32[]{:S(2)}) %collective-permute-start.1) | collective-permute-done | bytes 393248 | tf_op jit(solution)/shard_map/ppermute | solution.py:53
  24.3 0.3 collective-permute-done.3
  24.7 0.0 copy-start.11
  24.7 0.2 pad_maximum_fusion.refs_0_.refs_4_
  24.9 2.8 %collective-permute-start.5 = (bf16[2,4,64,1536]{3,2,1,0:T(8,128)(2,1)S(1)}, bf16[2,4,64,1536]{3,2,1,0:T(8,128)(2,1)S(1)}, u32[]{:S(2)}, u32[]{:S(2)}) collective-permute-start(bf16[2,4,64,1536]{3,2,1,0:T(8,128)(2,1)S(1)} %pad_maximum_fusion.refs_0_.refs_4_), channel_id=1, source_target_pairs={{0,96},{1,13},{2,98},{3,15},{4,100},{5,1},{6,102},{7,3},{8,104},{9... | collective-permute-start | bytes 4718600 | tf_op jit(solution)/shard_map/ppermute | solution.py:53
  27.8 0.0 collective-permute-start.4
  27.8 0.8 collective-permute-start.6
  28.5 3.9 %collective-permute-start.7 = (bf16[192,256]{1,0:T(8,128)(2,1)S(1)}, bf16[192,256]{1,0:T(8,128)(2,1)S(1)}, u32[]{:S(2)}, u32[]{:S(2)}) collective-permute-start(bf16[192,256]{1,0:T(8,128)(2,1)S(1)} %copy-done.22), channel_id=1, source_target_pairs={{0,64},{16,80},{32,96},{48,112},{64,0},{80,16},{96,32},{112,48},{1... | collective-permute-start | bytes 294920 | tf_op jit(solution)/shard_map/ppermute | solution.py:21
  32.5 0.2 collective-permute-start.8
  32.7 21.6 %collective-permute-done.6 = bf16[192,256]{1,0:T(8,128)(2,1)S(1)} collective-permute-done((bf16[192,256]{1,0:T(8,128)(2,1)S(1)}, bf16[192,256]{1,0:T(8,128)(2,1)S(1)}, u32[]{:S(2)}, u32[]{:S(2)}) %collective-permute-start.6) | collective-permute-done | bytes 98336 | tf_op jit(solution)/shard_map/ppermute | solution.py:21
  54.3 2.9 %collective-permute-start.9 = (bf16[192,256]{1,0:T(8,128)(2,1)S(1)}, bf16[192,256]{1,0:T(8,128)(2,1)S(1)}, u32[]{:S(2)}, u32[]{:S(2)}) collective-permute-start(bf16[192,256]{1,0:T(8,128)(2,1)S(1)} %copy-done.20), channel_id=1, source_target_pairs={{0,16},{16,0},{32,48},{48,32},{64,80},{80,64},{96,112},{112,96},{1... | collective-permute-start | bytes 294920 | tf_op jit(solution)/shard_map/ppermute | solution.py:21
  57.1 0.0 collective-permute-start.10
  57.2 3.4 %collective-permute-start.11 = (bf16[192,256]{1,0:T(8,128)(2,1)S(1)}, bf16[192,256]{1,0:T(8,128)(2,1)S(1)}, u32[]{:S(2)}, u32[]{:S(2)}) collective-permute-start(bf16[192,256]{1,0:T(8,128)(2,1)S(1)} %copy-done.18), channel_id=1, source_target_pairs={{0,80},{16,64},{32,112},{48,96},{64,16},{80,0},{96,48},{112,32},{1... | collective-permute-start | bytes 294920 | tf_op jit(solution)/shard_map/ppermute | solution.py:21
  60.6 2.3 %collective-permute-start.12 = (bf16[192,256]{1,0:T(8,128)(2,1)S(1)}, bf16[192,256]{1,0:T(8,128)(2,1)S(1)}, u32[]{:S(2)}, u32[]{:S(2)}) collective-permute-start(bf16[192,256]{1,0:T(8,128)(2,1)S(1)} %copy-done.17), channel_id=1, source_target_pairs={{0,112},{16,96},{32,16},{48,0},{64,48},{80,32},{96,80},{112,64},{1... | collective-permute-start | bytes 294920 | tf_op jit(solution)/shard_map/ppermute | solution.py:21
  62.9 3.5 %collective-permute-done.10 = bf16[192,256]{1,0:T(8,128)(2,1)S(1)} collective-permute-done((bf16[192,256]{1,0:T(8,128)(2,1)S(1)}, bf16[192,256]{1,0:T(8,128)(2,1)S(1)}, u32[]{:S(2)}, u32[]{:S(2)}) %collective-permute-start.10) | collective-permute-done | bytes 98336 | tf_op jit(solution)/shard_map/ppermute | solution.py:21
  66.4 0.0 collective-permute-done.11
  66.4 1.2 collective-permute-done.12
  67.6 0.0 collective-permute-done.5.refs_2_.refs_6_
  67.6 0.0 collective-permute-done.4.refs_1_.refs_5_
  67.7 0.1 slice.6
  67.7 0.1 slice.7
  67.8 1.0 copy-done.2
  68.8 2.5 %collective-permute-start.15 = (bf16[1,4,64,1536]{3,2,1,0:T(8,128)(2,1)S(1)}, bf16[1,4,64,1536]{3,2,1,0:T(8,128)(2,1)}, u32[]{:S(2)}, u32[]{:S(2)}) collective-permute-start(bf16[1,4,64,1536]{3,2,1,0:T(8,128)(2,1)S(1)} %slice.7), channel_id=1, source_target_pairs={{0,96},{1,13},{2,98},{3,15},{4,100},{5,1},{6,102},{7,3},{8,104},{9... | collective-permute-start | bytes 2359304 | tf_op jit(solution)/shard_map/ppermute | solution.py:53
  71.3 0.6 collective-permute-start.14
  71.9 12.8 %shard_map.51 = (bf16[6,2,192,256]{3,2,1,0:T(8,128)(2,1)}, bf16[6,2,192,256]{3,2,1,0:T(8,128)(2,1)}) custom-call(s32[5]{0:T(128)} %stack.74.at, bf16[768,1536]{1,0:T(8,128)(2,1)} %bitcast.45, bf16[2,4,64,1536]{3,2,1,0:T(8,128)(2,1)} %copy-done, bf16[2,4,64,1536]{3,2,1,0:T(8,128)(2,1)} %copy-done.3, bf16[2,4,64,1536]{3,2,1,0:T(8,128)(2,1)} %copy-done.2), custom_call_target="tpu_custom_call" | custom-call | flops 3623878656 | bytes 9437184 | tf_op jit(solution)/shard_map/pallas_call | solution.py:241
  84.7 0.1 collective-permute-start.13
  84.9 1.3 collective-permute-start.20
  86.2 1.6 %collective-permute-done.13.other = bf16[6,2,192,256]{3,2,1,0:T(8,128)(2,1)S(1)} collective-permute-done((bf16[6,2,192,256]{3,2,1,0:T(8,128)(2,1)}, bf16[6,2,192,256]{3,2,1,0:T(8,128)(2,1)S(1)}, u32[]{:S(2)}, u32[]{:S(2)}) %collective-permute-start.13) | collective-permute-done | bytes 1179680 | tf_op jit(solution)/shard_map/ppermute | solution.py:21
  87.8 7.0 %shard_map.52 = (bf16[2,2,192,256]{3,2,1,0:T(8,128)(2,1)}, bf16[2,2,192,256]{3,2,1,0:T(8,128)(2,1)}) custom-call(s32[5]{0:T(128)} %stack.74.at, bf16[768,1536]{1,0:T(8,128)(2,1)} %bitcast.46, bf16[1,4,64,1536]{3,2,1,0:T(8,128)(2,1)} %copy-done.13, bf16[1,4,64,1536]{3,2,1,0:T(8,128)(2,1)} %collective-permute-done.15.refs_1_.refs_8_), custom_call_target="tpu_custom_call" | custom-call | flops 1207959552 | bytes 4718592 | tf_op jit(solution)/shard_map/pallas_call | solution.py:241
  94.8 0.2 collective-permute-start.16
  95.1 1.8 %collective-permute-done.16.other2 = bf16[2,2,192,256]{3,2,1,0:T(8,128)(2,1)S(1)} collective-permute-done((bf16[2,2,192,256]{3,2,1,0:T(8,128)(2,1)}, bf16[2,2,192,256]{3,2,1,0:T(8,128)(2,1)S(1)}, u32[]{:S(2)}, u32[]{:S(2)}) %collective-permute-start.16) | collective-permute-done | bytes 393248 | tf_op jit(solution)/shard_map/ppermute | solution.py:21
  96.9 0.8 copy-done.7
  97.6 3.5 %shard_map.53 = (bf16[4,192,256]{2,1,0:T(8,128)(2,1)}, bf16[4,192,256]{2,1,0:T(8,128)(2,1)}, bf16[4,192,256]{2,1,0:T(8,128)(2,1)}, bf16[4,192,256]{2,1,0:T(8,128)(2,1)}) custom-call(s32[5]{0:T(128)} %stack.74.at, bf16[6,2,192,256]{3,2,1,0:T(8,128)(2,1)} %get-tuple-element.89.mine, bf16[2,2,192,256]{3,2,1,0:T(8,128)(2,1)} %get-tuple-element.93.mine2, ...), custom_call_target="tpu_custom_call" | custom-call | flops 1572864 | bytes 4718592 | tf_op jit(solution)/shard_map/pallas_call | solution.py:256
  101.1 4.0 %collective-permute-done.20.refs_1_ = bf16[2,4,192,256]{3,2,1,0:T(8,128)(2,1)S(1)} collective-permute-done((bf16[2,4,192,256]{3,2,1,0:T(8,128)(2,1)S(1)}, bf16[2,4,192,256]{3,2,1,0:T(8,128)(2,1)S(1)}, u32[]{:S(2)}, u32[]{:S(2)}) %collective-permute-start.20) | collective-permute-done | bytes 786464 | tf_op jit(solution)/shard_map/ppermute | solution.py:21
  105.1 0.0 collective-permute-start.21
  105.1 0.5 collective-permute-start.22
  105.6 2.1 %collective-permute-start.17 = (bf16[4,192,256]{2,1,0:T(8,128)(2,1)}, bf16[4,192,256]{2,1,0:T(8,128)(2,1)S(1)}, u32[]{:S(2)}, u32[]{:S(2)}) collective-permute-start(bf16[4,192,256]{2,1,0:T(8,128)(2,1)} %get-tuple-element.97), channel_id=1, source_target_pairs={{0,16},{16,0},{32,48},{48,32},{64,80},{80,64},{96,112},{112,96},{1... | collective-permute-start | bytes 1179656 | tf_op jit(solution)/shard_map/ppermute | solution.py:21
  107.7 1.0 collective-permute-start.18
  108.7 1.0 collective-permute-start.19
  109.7 0.9 copy-done.15
  110.6 0.9 copy-done.16
  111.5 12.2 %shard_map.54 = bf16[768,1536]{1,0:T(8,128)(2,1)} custom-call(s32[5]{0:T(128)} %stack.74.at, bf16[2,4,192,256]{3,2,1,0:T(8,128)(2,1)} %bitcast.44, bf16[2,4,192,256]{3,2,1,0:T(8,128)(2,1)} %copy-done.14, bf16[2,4,192,256]{3,2,1,0:T(8,128)(2,1)} %copy-done.15, bf16[2,4,192,256]{3,2,1,0:T(8,128)(2,1)} %copy-done.16, bf16[2,4,64,1536]{3,2,1,0:T(8,128)(2,1)} %copy-done, ...), custom_call_target="tpu_custom_call" | custom-call | flops 4831838208 | bytes 11010048 | tf_op jit(solution)/shard_map/pallas_call | solution.py:263
  123.7 0.0 copy-start.4
  123.7 2.7 %collective-permute-done.18.r10 = bf16[4,192,256]{2,1,0:T(8,128)(2,1)S(1)} collective-permute-done((bf16[4,192,256]{2,1,0:T(8,128)(2,1)}, bf16[4,192,256]{2,1,0:T(8,128)(2,1)S(1)}, u32[]{:S(2)}, u32[]{:S(2)}) %collective-permute-start.18) | collective-permute-done | bytes 393248 | tf_op jit(solution)/shard_map/ppermute | solution.py:21
  126.4 0.4 collective-permute-done.19.r11
  126.9 0.3 copy-done.5
  127.2 0.8 copy-done.6
  128.0 2.3 %shard_map.55 = (bf16[2,192,256]{2,1,0:T(8,128)(2,1)}, bf16[2,192,256]{2,1,0:T(8,128)(2,1)}, bf16[2,192,256]{2,1,0:T(8,128)(2,1)}, bf16[2,192,256]{2,1,0:T(8,128)(2,1)}) custom-call(bf16[4,192,256]{2,1,0:T(8,128)(2,1)} %get-tuple-element.96.r00, bf16[4,192,256]{2,1,0:T(8,128)(2,1)} %copy-done.4, bf16[4,192,256]{2,1,0:T(8,128)(2,1)} %copy-done.5, ...), custom_call_target="tpu_custom_call" | custom-call | flops 786432 | bytes 2359296 | tf_op jit(solution)/shard_map/pallas_call | solution.py:271
  130.2 1.7 %collective-permute-start.23 = (bf16[2,192,256]{2,1,0:T(8,128)(2,1)}, bf16[2,192,256]{2,1,0:T(8,128)(2,1)S(1)}, u32[]{:S(2)}, u32[]{:S(2)}) collective-permute-start(bf16[2,192,256]{2,1,0:T(8,128)(2,1)} %get-tuple-element.114), channel_id=1, source_target_pairs={{0,32},{16,48},{32,64},{48,80},{64,96},{80,112},{96,0},{112,16},{1... | collective-permute-start | bytes 589832 | tf_op jit(solution)/shard_map/ppermute | solution.py:21
  131.9 3.0 %collective-permute-start.24 = (bf16[2,192,256]{2,1,0:T(8,128)(2,1)}, bf16[2,192,256]{2,1,0:T(8,128)(2,1)S(1)}, u32[]{:S(2)}, u32[]{:S(2)}) collective-permute-start(bf16[2,192,256]{2,1,0:T(8,128)(2,1)} %get-tuple-element.115), channel_id=1, source_target_pairs={{0,64},{16,80},{32,96},{48,112},{64,0},{80,16},{96,32},{112,48},{1... | collective-permute-start | bytes 589832 | tf_op jit(solution)/shard_map/ppermute | solution.py:21
  134.9 4.0 %collective-permute-done.23.p1 = bf16[2,192,256]{2,1,0:T(8,128)(2,1)S(1)} collective-permute-done((bf16[2,192,256]{2,1,0:T(8,128)(2,1)}, bf16[2,192,256]{2,1,0:T(8,128)(2,1)S(1)}, u32[]{:S(2)}, u32[]{:S(2)}) %collective-permute-start.23) | collective-permute-done | bytes 196640 | tf_op jit(solution)/shard_map/ppermute | solution.py:21
  138.9 4.5 %collective-permute-done.24.p2 = bf16[2,192,256]{2,1,0:T(8,128)(2,1)S(1)} collective-permute-done((bf16[2,192,256]{2,1,0:T(8,128)(2,1)}, bf16[2,192,256]{2,1,0:T(8,128)(2,1)S(1)}, u32[]{:S(2)}, u32[]{:S(2)}) %collective-permute-start.24) | collective-permute-done | bytes 196640 | tf_op jit(solution)/shard_map/ppermute | solution.py:21
  143.4 0.7 copy-done.9
  144.1 0.1 copy-done.10
  144.2 3.0 %shard_map.56 = bf16[256,1536]{1,0:T(8,128)(2,1)} custom-call(s32[5]{0:T(128)} %stack.74.at, f32[256,1536]{1,0:T(8,128)} %get-tuple-element.60.slope, bf16[2,192,256]{2,1,0:T(8,128)(2,1)} %get-tuple-element.113.p0, bf16[2,192,256]{2,1,0:T(8,128)(2,1)} %copy-done.8, bf16[2,192,256]{2,1,0:T(8,128)(2,1)} %copy-done.9, bf16[2,192,256]{2,1,0:T(8,128)(2,1)} %copy-done.10), custom_call_target="tpu_custom_call" | custom-call | flops 201326592 | bytes 3145728 | tf_op jit(solution)/shard_map/pallas_call | solution.py:275
  (56 shorter events, 0.2 us)
Async XLA Ops:
  0.6 9.2 %collective-permute-start = (bf16[64,1536]{1,0:T(8,128)(2,1)}, bf16[64,1536]{1,0:T(8,128)(2,1)S(1)}, u32[]{:S(2)}, u32[]{:S(2)}) collective-permute-start(bf16[64,1536]{1,0:T(8,128)(2,1)} %param.4), channel_id=1, source_target_pairs={{0,16},{16,0},{32,48},{48,32},{64,80},{80,64},{96,112},{112,96},{1... | collective-permute-start | bytes 589832 | tf_op jit(solution)/shard_map/ppermute | solution.py:21
  10.8 9.5 %collective-permute-start.2 = (bf16[2,64,1536]{2,1,0:T(8,128)(2,1)S(1)}, bf16[2,64,1536]{2,1,0:T(8,128)(2,1)S(1)}, u32[]{:S(2)}, u32[]{:S(2)}) collective-permute-start(bf16[2,64,1536]{2,1,0:T(8,128)(2,1)S(1)} %get-tuple-element.119), channel_id=1, source_target_pairs={{0,8},{1,65},{2,10},{3,67},{4,12},{5,69},{6,14},{7,71},{8,0},{9,73... | collective-permute-start | bytes 1179656 | tf_op jit(solution)/shard_map/ppermute | solution.py:53
  14.0 10.3 %collective-permute-start.1 = (bf16[2,64,1536]{2,1,0:T(8,128)(2,1)S(1)}, bf16[2,64,1536]{2,1,0:T(8,128)(2,1)S(1)}, u32[]{:S(2)}, u32[]{:S(2)}) collective-permute-start(bf16[2,64,1536]{2,1,0:T(8,128)(2,1)S(1)} %get-tuple-element.119), channel_id=1, source_target_pairs={{0,4},{1,33},{2,6},{3,35},{4,8},{5,37},{6,10},{7,39},{8,12},{9,41}... | collective-permute-start | bytes 1179656 | tf_op jit(solution)/shard_map/ppermute | solution.py:53
  14.7 10.0 %collective-permute-start.3 = (bf16[2,64,1536]{2,1,0:T(8,128)(2,1)S(1)}, bf16[2,64,1536]{2,1,0:T(8,128)(2,1)S(1)}, u32[]{:S(2)}, u32[]{:S(2)}) collective-permute-start(bf16[2,64,1536]{2,1,0:T(8,128)(2,1)S(1)} %get-tuple-element.119), channel_id=1, source_target_pairs={{0,12},{1,97},{2,14},{3,99},{4,0},{5,101},{6,2},{7,103},{8,4},{9,1... | collective-permute-start | bytes 1179656 | tf_op jit(solution)/shard_map/ppermute | solution.py:53
  24.7 3.1 %copy-start.23 = (bf16[192,256]{1,0:T(8,128)(2,1)S(1)}, bf16[192,256]{1,0:T(8,128)(2,1)}, u32[]{:S(2)}) copy-start(bf16[192,256]{1,0:T(8,128)(2,1)} %get-tuple-element.80) | copy-start | bytes 294916
  24.7 3.9 %copy-start.22 = (bf16[192,256]{1,0:T(8,128)(2,1)S(1)}, bf16[192,256]{1,0:T(8,128)(2,1)}, u32[]{:S(2)}) copy-start(bf16[192,256]{1,0:T(8,128)(2,1)} %get-tuple-element.81) | copy-start | bytes 294916
  24.7 7.8 %copy-start.21 = (bf16[192,256]{1,0:T(8,128)(2,1)S(1)}, bf16[192,256]{1,0:T(8,128)(2,1)}, u32[]{:S(2)}) copy-start(bf16[192,256]{1,0:T(8,128)(2,1)} %get-tuple-element.82) | copy-start | bytes 294916
  24.7 29.6 %copy-start.20 = (bf16[192,256]{1,0:T(8,128)(2,1)S(1)}, bf16[192,256]{1,0:T(8,128)(2,1)}, u32[]{:S(2)}) copy-start(bf16[192,256]{1,0:T(8,128)(2,1)} %get-tuple-element.83) | copy-start | bytes 294916
  24.7 32.5 %copy-start.19 = (bf16[192,256]{1,0:T(8,128)(2,1)S(1)}, bf16[192,256]{1,0:T(8,128)(2,1)}, u32[]{:S(2)}) copy-start(bf16[192,256]{1,0:T(8,128)(2,1)} %get-tuple-element.84) | copy-start | bytes 294916
  24.7 32.5 %copy-start.18 = (bf16[192,256]{1,0:T(8,128)(2,1)S(1)}, bf16[192,256]{1,0:T(8,128)(2,1)}, u32[]{:S(2)}) copy-start(bf16[192,256]{1,0:T(8,128)(2,1)} %get-tuple-element.85) | copy-start | bytes 294916
  24.7 35.9 %copy-start.17 = (bf16[192,256]{1,0:T(8,128)(2,1)S(1)}, bf16[192,256]{1,0:T(8,128)(2,1)}, u32[]{:S(2)}) copy-start(bf16[192,256]{1,0:T(8,128)(2,1)} %get-tuple-element.86) | copy-start | bytes 294916
  24.7 42.9 %copy-start.11 = (bf16[192,256]{1,0:T(8,128)(2,1)S(1)}, bf16[192,256]{1,0:T(8,128)(2,1)}, u32[]{:S(2)}) copy-start(bf16[192,256]{1,0:T(8,128)(2,1)} %get-tuple-element.100) | copy-start | bytes 294916
  24.9 42.9 %copy-start = (bf16[2,4,64,1536]{3,2,1,0:T(8,128)(2,1)}, bf16[2,4,64,1536]{3,2,1,0:T(8,128)(2,1)S(1)}, u32[]{:S(2)}) copy-start(bf16[2,4,64,1536]{3,2,1,0:T(8,128)(2,1)S(1)} %pad_maximum_fusion.refs_0_.refs_4_) | copy-start | bytes 4718596
  24.9 42.7 %collective-permute-start.5 = (bf16[2,4,64,1536]{3,2,1,0:T(8,128)(2,1)S(1)}, bf16[2,4,64,1536]{3,2,1,0:T(8,128)(2,1)S(1)}, u32[]{:S(2)}, u32[]{:S(2)}) collective-permute-start(bf16[2,4,64,1536]{3,2,1,0:T(8,128)(2,1)S(1)} %pad_maximum_fusion.refs_0_.refs_4_), channel_id=1, source_target_pairs={{0,96},{1,13},{2,98},{3,15},{4,100},{5,1},{6,102},{7,3},{8,104},{9... | collective-permute-start | bytes 4718600 | tf_op jit(solution)/shard_map/ppermute | solution.py:53
  27.8 39.9 %collective-permute-start.4 = (bf16[2,4,64,1536]{3,2,1,0:T(8,128)(2,1)S(1)}, bf16[2,4,64,1536]{3,2,1,0:T(8,128)(2,1)S(1)}, u32[]{:S(2)}, u32[]{:S(2)}) collective-permute-start(bf16[2,4,64,1536]{3,2,1,0:T(8,128)(2,1)S(1)} %pad_maximum_fusion.refs_0_.refs_4_), channel_id=1, source_target_pairs={{0,32},{1,5},{2,34},{3,7},{4,36},{5,9},{6,38},{7,11},{8,40},{9,13}... | collective-permute-start | bytes 4718600 | tf_op jit(solution)/shard_map/ppermute | solution.py:53
  27.8 26.5 %collective-permute-start.6 = (bf16[192,256]{1,0:T(8,128)(2,1)S(1)}, bf16[192,256]{1,0:T(8,128)(2,1)S(1)}, u32[]{:S(2)}, u32[]{:S(2)}) collective-permute-start(bf16[192,256]{1,0:T(8,128)(2,1)S(1)} %copy-done.23), channel_id=1, source_target_pairs={{0,32},{16,48},{32,64},{48,80},{64,96},{80,112},{96,0},{112,16},{1... | collective-permute-start | bytes 294920 | tf_op jit(solution)/shard_map/ppermute | solution.py:21
  28.5 28.6 %collective-permute-start.7 = (bf16[192,256]{1,0:T(8,128)(2,1)S(1)}, bf16[192,256]{1,0:T(8,128)(2,1)S(1)}, u32[]{:S(2)}, u32[]{:S(2)}) collective-permute-start(bf16[192,256]{1,0:T(8,128)(2,1)S(1)} %copy-done.22), channel_id=1, source_target_pairs={{0,64},{16,80},{32,96},{48,112},{64,0},{80,16},{96,32},{112,48},{1... | collective-permute-start | bytes 294920 | tf_op jit(solution)/shard_map/ppermute | solution.py:21
  32.5 24.7 %collective-permute-start.8 = (bf16[192,256]{1,0:T(8,128)(2,1)S(1)}, bf16[192,256]{1,0:T(8,128)(2,1)S(1)}, u32[]{:S(2)}, u32[]{:S(2)}) collective-permute-start(bf16[192,256]{1,0:T(8,128)(2,1)S(1)} %copy-done.21), channel_id=1, source_target_pairs={{0,96},{16,112},{32,0},{48,16},{64,32},{80,48},{96,64},{112,80},{1... | collective-permute-start | bytes 294920 | tf_op jit(solution)/shard_map/ppermute | solution.py:21
  54.3 6.3 %collective-permute-start.9 = (bf16[192,256]{1,0:T(8,128)(2,1)S(1)}, bf16[192,256]{1,0:T(8,128)(2,1)S(1)}, u32[]{:S(2)}, u32[]{:S(2)}) collective-permute-start(bf16[192,256]{1,0:T(8,128)(2,1)S(1)} %copy-done.20), channel_id=1, source_target_pairs={{0,16},{16,0},{32,48},{48,32},{64,80},{80,64},{96,112},{112,96},{1... | collective-permute-start | bytes 294920 | tf_op jit(solution)/shard_map/ppermute | solution.py:21
  57.1 9.3 %collective-permute-start.10 = (bf16[192,256]{1,0:T(8,128)(2,1)S(1)}, bf16[192,256]{1,0:T(8,128)(2,1)S(1)}, u32[]{:S(2)}, u32[]{:S(2)}) collective-permute-start(bf16[192,256]{1,0:T(8,128)(2,1)S(1)} %copy-done.19), channel_id=1, source_target_pairs={{0,48},{16,32},{32,80},{48,64},{64,112},{80,96},{96,16},{112,0},{1... | collective-permute-start | bytes 294920 | tf_op jit(solution)/shard_map/ppermute | solution.py:21
  57.2 9.3 %collective-permute-start.11 = (bf16[192,256]{1,0:T(8,128)(2,1)S(1)}, bf16[192,256]{1,0:T(8,128)(2,1)S(1)}, u32[]{:S(2)}, u32[]{:S(2)}) collective-permute-start(bf16[192,256]{1,0:T(8,128)(2,1)S(1)} %copy-done.18), channel_id=1, source_target_pairs={{0,80},{16,64},{32,112},{48,96},{64,16},{80,0},{96,48},{112,32},{1... | collective-permute-start | bytes 294920 | tf_op jit(solution)/shard_map/ppermute | solution.py:21
  60.6 7.0 %collective-permute-start.12 = (bf16[192,256]{1,0:T(8,128)(2,1)S(1)}, bf16[192,256]{1,0:T(8,128)(2,1)S(1)}, u32[]{:S(2)}, u32[]{:S(2)}) collective-permute-start(bf16[192,256]{1,0:T(8,128)(2,1)S(1)} %copy-done.17), channel_id=1, source_target_pairs={{0,112},{16,96},{32,16},{48,0},{64,48},{80,32},{96,80},{112,64},{1... | collective-permute-start | bytes 294920 | tf_op jit(solution)/shard_map/ppermute | solution.py:21
  67.6 1.2 copy-start.2
  67.6 4.2 %copy-start.3 = (bf16[2,4,64,1536]{3,2,1,0:T(8,128)(2,1)}, bf16[2,4,64,1536]{3,2,1,0:T(8,128)(2,1)S(1)}, u32[]{:S(2)}) copy-start(bf16[2,4,64,1536]{3,2,1,0:T(8,128)(2,1)S(1)} %collective-permute-done.4.refs_1_.refs_5_) | copy-start | bytes 4718596
  68.8 17.4 %collective-permute-start.15 = (bf16[1,4,64,1536]{3,2,1,0:T(8,128)(2,1)S(1)}, bf16[1,4,64,1536]{3,2,1,0:T(8,128)(2,1)}, u32[]{:S(2)}, u32[]{:S(2)}) collective-permute-start(bf16[1,4,64,1536]{3,2,1,0:T(8,128)(2,1)S(1)} %slice.7), channel_id=1, source_target_pairs={{0,96},{1,13},{2,98},{3,15},{4,100},{5,1},{6,102},{7,3},{8,104},{9... | collective-permute-start | bytes 2359304 | tf_op jit(solution)/shard_map/ppermute | solution.py:53
  71.3 14.9 %collective-permute-start.14 = (bf16[1,4,64,1536]{3,2,1,0:T(8,128)(2,1)S(1)}, bf16[1,4,64,1536]{3,2,1,0:T(8,128)(2,1)S(1)}, u32[]{:S(2)}, u32[]{:S(2)}) collective-permute-start(bf16[1,4,64,1536]{3,2,1,0:T(8,128)(2,1)S(1)} %slice.6), channel_id=1, source_target_pairs={{0,32},{1,5},{2,34},{3,7},{4,36},{5,9},{6,38},{7,11},{8,40},{9,13}... | collective-permute-start | bytes 2359304 | tf_op jit(solution)/shard_map/ppermute | solution.py:53
  84.7 3.1 %collective-permute-start.13 = (bf16[6,2,192,256]{3,2,1,0:T(8,128)(2,1)}, bf16[6,2,192,256]{3,2,1,0:T(8,128)(2,1)S(1)}, u32[]{:S(2)}, u32[]{:S(2)}) collective-permute-start(bf16[6,2,192,256]{3,2,1,0:T(8,128)(2,1)} %get-tuple-element.90), channel_id=1, source_target_pairs={{0,1},{1,0},{2,3},{3,2},{4,5},{5,4},{6,7},{7,6},{8,9},{9,8},{10,11... | collective-permute-start | bytes 3538952 | tf_op jit(solution)/shard_map/ppermute | solution.py:21
  84.9 20.2 %copy-start.12 = (bf16[8,192,256]{2,1,0:T(8,128)(2,1)}, bf16[8,192,256]{2,1,0:T(8,128)(2,1)S(1)}, u32[]{:S(2)}) copy-start(bf16[8,192,256]{2,1,0:T(8,128)(2,1)S(1)} %bitcast_dynamic-update-slice_fusion) | copy-start | bytes 2359300
  84.9 20.2 %collective-permute-start.20 = (bf16[2,4,192,256]{3,2,1,0:T(8,128)(2,1)S(1)}, bf16[2,4,192,256]{3,2,1,0:T(8,128)(2,1)S(1)}, u32[]{:S(2)}, u32[]{:S(2)}) collective-permute-start(bf16[2,4,192,256]{3,2,1,0:T(8,128)(2,1)S(1)} %bitcast.42), channel_id=1, source_target_pairs={{0,2},{1,3},{2,0},{3,1},{4,6},{5,7},{6,4},{7,5},{8,10},{9,11},{10,... | collective-permute-start | bytes 2359304 | tf_op jit(solution)/shard_map/ppermute | solution.py:21
  86.2 1.6 %copy-start.13 = (bf16[1,4,64,1536]{3,2,1,0:T(8,128)(2,1)}, bf16[1,4,64,1536]{3,2,1,0:T(8,128)(2,1)S(1)}, u32[]{:S(2)}) copy-start(bf16[1,4,64,1536]{3,2,1,0:T(8,128)(2,1)S(1)} %collective-permute-done.14.refs_0_.refs_7_) | copy-start | bytes 2359300
  87.8 7.0 %copy-start.1 = (bf16[6,2,192,256]{3,2,1,0:T(8,128)(2,1)}, bf16[6,2,192,256]{3,2,1,0:T(8,128)(2,1)S(1)}, u32[]{:S(2)}) copy-start(bf16[6,2,192,256]{3,2,1,0:T(8,128)(2,1)S(1)} %collective-permute-done.13.other) | copy-start | bytes 3538948
  94.8 2.0 %collective-permute-start.16 = (bf16[2,2,192,256]{3,2,1,0:T(8,128)(2,1)}, bf16[2,2,192,256]{3,2,1,0:T(8,128)(2,1)S(1)}, u32[]{:S(2)}, u32[]{:S(2)}) collective-permute-start(bf16[2,2,192,256]{3,2,1,0:T(8,128)(2,1)} %get-tuple-element.95), channel_id=1, source_target_pairs={{0,1},{1,0},{2,3},{3,2},{4,5},{5,4},{6,7},{7,6},{8,9},{9,8},{10,11... | collective-permute-start | bytes 1179656 | tf_op jit(solution)/shard_map/ppermute | solution.py:21
  96.9 0.8 copy-start.7
  105.1 4.6 %copy-start.14 = (bf16[2,4,192,256]{3,2,1,0:T(8,128)(2,1)}, bf16[2,4,192,256]{3,2,1,0:T(8,128)(2,1)S(1)}, u32[]{:S(2)}) copy-start(bf16[2,4,192,256]{3,2,1,0:T(8,128)(2,1)S(1)} %collective-permute-done.20.refs_1_) | copy-start | bytes 2359300
  105.1 4.6 %collective-permute-start.21 = (bf16[2,4,192,256]{3,2,1,0:T(8,128)(2,1)S(1)}, bf16[2,4,192,256]{3,2,1,0:T(8,128)(2,1)S(1)}, u32[]{:S(2)}, u32[]{:S(2)}) collective-permute-start(bf16[2,4,192,256]{3,2,1,0:T(8,128)(2,1)S(1)} %bitcast.43), channel_id=1, source_target_pairs={{0,1},{1,0},{2,3},{3,2},{4,5},{5,4},{6,7},{7,6},{8,9},{9,8},{10,11... | collective-permute-start | bytes 2359304 | tf_op jit(solution)/shard_map/ppermute | solution.py:21
  105.1 4.6 %collective-permute-start.22 = (bf16[2,4,192,256]{3,2,1,0:T(8,128)(2,1)S(1)}, bf16[2,4,192,256]{3,2,1,0:T(8,128)(2,1)S(1)}, u32[]{:S(2)}, u32[]{:S(2)}) collective-permute-start(bf16[2,4,192,256]{3,2,1,0:T(8,128)(2,1)S(1)} %collective-permute-done.20.refs_1_), channel_id=1, source_target_pairs={{0,1},{1,0},{2,3},{3,2},{4,5},{5,4},{6,7},{7,6},{8,9},{9,8},{10,11... | collective-permute-start | bytes 2359304 | tf_op jit(solution)/shard_map/ppermute | solution.py:21
  105.6 18.1 %collective-permute-start.17 = (bf16[4,192,256]{2,1,0:T(8,128)(2,1)}, bf16[4,192,256]{2,1,0:T(8,128)(2,1)S(1)}, u32[]{:S(2)}, u32[]{:S(2)}) collective-permute-start(bf16[4,192,256]{2,1,0:T(8,128)(2,1)} %get-tuple-element.97), channel_id=1, source_target_pairs={{0,16},{16,0},{32,48},{48,32},{64,80},{80,64},{96,112},{112,96},{1... | collective-permute-start | bytes 1179656 | tf_op jit(solution)/shard_map/ppermute | solution.py:21
  107.7 18.8 %collective-permute-start.18 = (bf16[4,192,256]{2,1,0:T(8,128)(2,1)}, bf16[4,192,256]{2,1,0:T(8,128)(2,1)S(1)}, u32[]{:S(2)}, u32[]{:S(2)}) collective-permute-start(bf16[4,192,256]{2,1,0:T(8,128)(2,1)} %get-tuple-element.98), channel_id=1, source_target_pairs={{0,2},{1,3},{2,0},{3,1},{4,6},{5,7},{6,4},{7,5},{8,10},{9,11},{10,... | collective-permute-start | bytes 1179656 | tf_op jit(solution)/shard_map/ppermute | solution.py:21
  108.7 18.2 %collective-permute-start.19 = (bf16[4,192,256]{2,1,0:T(8,128)(2,1)}, bf16[4,192,256]{2,1,0:T(8,128)(2,1)S(1)}, u32[]{:S(2)}, u32[]{:S(2)}) collective-permute-start(bf16[4,192,256]{2,1,0:T(8,128)(2,1)} %get-tuple-element.99), channel_id=1, source_target_pairs={{0,18},{1,19},{2,16},{3,17},{16,2},{17,3},{18,0},{19,1},{32,50},{3... | collective-permute-start | bytes 1179656 | tf_op jit(solution)/shard_map/ppermute | solution.py:21
  109.7 0.9 copy-start.15
  110.6 0.9 copy-start.16
  123.7 3.1 %copy-start.4 = (bf16[4,192,256]{2,1,0:T(8,128)(2,1)}, bf16[4,192,256]{2,1,0:T(8,128)(2,1)S(1)}, u32[]{:S(2)}) copy-start(bf16[4,192,256]{2,1,0:T(8,128)(2,1)S(1)} %collective-permute-done.17.r01) | copy-start | bytes 1179652
  126.4 0.7 copy-start.5
  127.2 0.8 copy-start.6
  130.2 8.7 %collective-permute-start.23 = (bf16[2,192,256]{2,1,0:T(8,128)(2,1)}, bf16[2,192,256]{2,1,0:T(8,128)(2,1)S(1)}, u32[]{:S(2)}, u32[]{:S(2)}) collective-permute-start(bf16[2,192,256]{2,1,0:T(8,128)(2,1)} %get-tuple-element.114), channel_id=1, source_target_pairs={{0,32},{16,48},{32,64},{48,80},{64,96},{80,112},{96,0},{112,16},{1... | collective-permute-start | bytes 589832 | tf_op jit(solution)/shard_map/ppermute | solution.py:21
  131.9 11.5 %collective-permute-start.24 = (bf16[2,192,256]{2,1,0:T(8,128)(2,1)}, bf16[2,192,256]{2,1,0:T(8,128)(2,1)S(1)}, u32[]{:S(2)}, u32[]{:S(2)}) collective-permute-start(bf16[2,192,256]{2,1,0:T(8,128)(2,1)} %get-tuple-element.115), channel_id=1, source_target_pairs={{0,64},{16,80},{32,96},{48,112},{64,0},{80,16},{96,32},{112,48},{1... | collective-permute-start | bytes 589832 | tf_op jit(solution)/shard_map/ppermute | solution.py:21
  134.9 8.5 %collective-permute-start.25 = (bf16[2,192,256]{2,1,0:T(8,128)(2,1)}, bf16[2,192,256]{2,1,0:T(8,128)(2,1)S(1)}, u32[]{:S(2)}, u32[]{:S(2)}) collective-permute-start(bf16[2,192,256]{2,1,0:T(8,128)(2,1)} %get-tuple-element.116), channel_id=1, source_target_pairs={{0,96},{16,112},{32,0},{48,16},{64,32},{80,48},{96,64},{112,80},{1... | collective-permute-start | bytes 589832 | tf_op jit(solution)/shard_map/ppermute | solution.py:21
  138.9 4.5 %copy-start.8 = (bf16[2,192,256]{2,1,0:T(8,128)(2,1)}, bf16[2,192,256]{2,1,0:T(8,128)(2,1)S(1)}, u32[]{:S(2)}) copy-start(bf16[2,192,256]{2,1,0:T(8,128)(2,1)S(1)} %collective-permute-done.23.p1) | copy-start | bytes 589828
  143.4 0.7 copy-start.9
  143.4 0.8 copy-start.10

commit v3 on v2

--- a/solution.py
+++ b/solution.py
@@ -68,12 +68,14 @@
     )
 
 
-def one_hot(at, rows):
-    q = lax.broadcasted_iota(jnp.int32, (rows, 256), 0)
-    u = lax.broadcasted_iota(jnp.int32, (rows, 256), 1)
-    i, r = q // 32, q % 32
-    s = ((at[0] - i // 2) & 3) * 2 + ((at[1] + i) & 1)
-    return jnp.where(u == r * 8 + s, 1.0, 0.0).astype(bf16)
+def one_hot():
+    q = lax.broadcasted_iota(jnp.int32, (256, 256), 0)
+    u = lax.broadcasted_iota(jnp.int32, (256, 256), 1)
+    return jnp.where(u == (q % 32) * 8 + q // 32, 1.0, 0.0).astype(bf16)
+
+
+def group(at, k, z):
+    return ((at[0] - k) & 3) * 2 + (at[1] ^ z)
 
 
 def token_rows(y, k):
@@ -81,8 +83,8 @@
 
 
 def pack_body(at, pre, *outs):
-    slope, parts = outs[0], outs[1:]
-    pick = one_hot(at, 256)
+    slope, parts = outs
+    pick = one_hot()
     for j in range(pre.shape[1] // 256):
         cols = slice(256 * j, 256 * j + 256)
         u = jnp.concatenate([pre[token_rows(at[2], k), cols] for k in range(4)], 0)
@@ -95,7 +97,7 @@
         turned = lax.dot_general(pick, hidden, (((1,), (1,)), ((), ())), preferred_element_type=f32)
         turned = turned.astype(bf16)
         for i in range(8):
-            parts[i][32 * j : 32 * j + 32, :] = turned[32 * i : 32 * i + 32, :]
+            parts[i, 32 * j : 32 * j + 32, :] = turned[32 * i : 32 * i + 32, :]
 
 
 def load_grads(at, pieces, held, sems):
@@ -121,29 +123,46 @@
 
 
 def input_body(count, at, w, *refs):
-    pieces, (mine, theirs, held, sems) = refs[:count], refs[count:]
-    blocks = [(n, z) for n, p in enumerate(pieces) for z in range(p.shape[0])]
-    copies = [
-        pltpu.make_async_copy(pieces[n].at[z], held.at[i], sems.at[i]) for i, (n, z) in enumerate(blocks)
-    ]
-    for c in copies:
-        c.start()
+    pieces, (mine, theirs, held, sums, in_sems, out_sems) = refs[:count], refs[count:]
+    blocks = [p.at[z] for p in pieces for z in range(p.shape[0])]
+    for i, src in enumerate(blocks):
+        pltpu.make_async_copy(src, held.at[i], in_sems.at[i]).start()
     rows = w.shape[0] // 4
-    for i, c in enumerate(copies):
-        c.wait()
+
+    def leaving(i):
+        slot = i % 2
+        return [
+            pltpu.make_async_copy(sums.at[slot, n], out.at[i], out_sems.at[slot, n])
+            for n, out in enumerate((mine, theirs))
+        ]
+
+    @pl.loop(0, len(blocks))
+    def _(i):
+        pltpu.make_async_copy(blocks[0], held.at[i], in_sems.at[i]).wait()
+
+        @pl.when(i >= 2)
+        def _():
+            for c in leaving(i - 2):
+                c.wait()
+
         part = lax.dot_general(
             w[...], held[i].reshape(256, -1), (((1,), (1,)), ((), ())), preferred_element_type=f32
         ).astype(bf16)
-        for core in range(2):
-
-            @pl.when(at[4] == core)
-            def _():
-                for n in range(4):
-                    out = mine if n % 2 == core else theirs
-                    out[i, at[3] ^ (n // 2)] = part[n * rows : n * rows + rows]
-
-
-def core_sum_body(at, mine, mine2, other, other2, *outs):
+        for n in range(4):
+            sums[i % 2, at[4] ^ (n % 2), n // 2] = part[n * rows : n * rows + rows]
+        for c in leaving(i):
+            c.start()
+
+    for i in range(len(blocks) - 2, len(blocks)):
+        for c in leaving(i):
+            c.wait()
+
+
+def core_sum_body(at, mine, mine2, other, other2, out, held, sems):
+    def leaving(k, z):
+        n = 2 * k + z
+        return pltpu.make_async_copy(held.at[n], out.at[group(at, k, z)], sems.at[n])
+
     def block(early, late, k, z, lo):
         if k == 2:
             return late[z, lo]
@@ -156,26 +175,27 @@
             by_x, by_y = (mine, mine2), (other, other2)
             if core:
                 by_x, by_y = by_y, by_x
-            for lo in range(2):
-                for z in range(2):
+            for z in range(2):
+                for lo in range(2):
                     y = [block(*by_y, k, z, lo) for k in range(4)]
                     for k in range(4):
                         turned = jnp.concatenate([v[:, 64 * k : 64 * k + 64] for v in y], 1)
                         total = block(*by_x, k, z, lo).astype(f32) + turned.astype(f32)
-                        outs[lo * 2 + z][k] = total.astype(bf16)
-
-
-def z_sum_body(r00, r01, r10, r11, *outs):
-    for k in range(4):
-        outs[k][0] = (r00[k].astype(f32) + r10[k].astype(f32)).astype(bf16)
-        outs[k][1] = (r01[k].astype(f32) + r11[k].astype(f32)).astype(bf16)
-
-
-def finish_body(at, slope, p0, p1, p2, p3, out):
-    pick = one_hot(at, 256)
+                        held[2 * k + z, lo] = total.astype(bf16)
+                for k in range(4):
+                    leaving(k, z).start()
+
+    for z in range(2):
+        for k in range(4):
+            leaving(k, z).wait()
+
+
+def finish_body(at, slope, parts, out):
+    pick = one_hot()
     for j in range(out.shape[1] // 256):
-        cols = slice(256 * j, 256 * j + 256)
-        v = jnp.concatenate([p[z, 32 * j : 32 * j + 32, :] for p in (p0, p1, p2, p3) for z in range(2)], 0)
+        cols, units = slice(256 * j, 256 * j + 256), slice(32 * j, 32 * j + 32)
+        v = [(parts[n, 0, units, :].astype(f32) + parts[n, 1, units, :].astype(f32)) for n in range(8)]
+        v = jnp.concatenate(v, 0).astype(bf16)
         total = lax.dot_general(v, pick, (((0,), (0,)), ((), ())), preferred_element_type=f32)
         result = (total * slope[:, cols]).astype(bf16)
         for k in range(4):
@@ -187,7 +207,7 @@
     load_grads(at, pieces, held, sems)
     rows = out.shape[0] // 4
     lhs = jnp.concatenate(
-        [jnp.concatenate([h[z, k] for k in range(4) for z in range(2)], 1) for h in hidden], 0
+        [jnp.concatenate([h[group(at, k, z)] for k in range(4) for z in range(2)], 1) for h in hidden], 0
     )
 
     @pl.loop(0, out.shape[1] // 256)
@@ -211,9 +231,9 @@
     grad_scratch = [pltpu.VMEM((4, 2, 4, tokens // 4, features), bf16), pltpu.SemaphoreType.DMA((8,))]
     product = 2 * 4 * rows * 8 * tokens * features
 
-    slope, *parts = call(
+    slope, parts = call(
         pack_body,
-        [((tokens, columns), f32)] + [(block, bf16)] * 8,
+        [((tokens, columns), f32), ((8,) + block, bf16)],
         [SMEM, VMEM],
         (2 * tokens * 256 * columns, 8 * tokens * columns),
     )(at, pre_act)
@@ -221,19 +241,12 @@
     other, parts = lax.optimization_barrier((swap_z_hi(grad_out), parts))
     both = jnp.stack([grad_out, other])
     p0 = jnp.stack([both] + [send_by_core(both, k, True) for k in (1, 2, 3)], 1)
-    p0, parts = lax.optimization_barrier((p0, parts))
     p1, p3 = send_by_core(p0, 1, False), send_by_core(p0, 3, False)
 
-    got = [None] * 8
-    for k in range(4):
-        for z in range(2):
-            to = lambda i, k=k, z=z: ((i // 2 - k) % 4) * 2 + (i % 2 ^ z)
-            moved = parts[2 * k + z] if k == z == 0 else send(parts[2 * k + z], "gx", 8, to)
-            got[4 * z + (4 - k) % 4] = moved
-    p1, p3, got = lax.optimization_barrier((p1, p3, got))
+    own = lax.all_to_all(parts, "gx", 0, 0, tiled=True)
+    p1, p3, own = lax.optimization_barrier((p1, p3, own))
     p2p, p2m = send_by_core(p1[:1], 1, False), send_by_core(p3[1:], 3, False)
     pieces = p0, p1, p3, p2p, p2m
-    own = jnp.stack(got).reshape((2, 4) + block)
     far = swap_z_lo(own)
 
     def input_part(*given):
@@ -243,22 +256,32 @@
             [((count, 2) + block, bf16)] * 2,
             [SMEM, VMEM] + [ANY] * len(given),
             (product * count // 8, 2 * (4 * rows * features + count * (4 * rows + features) * tokens)),
+            out_specs=[ANY] * 2,
             scratch=[
                 pltpu.VMEM((count, 4, tokens // 4, features), bf16),
+                pltpu.VMEM((2, 2, 2) + block, bf16),
                 pltpu.SemaphoreType.DMA((count,)),
+                pltpu.SemaphoreType.DMA((2, 2)),
             ],
         )(at, w, *given)
 
     mine, theirs = input_part(p0, p1, p3)
-    other, p2p, p2m = lax.optimization_barrier((swap_core(theirs), p2p, p2m))
+    other = swap_core(theirs)
     mine2, theirs2 = input_part(p2p, p2m)
     size = 2 * 4 * rows * tokens
-    r00, r01, r10, r11 = call(
-        core_sum_body, [((4,) + block, bf16)] * 4, [SMEM] + [VMEM] * 4, (4 * size, 12 * size)
+    (sums,) = call(
+        core_sum_body,
+        [((8, 2) + block, bf16)],
+        [SMEM] + [VMEM] * 4,
+        (4 * size, 12 * size),
+        out_specs=[ANY],
+        scratch=[pltpu.VMEM((8, 2) + block, bf16), pltpu.SemaphoreType.DMA((8,))],
     )(at, mine, mine2, other, swap_core(theirs2))
-    q01, q10 = swap_z_hi(r01), swap_z_lo(r10)
-    q11 = send(r11, ("gx", "gz"), 32, lambda i: i ^ 6)
-    own, far, _ = lax.optimization_barrier((own, far, r00))
+    same_core = [[2 * (2 * i + k) + c for i in range(8) for k in range(2)] for c in range(2)]
+    back = lax.all_to_all(
+        sums.reshape((16,) + block), ("gx", "gz"), 0, 0, tiled=True, axis_index_groups=same_core
+    )
+    own, far, _ = lax.optimization_barrier((own, far, sums))
     hidden = [own, far, swap_core(own), swap_core(far)]
     (weight_grad,) = call(
         weight_body,
@@ -267,17 +290,13 @@
         (product, 2 * (8 * rows * features + 2048 * features)),
         scratch=grad_scratch,
     )(at, *hidden, *pieces)
-    q01, q10, q11, weight_grad = lax.optimization_barrier((q01, q10, q11, weight_grad))
-    sums = call(z_sum_body, [((2,) + block, bf16)] * 4, [VMEM] * 4, (2 * size, 6 * size))(
-        r00, q01, q10, q11
-    )
-    back = [sums[0]] + [send_x(sums[4 - k], k) for k in (1, 2, 3)]
+    back, weight_grad = lax.optimization_barrier((back, weight_grad))
     (pre_grad,) = call(
         finish_body,
         [((tokens, columns), bf16)],
-        [SMEM] + [VMEM] * 5,
+        [SMEM] + [VMEM] * 2,
         (2 * tokens * 256 * columns, 8 * tokens * columns),
-    )(at, slope, *back)
+    )(at, slope, back.reshape((8, 2) + block))
     return pre_grad, weight_grad.reshape(weight.shape)
 
 

time: 147 us -> 122 us (0.83)
  blocking collectives: 0 us -> 32.8 us
  waiting for transfers between devices: 53.4 us -> 22.9 us
  starting transfers between devices: 40.8 us -> 20.9 us
  Pallas kernels: 44.5 us -> 36.2 us
    ppermute x19 -> x6, waiting for transfers between devices: 46 us -> 7.14 us  [send(): return lax.ppermute(v, axis, [(i, to(i)) for i in range(count)])]
    all_to_all x0 -> x1, blocking collectives: none -> 32.8 us  [per_device(): own = lax.all_to_all(parts, 'gx', 0, 0, tiled=True)]
    ppermute x19 -> x6, starting transfers between devices: 28.4 us -> 5.81 us  [send(): return lax.ppermute(v, axis, [(i, to(i)) for i in range(count)])]
    all_to_all x0 -> x1, waiting for transfers between devices: none -> 6.92 us  [per_device(): lax.all_to_all(sums.reshape((16,) + block), ('gx', 'gz'), 0, 0, tiled=Tru...]
    pallas_call x2, Pallas kernels: 19.8 us -> 13.8 us  [input_part(): call(functools.partial(input_body, len(given)), [((count, 2) + block, bf1...]
    all_to_all x0 -> x1, starting transfers between devices: none -> 3.72 us  [per_device(): lax.all_to_all(sums.reshape((16,) + block), ('gx', 'gz'), 0, 0, tiled=Tru...]
    pallas_call x4 -> x3, Pallas kernels: 12.5 us -> 10.3 us  [the longest x1 3.68 us: per_device(): call(pack_body, [((tokens, columns), f32), ((8,) + block, bf16)], [SMEM,...]
    unnamed x55 -> x22, local copies, waits for them, and re-layouts: 5.51 us -> 5.66 us
  transfers between devices with their start and end apart: 26 -> 14, of which waited for: 14 -> 11; matrix products, arithmetic and copies ran while one was open for 0% -> 0% of each run, Pallas kernels for 27% -> 27%
where the time goes in v3:
time: 122 us; the launch traced here: 121 us
  Pallas kernels  36.2 us (30%)
  blocking collectives  32.8 us (27%)
  waiting for transfers between devices  22.9 us (19%)
  starting transfers between devices  20.9 us (17%)
  local copies, waits for them, and re-layouts  6.34 us (5%)
    all_to_all x1, blocking collectives, per_device(): own = lax.all_to_all(parts, 'gx', 0, 0, tiled=True)  32.8 us
    pallas_call x2, Pallas kernels, input_part(): call(functools.partial(input_body, len(given)), [((count, 2) + block, bf1...  13.8 us
    pallas_call x1, Pallas kernels, per_device(): call(weight_body, [((4 * rows, features), bf16)], [SMEM] + [VMEM] * 4 + [...  12.2 us
    ppermute x7, starting transfers between devices, send_by_core(): return lax.ppermute(v, ('gx', 'gy', 'gz'), pairs)  11.4 us
    ppermute x7, waiting for transfers between devices, send_by_core(): return lax.ppermute(v, ('gx', 'gy', 'gz'), pairs)  8.87 us
    ppermute x6, waiting for transfers between devices, send(): return lax.ppermute(v, axis, [(i, to(i)) for i in range(count)])  7.14 us
    all_to_all x1, waiting for transfers between devices, per_device(): lax.all_to_all(sums.reshape((16,) + block), ('gx', 'gz'), 0, 0, tiled=Tru...  6.92 us
    ppermute x6, starting transfers between devices, send(): return lax.ppermute(v, axis, [(i, to(i)) for i in range(count)])  5.81 us
  transfers between devices with their start and end apart: 14, of which 11 were waited for; matrix products, arithmetic and copies ran while one was open for 0% of the time, Pallas kernels for 27%

profile of v3, /device:TPU:0, one launch (start us, length us, event | category | flops | bytes accessed | tf_op | source)
XLA Modules:
  0.0 121.2 jit_solution(10092002888825970263)
XLA Ops:
  0.6 4.0 %collective-permute-start = (bf16[64,1536]{1,0:T(8,128)(2,1)}, bf16[64,1536]{1,0:T(8,128)(2,1)S(1)}, u32[]{:S(2)}, u32[]{:S(2)}) collective-permute-start(bf16[64,1536]{1,0:T(8,128)(2,1)} %param.4), channel_id=1, source_target_pairs={{0,16},{16,0},{32,48},{48,32},{64,80},{80,64},{96,112},{112,96},{1... | collective-permute-start | bytes 589832 | tf_op jit(solution)/shard_map/ppermute | solution.py:21
  4.7 0.6 stack.47.at
  5.2 3.7 %shard_map.50 = (f32[256,1536]{1,0:T(8,128)}, bf16[8,192,256]{2,1,0:T(8,128)(2,1)}) custom-call(s32[5]{0:T(128)} %stack.47.at, bf16[256,1536]{1,0:T(8,128)(2,1)} %pre.1), custom_call_target="tpu_custom_call" | custom-call | flops 201326592 | bytes 3145728 | tf_op jit(solution)/shard_map/pallas_call | solution.py:234
  8.9 0.9 collective-permute-done
  9.8 1.0 fusion
  10.8 3.3 %collective-permute-start.2 = (bf16[2,64,1536]{2,1,0:T(8,128)(2,1)S(1)}, bf16[2,64,1536]{2,1,0:T(8,128)(2,1)S(1)}, u32[]{:S(2)}, u32[]{:S(2)}) collective-permute-start(bf16[2,64,1536]{2,1,0:T(8,128)(2,1)S(1)} %get-tuple-element.33), channel_id=1, source_target_pairs={{0,8},{1,65},{2,10},{3,67},{4,12},{5,69},{6,14},{7,71},{8,0},{9,73... | collective-permute-start | bytes 1179656 | tf_op jit(solution)/shard_map/ppermute | solution.py:53
  14.0 0.7 collective-permute-start.1
  14.7 2.6 %collective-permute-start.3 = (bf16[2,64,1536]{2,1,0:T(8,128)(2,1)S(1)}, bf16[2,64,1536]{2,1,0:T(8,128)(2,1)S(1)}, u32[]{:S(2)}, u32[]{:S(2)}) collective-permute-start(bf16[2,64,1536]{2,1,0:T(8,128)(2,1)S(1)} %get-tuple-element.33), channel_id=1, source_target_pairs={{0,12},{1,97},{2,14},{3,99},{4,0},{5,101},{6,2},{7,103},{8,4},{9,1... | collective-permute-start | bytes 1179656 | tf_op jit(solution)/shard_map/ppermute | solution.py:53
  17.3 3.0 %collective-permute-done.2 = bf16[2,64,1536]{2,1,0:T(8,128)(2,1)S(1)} collective-permute-done((bf16[2,64,1536]{2,1,0:T(8,128)(2,1)S(1)}, bf16[2,64,1536]{2,1,0:T(8,128)(2,1)S(1)}, u32[]{:S(2)}, u32[]{:S(2)}) %collective-permute-start.2) | collective-permute-done | bytes 393248 | tf_op jit(solution)/shard_map/ppermute | solution.py:53
  20.2 4.1 %collective-permute-done.1 = bf16[2,64,1536]{2,1,0:T(8,128)(2,1)S(1)} collective-permute-done((bf16[2,64,1536]{2,1,0:T(8,128)(2,1)S(1)}, bf16[2,64,1536]{2,1,0:T(8,128)(2,1)S(1)}, u32[]{:S(2)}, u32[]{:S(2)}) %collective-permute-start.1) | collective-permute-done | bytes 393248 | tf_op jit(solution)/shard_map/ppermute | solution.py:53
  24.3 0.3 collective-permute-done.3
  24.7 0.0 copy-start.3
  24.7 0.2 pad_maximum_fusion.refs_0_.refs_4_
  24.9 0.0 copy-start.1
  24.9 2.8 %collective-permute-start.5 = (bf16[2,4,64,1536]{3,2,1,0:T(8,128)(2,1)S(1)}, bf16[2,4,64,1536]{3,2,1,0:T(8,128)(2,1)S(1)}, u32[]{:S(2)}, u32[]{:S(2)}) collective-permute-start(bf16[2,4,64,1536]{3,2,1,0:T(8,128)(2,1)S(1)} %pad_maximum_fusion.refs_0_.refs_4_), channel_id=1, source_target_pairs={{0,96},{1,13},{2,98},{3,15},{4,100},{5,1},{6,102},{7,3},{8,104},{9... | collective-permute-start | bytes 4718600 | tf_op jit(solution)/shard_map/ppermute | solution.py:53
  27.7 0.0 collective-permute-start.4
  27.7 0.0 copy-done.3
  27.7 32.8 %all_to_all.10.refs_0_ = bf16[8,192,256]{2,1,0:T(8,128)(2,1)} all-to-all(bf16[8,192,256]{2,1,0:T(8,128)(2,1)S(1)} %copy-done.3), channel_id=1, replica_groups=mesh['gx'=8,'gy'=4,'gz'=4] {'gx'}, dimensions={0} | all-to-all | bytes 1572864 | tf_op jit(solution)/shard_map/all_to_all | solution.py:246
  60.6 0.0 collective-permute-done.5.refs_2_.refs_6_
  60.6 0.0 copy-start.5
  60.6 0.0 collective-permute-done.4.refs_1_.refs_5_
  60.6 0.0 copy-start.6
  60.6 0.1 slice.6
  60.6 0.0 copy-done.1
  60.7 0.1 slice.7
  60.7 1.1 copy-done.5
  61.8 0.4 copy-done.6
  62.2 0.0 collective-permute-start.7
  62.2 2.0 %collective-permute-start.6 = (bf16[1,4,64,1536]{3,2,1,0:T(8,128)(2,1)S(1)}, bf16[1,4,64,1536]{3,2,1,0:T(8,128)(2,1)S(1)}, u32[]{:S(2)}, u32[]{:S(2)}) collective-permute-start(bf16[1,4,64,1536]{3,2,1,0:T(8,128)(2,1)S(1)} %slice.6), channel_id=1, source_target_pairs={{0,32},{1,5},{2,34},{3,7},{4,36},{5,9},{6,38},{7,11},{8,40},{9,13}... | collective-permute-start | bytes 2359304 | tf_op jit(solution)/shard_map/ppermute | solution.py:53
  64.2 8.5 %shard_map.51 = (bf16[6,2,192,256]{3,2,1,0:T(8,128)(2,1)}, bf16[6,2,192,256]{3,2,1,0:T(8,128)(2,1)}) custom-call(s32[5]{0:T(128)} %stack.47.at, bf16[768,1536]{1,0:T(8,128)(2,1)} %bitcast.29, bf16[2,4,64,1536]{3,2,1,0:T(8,128)(2,1)} %copy-done.1, bf16[2,4,64,1536]{3,2,1,0:T(8,128)(2,1)} %copy-done.6, bf16[2,4,64,1536]{3,2,1,0:T(8,128)(2,1)} %copy-done.5), custom_call_target="tpu_custom_call" | custom-call | flops 3623878656 | bytes 9437184 | tf_op jit(solution)/shard_map/pallas_call | solution.py:254
  72.8 0.1 collective-permute-start.8
  72.9 1.1 collective-permute-start.10
  74.0 0.2 collective-permute-done.7.refs_1_.refs_8_
  74.2 0.0 copy-start.7
  74.2 1.2 collective-permute-done.6.refs_0_.refs_7_
  75.4 0.0 copy-done.7
  75.4 0.0 copy-start.8
  75.4 0.9 copy-done.8
  76.3 5.3 %shard_map.52 = (bf16[2,2,192,256]{3,2,1,0:T(8,128)(2,1)}, bf16[2,2,192,256]{3,2,1,0:T(8,128)(2,1)}) custom-call(s32[5]{0:T(128)} %stack.47.at, bf16[768,1536]{1,0:T(8,128)(2,1)} %bitcast.30, bf16[1,4,64,1536]{3,2,1,0:T(8,128)(2,1)} %copy-done.8, bf16[1,4,64,1536]{3,2,1,0:T(8,128)(2,1)} %copy-done.7), custom_call_target="tpu_custom_call" | custom-call | flops 1207959552 | bytes 4718592 | tf_op jit(solution)/shard_map/pallas_call | solution.py:254
  81.6 0.1 collective-permute-start.9
  81.7 1.9 %collective-permute-done.9.other2 = bf16[2,2,192,256]{3,2,1,0:T(8,128)(2,1)S(1)} collective-permute-done((bf16[2,2,192,256]{3,2,1,0:T(8,128)(2,1)}, bf16[2,2,192,256]{3,2,1,0:T(8,128)(2,1)S(1)}, u32[]{:S(2)}, u32[]{:S(2)}) %collective-permute-start.9) | collective-permute-done | bytes 393248 | tf_op jit(solution)/shard_map/ppermute | solution.py:21
  83.6 0.0 copy-start.4
  83.6 0.0 collective-permute-done.8.other
  83.6 0.0 copy-start.2
  83.6 0.8 copy-done.4
  84.3 0.5 copy-done.2
  84.8 3.4 %shard_map.53 = bf16[8,2,192,256]{3,2,1,0:T(8,128)(2,1)} custom-call(s32[5]{0:T(128)} %stack.47.at, bf16[6,2,192,256]{3,2,1,0:T(8,128)(2,1)} %get-tuple-element.23.mine, bf16[2,2,192,256]{3,2,1,0:T(8,128)(2,1)} %get-tuple-element.24.mine2, bf16[6,2,192,256]{3,2,1,0:T(8,128)(2,1)} %copy-done.2, bf16[2,2,192,256]{3,2,1,0:T(8,128)(2,1)} %copy-done.4), custom_call_target="tpu_custom_call" | custom-call | flops 1572864 | bytes 4718592 | tf_op jit(solution)/shard_map/pallas_call | solution.py:272
  88.2 3.7 %all-to-all-start.1 = ((bf16[16,192,256]{2,1,0:T(8,128)(2,1)}), bf16[16,192,256]{2,1,0:T(8,128)(2,1)S(1)}, u32[]{:S(2)}, u32[]{:S(2)}) async-start(bf16[16,192,256]{2,1,0:T(8,128)(2,1)} %bitcast.22), calls=%async_computation.1 | async-start | bytes 3145728 | tf_op jit(solution)/shard_map/all_to_all | solution.py:281
  91.9 1.2 %collective-permute-done.10.refs_1_ = bf16[8,192,256]{2,1,0:T(8,128)(2,1)} collective-permute-done((bf16[8,192,256]{2,1,0:T(8,128)(2,1)}, bf16[8,192,256]{2,1,0:T(8,128)(2,1)}, u32[]{:S(2)}, u32[]{:S(2)}) %collective-permute-start.10) | collective-permute-done | bytes 786464 | tf_op jit(solution)/shard_map/ppermute | solution.py:21
  93.1 0.0 collective-permute-start.11
  93.1 0.5 collective-permute-start.12
  93.6 2.0 %collective-permute-done.11.refs_2_ = bf16[8,192,256]{2,1,0:T(8,128)(2,1)S(1)} collective-permute-done((bf16[8,192,256]{2,1,0:T(8,128)(2,1)}, bf16[8,192,256]{2,1,0:T(8,128)(2,1)S(1)}, u32[]{:S(2)}, u32[]{:S(2)}) %collective-permute-start.11) | collective-permute-done | bytes 786464 | tf_op jit(solution)/shard_map/ppermute | solution.py:21
  95.6 0.0 copy-start.9
  95.6 1.1 collective-permute-done.12.refs_3_
  96.8 0.0 copy-done.9
  96.8 0.0 copy-start.10
  96.8 0.9 copy-done.10
  97.7 12.2 %shard_map.54 = bf16[768,1536]{1,0:T(8,128)(2,1)} custom-call(s32[5]{0:T(128)} %stack.47.at, bf16[8,192,256]{2,1,0:T(8,128)(2,1)} %all_to_all.10.refs_0_, bf16[8,192,256]{2,1,0:T(8,128)(2,1)} %collective-permute-done.10.refs_1_, bf16[8,192,256]{2,1,0:T(8,128)(2,1)} %copy-done.9, bf16[8,192,256]{2,1,0:T(8,128)(2,1)} %copy-done.10, ...), custom_call_target="tpu_custom_call" | custom-call | flops 4831838208 | bytes 11010048 | tf_op jit(solution)/shard_map/pallas_call | solution.py:286
  109.9 6.9 %all-to-all-done.1 = bf16[16,192,256]{2,1,0:T(8,128)(2,1)S(1)} async-done(((bf16[16,192,256]{2,1,0:T(8,128)(2,1)}), bf16[16,192,256]{2,1,0:T(8,128)(2,1)S(1)}, u32[]{:S(2)}, u32[]{:S(2)}) %all-to-all-start.1) | async-done | bytes 1572896 | tf_op jit(solution)/shard_map/all_to_all | solution.py:281
  116.8 0.0 copy-start
  116.8 1.1 copy-done
  117.9 3.2 %shard_map.55 = bf16[256,1536]{1,0:T(8,128)(2,1)} custom-call(s32[5]{0:T(128)} %stack.47.at, f32[256,1536]{1,0:T(8,128)} %get-tuple-element.17.slope, bf16[8,2,192,256]{3,2,1,0:T(8,128)(2,1)} %bitcast.23), custom_call_target="tpu_custom_call" | custom-call | flops 201326592 | bytes 3145728 | tf_op jit(solution)/shard_map/pallas_call | solution.py:294
Async XLA Ops:
  0.6 9.2 %collective-permute-start = (bf16[64,1536]{1,0:T(8,128)(2,1)}, bf16[64,1536]{1,0:T(8,128)(2,1)S(1)}, u32[]{:S(2)}, u32[]{:S(2)}) collective-permute-start(bf16[64,1536]{1,0:T(8,128)(2,1)} %param.4), channel_id=1, source_target_pairs={{0,16},{16,0},{32,48},{48,32},{64,80},{80,64},{96,112},{112,96},{1... | collective-permute-start | bytes 589832 | tf_op jit(solution)/shard_map/ppermute | solution.py:21
  10.8 9.5 %collective-permute-start.2 = (bf16[2,64,1536]{2,1,0:T(8,128)(2,1)S(1)}, bf16[2,64,1536]{2,1,0:T(8,128)(2,1)S(1)}, u32[]{:S(2)}, u32[]{:S(2)}) collective-permute-start(bf16[2,64,1536]{2,1,0:T(8,128)(2,1)S(1)} %get-tuple-element.33), channel_id=1, source_target_pairs={{0,8},{1,65},{2,10},{3,67},{4,12},{5,69},{6,14},{7,71},{8,0},{9,73... | collective-permute-start | bytes 1179656 | tf_op jit(solution)/shard_map/ppermute | solution.py:53
  14.0 10.3 %collective-permute-start.1 = (bf16[2,64,1536]{2,1,0:T(8,128)(2,1)S(1)}, bf16[2,64,1536]{2,1,0:T(8,128)(2,1)S(1)}, u32[]{:S(2)}, u32[]{:S(2)}) collective-permute-start(bf16[2,64,1536]{2,1,0:T(8,128)(2,1)S(1)} %get-tuple-element.33), channel_id=1, source_target_pairs={{0,4},{1,33},{2,6},{3,35},{4,8},{5,37},{6,10},{7,39},{8,12},{9,41}... | collective-permute-start | bytes 1179656 | tf_op jit(solution)/shard_map/ppermute | solution.py:53
  14.7 10.0 %collective-permute-start.3 = (bf16[2,64,1536]{2,1,0:T(8,128)(2,1)S(1)}, bf16[2,64,1536]{2,1,0:T(8,128)(2,1)S(1)}, u32[]{:S(2)}, u32[]{:S(2)}) collective-permute-start(bf16[2,64,1536]{2,1,0:T(8,128)(2,1)S(1)} %get-tuple-element.33), channel_id=1, source_target_pairs={{0,12},{1,97},{2,14},{3,99},{4,0},{5,101},{6,2},{7,103},{8,4},{9,1... | collective-permute-start | bytes 1179656 | tf_op jit(solution)/shard_map/ppermute | solution.py:53
  24.7 3.0 %copy-start.3 = (bf16[8,192,256]{2,1,0:T(8,128)(2,1)S(1)}, bf16[8,192,256]{2,1,0:T(8,128)(2,1)}, u32[]{:S(2)}) copy-start(bf16[8,192,256]{2,1,0:T(8,128)(2,1)} %get-tuple-element.20) | copy-start | bytes 2359300
  24.9 35.8 %copy-start.1 = (bf16[2,4,64,1536]{3,2,1,0:T(8,128)(2,1)}, bf16[2,4,64,1536]{3,2,1,0:T(8,128)(2,1)S(1)}, u32[]{:S(2)}) copy-start(bf16[2,4,64,1536]{3,2,1,0:T(8,128)(2,1)S(1)} %pad_maximum_fusion.refs_0_.refs_4_) | copy-start | bytes 4718596
  24.9 35.7 %collective-permute-start.5 = (bf16[2,4,64,1536]{3,2,1,0:T(8,128)(2,1)S(1)}, bf16[2,4,64,1536]{3,2,1,0:T(8,128)(2,1)S(1)}, u32[]{:S(2)}, u32[]{:S(2)}) collective-permute-start(bf16[2,4,64,1536]{3,2,1,0:T(8,128)(2,1)S(1)} %pad_maximum_fusion.refs_0_.refs_4_), channel_id=1, source_target_pairs={{0,96},{1,13},{2,98},{3,15},{4,100},{5,1},{6,102},{7,3},{8,104},{9... | collective-permute-start | bytes 4718600 | tf_op jit(solution)/shard_map/ppermute | solution.py:53
  27.7 32.8 %collective-permute-start.4 = (bf16[2,4,64,1536]{3,2,1,0:T(8,128)(2,1)S(1)}, bf16[2,4,64,1536]{3,2,1,0:T(8,128)(2,1)S(1)}, u32[]{:S(2)}, u32[]{:S(2)}) collective-permute-start(bf16[2,4,64,1536]{3,2,1,0:T(8,128)(2,1)S(1)} %pad_maximum_fusion.refs_0_.refs_4_), channel_id=1, source_target_pairs={{0,32},{1,5},{2,34},{3,7},{4,36},{5,9},{6,38},{7,11},{8,40},{9,13}... | collective-permute-start | bytes 4718600 | tf_op jit(solution)/shard_map/ppermute | solution.py:53
  60.6 1.2 copy-start.5
  60.6 1.6 %copy-start.6 = (bf16[2,4,64,1536]{3,2,1,0:T(8,128)(2,1)}, bf16[2,4,64,1536]{3,2,1,0:T(8,128)(2,1)S(1)}, u32[]{:S(2)}) copy-start(bf16[2,4,64,1536]{3,2,1,0:T(8,128)(2,1)S(1)} %collective-permute-done.4.refs_1_.refs_5_) | copy-start | bytes 4718596
  62.2 12.0 %collective-permute-start.7 = (bf16[1,4,64,1536]{3,2,1,0:T(8,128)(2,1)S(1)}, bf16[1,4,64,1536]{3,2,1,0:T(8,128)(2,1)S(1)}, u32[]{:S(2)}, u32[]{:S(2)}) collective-permute-start(bf16[1,4,64,1536]{3,2,1,0:T(8,128)(2,1)S(1)} %slice.7), channel_id=1, source_target_pairs={{0,96},{1,13},{2,98},{3,15},{4,100},{5,1},{6,102},{7,3},{8,104},{9... | collective-permute-start | bytes 2359304 | tf_op jit(solution)/shard_map/ppermute | solution.py:53
  62.2 13.2 %collective-permute-start.6 = (bf16[1,4,64,1536]{3,2,1,0:T(8,128)(2,1)S(1)}, bf16[1,4,64,1536]{3,2,1,0:T(8,128)(2,1)S(1)}, u32[]{:S(2)}, u32[]{:S(2)}) collective-permute-start(bf16[1,4,64,1536]{3,2,1,0:T(8,128)(2,1)S(1)} %slice.6), channel_id=1, source_target_pairs={{0,32},{1,5},{2,34},{3,7},{4,36},{5,9},{6,38},{7,11},{8,40},{9,13}... | collective-permute-start | bytes 2359304 | tf_op jit(solution)/shard_map/ppermute | solution.py:53
  72.8 10.8 %collective-permute-start.8 = (bf16[6,2,192,256]{3,2,1,0:T(8,128)(2,1)}, bf16[6,2,192,256]{3,2,1,0:T(8,128)(2,1)S(1)}, u32[]{:S(2)}, u32[]{:S(2)}) collective-permute-start(bf16[6,2,192,256]{3,2,1,0:T(8,128)(2,1)} %get-tuple-element.25), channel_id=1, source_target_pairs={{0,1},{1,0},{2,3},{3,2},{4,5},{5,4},{6,7},{7,6},{8,9},{9,8},{10,11... | collective-permute-start | bytes 3538952 | tf_op jit(solution)/shard_map/ppermute | solution.py:21
  72.9 20.3 %collective-permute-start.10 = (bf16[8,192,256]{2,1,0:T(8,128)(2,1)}, bf16[8,192,256]{2,1,0:T(8,128)(2,1)}, u32[]{:S(2)}, u32[]{:S(2)}) collective-permute-start(bf16[8,192,256]{2,1,0:T(8,128)(2,1)} %all_to_all.10.refs_0_), channel_id=1, source_target_pairs={{0,2},{1,3},{2,0},{3,1},{4,6},{5,7},{6,4},{7,5},{8,10},{9,11},{10,... | collective-permute-start | bytes 2359304 | tf_op jit(solution)/shard_map/ppermute | solution.py:21
  74.2 1.2 %copy-start.7 = (bf16[1,4,64,1536]{3,2,1,0:T(8,128)(2,1)}, bf16[1,4,64,1536]{3,2,1,0:T(8,128)(2,1)S(1)}, u32[]{:S(2)}) copy-start(bf16[1,4,64,1536]{3,2,1,0:T(8,128)(2,1)S(1)} %collective-permute-done.7.refs_1_.refs_8_) | copy-start | bytes 2359300
  75.4 0.9 copy-start.8
  81.6 2.0 %collective-permute-start.9 = (bf16[2,2,192,256]{3,2,1,0:T(8,128)(2,1)}, bf16[2,2,192,256]{3,2,1,0:T(8,128)(2,1)S(1)}, u32[]{:S(2)}, u32[]{:S(2)}) collective-permute-start(bf16[2,2,192,256]{3,2,1,0:T(8,128)(2,1)} %get-tuple-element.26), channel_id=1, source_target_pairs={{0,1},{1,0},{2,3},{3,2},{4,5},{5,4},{6,7},{7,6},{8,9},{9,8},{10,11... | collective-permute-start | bytes 1179656 | tf_op jit(solution)/shard_map/ppermute | solution.py:21
  83.6 0.8 copy-start.4
  83.6 1.2 %copy-start.2 = (bf16[6,2,192,256]{3,2,1,0:T(8,128)(2,1)}, bf16[6,2,192,256]{3,2,1,0:T(8,128)(2,1)S(1)}, u32[]{:S(2)}) copy-start(bf16[6,2,192,256]{3,2,1,0:T(8,128)(2,1)S(1)} %collective-permute-done.8.other) | copy-start | bytes 3538948
  88.2 28.6 %all-to-all-start.1 = ((bf16[16,192,256]{2,1,0:T(8,128)(2,1)}), bf16[16,192,256]{2,1,0:T(8,128)(2,1)S(1)}, u32[]{:S(2)}, u32[]{:S(2)}) async-start(bf16[16,192,256]{2,1,0:T(8,128)(2,1)} %bitcast.22), calls=%async_computation.1 | async-start | bytes 3145728 | tf_op jit(solution)/shard_map/all_to_all | solution.py:281
  93.1 2.5 %collective-permute-start.11 = (bf16[8,192,256]{2,1,0:T(8,128)(2,1)}, bf16[8,192,256]{2,1,0:T(8,128)(2,1)S(1)}, u32[]{:S(2)}, u32[]{:S(2)}) collective-permute-start(bf16[8,192,256]{2,1,0:T(8,128)(2,1)} %all_to_all.10.refs_0_), channel_id=1, source_target_pairs={{0,1},{1,0},{2,3},{3,2},{4,5},{5,4},{6,7},{7,6},{8,9},{9,8},{10,11... | collective-permute-start | bytes 2359304 | tf_op jit(solution)/shard_map/ppermute | solution.py:21
  93.1 3.6 %collective-permute-start.12 = (bf16[8,192,256]{2,1,0:T(8,128)(2,1)}, bf16[8,192,256]{2,1,0:T(8,128)(2,1)S(1)}, u32[]{:S(2)}, u32[]{:S(2)}) collective-permute-start(bf16[8,192,256]{2,1,0:T(8,128)(2,1)} %collective-permute-done.10.refs_1_), channel_id=1, source_target_pairs={{0,1},{1,0},{2,3},{3,2},{4,5},{5,4},{6,7},{7,6},{8,9},{9,8},{10,11... | collective-permute-start | bytes 2359304 | tf_op jit(solution)/shard_map/ppermute | solution.py:21
  95.6 1.1 copy-start.9
  96.8 0.9 copy-start.10
  116.8 1.1 copy-start

commit v4 on v3

--- a/solution.py
+++ b/solution.py
@@ -14,7 +14,7 @@
 MIB = 1024 * 1024
 VMEM = pl.BlockSpec(memory_space=pltpu.VMEM)
 SMEM = pl.BlockSpec(memory_space=pltpu.SMEM)
-ANY = pl.BlockSpec(memory_space=pl.ANY)
+HBM = pl.BlockSpec(memory_space=pltpu.HBM)
 
 
 def send(v, axis, count, to):
@@ -240,11 +240,12 @@
 
     other, parts = lax.optimization_barrier((swap_z_hi(grad_out), parts))
     both = jnp.stack([grad_out, other])
-    p0 = jnp.stack([both] + [send_by_core(both, k, True) for k in (1, 2, 3)], 1)
+    first = [send_by_core(both, k, True) for k in (1, 2, 3)]
+    own = lax.all_to_all(parts, "gx", 0, 0, tiled=True)
+    first, own = lax.optimization_barrier((first, own))
+    p0 = jnp.stack([both] + first, 1)
     p1, p3 = send_by_core(p0, 1, False), send_by_core(p0, 3, False)
 
-    own = lax.all_to_all(parts, "gx", 0, 0, tiled=True)
-    p1, p3, own = lax.optimization_barrier((p1, p3, own))
     p2p, p2m = send_by_core(p1[:1], 1, False), send_by_core(p3[1:], 3, False)
     pieces = p0, p1, p3, p2p, p2m
     far = swap_z_lo(own)
@@ -254,9 +255,9 @@
         return call(
             functools.partial(input_body, len(given)),
             [((count, 2) + block, bf16)] * 2,
-            [SMEM, VMEM] + [ANY] * len(given),
+            [SMEM, VMEM] + [HBM] * len(given),
             (product * count // 8, 2 * (4 * rows * features + count * (4 * rows + features) * tokens)),
-            out_specs=[ANY] * 2,
+            out_specs=[HBM] * 2,
             scratch=[
                 pltpu.VMEM((count, 4, tokens // 4, features), bf16),
                 pltpu.VMEM((2, 2, 2) + block, bf16),
@@ -265,8 +266,11 @@
             ],
         )(at, w, *given)
 
-    mine, theirs = input_part(p0, p1, p3)
+    early = lax.optimization_barrier((p0, p1, p3, far))
+    mine, theirs = input_part(*early[:3])
     other = swap_core(theirs)
+    hidden = [own, far, swap_core(own), swap_core(far)]
+    p2p, p2m, hidden = lax.optimization_barrier((p2p, p2m, hidden))
     mine2, theirs2 = input_part(p2p, p2m)
     size = 2 * 4 * rows * tokens
     (sums,) = call(
@@ -274,19 +278,18 @@
         [((8, 2) + block, bf16)],
         [SMEM] + [VMEM] * 4,
         (4 * size, 12 * size),
-        out_specs=[ANY],
+        out_specs=[HBM],
         scratch=[pltpu.VMEM((8, 2) + block, bf16), pltpu.SemaphoreType.DMA((8,))],
     )(at, mine, mine2, other, swap_core(theirs2))
     same_core = [[2 * (2 * i + k) + c for i in range(8) for k in range(2)] for c in range(2)]
     back = lax.all_to_all(
         sums.reshape((16,) + block), ("gx", "gz"), 0, 0, tiled=True, axis_index_groups=same_core
     )
-    own, far, _ = lax.optimization_barrier((own, far, sums))
-    hidden = [own, far, swap_core(own), swap_core(far)]
+    hidden, _ = lax.optimization_barrier((hidden, sums))
     (weight_grad,) = call(
         weight_body,
         [((4 * rows, features), bf16)],
-        [SMEM] + [VMEM] * 4 + [ANY] * 5,
+        [SMEM] + [VMEM] * 4 + [HBM] * 5,
         (product, 2 * (8 * rows * features + 2048 * features)),
         scratch=grad_scratch,
     )(at, *hidden, *pieces)

time: 122 us -> 119 us (0.975)
  blocking collectives: 32.8 us -> 0 us
  waiting for transfers between devices: 22.9 us -> 47.4 us
  starting transfers between devices: 20.9 us -> 30.6 us
  local copies, waits for them, and re-layouts: 6.34 us -> 3.38 us
    all_to_all x1 -> x0, blocking collectives: 32.8 us -> none  [per_device(): own = lax.all_to_all(parts, 'gx', 0, 0, tiled=True)]
    ppermute x6, waiting for transfers between devices: 7.14 us -> 20.5 us  [send(): return lax.ppermute(v, axis, [(i, to(i)) for i in range(count)])]
    all_to_all x0 -> x1, starting transfers between devices: none -> 6.98 us  [per_device(): own = lax.all_to_all(parts, 'gx', 0, 0, tiled=True)]
    all_to_all x1, waiting for transfers between devices: 6.92 us -> 12.8 us  [per_device(): lax.all_to_all(sums.reshape((16,) + block), ('gx', 'gz'), 0, 0, tiled=Tru...]
    all_to_all x0 -> x1, waiting for transfers between devices: none -> 5.05 us  [per_device(): own = lax.all_to_all(parts, 'gx', 0, 0, tiled=True)]
    ppermute x6, starting transfers between devices: 5.81 us -> 9.11 us  [send(): return lax.ppermute(v, axis, [(i, to(i)) for i in range(count)])]
    unnamed x22 -> x18, local copies, waits for them, and re-layouts: 5.66 us -> 2.62 us
  transfers between devices with their start and end apart: 14 -> 15, of which waited for: 11 -> 9; matrix products, arithmetic and copies ran while one was open for 0% -> 1% of each run, Pallas kernels for 27% -> 25%
where the time goes in v4:
time: 119 us
  waiting for transfers between devices  47.4 us (40%)
  Pallas kernels  36.2 us (30%)
  starting transfers between devices  30.6 us (26%)
  local copies, waits for them, and re-layouts  3.38 us (3%)
    ppermute x6, waiting for transfers between devices, send(): return lax.ppermute(v, axis, [(i, to(i)) for i in range(count)])  20.5 us
    pallas_call x2, Pallas kernels, input_part(): call(functools.partial(input_body, len(given)), [((count, 2) + block, bf1...  13.8 us
    all_to_all x1, waiting for transfers between devices, per_device(): lax.all_to_all(sums.reshape((16,) + block), ('gx', 'gz'), 0, 0, tiled=Tru...  12.8 us
    pallas_call x1, Pallas kernels, per_device(): call(weight_body, [((4 * rows, features), bf16)], [SMEM] + [VMEM] * 4 + [...  12.2 us
    ppermute x7, starting transfers between devices, send_by_core(): return lax.ppermute(v, ('gx', 'gy', 'gz'), pairs)  10.8 us
    ppermute x6, starting transfers between devices, send(): return lax.ppermute(v, axis, [(i, to(i)) for i in range(count)])  9.11 us
    ppermute x7, waiting for transfers between devices, send_by_core(): return lax.ppermute(v, ('gx', 'gy', 'gz'), pairs)  9.07 us
    all_to_all x1, starting transfers between devices, per_device(): own = lax.all_to_all(parts, 'gx', 0, 0, tiled=True)  6.98 us
  transfers between devices with their start and end apart: 15, of which 9 were waited for; matrix products, arithmetic and copies ran while one was open for 1% of the time, Pallas kernels for 25%

profile of v4, /device:TPU:0, one launch (start us, length us, event | category | flops | bytes accessed | tf_op | source)
XLA Modules:
  0.0 118.6 jit_solution(17230954754535595782)
XLA Ops:
  0.6 0.0 copy-start.7
  0.6 4.0 %collective-permute-start = (bf16[64,1536]{1,0:T(8,128)(2,1)}, bf16[64,1536]{1,0:T(8,128)(2,1)S(1)}, u32[]{:S(2)}, u32[]{:S(2)}) collective-permute-start(bf16[64,1536]{1,0:T(8,128)(2,1)} %param.4), channel_id=1, source_target_pairs={{0,16},{16,0},{32,48},{48,32},{64,80},{80,64},{96,112},{112,96},{1... | collective-permute-start | bytes 589832 | tf_op jit(solution)/shard_map/ppermute | solution.py:21
  4.7 0.7 stack.47.at
  5.3 3.7 %shard_map.50 = (f32[256,1536]{1,0:T(8,128)}, bf16[8,192,256]{2,1,0:T(8,128)(2,1)}) custom-call(s32[5]{0:T(128)} %stack.47.at, bf16[256,1536]{1,0:T(8,128)(2,1)} %pre.1), custom_call_target="tpu_custom_call" | custom-call | flops 201326592 | bytes 3145728 | tf_op jit(solution)/shard_map/pallas_call | solution.py:234
  9.0 0.8 collective-permute-done
  9.8 7.0 %all-to-all-start = ((bf16[8,192,256]{2,1,0:T(8,128)(2,1)}), bf16[8,192,256]{2,1,0:T(8,128)(2,1)S(1)}, u32[]{:S(2)}, u32[]{:S(2)}) async-start(bf16[8,192,256]{2,1,0:T(8,128)(2,1)} %get-tuple-element.32), calls=%async_computation | async-start | bytes 1572864 | tf_op jit(solution)/shard_map/all_to_all | solution.py:244
  16.8 0.0 copy-done.7
  16.8 0.1 fusion
  16.8 3.3 %collective-permute-start.2 = (bf16[2,64,1536]{2,1,0:T(8,128)(2,1)S(1)}, bf16[2,64,1536]{2,1,0:T(8,128)(2,1)S(1)}, u32[]{:S(2)}, u32[]{:S(2)}) collective-permute-start(bf16[2,64,1536]{2,1,0:T(8,128)(2,1)S(1)} %get-tuple-element.57), channel_id=1, source_target_pairs={{0,8},{1,65},{2,10},{3,67},{4,12},{5,69},{6,14},{7,71},{8,0},{9,73... | collective-permute-start | bytes 1179656 | tf_op jit(solution)/shard_map/ppermute | solution.py:53
  20.1 0.7 collective-permute-start.1
  20.8 2.6 %collective-permute-start.3 = (bf16[2,64,1536]{2,1,0:T(8,128)(2,1)S(1)}, bf16[2,64,1536]{2,1,0:T(8,128)(2,1)S(1)}, u32[]{:S(2)}, u32[]{:S(2)}) collective-permute-start(bf16[2,64,1536]{2,1,0:T(8,128)(2,1)S(1)} %get-tuple-element.57), channel_id=1, source_target_pairs={{0,12},{1,97},{2,14},{3,99},{4,0},{5,101},{6,2},{7,103},{8,4},{9,1... | collective-permute-start | bytes 1179656 | tf_op jit(solution)/shard_map/ppermute | solution.py:53
  23.4 3.0 %collective-permute-done.2 = bf16[2,64,1536]{2,1,0:T(8,128)(2,1)S(1)} collective-permute-done((bf16[2,64,1536]{2,1,0:T(8,128)(2,1)S(1)}, bf16[2,64,1536]{2,1,0:T(8,128)(2,1)S(1)}, u32[]{:S(2)}, u32[]{:S(2)}) %collective-permute-start.2) | collective-permute-done | bytes 393248 | tf_op jit(solution)/shard_map/ppermute | solution.py:53
  26.3 4.1 %collective-permute-done.1 = bf16[2,64,1536]{2,1,0:T(8,128)(2,1)S(1)} collective-permute-done((bf16[2,64,1536]{2,1,0:T(8,128)(2,1)S(1)}, bf16[2,64,1536]{2,1,0:T(8,128)(2,1)S(1)}, u32[]{:S(2)}, u32[]{:S(2)}) %collective-permute-start.1) | collective-permute-done | bytes 393248 | tf_op jit(solution)/shard_map/ppermute | solution.py:53
  30.4 0.3 collective-permute-done.3
  30.8 5.0 %all-to-all-done.refs_0_ = bf16[8,192,256]{2,1,0:T(8,128)(2,1)S(1)} async-done(((bf16[8,192,256]{2,1,0:T(8,128)(2,1)}), bf16[8,192,256]{2,1,0:T(8,128)(2,1)S(1)}, u32[]{:S(2)}, u32[]{:S(2)}) %all-to-all-start) | async-done | bytes 786464 | tf_op jit(solution)/shard_map/all_to_all | solution.py:244
  35.8 0.0 copy-start.3
  35.8 0.2 pad_maximum_fusion.refs_0_.refs_4_
  36.0 0.0 copy-start.1
  36.0 0.3 collective-permute-start.5
  36.3 1.8 %collective-permute-start.4 = (bf16[2,4,64,1536]{3,2,1,0:T(8,128)(2,1)S(1)}, bf16[2,4,64,1536]{3,2,1,0:T(8,128)(2,1)S(1)}, u32[]{:S(2)}, u32[]{:S(2)}) collective-permute-start(bf16[2,4,64,1536]{3,2,1,0:T(8,128)(2,1)S(1)} %pad_maximum_fusion.refs_0_.refs_4_), channel_id=1, source_target_pairs={{0,32},{1,5},{2,34},{3,7},{4,36},{5,9},{6,38},{7,11},{8,40},{9,13}... | collective-permute-start | bytes 4718600 | tf_op jit(solution)/shard_map/ppermute | solution.py:53
  38.1 1.0 collective-permute-start.6
  39.1 0.0 copy-done.3
  39.1 1.0 collective-permute-start.9
  40.1 18.2 %collective-permute-done.6.refs_1_ = bf16[8,192,256]{2,1,0:T(8,128)(2,1)S(1)} collective-permute-done((bf16[8,192,256]{2,1,0:T(8,128)(2,1)S(1)}, bf16[8,192,256]{2,1,0:T(8,128)(2,1)S(1)}, u32[]{:S(2)}, u32[]{:S(2)}) %collective-permute-start.6) | collective-permute-done | bytes 786464 | tf_op jit(solution)/shard_map/ppermute | solution.py:21
  58.3 0.0 copy-start.8
  58.3 0.1 collective-permute-start.10
  58.4 0.0 collective-permute-done.5.refs_2_.refs_6_
  58.4 0.0 copy-start.5
  58.4 0.1 slice.9
  58.4 1.3 %collective-permute-start.8 = (bf16[1,4,64,1536]{3,2,1,0:T(8,128)(2,1)S(1)}, bf16[1,4,64,1536]{3,2,1,0:T(8,128)(2,1)}, u32[]{:S(2)}, u32[]{:S(2)}) collective-permute-start(bf16[1,4,64,1536]{3,2,1,0:T(8,128)(2,1)S(1)} %slice.9), channel_id=1, source_target_pairs={{0,96},{1,13},{2,98},{3,15},{4,100},{5,1},{6,102},{7,3},{8,104},{9... | collective-permute-start | bytes 2359304 | tf_op jit(solution)/shard_map/ppermute | solution.py:53
  59.7 0.0 collective-permute-done.4.refs_1_.refs_5_
  59.7 0.0 copy-start.6
  59.7 0.1 slice.8
  59.8 0.9 collective-permute-start.7
  60.7 0.0 copy-done.1
  60.7 0.0 copy-done.5
  60.7 0.2 copy-done.6
  60.9 8.5 %shard_map.51 = (bf16[6,2,192,256]{3,2,1,0:T(8,128)(2,1)}, bf16[6,2,192,256]{3,2,1,0:T(8,128)(2,1)}) custom-call(s32[5]{0:T(128)} %stack.47.at, bf16[768,1536]{1,0:T(8,128)(2,1)} %bitcast.29, bf16[2,4,64,1536]{3,2,1,0:T(8,128)(2,1)} %copy-done.1, bf16[2,4,64,1536]{3,2,1,0:T(8,128)(2,1)} %copy-done.6, bf16[2,4,64,1536]{3,2,1,0:T(8,128)(2,1)} %copy-done.5), custom_call_target="tpu_custom_call" | custom-call | flops 3623878656 | bytes 9437184 | tf_op jit(solution)/shard_map/pallas_call | solution.py:255
  69.4 0.0 copy-done.8
  69.4 2.1 %collective-permute-start.11 = (bf16[6,2,192,256]{3,2,1,0:T(8,128)(2,1)}, bf16[6,2,192,256]{3,2,1,0:T(8,128)(2,1)S(1)}, u32[]{:S(2)}, u32[]{:S(2)}) collective-permute-start(bf16[6,2,192,256]{3,2,1,0:T(8,128)(2,1)} %get-tuple-element.44), channel_id=1, source_target_pairs={{0,1},{1,0},{2,3},{3,2},{4,5},{5,4},{6,7},{7,6},{8,9},{9,8},{10,11... | collective-permute-start | bytes 3538952 | tf_op jit(solution)/shard_map/ppermute | solution.py:21
  71.5 0.0 collective-permute-done.9.refs_2_
  71.5 0.0 collective-permute-done.10.refs_3_
  71.5 0.0 collective-permute-done.8.refs_1_.refs_8_
  71.5 1.7 %collective-permute-done.7.refs_0_.refs_7_ = bf16[1,4,64,1536]{3,2,1,0:T(8,128)(2,1)} collective-permute-done((bf16[1,4,64,1536]{3,2,1,0:T(8,128)(2,1)S(1)}, bf16[1,4,64,1536]{3,2,1,0:T(8,128)(2,1)}, u32[]{:S(2)}, u32[]{:S(2)}) %collective-permute-start.7) | collective-permute-done | bytes 786464 | tf_op jit(solution)/shard_map/ppermute | solution.py:53
  73.2 5.2 %shard_map.52 = (bf16[2,2,192,256]{3,2,1,0:T(8,128)(2,1)}, bf16[2,2,192,256]{3,2,1,0:T(8,128)(2,1)}) custom-call(s32[5]{0:T(128)} %stack.47.at, bf16[768,1536]{1,0:T(8,128)(2,1)} %bitcast.30, bf16[1,4,64,1536]{3,2,1,0:T(8,128)(2,1)} %collective-permute-done.7.refs_0_.refs_7_, bf16[1,4,64,1536]{3,2,1,0:T(8,128)(2,1)} %collective-permute-done.8.refs_1_.refs_8_), custom_call_target="tpu_custom_call" | custom-call | flops 1207959552 | bytes 4718592 | tf_op jit(solution)/shard_map/pallas_call | solution.py:255
  78.4 0.9 collective-permute-start.12
  79.3 1.6 %collective-permute-done.12.other2 = bf16[2,2,192,256]{3,2,1,0:T(8,128)(2,1)S(1)} collective-permute-done((bf16[2,2,192,256]{3,2,1,0:T(8,128)(2,1)}, bf16[2,2,192,256]{3,2,1,0:T(8,128)(2,1)S(1)}, u32[]{:S(2)}, u32[]{:S(2)}) %collective-permute-start.12) | collective-permute-done | bytes 393248 | tf_op jit(solution)/shard_map/ppermute | solution.py:21
  80.9 0.0 copy-start.4
  80.9 0.0 collective-permute-done.11.other
  80.9 0.0 copy-start.2
  80.9 0.7 copy-done.4
  81.6 0.5 copy-done.2
  82.1 3.4 %shard_map.53 = bf16[8,2,192,256]{3,2,1,0:T(8,128)(2,1)} custom-call(s32[5]{0:T(128)} %stack.47.at, bf16[6,2,192,256]{3,2,1,0:T(8,128)(2,1)} %get-tuple-element.40.mine, bf16[2,2,192,256]{3,2,1,0:T(8,128)(2,1)} %get-tuple-element.43.mine2, bf16[6,2,192,256]{3,2,1,0:T(8,128)(2,1)} %copy-done.2, bf16[2,2,192,256]{3,2,1,0:T(8,128)(2,1)} %copy-done.4), custom_call_target="tpu_custom_call" | custom-call | flops 1572864 | bytes 4718592 | tf_op jit(solution)/shard_map/pallas_call | solution.py:276
  85.5 3.7 %all-to-all-start.1 = ((bf16[16,192,256]{2,1,0:T(8,128)(2,1)}), bf16[16,192,256]{2,1,0:T(8,128)(2,1)S(1)}, u32[]{:S(2)}, u32[]{:S(2)}) async-start(bf16[16,192,256]{2,1,0:T(8,128)(2,1)} %bitcast.22), calls=%async_computation.1 | async-start | bytes 3145728 | tf_op jit(solution)/shard_map/all_to_all | solution.py:285
  89.2 12.2 %shard_map.54 = bf16[768,1536]{1,0:T(8,128)(2,1)} custom-call(s32[5]{0:T(128)} %stack.47.at, bf16[8,192,256]{2,1,0:T(8,128)(2,1)} %copy-done.3, bf16[8,192,256]{2,1,0:T(8,128)(2,1)} %copy-done.8, bf16[8,192,256]{2,1,0:T(8,128)(2,1)} %collective-permute-done.9.refs_2_, bf16[8,192,256]{2,1,0:T(8,128)(2,1)} %collective-permute-done.10.refs_3_, ...), custom_call_target="tpu_custom_call" | custom-call | flops 4831838208 | bytes 11010048 | tf_op jit(solution)/shard_map/pallas_call | solution.py:289
  101.4 12.8 %all-to-all-done.1 = bf16[16,192,256]{2,1,0:T(8,128)(2,1)S(1)} async-done(((bf16[16,192,256]{2,1,0:T(8,128)(2,1)}), bf16[16,192,256]{2,1,0:T(8,128)(2,1)S(1)}, u32[]{:S(2)}, u32[]{:S(2)}) %all-to-all-start.1) | async-done | bytes 1572896 | tf_op jit(solution)/shard_map/all_to_all | solution.py:285
  114.2 0.0 copy-start
  114.2 1.1 copy-done
  115.4 3.2 %shard_map.55 = bf16[256,1536]{1,0:T(8,128)(2,1)} custom-call(s32[5]{0:T(128)} %stack.47.at, f32[256,1536]{1,0:T(8,128)} %get-tuple-element.29.slope, bf16[8,2,192,256]{3,2,1,0:T(8,128)(2,1)} %bitcast.23), custom_call_target="tpu_custom_call" | custom-call | flops 201326592 | bytes 3145728 | tf_op jit(solution)/shard_map/pallas_call | solution.py:297
Async XLA Ops:
  0.6 16.1 %copy-start.7 = (bf16[64,1536]{1,0:T(8,128)(2,1)S(1)}, bf16[64,1536]{1,0:T(8,128)(2,1)}, u32[]{:S(2)}) copy-start(bf16[64,1536]{1,0:T(8,128)(2,1)} %param.4) | copy-start | bytes 589828
  0.6 9.2 %collective-permute-start = (bf16[64,1536]{1,0:T(8,128)(2,1)}, bf16[64,1536]{1,0:T(8,128)(2,1)S(1)}, u32[]{:S(2)}, u32[]{:S(2)}) collective-permute-start(bf16[64,1536]{1,0:T(8,128)(2,1)} %param.4), channel_id=1, source_target_pairs={{0,16},{16,0},{32,48},{48,32},{64,80},{80,64},{96,112},{112,96},{1... | collective-permute-start | bytes 589832 | tf_op jit(solution)/shard_map/ppermute | solution.py:21
  9.8 26.0 %all-to-all-start = ((bf16[8,192,256]{2,1,0:T(8,128)(2,1)}), bf16[8,192,256]{2,1,0:T(8,128)(2,1)S(1)}, u32[]{:S(2)}, u32[]{:S(2)}) async-start(bf16[8,192,256]{2,1,0:T(8,128)(2,1)} %get-tuple-element.32), calls=%async_computation | async-start | bytes 1572864 | tf_op jit(solution)/shard_map/all_to_all | solution.py:244
  16.8 9.5 %collective-permute-start.2 = (bf16[2,64,1536]{2,1,0:T(8,128)(2,1)S(1)}, bf16[2,64,1536]{2,1,0:T(8,128)(2,1)S(1)}, u32[]{:S(2)}, u32[]{:S(2)}) collective-permute-start(bf16[2,64,1536]{2,1,0:T(8,128)(2,1)S(1)} %get-tuple-element.57), channel_id=1, source_target_pairs={{0,8},{1,65},{2,10},{3,67},{4,12},{5,69},{6,14},{7,71},{8,0},{9,73... | collective-permute-start | bytes 1179656 | tf_op jit(solution)/shard_map/ppermute | solution.py:53
  20.1 10.3 %collective-permute-start.1 = (bf16[2,64,1536]{2,1,0:T(8,128)(2,1)S(1)}, bf16[2,64,1536]{2,1,0:T(8,128)(2,1)S(1)}, u32[]{:S(2)}, u32[]{:S(2)}) collective-permute-start(bf16[2,64,1536]{2,1,0:T(8,128)(2,1)S(1)} %get-tuple-element.57), channel_id=1, source_target_pairs={{0,4},{1,33},{2,6},{3,35},{4,8},{5,37},{6,10},{7,39},{8,12},{9,41}... | collective-permute-start | bytes 1179656 | tf_op jit(solution)/shard_map/ppermute | solution.py:53
  20.8 10.0 %collective-permute-start.3 = (bf16[2,64,1536]{2,1,0:T(8,128)(2,1)S(1)}, bf16[2,64,1536]{2,1,0:T(8,128)(2,1)S(1)}, u32[]{:S(2)}, u32[]{:S(2)}) collective-permute-start(bf16[2,64,1536]{2,1,0:T(8,128)(2,1)S(1)} %get-tuple-element.57), channel_id=1, source_target_pairs={{0,12},{1,97},{2,14},{3,99},{4,0},{5,101},{6,2},{7,103},{8,4},{9,1... | collective-permute-start | bytes 1179656 | tf_op jit(solution)/shard_map/ppermute | solution.py:53
  35.8 3.3 %copy-start.3 = (bf16[8,192,256]{2,1,0:T(8,128)(2,1)}, bf16[8,192,256]{2,1,0:T(8,128)(2,1)S(1)}, u32[]{:S(2)}) copy-start(bf16[8,192,256]{2,1,0:T(8,128)(2,1)S(1)} %all-to-all-done.refs_0_) | copy-start | bytes 2359300
  36.0 24.7 %copy-start.1 = (bf16[2,4,64,1536]{3,2,1,0:T(8,128)(2,1)}, bf16[2,4,64,1536]{3,2,1,0:T(8,128)(2,1)S(1)}, u32[]{:S(2)}) copy-start(bf16[2,4,64,1536]{3,2,1,0:T(8,128)(2,1)S(1)} %pad_maximum_fusion.refs_0_.refs_4_) | copy-start | bytes 4718596
  36.0 22.4 %collective-permute-start.5 = (bf16[2,4,64,1536]{3,2,1,0:T(8,128)(2,1)S(1)}, bf16[2,4,64,1536]{3,2,1,0:T(8,128)(2,1)S(1)}, u32[]{:S(2)}, u32[]{:S(2)}) collective-permute-start(bf16[2,4,64,1536]{3,2,1,0:T(8,128)(2,1)S(1)} %pad_maximum_fusion.refs_0_.refs_4_), channel_id=1, source_target_pairs={{0,96},{1,13},{2,98},{3,15},{4,100},{5,1},{6,102},{7,3},{8,104},{9... | collective-permute-start | bytes 4718600 | tf_op jit(solution)/shard_map/ppermute | solution.py:53
  36.3 23.4 %collective-permute-start.4 = (bf16[2,4,64,1536]{3,2,1,0:T(8,128)(2,1)S(1)}, bf16[2,4,64,1536]{3,2,1,0:T(8,128)(2,1)S(1)}, u32[]{:S(2)}, u32[]{:S(2)}) collective-permute-start(bf16[2,4,64,1536]{3,2,1,0:T(8,128)(2,1)S(1)} %pad_maximum_fusion.refs_0_.refs_4_), channel_id=1, source_target_pairs={{0,32},{1,5},{2,34},{3,7},{4,36},{5,9},{6,38},{7,11},{8,40},{9,13}... | collective-permute-start | bytes 4718600 | tf_op jit(solution)/shard_map/ppermute | solution.py:53
  38.1 20.1 %collective-permute-start.6 = (bf16[8,192,256]{2,1,0:T(8,128)(2,1)S(1)}, bf16[8,192,256]{2,1,0:T(8,128)(2,1)S(1)}, u32[]{:S(2)}, u32[]{:S(2)}) collective-permute-start(bf16[8,192,256]{2,1,0:T(8,128)(2,1)S(1)} %all-to-all-done.refs_0_), channel_id=1, source_target_pairs={{0,2},{1,3},{2,0},{3,1},{4,6},{5,7},{6,4},{7,5},{8,10},{9,11},{10,... | collective-permute-start | bytes 2359304 | tf_op jit(solution)/shard_map/ppermute | solution.py:21
  39.1 32.4 %collective-permute-start.9 = (bf16[8,192,256]{2,1,0:T(8,128)(2,1)S(1)}, bf16[8,192,256]{2,1,0:T(8,128)(2,1)}, u32[]{:S(2)}, u32[]{:S(2)}) collective-permute-start(bf16[8,192,256]{2,1,0:T(8,128)(2,1)S(1)} %all-to-all-done.refs_0_), channel_id=1, source_target_pairs={{0,1},{1,0},{2,3},{3,2},{4,5},{5,4},{6,7},{7,6},{8,9},{9,8},{10,11... | collective-permute-start | bytes 2359304 | tf_op jit(solution)/shard_map/ppermute | solution.py:21
  58.3 11.2 %copy-start.8 = (bf16[8,192,256]{2,1,0:T(8,128)(2,1)}, bf16[8,192,256]{2,1,0:T(8,128)(2,1)S(1)}, u32[]{:S(2)}) copy-start(bf16[8,192,256]{2,1,0:T(8,128)(2,1)S(1)} %collective-permute-done.6.refs_1_) | copy-start | bytes 2359300
  58.3 13.2 %collective-permute-start.10 = (bf16[8,192,256]{2,1,0:T(8,128)(2,1)S(1)}, bf16[8,192,256]{2,1,0:T(8,128)(2,1)}, u32[]{:S(2)}, u32[]{:S(2)}) collective-permute-start(bf16[8,192,256]{2,1,0:T(8,128)(2,1)S(1)} %collective-permute-done.6.refs_1_), channel_id=1, source_target_pairs={{0,1},{1,0},{2,3},{3,2},{4,5},{5,4},{6,7},{7,6},{8,9},{9,8},{10,11... | collective-permute-start | bytes 2359304 | tf_op jit(solution)/shard_map/ppermute | solution.py:21
  58.4 2.3 %copy-start.5 = (bf16[2,4,64,1536]{3,2,1,0:T(8,128)(2,1)}, bf16[2,4,64,1536]{3,2,1,0:T(8,128)(2,1)S(1)}, u32[]{:S(2)}) copy-start(bf16[2,4,64,1536]{3,2,1,0:T(8,128)(2,1)S(1)} %collective-permute-done.5.refs_2_.refs_6_) | copy-start | bytes 4718596
  58.4 13.1 %collective-permute-start.8 = (bf16[1,4,64,1536]{3,2,1,0:T(8,128)(2,1)S(1)}, bf16[1,4,64,1536]{3,2,1,0:T(8,128)(2,1)}, u32[]{:S(2)}, u32[]{:S(2)}) collective-permute-start(bf16[1,4,64,1536]{3,2,1,0:T(8,128)(2,1)S(1)} %slice.9), channel_id=1, source_target_pairs={{0,96},{1,13},{2,98},{3,15},{4,100},{5,1},{6,102},{7,3},{8,104},{9... | collective-permute-start | bytes 2359304 | tf_op jit(solution)/shard_map/ppermute | solution.py:53
  59.7 1.2 copy-start.6
  59.8 13.4 %collective-permute-start.7 = (bf16[1,4,64,1536]{3,2,1,0:T(8,128)(2,1)S(1)}, bf16[1,4,64,1536]{3,2,1,0:T(8,128)(2,1)}, u32[]{:S(2)}, u32[]{:S(2)}) collective-permute-start(bf16[1,4,64,1536]{3,2,1,0:T(8,128)(2,1)S(1)} %slice.8), channel_id=1, source_target_pairs={{0,32},{1,5},{2,34},{3,7},{4,36},{5,9},{6,38},{7,11},{8,40},{9,13}... | collective-permute-start | bytes 2359304 | tf_op jit(solution)/shard_map/ppermute | solution.py:53
  69.4 11.5 %collective-permute-start.11 = (bf16[6,2,192,256]{3,2,1,0:T(8,128)(2,1)}, bf16[6,2,192,256]{3,2,1,0:T(8,128)(2,1)S(1)}, u32[]{:S(2)}, u32[]{:S(2)}) collective-permute-start(bf16[6,2,192,256]{3,2,1,0:T(8,128)(2,1)} %get-tuple-element.44), channel_id=1, source_target_pairs={{0,1},{1,0},{2,3},{3,2},{4,5},{5,4},{6,7},{7,6},{8,9},{9,8},{10,11... | collective-permute-start | bytes 3538952 | tf_op jit(solution)/shard_map/ppermute | solution.py:21
  78.4 2.5 %collective-permute-start.12 = (bf16[2,2,192,256]{3,2,1,0:T(8,128)(2,1)}, bf16[2,2,192,256]{3,2,1,0:T(8,128)(2,1)S(1)}, u32[]{:S(2)}, u32[]{:S(2)}) collective-permute-start(bf16[2,2,192,256]{3,2,1,0:T(8,128)(2,1)} %get-tuple-element.45), channel_id=1, source_target_pairs={{0,1},{1,0},{2,3},{3,2},{4,5},{5,4},{6,7},{7,6},{8,9},{9,8},{10,11... | collective-permute-start | bytes 1179656 | tf_op jit(solution)/shard_map/ppermute | solution.py:21
  80.9 0.7 copy-start.4
  80.9 1.2 %copy-start.2 = (bf16[6,2,192,256]{3,2,1,0:T(8,128)(2,1)}, bf16[6,2,192,256]{3,2,1,0:T(8,128)(2,1)S(1)}, u32[]{:S(2)}) copy-start(bf16[6,2,192,256]{3,2,1,0:T(8,128)(2,1)S(1)} %collective-permute-done.11.other) | copy-start | bytes 3538948
  85.5 28.7 %all-to-all-start.1 = ((bf16[16,192,256]{2,1,0:T(8,128)(2,1)}), bf16[16,192,256]{2,1,0:T(8,128)(2,1)S(1)}, u32[]{:S(2)}, u32[]{:S(2)}) async-start(bf16[16,192,256]{2,1,0:T(8,128)(2,1)} %bitcast.22), calls=%async_computation.1 | async-start | bytes 3145728 | tf_op jit(solution)/shard_map/all_to_all | solution.py:285
  114.2 1.1 copy-start

commit v5 on v4

--- a/solution.py
+++ b/solution.py
@@ -53,7 +53,7 @@
     return lax.ppermute(v, ("gx", "gy", "gz"), pairs)
 
 
-def call(body, out_shape, in_specs, cost, out_specs=None, scratch=(), limit=56):
+def call(body, out_shape, in_specs, cost, out_specs=None, scratch=(), aliases={}, limit=56):
     if out_specs is None:
         out_specs = [VMEM] * len(out_shape)
     flops, moved = cost
@@ -63,6 +63,7 @@
         in_specs=in_specs,
         out_specs=out_specs,
         scratch_shapes=list(scratch),
+        input_output_aliases=aliases,
         compiler_params=pltpu.CompilerParams(vmem_limit_bytes=limit * MIB),
         cost_estimate=pl.CostEstimate(flops=flops, bytes_accessed=moved, transcendentals=0),
     )
@@ -101,14 +102,16 @@
 
 
 def load_grads(at, pieces, held, sems):
-    p0, p1, p3, p2p, p2m = pieces
-    todo = [(p0, 0, 0), (p0, 0, 1), (p1, 1, 0), (p1, 1, 1), (p3, 3, 0), (p3, 3, 1), (p2p, 2, 0), (p2m, 2, 1)]
+    low, high, full = pl.ds(0, 2), pl.ds(2, 2), pl.ds(0, 4)
+    p0, p1, p3, r0, up, down, r2p, r2m = pieces
+    todo = [(p0, 0, 0, full), (p1, 1, 0, full), (p3, 3, 0, full), (up.at[low], 2, 0, low), (down.at[low], 2, 0, high)]
+    todo += [(r0, 0, 1, full), (up.at[pl.ds(2, 4)], 1, 1, full), (down.at[pl.ds(2, 4)], 3, 1, full)]
+    todo += [(r2p, 2, 1, low), (r2m, 2, 1, high)]
 
     def copies(core):
         made = []
-        for n, (src, k, z) in enumerate(todo):
-            src = src.at[z if src.shape[0] == 2 else 0]
-            dst = held.at[k, z] if core == 0 else held.at[:, z, k]
+        for n, (src, k, z, part) in enumerate(todo):
+            dst = held.at[k, z, part] if core == 0 else held.at[part, z, k]
             made.append(pltpu.make_async_copy(src, dst, sems.at[n]))
         return made
 
@@ -122,23 +125,32 @@
                 c.wait()
 
 
-def input_body(count, at, w, *refs):
-    pieces, (mine, theirs, held, sums, in_sems, out_sems) = refs[:count], refs[count:]
-    blocks = [p.at[z] for p in pieces for z in range(p.shape[0])]
-    for i, src in enumerate(blocks):
-        pltpu.make_async_copy(src, held.at[i], in_sems.at[i]).start()
-    rows = w.shape[0] // 4
+def input_body(halves, at, w_hbm, *refs):
+    count = len(halves) // 2
+    pieces, (mine, theirs, w, held, sums, w_sem, in_sems, out_sems) = refs[:-8], refs[-8:]
+    load = pltpu.make_async_copy(w_hbm, w, w_sem)
+    load.start()
+    sources = [pieces[n].at[pl.ds(start, 2)] for n, start in halves]
+
+    def coming(i, half, src):
+        return pltpu.make_async_copy(src, held.at[i, pl.ds(2 * half, 2)], in_sems.at[i, half])
 
     def leaving(i):
         slot = i % 2
         return [
-            pltpu.make_async_copy(sums.at[slot, n], out.at[i], out_sems.at[slot, n])
+            pltpu.make_async_copy(sums.at[slot, at[4] ^ n], out.at[i], out_sems.at[slot, n])
             for n, out in enumerate((mine, theirs))
         ]
 
-    @pl.loop(0, len(blocks))
+    for n, src in enumerate(sources):
+        coming(n // 2, n % 2, src).start()
+    load.wait()
+    rows = w.shape[0] // 4
+
+    @pl.loop(0, count)
     def _(i):
-        pltpu.make_async_copy(blocks[0], held.at[i], in_sems.at[i]).wait()
+        for half in range(2):
+            coming(i, half, sources[half]).wait()
 
         @pl.when(i >= 2)
         def _():
@@ -149,45 +161,35 @@
             w[...], held[i].reshape(256, -1), (((1,), (1,)), ((), ())), preferred_element_type=f32
         ).astype(bf16)
         for n in range(4):
-            sums[i % 2, at[4] ^ (n % 2), n // 2] = part[n * rows : n * rows + rows]
+            sums[i % 2, n % 2, n // 2] = part[n * rows : n * rows + rows]
         for c in leaving(i):
             c.start()
 
-    for i in range(len(blocks) - 2, len(blocks)):
+    for i in range(max(count - 2, 0), count):
         for c in leaving(i):
             c.wait()
 
 
-def core_sum_body(at, mine, mine2, other, other2, out, held, sems):
-    def leaving(k, z):
-        n = 2 * k + z
-        return pltpu.make_async_copy(held.at[n], out.at[group(at, k, z)], sems.at[n])
-
-    def block(early, late, k, z, lo):
-        if k == 2:
-            return late[z, lo]
-        return early[2 * (k - k // 3) + z, lo]
+def core_sum_body(z, places, at, *refs):
+    mine, other, (out, held, sems) = refs[: len(refs) // 2 - 1 - z], refs[len(refs) // 2 - 1 - z : -3 - z], refs[-3:]
+
+    def leaving(k):
+        return pltpu.make_async_copy(held.at[k], out.at[group(at, k, z)], sems.at[k])
 
     for core in range(2):
 
         @pl.when(at[4] == core)
         def _():
-            by_x, by_y = (mine, mine2), (other, other2)
-            if core:
-                by_x, by_y = by_y, by_x
-            for z in range(2):
-                for lo in range(2):
-                    y = [block(*by_y, k, z, lo) for k in range(4)]
-                    for k in range(4):
-                        turned = jnp.concatenate([v[:, 64 * k : 64 * k + 64] for v in y], 1)
-                        total = block(*by_x, k, z, lo).astype(f32) + turned.astype(f32)
-                        held[2 * k + z, lo] = total.astype(bf16)
-                for k in range(4):
-                    leaving(k, z).start()
-
-    for z in range(2):
-        for k in range(4):
-            leaving(k, z).wait()
+            by_x, by_y = (other, mine) if core else (mine, other)
+            for lo in range(2):
+                for k, (n, i) in enumerate(places):
+                    turned = jnp.concatenate([by_y[m][j, lo, :, 64 * k : 64 * k + 64] for m, j in places], 1)
+                    held[k, lo] = (by_x[n][i, lo].astype(f32) + turned.astype(f32)).astype(bf16)
+                    if lo:
+                        leaving(k).start()
+
+    for k in range(4):
+        leaving(k).wait()
 
 
 def finish_body(at, slope, parts, out):
@@ -203,7 +205,7 @@
 
 
 def weight_body(at, *refs):
-    hidden, pieces, (out, held, sems) = refs[:4], refs[4:9], refs[9:]
+    hidden, pieces, (out, held, sems) = refs[:4], refs[4:12], refs[12:]
     load_grads(at, pieces, held, sems)
     rows = out.shape[0] // 4
     lhs = jnp.concatenate(
@@ -228,7 +230,7 @@
     at = jnp.stack([gx // 2, gx % 2, y, gz // 2, gz % 2]).astype(jnp.int32)
     w = weight.reshape(4 * rows, features)
     block = (rows, tokens)
-    grad_scratch = [pltpu.VMEM((4, 2, 4, tokens // 4, features), bf16), pltpu.SemaphoreType.DMA((8,))]
+    grad_scratch = [pltpu.VMEM((4, 2, 4, tokens // 4, features), bf16), pltpu.SemaphoreType.DMA((10,))]
     product = 2 * 4 * rows * 8 * tokens * features
 
     slope, parts = call(
@@ -238,58 +240,74 @@
         (2 * tokens * 256 * columns, 8 * tokens * columns),
     )(at, pre_act)
 
-    other, parts = lax.optimization_barrier((swap_z_hi(grad_out), parts))
-    both = jnp.stack([grad_out, other])
-    first = [send_by_core(both, k, True) for k in (1, 2, 3)]
+    other = swap_z_hi(grad_out)
+    first = [send_by_core(grad_out, k, True) for k in (1, 2, 3)]
+    first, other = lax.optimization_barrier((first, other))
+    p0 = jnp.stack([grad_out] + first)
+    p1, p3 = send_by_core(p0, 1, False), send_by_core(p0, 3, False)
+    r0 = jnp.stack([other] + [send_by_core(other, k, True) for k in (1, 2, 3)])
+    p1, p3, r0, parts = lax.optimization_barrier((p1, p3, r0, parts))
+    up = send_by_core(jnp.concatenate([p1[:2], r0]), 1, False)
+    down = send_by_core(jnp.concatenate([p3[2:], r0]), 3, False)
     own = lax.all_to_all(parts, "gx", 0, 0, tiled=True)
-    first, own = lax.optimization_barrier((first, own))
-    p0 = jnp.stack([both] + first, 1)
-    p1, p3 = send_by_core(p0, 1, False), send_by_core(p0, 3, False)
-
-    p2p, p2m = send_by_core(p1[:1], 1, False), send_by_core(p3[1:], 3, False)
-    pieces = p0, p1, p3, p2p, p2m
-    far = swap_z_lo(own)
-
-    def input_part(*given):
-        count = sum(p.shape[0] for p in given)
+    def input_part(halves, *given):
+        count = len(halves) // 2
         return call(
-            functools.partial(input_body, len(given)),
+            functools.partial(input_body, halves),
             [((count, 2) + block, bf16)] * 2,
-            [SMEM, VMEM] + [HBM] * len(given),
+            [SMEM, HBM] + [HBM] * len(given),
             (product * count // 8, 2 * (4 * rows * features + count * (4 * rows + features) * tokens)),
             out_specs=[HBM] * 2,
             scratch=[
+                pltpu.VMEM((4 * rows, features), bf16),
                 pltpu.VMEM((count, 4, tokens // 4, features), bf16),
                 pltpu.VMEM((2, 2, 2) + block, bf16),
-                pltpu.SemaphoreType.DMA((count,)),
+                pltpu.SemaphoreType.DMA,
+                pltpu.SemaphoreType.DMA((count, 2)),
                 pltpu.SemaphoreType.DMA((2, 2)),
             ],
         )(at, w, *given)
 
-    early = lax.optimization_barrier((p0, p1, p3, far))
-    mine, theirs = input_part(*early[:3])
-    other = swap_core(theirs)
+    def core_sum(z, places, mine, other, *into):
+        return call(
+            functools.partial(core_sum_body, z, places),
+            [((8, 2) + block, bf16)],
+            [SMEM] + [VMEM] * (2 * len(mine)) + [HBM] * len(into),
+            (8 * rows * tokens, 24 * rows * tokens),
+            out_specs=[HBM],
+            scratch=[pltpu.VMEM((4, 2) + block, bf16), pltpu.SemaphoreType.DMA((4,))],
+            aliases={1 + 2 * len(mine): 0} if into else {},
+        )(at, *mine, *other, *into)[0]
+
+    mine0, theirs0 = input_part([(n, at) for n in range(3) for at in (0, 2)], p0, p1, p3)
+    up, down, other0, own = lax.optimization_barrier((up, down, swap_core(theirs0), own))
+    r2p, r2m = send_by_core(up[2:4], 1, False), send_by_core(down[4:], 3, False)
+    pieces = p0, p1, p3, r0, up, down, r2p, r2m
+    mine1, theirs1 = input_part(
+        [(1, 0), (2, 0), (0, 0), (0, 2), (1, 2), (1, 4), (2, 2), (2, 4)], r0, up, down
+    )
+    far = swap_z_lo(own)
+    mine2, theirs2 = input_part([(0, 0), (1, 0)], r2p, r2m)
+    theirs1, _ = lax.optimization_barrier((theirs1, theirs2))
+    other1 = swap_core(theirs1)
+    sums = core_sum(0, ((0, 0), (0, 1), (1, 0), (0, 2)), [mine0, mine1], [other0, other1])
+    sums = core_sum(
+        1,
+        ((0, 1), (0, 2), (1, 0), (0, 3)),
+        [mine1, mine2],
+        [other1, swap_core(theirs2)],
+        sums,
+    )
+    own, far, _ = lax.optimization_barrier((own, far, sums))
     hidden = [own, far, swap_core(own), swap_core(far)]
-    p2p, p2m, hidden = lax.optimization_barrier((p2p, p2m, hidden))
-    mine2, theirs2 = input_part(p2p, p2m)
-    size = 2 * 4 * rows * tokens
-    (sums,) = call(
-        core_sum_body,
-        [((8, 2) + block, bf16)],
-        [SMEM] + [VMEM] * 4,
-        (4 * size, 12 * size),
-        out_specs=[HBM],
-        scratch=[pltpu.VMEM((8, 2) + block, bf16), pltpu.SemaphoreType.DMA((8,))],
-    )(at, mine, mine2, other, swap_core(theirs2))
     same_core = [[2 * (2 * i + k) + c for i in range(8) for k in range(2)] for c in range(2)]
     back = lax.all_to_all(
         sums.reshape((16,) + block), ("gx", "gz"), 0, 0, tiled=True, axis_index_groups=same_core
     )
-    hidden, _ = lax.optimization_barrier((hidden, sums))
     (weight_grad,) = call(
         weight_body,
         [((4 * rows, features), bf16)],
-        [SMEM] + [VMEM] * 4 + [HBM] * 5,
+        [SMEM] + [VMEM] * 4 + [HBM] * 8,
         (product, 2 * (8 * rows * features + 2048 * features)),
         scratch=grad_scratch,
     )(at, *hidden, *pieces)

time: 119 us -> 135 us (1.13)
  the two profiles are of different devices: /device:TPU:0 before, /device:TPU:31 now
where the time goes in v5:
time: 135 us; the launch traced here: 134 us
  starting transfers between devices  46.9 us (35%)
  Pallas kernels  42.2 us (31%)
  waiting for transfers between devices  33.8 us (25%)
  local copies, waits for them, and re-layouts  9.22 us (7%)
    ppermute x7, waiting for transfers between devices, send(): return lax.ppermute(v, axis, [(i, to(i)) for i in range(count)])  25.1 us
    ppermute x7, starting transfers between devices, send(): return lax.ppermute(v, axis, [(i, to(i)) for i in range(count)])  23.1 us
    pallas_call x3, Pallas kernels, input_part(): call(functools.partial(input_body, halves), [((count, 2) + block, bf16)]...  17.6 us
    ppermute x12, starting transfers between devices, send_by_core(): return lax.ppermute(v, ('gx', 'gy', 'gz'), pairs)  13.9 us
    pallas_call x1, Pallas kernels, per_device(): call(weight_body, [((4 * rows, features), bf16)], [SMEM] + [VMEM] * 4 + [...  12.2 us
    ppermute x12, waiting for transfers between devices, send_by_core(): return lax.ppermute(v, ('gx', 'gy', 'gz'), pairs)  8.71 us
    unnamed x28, local copies, waits for them, and re-layouts  6.23 us
    pallas_call x2, Pallas kernels, core_sum(): call(functools.partial(core_sum_body, z, places), [((8, 2) + block, bf16)...  5.53 us
  transfers between devices with their start and end apart: 21, of which 10 were waited for; matrix products, arithmetic and copies ran while one was open for 1% of the time, Pallas kernels for 26%

profile of v5, /device:TPU:31, one launch (start us, length us, event | category | flops | bytes accessed | tf_op | source)
XLA Modules:
  0.0 134.4 jit_solution(1579144224833510130)
XLA Ops:
  0.6 1.2 collective-permute-start.1
  1.8 1.8 %collective-permute-start = (bf16[64,1536]{1,0:T(8,128)(2,1)}, bf16[64,1536]{1,0:T(8,128)(2,1)S(1)}, u32[]{:S(2)}, u32[]{:S(2)}) collective-permute-start(bf16[64,1536]{1,0:T(8,128)(2,1)} %param.4), channel_id=1, source_target_pairs={{0,4},{1,33},{2,6},{3,35},{4,8},{5,37},{6,10},{7,39},{8,12},{9,41}... | collective-permute-start | bytes 589832 | tf_op jit(solution)/shard_map/ppermute | solution.py:53
  3.7 3.6 %collective-permute-start.3 = (bf16[64,1536]{1,0:T(8,128)(2,1)}, bf16[64,1536]{1,0:T(8,128)(2,1)S(1)}, u32[]{:S(2)}, u32[]{:S(2)}) collective-permute-start(bf16[64,1536]{1,0:T(8,128)(2,1)} %param.4), channel_id=1, source_target_pairs={{0,16},{16,0},{32,48},{48,32},{64,80},{80,64},{96,112},{112,96},{1... | collective-permute-start | bytes 589832 | tf_op jit(solution)/shard_map/ppermute | solution.py:21
  7.2 0.0 collective-permute-start.2
  7.3 0.0 collective-permute-done.1
  7.3 0.0 collective-permute-done
  7.3 4.3 %collective-permute-done.3 = bf16[64,1536]{1,0:T(8,128)(2,1)S(1)} collective-permute-done((bf16[64,1536]{1,0:T(8,128)(2,1)}, bf16[64,1536]{1,0:T(8,128)(2,1)S(1)}, u32[]{:S(2)}, u32[]{:S(2)}) %collective-permute-start.3) | collective-permute-done | bytes 196640 | tf_op jit(solution)/shard_map/ppermute | solution.py:21
  11.6 1.9 %collective-permute-done.2 = bf16[64,1536]{1,0:T(8,128)(2,1)S(1)} collective-permute-done((bf16[64,1536]{1,0:T(8,128)(2,1)}, bf16[64,1536]{1,0:T(8,128)(2,1)S(1)}, u32[]{:S(2)}, u32[]{:S(2)}) %collective-permute-start.2) | collective-permute-done | bytes 196640 | tf_op jit(solution)/shard_map/ppermute | solution.py:53
  13.5 1.0 pad_maximum_fusion.2.refs_0_.refs_4_
  14.5 0.2 collective-permute-start.5
  14.8 2.5 %collective-permute-start.4 = (bf16[4,64,1536]{2,1,0:T(8,128)(2,1)S(1)}, bf16[4,64,1536]{2,1,0:T(8,128)(2,1)S(1)}, u32[]{:S(2)}, u32[]{:S(2)}) collective-permute-start(bf16[4,64,1536]{2,1,0:T(8,128)(2,1)S(1)} %pad_maximum_fusion.2.refs_0_.refs_4_), channel_id=1, source_target_pairs={{0,32},{1,5},{2,34},{3,7},{4,36},{5,9},{6,38},{7,11},{8,40},{9,13}... | collective-permute-start | bytes 2359304 | tf_op jit(solution)/shard_map/ppermute | solution.py:53
  17.3 0.0 collective-permute-start.8
  17.3 0.6 collective-permute-start.7
  17.8 2.1 %collective-permute-start.6 = (bf16[64,1536]{1,0:T(8,128)(2,1)S(1)}, bf16[64,1536]{1,0:T(8,128)(2,1)S(1)}, u32[]{:S(2)}, u32[]{:S(2)}) collective-permute-start(bf16[64,1536]{1,0:T(8,128)(2,1)S(1)} %collective-permute-done.3), channel_id=1, source_target_pairs={{0,4},{1,33},{2,6},{3,35},{4,8},{5,37},{6,10},{7,39},{8,12},{9,41}... | collective-permute-start | bytes 589832 | tf_op jit(solution)/shard_map/ppermute | solution.py:53
  20.0 0.6 stack.53.at
  20.6 3.7 %shard_map.50 = (f32[256,1536]{1,0:T(8,128)}, bf16[8,192,256]{2,1,0:T(8,128)(2,1)}) custom-call(s32[5]{0:T(128)} %stack.53.at, bf16[256,1536]{1,0:T(8,128)(2,1)} %pre.1), custom_call_target="tpu_custom_call" | custom-call | flops 201326592 | bytes 3145728 | tf_op jit(solution)/shard_map/pallas_call | solution.py:236
  24.2 3.2 %collective-permute-done.8 = bf16[64,1536]{1,0:T(8,128)(2,1)S(1)} collective-permute-done((bf16[64,1536]{1,0:T(8,128)(2,1)S(1)}, bf16[64,1536]{1,0:T(8,128)(2,1)S(1)}, u32[]{:S(2)}, u32[]{:S(2)}) %collective-permute-start.8) | collective-permute-done | bytes 196640 | tf_op jit(solution)/shard_map/ppermute | solution.py:53
  27.4 0.0 collective-permute-done.7
  27.4 2.7 %collective-permute-done.6 = bf16[64,1536]{1,0:T(8,128)(2,1)S(1)} collective-permute-done((bf16[64,1536]{1,0:T(8,128)(2,1)S(1)}, bf16[64,1536]{1,0:T(8,128)(2,1)S(1)}, u32[]{:S(2)}, u32[]{:S(2)}) %collective-permute-start.6) | collective-permute-done | bytes 196640 | tf_op jit(solution)/shard_map/ppermute | solution.py:53
  30.2 0.1 pad_maximum_fusion.3.refs_0_.refs_7_
  30.3 0.9 collective-permute-done.5.refs_2_.refs_6_
  31.2 0.0 collective-permute-done.4.refs_1_.refs_5_
  31.2 0.9 copy-done.7
  32.1 0.3 copy-done.8
  32.4 0.2 pad_maximum_fusion
  32.6 0.1 collective-permute-start.10
  32.7 2.7 %collective-permute-start.9 = (bf16[6,64,1536]{2,1,0:T(8,128)(2,1)S(1)}, bf16[6,64,1536]{2,1,0:T(8,128)(2,1)}, u32[]{:S(2)}, u32[]{:S(2)}) collective-permute-start(bf16[6,64,1536]{2,1,0:T(8,128)(2,1)S(1)} %get-tuple-element.53), channel_id=1, source_target_pairs={{0,32},{1,5},{2,34},{3,7},{4,36},{5,9},{6,38},{7,11},{8,40},{9,13}... | collective-permute-start | bytes 3538952 | tf_op jit(solution)/shard_map/ppermute | solution.py:53
  35.3 4.4 %all-to-all-start = ((bf16[8,192,256]{2,1,0:T(8,128)(2,1)}), bf16[8,192,256]{2,1,0:T(8,128)(2,1)S(1)}, u32[]{:S(2)}, u32[]{:S(2)}) async-start(bf16[8,192,256]{2,1,0:T(8,128)(2,1)} %get-tuple-element.37), calls=%async_computation | async-start | bytes 1572864 | tf_op jit(solution)/shard_map/all_to_all | solution.py:252
  39.7 6.2 %shard_map.51 = (bf16[3,2,192,256]{3,2,1,0:T(8,128)(2,1)}, bf16[3,2,192,256]{3,2,1,0:T(8,128)(2,1)}) custom-call(s32[5]{0:T(128)} %stack.53.at, bf16[768,1536]{1,0:T(8,128)(2,1)} %bitcast.19, bf16[4,64,1536]{2,1,0:T(8,128)(2,1)} %copy-done.3, bf16[4,64,1536]{2,1,0:T(8,128)(2,1)} %copy-done.8, bf16[4,64,1536]{2,1,0:T(8,128)(2,1)} %copy-done.7), custom_call_target="tpu_custom_call" | custom-call | flops 1811939328 | bytes 5898240 | tf_op jit(solution)/shard_map/pallas_call | solution.py:255
  45.9 4.3 %collective-permute-start.11 = (bf16[3,2,192,256]{3,2,1,0:T(8,128)(2,1)}, bf16[3,2,192,256]{3,2,1,0:T(8,128)(2,1)}, u32[]{:S(2)}, u32[]{:S(2)}) collective-permute-start(bf16[3,2,192,256]{3,2,1,0:T(8,128)(2,1)} %get-tuple-element.36), channel_id=1, source_target_pairs={{0,1},{1,0},{2,3},{3,2},{4,5},{5,4},{6,7},{7,6},{8,9},{9,8},{10,11... | collective-permute-start | bytes 1769480 | tf_op jit(solution)/shard_map/ppermute | solution.py:21
  50.2 2.0 %collective-permute-done.11.refs_2_ = bf16[3,2,192,256]{3,2,1,0:T(8,128)(2,1)} collective-permute-done((bf16[3,2,192,256]{3,2,1,0:T(8,128)(2,1)}, bf16[3,2,192,256]{3,2,1,0:T(8,128)(2,1)}, u32[]{:S(2)}, u32[]{:S(2)}) %collective-permute-start.11) | collective-permute-done | bytes 589856 | tf_op jit(solution)/shard_map/ppermute | solution.py:21
  52.2 0.0 all-to-all-done.refs_0_
  52.2 0.0 collective-permute-done.10.refs_2_.refs_9_
  52.2 0.0 collective-permute-done.9.refs_1_.refs_8_
  52.2 1.3 slice.14
  53.5 1.0 slice.15
  54.6 0.3 collective-permute-start.13
  54.9 2.4 %collective-permute-start.12 = (bf16[2,64,1536]{2,1,0:T(8,128)(2,1)S(1)}, bf16[2,64,1536]{2,1,0:T(8,128)(2,1)S(1)}, u32[]{:S(2)}, u32[]{:S(2)}) collective-permute-start(bf16[2,64,1536]{2,1,0:T(8,128)(2,1)S(1)} %slice.14), channel_id=1, source_target_pairs={{0,32},{1,5},{2,34},{3,7},{4,36},{5,9},{6,38},{7,11},{8,40},{9,13}... | collective-permute-start | bytes 1179656 | tf_op jit(solution)/shard_map/ppermute | solution.py:53
  57.3 7.3 %shard_map.52 = (bf16[4,2,192,256]{3,2,1,0:T(8,128)(2,1)}, bf16[4,2,192,256]{3,2,1,0:T(8,128)(2,1)}) custom-call(s32[5]{0:T(128)} %stack.53.at, bf16[768,1536]{1,0:T(8,128)(2,1)} %bitcast.20, bf16[4,64,1536]{2,1,0:T(8,128)(2,1)} %copy-done.2, bf16[6,64,1536]{2,1,0:T(8,128)(2,1)} %collective-permute-done.9.refs_1_.refs_8_, ...), custom_call_target="tpu_custom_call" | custom-call | flops 2415919104 | bytes 7077888 | tf_op jit(solution)/shard_map/pallas_call | solution.py:255
  64.6 0.0 copy-start.11
  64.6 0.0 collective-permute-done.13.refs_1_.refs_11_
  64.6 0.7 copy-done.5
  65.3 0.7 copy-done.6
  66.1 4.1 %shard_map.53 = (bf16[1,2,192,256]{3,2,1,0:T(8,128)(2,1)}, bf16[1,2,192,256]{3,2,1,0:T(8,128)(2,1)}) custom-call(s32[5]{0:T(128)} %stack.53.at, bf16[768,1536]{1,0:T(8,128)(2,1)} %bitcast.21, bf16[2,64,1536]{2,1,0:T(8,128)(2,1)} %copy-done.6, bf16[2,64,1536]{2,1,0:T(8,128)(2,1)} %copy-done.5), custom_call_target="tpu_custom_call" | custom-call | flops 603979776 | bytes 3538944 | tf_op jit(solution)/shard_map/pallas_call | solution.py:255
  70.2 10.9 %collective-permute-start.14 = (bf16[4,2,192,256]{3,2,1,0:T(8,128)(2,1)S(1)}, bf16[4,2,192,256]{3,2,1,0:T(8,128)(2,1)S(1)}, u32[]{:S(2)}, u32[]{:S(2)}) collective-permute-start(bf16[4,2,192,256]{3,2,1,0:T(8,128)(2,1)S(1)} %copy-done.11), channel_id=1, source_target_pairs={{0,1},{1,0},{2,3},{3,2},{4,5},{5,4},{6,7},{7,6},{8,9},{9,8},{10,11... | collective-permute-start | bytes 2359304 | tf_op jit(solution)/shard_map/ppermute | solution.py:21
  81.1 0.7 collective-permute-start.16
  81.9 0.4 collective-permute-start.15
  82.2 0.8 collective-permute-done.14.refs_3_.refs_2_
  83.0 0.9 copy-done.1
  83.9 2.9 %shard_map.54.refs_4_ = bf16[8,2,192,256]{3,2,1,0:T(8,128)(2,1)} custom-call(s32[5]{0:T(128)} %stack.53.at, bf16[3,2,192,256]{3,2,1,0:T(8,128)(2,1)} %get-tuple-element.45.refs_0_, bf16[4,2,192,256]{3,2,1,0:T(8,128)(2,1)} %get-tuple-element.40.refs_1_.refs_0_, bf16[3,2,192,256]{3,2,1,0:T(8,128)(2,1)} %collective-permute-done.11.refs_2_, ...), custom_call_target="tpu_custom_call" | custom-call | flops 393216 | bytes 1179648 | tf_op jit(solution)/shard_map/pallas_call | solution.py:272
  86.8 0.0 collective-permute-done.15.refs_3_
  86.8 0.7 copy-done.9
  87.5 2.7 %shard_map.55 = bf16[8,2,192,256]{3,2,1,0:T(8,128)(2,1)} custom-call(s32[5]{0:T(128)} %stack.53.at, bf16[4,2,192,256]{3,2,1,0:T(8,128)(2,1)} %get-tuple-element.40.refs_1_.refs_0_, bf16[1,2,192,256]{3,2,1,0:T(8,128)(2,1)} %get-tuple-element.41.refs_1_, bf16[4,2,192,256]{3,2,1,0:T(8,128)(2,1)} %copy-done.1, ...), custom_call_target="tpu_custom_call", output_to_operand_aliasing={{}: (5, {})} | custom-call | flops 393216 | bytes 1179648 | tf_op jit(solution)/shard_map/pallas_call | solution.py:272
  90.1 5.5 %all-to-all-start.1 = ((bf16[16,192,256]{2,1,0:T(8,128)(2,1)}), bf16[16,192,256]{2,1,0:T(8,128)(2,1)S(1)}, u32[]{:S(2)}, u32[]{:S(2)}) async-start(bf16[16,192,256]{2,1,0:T(8,128)(2,1)} %bitcast.17), calls=%async_computation.1 | async-start | bytes 3145728 | tf_op jit(solution)/shard_map/all_to_all | solution.py:304
  95.6 15.1 %collective-permute-done.16.refs_1_ = bf16[8,192,256]{2,1,0:T(8,128)(2,1)S(1)} collective-permute-done((bf16[8,192,256]{2,1,0:T(8,128)(2,1)S(1)}, bf16[8,192,256]{2,1,0:T(8,128)(2,1)S(1)}, u32[]{:S(2)}, u32[]{:S(2)}) %collective-permute-start.16) | collective-permute-done | bytes 786464 | tf_op jit(solution)/shard_map/ppermute | solution.py:21
  110.7 3.1 %collective-permute-start.17 = (bf16[8,192,256]{2,1,0:T(8,128)(2,1)S(1)}, bf16[8,192,256]{2,1,0:T(8,128)(2,1)S(1)}, u32[]{:S(2)}, u32[]{:S(2)}) collective-permute-start(bf16[8,192,256]{2,1,0:T(8,128)(2,1)S(1)} %all-to-all-done.refs_0_), channel_id=1, source_target_pairs={{0,1},{1,0},{2,3},{3,2},{4,5},{5,4},{6,7},{7,6},{8,9},{9,8},{10,11... | collective-permute-start | bytes 2359304 | tf_op jit(solution)/shard_map/ppermute | solution.py:21
  113.8 0.1 collective-permute-start.18
  113.9 1.8 %collective-permute-done.17.refs_2_ = bf16[8,192,256]{2,1,0:T(8,128)(2,1)S(1)} collective-permute-done((bf16[8,192,256]{2,1,0:T(8,128)(2,1)S(1)}, bf16[8,192,256]{2,1,0:T(8,128)(2,1)S(1)}, u32[]{:S(2)}, u32[]{:S(2)}) %collective-permute-start.17) | collective-permute-done | bytes 786464 | tf_op jit(solution)/shard_map/ppermute | solution.py:21
  115.7 1.1 collective-permute-done.18.refs_3_
  116.8 0.9 copy-done.13
  117.7 12.2 %shard_map.56 = bf16[768,1536]{1,0:T(8,128)(2,1)} custom-call(s32[5]{0:T(128)} %stack.53.at, bf16[8,192,256]{2,1,0:T(8,128)(2,1)} %copy-done.4, bf16[8,192,256]{2,1,0:T(8,128)(2,1)} %copy-done.10, bf16[8,192,256]{2,1,0:T(8,128)(2,1)} %copy-done.12, bf16[8,192,256]{2,1,0:T(8,128)(2,1)} %copy-done.13, bf16[4,64,1536]{2,1,0:T(8,128)(2,1)} %copy-done.3, ...), custom_call_target="tpu_custom_call" | custom-call | flops 4831838208 | bytes 11010048 | tf_op jit(solution)/shard_map/pallas_call | solution.py:307
  130.0 0.0 all-to-all-done.1
  130.0 1.1 copy-done
  131.1 3.2 %shard_map.57 = bf16[256,1536]{1,0:T(8,128)(2,1)} custom-call(s32[5]{0:T(128)} %stack.53.at, f32[256,1536]{1,0:T(8,128)} %get-tuple-element.27.slope, bf16[8,2,192,256]{3,2,1,0:T(8,128)(2,1)} %bitcast.18), custom_call_target="tpu_custom_call" | custom-call | flops 201326592 | bytes 3145728 | tf_op jit(solution)/shard_map/pallas_call | solution.py:315
  (22 shorter events, 0.1 us)
Async XLA Ops:
  0.6 6.6 %collective-permute-start.1 = (bf16[64,1536]{1,0:T(8,128)(2,1)}, bf16[64,1536]{1,0:T(8,128)(2,1)S(1)}, u32[]{:S(2)}, u32[]{:S(2)}) collective-permute-start(bf16[64,1536]{1,0:T(8,128)(2,1)} %param.4), channel_id=1, source_target_pairs={{0,8},{1,65},{2,10},{3,67},{4,12},{5,69},{6,14},{7,71},{8,0},{9,73... | collective-permute-start | bytes 589832 | tf_op jit(solution)/shard_map/ppermute | solution.py:53
  1.8 5.4 %collective-permute-start = (bf16[64,1536]{1,0:T(8,128)(2,1)}, bf16[64,1536]{1,0:T(8,128)(2,1)S(1)}, u32[]{:S(2)}, u32[]{:S(2)}) collective-permute-start(bf16[64,1536]{1,0:T(8,128)(2,1)} %param.4), channel_id=1, source_target_pairs={{0,4},{1,33},{2,6},{3,35},{4,8},{5,37},{6,10},{7,39},{8,12},{9,41}... | collective-permute-start | bytes 589832 | tf_op jit(solution)/shard_map/ppermute | solution.py:53
  3.7 7.9 %collective-permute-start.3 = (bf16[64,1536]{1,0:T(8,128)(2,1)}, bf16[64,1536]{1,0:T(8,128)(2,1)S(1)}, u32[]{:S(2)}, u32[]{:S(2)}) collective-permute-start(bf16[64,1536]{1,0:T(8,128)(2,1)} %param.4), channel_id=1, source_target_pairs={{0,16},{16,0},{32,48},{48,32},{64,80},{80,64},{96,112},{112,96},{1... | collective-permute-start | bytes 589832 | tf_op jit(solution)/shard_map/ppermute | solution.py:21
  7.2 6.2 %collective-permute-start.2 = (bf16[64,1536]{1,0:T(8,128)(2,1)}, bf16[64,1536]{1,0:T(8,128)(2,1)S(1)}, u32[]{:S(2)}, u32[]{:S(2)}) collective-permute-start(bf16[64,1536]{1,0:T(8,128)(2,1)} %param.4), channel_id=1, source_target_pairs={{0,12},{1,97},{2,14},{3,99},{4,0},{5,101},{6,2},{7,103},{8,4},{9,1... | collective-permute-start | bytes 589832 | tf_op jit(solution)/shard_map/ppermute | solution.py:53
  14.5 15.8 %copy-start.3 = (bf16[4,64,1536]{2,1,0:T(8,128)(2,1)}, bf16[4,64,1536]{2,1,0:T(8,128)(2,1)S(1)}, u32[]{:S(2)}) copy-start(bf16[4,64,1536]{2,1,0:T(8,128)(2,1)S(1)} %pad_maximum_fusion.2.refs_0_.refs_4_) | copy-start | bytes 2359300
  14.5 16.6 %collective-permute-start.5 = (bf16[4,64,1536]{2,1,0:T(8,128)(2,1)S(1)}, bf16[4,64,1536]{2,1,0:T(8,128)(2,1)S(1)}, u32[]{:S(2)}, u32[]{:S(2)}) collective-permute-start(bf16[4,64,1536]{2,1,0:T(8,128)(2,1)S(1)} %pad_maximum_fusion.2.refs_0_.refs_4_), channel_id=1, source_target_pairs={{0,96},{1,13},{2,98},{3,15},{4,100},{5,1},{6,102},{7,3},{8,104},{9... | collective-permute-start | bytes 2359304 | tf_op jit(solution)/shard_map/ppermute | solution.py:53
  14.8 16.4 %collective-permute-start.4 = (bf16[4,64,1536]{2,1,0:T(8,128)(2,1)S(1)}, bf16[4,64,1536]{2,1,0:T(8,128)(2,1)S(1)}, u32[]{:S(2)}, u32[]{:S(2)}) collective-permute-start(bf16[4,64,1536]{2,1,0:T(8,128)(2,1)S(1)} %pad_maximum_fusion.2.refs_0_.refs_4_), channel_id=1, source_target_pairs={{0,32},{1,5},{2,34},{3,7},{4,36},{5,9},{6,38},{7,11},{8,40},{9,13}... | collective-permute-start | bytes 2359304 | tf_op jit(solution)/shard_map/ppermute | solution.py:53
  17.3 10.2 %collective-permute-start.8 = (bf16[64,1536]{1,0:T(8,128)(2,1)S(1)}, bf16[64,1536]{1,0:T(8,128)(2,1)S(1)}, u32[]{:S(2)}, u32[]{:S(2)}) collective-permute-start(bf16[64,1536]{1,0:T(8,128)(2,1)S(1)} %collective-permute-done.3), channel_id=1, source_target_pairs={{0,12},{1,97},{2,14},{3,99},{4,0},{5,101},{6,2},{7,103},{8,4},{9,1... | collective-permute-start | bytes 589832 | tf_op jit(solution)/shard_map/ppermute | solution.py:53
  17.3 10.2 %collective-permute-start.7 = (bf16[64,1536]{1,0:T(8,128)(2,1)S(1)}, bf16[64,1536]{1,0:T(8,128)(2,1)S(1)}, u32[]{:S(2)}, u32[]{:S(2)}) collective-permute-start(bf16[64,1536]{1,0:T(8,128)(2,1)S(1)} %collective-permute-done.3), channel_id=1, source_target_pairs={{0,8},{1,65},{2,10},{3,67},{4,12},{5,69},{6,14},{7,71},{8,0},{9,73... | collective-permute-start | bytes 589832 | tf_op jit(solution)/shard_map/ppermute | solution.py:53
  17.8 12.3 %collective-permute-start.6 = (bf16[64,1536]{1,0:T(8,128)(2,1)S(1)}, bf16[64,1536]{1,0:T(8,128)(2,1)S(1)}, u32[]{:S(2)}, u32[]{:S(2)}) collective-permute-start(bf16[64,1536]{1,0:T(8,128)(2,1)S(1)} %collective-permute-done.3), channel_id=1, source_target_pairs={{0,4},{1,33},{2,6},{3,35},{4,8},{5,37},{6,10},{7,39},{8,12},{9,41}... | collective-permute-start | bytes 589832 | tf_op jit(solution)/shard_map/ppermute | solution.py:53
  30.3 2.3 %copy-start.2 = (bf16[4,64,1536]{2,1,0:T(8,128)(2,1)}, bf16[4,64,1536]{2,1,0:T(8,128)(2,1)S(1)}, u32[]{:S(2)}) copy-start(bf16[4,64,1536]{2,1,0:T(8,128)(2,1)S(1)} %pad_maximum_fusion.3.refs_0_.refs_7_) | copy-start | bytes 2359300
  31.2 0.9 copy-start.7
  31.2 1.2 copy-start.8
  32.6 19.6 %collective-permute-start.10 = (bf16[6,64,1536]{2,1,0:T(8,128)(2,1)S(1)}, bf16[6,64,1536]{2,1,0:T(8,128)(2,1)}, u32[]{:S(2)}, u32[]{:S(2)}) collective-permute-start(bf16[6,64,1536]{2,1,0:T(8,128)(2,1)S(1)} %get-tuple-element.52), channel_id=1, source_target_pairs={{0,96},{1,13},{2,98},{3,15},{4,100},{5,1},{6,102},{7,3},{8,104},{9... | collective-permute-start | bytes 3538952 | tf_op jit(solution)/shard_map/ppermute | solution.py:53
  32.7 19.6 %collective-permute-start.9 = (bf16[6,64,1536]{2,1,0:T(8,128)(2,1)S(1)}, bf16[6,64,1536]{2,1,0:T(8,128)(2,1)}, u32[]{:S(2)}, u32[]{:S(2)}) collective-permute-start(bf16[6,64,1536]{2,1,0:T(8,128)(2,1)S(1)} %get-tuple-element.53), channel_id=1, source_target_pairs={{0,32},{1,5},{2,34},{3,7},{4,36},{5,9},{6,38},{7,11},{8,40},{9,13}... | collective-permute-start | bytes 3538952 | tf_op jit(solution)/shard_map/ppermute | solution.py:53
  35.3 16.9 %all-to-all-start = ((bf16[8,192,256]{2,1,0:T(8,128)(2,1)}), bf16[8,192,256]{2,1,0:T(8,128)(2,1)S(1)}, u32[]{:S(2)}, u32[]{:S(2)}) async-start(bf16[8,192,256]{2,1,0:T(8,128)(2,1)} %get-tuple-element.37), calls=%async_computation | async-start | bytes 1572864 | tf_op jit(solution)/shard_map/all_to_all | solution.py:252
  45.9 6.3 %collective-permute-start.11 = (bf16[3,2,192,256]{3,2,1,0:T(8,128)(2,1)}, bf16[3,2,192,256]{3,2,1,0:T(8,128)(2,1)}, u32[]{:S(2)}, u32[]{:S(2)}) collective-permute-start(bf16[3,2,192,256]{3,2,1,0:T(8,128)(2,1)} %get-tuple-element.36), channel_id=1, source_target_pairs={{0,1},{1,0},{2,3},{3,2},{4,5},{5,4},{6,7},{7,6},{8,9},{9,8},{10,11... | collective-permute-start | bytes 1769480 | tf_op jit(solution)/shard_map/ppermute | solution.py:21
  52.2 58.5 %copy-start.4 = (bf16[8,192,256]{2,1,0:T(8,128)(2,1)}, bf16[8,192,256]{2,1,0:T(8,128)(2,1)S(1)}, u32[]{:S(2)}) copy-start(bf16[8,192,256]{2,1,0:T(8,128)(2,1)S(1)} %all-to-all-done.refs_0_) | copy-start | bytes 2359300
  54.6 10.0 %collective-permute-start.13 = (bf16[2,64,1536]{2,1,0:T(8,128)(2,1)S(1)}, bf16[2,64,1536]{2,1,0:T(8,128)(2,1)S(1)}, u32[]{:S(2)}, u32[]{:S(2)}) collective-permute-start(bf16[2,64,1536]{2,1,0:T(8,128)(2,1)S(1)} %slice.15), channel_id=1, source_target_pairs={{0,96},{1,13},{2,98},{3,15},{4,100},{5,1},{6,102},{7,3},{8,104},{9... | collective-permute-start | bytes 1179656 | tf_op jit(solution)/shard_map/ppermute | solution.py:53
  54.9 9.8 %collective-permute-start.12 = (bf16[2,64,1536]{2,1,0:T(8,128)(2,1)S(1)}, bf16[2,64,1536]{2,1,0:T(8,128)(2,1)S(1)}, u32[]{:S(2)}, u32[]{:S(2)}) collective-permute-start(bf16[2,64,1536]{2,1,0:T(8,128)(2,1)S(1)} %slice.14), channel_id=1, source_target_pairs={{0,32},{1,5},{2,34},{3,7},{4,36},{5,9},{6,38},{7,11},{8,40},{9,13}... | collective-permute-start | bytes 1179656 | tf_op jit(solution)/shard_map/ppermute | solution.py:53
  64.6 5.6 %copy-start.11 = (bf16[4,2,192,256]{3,2,1,0:T(8,128)(2,1)S(1)}, bf16[4,2,192,256]{3,2,1,0:T(8,128)(2,1)}, u32[]{:S(2)}) copy-start(bf16[4,2,192,256]{3,2,1,0:T(8,128)(2,1)} %get-tuple-element.44) | copy-start | bytes 2359300
  64.6 0.7 copy-start.5
  65.3 0.7 copy-start.6
  70.2 12.8 %collective-permute-start.14 = (bf16[4,2,192,256]{3,2,1,0:T(8,128)(2,1)S(1)}, bf16[4,2,192,256]{3,2,1,0:T(8,128)(2,1)S(1)}, u32[]{:S(2)}, u32[]{:S(2)}) collective-permute-start(bf16[4,2,192,256]{3,2,1,0:T(8,128)(2,1)S(1)} %copy-done.11), channel_id=1, source_target_pairs={{0,1},{1,0},{2,3},{3,2},{4,5},{5,4},{6,7},{7,6},{8,9},{9,8},{10,11... | collective-permute-start | bytes 2359304 | tf_op jit(solution)/shard_map/ppermute | solution.py:21
  81.1 29.6 %collective-permute-start.16 = (bf16[8,192,256]{2,1,0:T(8,128)(2,1)S(1)}, bf16[8,192,256]{2,1,0:T(8,128)(2,1)S(1)}, u32[]{:S(2)}, u32[]{:S(2)}) collective-permute-start(bf16[8,192,256]{2,1,0:T(8,128)(2,1)S(1)} %all-to-all-done.refs_0_), channel_id=1, source_target_pairs={{0,2},{1,3},{2,0},{3,1},{4,6},{5,7},{6,4},{7,5},{8,10},{9,11},{10,... | collective-permute-start | bytes 2359304 | tf_op jit(solution)/shard_map/ppermute | solution.py:21
  81.9 4.9 %collective-permute-start.15 = (bf16[1,2,192,256]{3,2,1,0:T(8,128)(2,1)}, bf16[1,2,192,256]{3,2,1,0:T(8,128)(2,1)S(1)}, u32[]{:S(2)}, u32[]{:S(2)}) collective-permute-start(bf16[1,2,192,256]{3,2,1,0:T(8,128)(2,1)} %get-tuple-element.43), channel_id=1, source_target_pairs={{0,1},{1,0},{2,3},{3,2},{4,5},{5,4},{6,7},{7,6},{8,9},{9,8},{10,11... | collective-permute-start | bytes 589832 | tf_op jit(solution)/shard_map/ppermute | solution.py:21
  83.0 0.9 copy-start.1
  86.8 0.7 copy-start.9
  90.1 39.9 %all-to-all-start.1 = ((bf16[16,192,256]{2,1,0:T(8,128)(2,1)}), bf16[16,192,256]{2,1,0:T(8,128)(2,1)S(1)}, u32[]{:S(2)}, u32[]{:S(2)}) async-start(bf16[16,192,256]{2,1,0:T(8,128)(2,1)} %bitcast.17), calls=%async_computation.1 | async-start | bytes 3145728 | tf_op jit(solution)/shard_map/all_to_all | solution.py:304
  110.7 6.1 %copy-start.10 = (bf16[8,192,256]{2,1,0:T(8,128)(2,1)}, bf16[8,192,256]{2,1,0:T(8,128)(2,1)S(1)}, u32[]{:S(2)}) copy-start(bf16[8,192,256]{2,1,0:T(8,128)(2,1)S(1)} %collective-permute-done.16.refs_1_) | copy-start | bytes 2359300
  110.7 5.0 %collective-permute-start.17 = (bf16[8,192,256]{2,1,0:T(8,128)(2,1)S(1)}, bf16[8,192,256]{2,1,0:T(8,128)(2,1)S(1)}, u32[]{:S(2)}, u32[]{:S(2)}) collective-permute-start(bf16[8,192,256]{2,1,0:T(8,128)(2,1)S(1)} %all-to-all-done.refs_0_), channel_id=1, source_target_pairs={{0,1},{1,0},{2,3},{3,2},{4,5},{5,4},{6,7},{7,6},{8,9},{9,8},{10,11... | collective-permute-start | bytes 2359304 | tf_op jit(solution)/shard_map/ppermute | solution.py:21
  113.8 3.0 %collective-permute-start.18 = (bf16[8,192,256]{2,1,0:T(8,128)(2,1)S(1)}, bf16[8,192,256]{2,1,0:T(8,128)(2,1)S(1)}, u32[]{:S(2)}, u32[]{:S(2)}) collective-permute-start(bf16[8,192,256]{2,1,0:T(8,128)(2,1)S(1)} %collective-permute-done.16.refs_1_), channel_id=1, source_target_pairs={{0,1},{1,0},{2,3},{3,2},{4,5},{5,4},{6,7},{7,6},{8,9},{9,8},{10,11... | collective-permute-start | bytes 2359304 | tf_op jit(solution)/shard_map/ppermute | solution.py:21
  115.7 1.1 copy-start.12
  116.8 0.9 copy-start.13
  130.0 1.2 copy-start

commit v6 on v4

--- a/solution.py
+++ b/solution.py
@@ -53,12 +53,13 @@
     return lax.ppermute(v, ("gx", "gy", "gz"), pairs)
 
 
-def call(body, out_shape, in_specs, cost, out_specs=None, scratch=(), limit=56):
+def call(body, out_shape, in_specs, cost, out_specs=None, scratch=(), grid=(), limit=56):
     if out_specs is None:
         out_specs = [VMEM] * len(out_shape)
     flops, moved = cost
     return pl.pallas_call(
         body,
+        grid=grid,
         out_shape=[jax.ShapeDtypeStruct(*s) for s in out_shape],
         in_specs=in_specs,
         out_specs=out_specs,
@@ -68,10 +69,13 @@
     )
 
 
-def one_hot():
+def one_hot(at=None):
     q = lax.broadcasted_iota(jnp.int32, (256, 256), 0)
     u = lax.broadcasted_iota(jnp.int32, (256, 256), 1)
-    return jnp.where(u == (q % 32) * 8 + q // 32, 1.0, 0.0).astype(bf16)
+    s = q // 32
+    if at is not None:
+        s = ((at[0] - s // 2) & 3) * 2 + ((at[1] + s) & 1)
+    return jnp.where(u == (q % 32) * 8 + s, 1.0, 0.0).astype(bf16)
 
 
 def group(at, k, z):
@@ -83,8 +87,8 @@
 
 
 def pack_body(at, pre, *outs):
-    slope, parts = outs
-    pick = one_hot()
+    slope, parts = outs[0], outs[1:]
+    pick = one_hot(at)
     for j in range(pre.shape[1] // 256):
         cols = slice(256 * j, 256 * j + 256)
         u = jnp.concatenate([pre[token_rows(at[2], k), cols] for k in range(4)], 0)
@@ -97,7 +101,7 @@
         turned = lax.dot_general(pick, hidden, (((1,), (1,)), ((), ())), preferred_element_type=f32)
         turned = turned.astype(bf16)
         for i in range(8):
-            parts[i, 32 * j : 32 * j + 32, :] = turned[32 * i : 32 * i + 32, :]
+            parts[i // 2][i % 2, 32 * j : 32 * j + 32, :] = turned[32 * i : 32 * i + 32, :]
 
 
 def load_grads(at, pieces, held, sems):
@@ -122,17 +126,20 @@
                 c.wait()
 
 
-def input_body(count, at, w, *refs):
-    pieces, (mine, theirs, held, sums, in_sems, out_sems) = refs[:count], refs[count:]
+def input_body(count, at, w_hbm, *refs):
+    pieces, (mine, theirs, w, held, sums, w_sem, in_sems, out_sems) = refs[:count], refs[count:]
+    load = pltpu.make_async_copy(w_hbm, w, w_sem)
+    load.start()
     blocks = [p.at[z] for p in pieces for z in range(p.shape[0])]
     for i, src in enumerate(blocks):
         pltpu.make_async_copy(src, held.at[i], in_sems.at[i]).start()
+    load.wait()
     rows = w.shape[0] // 4
 
     def leaving(i):
         slot = i % 2
         return [
-            pltpu.make_async_copy(sums.at[slot, n], out.at[i], out_sems.at[slot, n])
+            pltpu.make_async_copy(sums.at[slot, at[4] ^ n], out.at[i], out_sems.at[slot, n])
             for n, out in enumerate((mine, theirs))
         ]
 
@@ -149,7 +156,7 @@
             w[...], held[i].reshape(256, -1), (((1,), (1,)), ((), ())), preferred_element_type=f32
         ).astype(bf16)
         for n in range(4):
-            sums[i % 2, at[4] ^ (n % 2), n // 2] = part[n * rows : n * rows + rows]
+            sums[i % 2, n % 2, n // 2] = part[n * rows : n * rows + rows]
         for c in leaving(i):
             c.start()
 
@@ -163,10 +170,10 @@
         n = 2 * k + z
         return pltpu.make_async_copy(held.at[n], out.at[group(at, k, z)], sems.at[n])
 
-    def block(early, late, k, z, lo):
+    def block(early, late, k, z, lo, lanes=slice(None)):
         if k == 2:
-            return late[z, lo]
-        return early[2 * (k - k // 3) + z, lo]
+            return late[z, lo, :, lanes]
+        return early[2 * (k - k // 3) + z, lo, :, lanes]
 
     for core in range(2):
 
@@ -177,9 +184,9 @@
                 by_x, by_y = by_y, by_x
             for z in range(2):
                 for lo in range(2):
-                    y = [block(*by_y, k, z, lo) for k in range(4)]
                     for k in range(4):
-                        turned = jnp.concatenate([v[:, 64 * k : 64 * k + 64] for v in y], 1)
+                        lanes = pl.ds(64 * k, 64)
+                        turned = jnp.concatenate([block(*by_y, n, z, lo, lanes) for n in range(4)], 1)
                         total = block(*by_x, k, z, lo).astype(f32) + turned.astype(f32)
                         held[2 * k + z, lo] = total.astype(bf16)
                 for k in range(4):
@@ -191,15 +198,12 @@
 
 
 def finish_body(at, slope, parts, out):
-    pick = one_hot()
-    for j in range(out.shape[1] // 256):
-        cols, units = slice(256 * j, 256 * j + 256), slice(32 * j, 32 * j + 32)
-        v = [(parts[n, 0, units, :].astype(f32) + parts[n, 1, units, :].astype(f32)) for n in range(8)]
-        v = jnp.concatenate(v, 0).astype(bf16)
-        total = lax.dot_general(v, pick, (((0,), (0,)), ((), ())), preferred_element_type=f32)
-        result = (total * slope[:, cols]).astype(bf16)
-        for k in range(4):
-            out[token_rows(at[2], k), cols] = result[64 * k : 64 * k + 64, :]
+    v = [parts[n, 0].astype(f32) + parts[n, 1].astype(f32) for n in range(8)]
+    v = jnp.concatenate(v, 0).astype(bf16)
+    total = lax.dot_general(v, one_hot(), (((0,), (0,)), ((), ())), preferred_element_type=f32)
+    result = (total * slope[...]).astype(bf16)
+    for k in range(4):
+        out[token_rows(at[2], k), :] = result[64 * k : 64 * k + 64, :]
 
 
 def weight_body(at, *refs):
@@ -207,7 +211,7 @@
     load_grads(at, pieces, held, sems)
     rows = out.shape[0] // 4
     lhs = jnp.concatenate(
-        [jnp.concatenate([h[group(at, k, z)] for k in range(4) for z in range(2)], 1) for h in hidden], 0
+        [jnp.concatenate([h[z, k] for k in range(4) for z in range(2)], 1) for h in hidden], 0
     )
 
     @pl.loop(0, out.shape[1] // 256)
@@ -231,23 +235,25 @@
     grad_scratch = [pltpu.VMEM((4, 2, 4, tokens // 4, features), bf16), pltpu.SemaphoreType.DMA((8,))]
     product = 2 * 4 * rows * 8 * tokens * features
 
-    slope, parts = call(
+    slope, *parts = call(
         pack_body,
-        [((tokens, columns), f32), ((8,) + block, bf16)],
+        [((tokens, columns), f32)] + [((2,) + block, bf16)] * 4,
         [SMEM, VMEM],
         (2 * tokens * 256 * columns, 8 * tokens * columns),
     )(at, pre_act)
 
-    other, parts = lax.optimization_barrier((swap_z_hi(grad_out), parts))
-    both = jnp.stack([grad_out, other])
-    first = [send_by_core(both, k, True) for k in (1, 2, 3)]
-    own = lax.all_to_all(parts, "gx", 0, 0, tiled=True)
-    first, own = lax.optimization_barrier((first, own))
-    p0 = jnp.stack([both] + first, 1)
+    other = swap_z_hi(grad_out)
+    first = [[v] + [send_by_core(v, k, True) for k in (1, 2, 3)] for v in (grad_out, other)]
+
+    by_x = [parts[0]] + [send_x(parts[4 - k], k) for k in (1, 2, 3)]
+    first, by_x = lax.optimization_barrier((first, by_x))
+    p0 = jnp.stack([jnp.stack(v) for v in first])
     p1, p3 = send_by_core(p0, 1, False), send_by_core(p0, 3, False)
 
     p2p, p2m = send_by_core(p1[:1], 1, False), send_by_core(p3[1:], 3, False)
     pieces = p0, p1, p3, p2p, p2m
+    own = jnp.stack([p[0] for p in by_x])
+    own = jnp.stack([own, swap_z_hi(jnp.stack([p[1] for p in by_x]))])
     far = swap_z_lo(own)
 
     def input_part(*given):
@@ -255,22 +261,22 @@
         return call(
             functools.partial(input_body, len(given)),
             [((count, 2) + block, bf16)] * 2,
-            [SMEM, VMEM] + [HBM] * len(given),
+            [SMEM, HBM] + [HBM] * len(given),
             (product * count // 8, 2 * (4 * rows * features + count * (4 * rows + features) * tokens)),
             out_specs=[HBM] * 2,
             scratch=[
+                pltpu.VMEM((4 * rows, features), bf16),
                 pltpu.VMEM((count, 4, tokens // 4, features), bf16),
                 pltpu.VMEM((2, 2, 2) + block, bf16),
+                pltpu.SemaphoreType.DMA,
                 pltpu.SemaphoreType.DMA((count,)),
                 pltpu.SemaphoreType.DMA((2, 2)),
             ],
         )(at, w, *given)
 
-    early = lax.optimization_barrier((p0, p1, p3, far))
+    early = lax.optimization_barrier((p0, p1, p3, own))
     mine, theirs = input_part(*early[:3])
     other = swap_core(theirs)
-    hidden = [own, far, swap_core(own), swap_core(far)]
-    p2p, p2m, hidden = lax.optimization_barrier((p2p, p2m, hidden))
     mine2, theirs2 = input_part(p2p, p2m)
     size = 2 * 4 * rows * tokens
     (sums,) = call(
@@ -285,7 +291,8 @@
     back = lax.all_to_all(
         sums.reshape((16,) + block), ("gx", "gz"), 0, 0, tiled=True, axis_index_groups=same_core
     )
-    hidden, _ = lax.optimization_barrier((hidden, sums))
+    own, far, _ = lax.optimization_barrier((own, far, sums))
+    hidden = [own, far, swap_core(own), swap_core(far)]
     (weight_grad,) = call(
         weight_body,
         [((4 * rows, features), bf16)],
@@ -297,8 +304,14 @@
     (pre_grad,) = call(
         finish_body,
         [((tokens, columns), bf16)],
-        [SMEM] + [VMEM] * 2,
+        [
+            SMEM,
+            pl.BlockSpec((tokens, 256), lambda j: (0, j)),
+            pl.BlockSpec((8, 2, 32, tokens), lambda j: (0, 0, j, 0)),
+        ],
         (2 * tokens * 256 * columns, 8 * tokens * columns),
+        out_specs=[pl.BlockSpec((tokens, 256), lambda j: (0, j))],
+        grid=(columns // 256,),
     )(at, slope, back.reshape((8, 2) + block))
     return pre_grad, weight_grad.reshape(weight.shape)
 

time: 119 us -> 118 us (level)
  waiting for transfers between devices: 47.4 us -> 39 us
  local copies, waits for them, and re-layouts: 3.38 us -> 6.08 us
  Pallas kernels: 36.2 us -> 38.9 us
  other arithmetic: 0.25 us -> 2.37 us
    all_to_all x1 -> x0, starting transfers between devices: 6.98 us -> none  [per_device(): own = lax.all_to_all(parts, 'gx', 0, 0, tiled=True)]
    all_to_all x1, waiting for transfers between devices: 12.8 us -> 6.28 us  [per_device(): lax.all_to_all(sums.reshape((16,) + block), ('gx', 'gz'), 0, 0, tiled=Tru...]
    all_to_all x1 -> x0, waiting for transfers between devices: 5.05 us -> none  [per_device(): own = lax.all_to_all(parts, 'gx', 0, 0, tiled=True)]
    ppermute x7 -> x10, waiting for transfers between devices: 9.07 us -> 14.1 us  [send_by_core(): return lax.ppermute(v, ('gx', 'gy', 'gz'), pairs)]
    ppermute x7 -> x10, starting transfers between devices: 10.8 us -> 15.4 us  [send_by_core(): return lax.ppermute(v, ('gx', 'gy', 'gz'), pairs)]
    unnamed x18 -> x22, local copies, waits for them, and re-layouts: 2.62 us -> 5.32 us
    ppermute x6 -> x10, starting transfers between devices: 9.11 us -> 11.4 us  [send(): return lax.ppermute(v, axis, [(i, to(i)) for i in range(count)])]
    another operation x2 -> x5, other arithmetic: 0.25 us -> 2.37 us  [the longest x2 1.27 us: per_device(): p0 = jnp.stack([jnp.stack(v) for v in first])]
  transfers between devices with their start and end apart: 15 -> 21, of which waited for: 9 -> 10; matrix products, arithmetic and copies ran while one was open for 1% -> 2% of each run, Pallas kernels for 25% -> 28%
where the time goes in v6:
time: 118 us
  waiting for transfers between devices  39 us (33%)
  Pallas kernels  38.9 us (33%)
  starting transfers between devices  30.6 us (26%)
  local copies, waits for them, and re-layouts  6.08 us (5%)
  other arithmetic  2.37 us (2%)
    ppermute x10, waiting for transfers between devices, send(): return lax.ppermute(v, axis, [(i, to(i)) for i in range(count)])  18.7 us
    ppermute x10, starting transfers between devices, send_by_core(): return lax.ppermute(v, ('gx', 'gy', 'gz'), pairs)  15.4 us
    pallas_call x2, Pallas kernels, input_part(): call(functools.partial(input_body, len(given)), [((count, 2) + block, bf1...  14.2 us
    ppermute x10, waiting for transfers between devices, send_by_core(): return lax.ppermute(v, ('gx', 'gy', 'gz'), pairs)  14.1 us
    pallas_call x1, Pallas kernels, per_device(): call(weight_body, [((4 * rows, features), bf16)], [SMEM] + [VMEM] * 4 + [...  12.2 us
    ppermute x10, starting transfers between devices, send(): return lax.ppermute(v, axis, [(i, to(i)) for i in range(count)])  11.4 us
    all_to_all x1, waiting for transfers between devices, per_device(): lax.all_to_all(sums.reshape((16,) + block), ('gx', 'gz'), 0, 0, tiled=Tru...  6.28 us
    unnamed x22, local copies, waits for them, and re-layouts  5.32 us
  transfers between devices with their start and end apart: 21, of which 10 were waited for; matrix products, arithmetic and copies ran while one was open for 2% of the time, Pallas kernels for 28%

profile of v6, /device:TPU:0, one launch (start us, length us, event | category | flops | bytes accessed | tf_op | source)
XLA Modules:
  0.0 117.8 jit_solution(4660871521117103271)
XLA Ops:
  0.6 3.2 %collective-permute-start.2 = (bf16[64,1536]{1,0:T(8,128)(2,1)}, bf16[64,1536]{1,0:T(8,128)(2,1)S(1)}, u32[]{:S(2)}, u32[]{:S(2)}) collective-permute-start(bf16[64,1536]{1,0:T(8,128)(2,1)} %param.4), channel_id=1, source_target_pairs={{0,12},{1,97},{2,14},{3,99},{4,0},{5,101},{6,2},{7,103},{8,4},{9,1... | collective-permute-start | bytes 589832 | tf_op jit(solution)/shard_map/ppermute | solution.py:53
  3.8 0.6 collective-permute-start.1
  4.4 1.0 collective-permute-start
  5.4 3.9 %collective-permute-start.3 = (bf16[64,1536]{1,0:T(8,128)(2,1)}, bf16[64,1536]{1,0:T(8,128)(2,1)S(1)}, u32[]{:S(2)}, u32[]{:S(2)}) collective-permute-start(bf16[64,1536]{1,0:T(8,128)(2,1)} %param.4), channel_id=1, source_target_pairs={{0,16},{16,0},{32,48},{48,32},{64,80},{80,64},{96,112},{112,96},{1... | collective-permute-start | bytes 589832 | tf_op jit(solution)/shard_map/ppermute | solution.py:21
  9.3 0.6 stack.77.at
  9.9 3.7 %shard_map.50 = (f32[256,1536]{1,0:T(8,128)}, bf16[2,192,256]{2,1,0:T(8,128)(2,1)}, bf16[2,192,256]{2,1,0:T(8,128)(2,1)}, bf16[2,192,256]{2,1,0:T(8,128)(2,1)}, bf16[2,192,256]{2,1,0:T(8,128)(2,1)}) custom-call(s32[5]{0:T(128)} %stack.77.at, bf16[256,1536]{1,0:T(8,128)(2,1)} %pre.1), custom_call_target="tpu_custom_call" | custom-call | flops 201326592 | bytes 3145728 | tf_op jit(solution)/shard_map/pallas_call | solution.py:238
  13.6 1.5 %collective-permute-start.7 = (bf16[2,192,256]{2,1,0:T(8,128)(2,1)}, bf16[2,192,256]{2,1,0:T(8,128)(2,1)S(1)}, u32[]{:S(2)}, u32[]{:S(2)}) collective-permute-start(bf16[2,192,256]{2,1,0:T(8,128)(2,1)} %get-tuple-element.32), channel_id=1, source_target_pairs={{0,32},{16,48},{32,64},{48,80},{64,96},{80,112},{96,0},{112,16},{1... | collective-permute-start | bytes 589832 | tf_op jit(solution)/shard_map/ppermute | solution.py:21
  15.1 0.0 collective-permute-done.2
  15.1 2.7 %collective-permute-start.8 = (bf16[2,192,256]{2,1,0:T(8,128)(2,1)}, bf16[2,192,256]{2,1,0:T(8,128)(2,1)S(1)}, u32[]{:S(2)}, u32[]{:S(2)}) collective-permute-start(bf16[2,192,256]{2,1,0:T(8,128)(2,1)} %get-tuple-element.33), channel_id=1, source_target_pairs={{0,64},{16,80},{32,96},{48,112},{64,0},{80,16},{96,32},{112,48},{1... | collective-permute-start | bytes 589832 | tf_op jit(solution)/shard_map/ppermute | solution.py:21
  17.8 0.0 collective-permute-done.1
  17.8 1.4 %collective-permute-start.9 = (bf16[2,192,256]{2,1,0:T(8,128)(2,1)}, bf16[2,192,256]{2,1,0:T(8,128)(2,1)S(1)}, u32[]{:S(2)}, u32[]{:S(2)}) collective-permute-start(bf16[2,192,256]{2,1,0:T(8,128)(2,1)} %get-tuple-element.34), channel_id=1, source_target_pairs={{0,96},{16,112},{32,0},{48,16},{64,32},{80,48},{96,64},{112,80},{1... | collective-permute-start | bytes 589832 | tf_op jit(solution)/shard_map/ppermute | solution.py:21
  19.2 0.0 collective-permute-done.3
  19.3 2.3 %collective-permute-start.6 = (bf16[64,1536]{1,0:T(8,128)(2,1)S(1)}, bf16[64,1536]{1,0:T(8,128)(2,1)S(1)}, u32[]{:S(2)}, u32[]{:S(2)}) collective-permute-start(bf16[64,1536]{1,0:T(8,128)(2,1)S(1)} %collective-permute-done.3), channel_id=1, source_target_pairs={{0,12},{1,97},{2,14},{3,99},{4,0},{5,101},{6,2},{7,103},{8,4},{9,1... | collective-permute-start | bytes 589832 | tf_op jit(solution)/shard_map/ppermute | solution.py:53
  21.5 0.0 collective-permute-done
  21.5 1.7 %collective-permute-start.5 = (bf16[64,1536]{1,0:T(8,128)(2,1)S(1)}, bf16[64,1536]{1,0:T(8,128)(2,1)S(1)}, u32[]{:S(2)}, u32[]{:S(2)}) collective-permute-start(bf16[64,1536]{1,0:T(8,128)(2,1)S(1)} %collective-permute-done.3), channel_id=1, source_target_pairs={{0,8},{1,65},{2,10},{3,67},{4,12},{5,69},{6,14},{7,71},{8,0},{9,73... | collective-permute-start | bytes 589832 | tf_op jit(solution)/shard_map/ppermute | solution.py:53
  23.2 3.4 %collective-permute-done.7 = bf16[2,192,256]{2,1,0:T(8,128)(2,1)S(1)} collective-permute-done((bf16[2,192,256]{2,1,0:T(8,128)(2,1)}, bf16[2,192,256]{2,1,0:T(8,128)(2,1)S(1)}, u32[]{:S(2)}, u32[]{:S(2)}) %collective-permute-start.7) | collective-permute-done | bytes 196640 | tf_op jit(solution)/shard_map/ppermute | solution.py:21
  26.7 2.6 %collective-permute-start.4 = (bf16[64,1536]{1,0:T(8,128)(2,1)S(1)}, bf16[64,1536]{1,0:T(8,128)(2,1)S(1)}, u32[]{:S(2)}, u32[]{:S(2)}) collective-permute-start(bf16[64,1536]{1,0:T(8,128)(2,1)S(1)} %collective-permute-done.3), channel_id=1, source_target_pairs={{0,4},{1,33},{2,6},{3,35},{4,8},{5,37},{6,10},{7,39},{8,12},{9,41}... | collective-permute-start | bytes 589832 | tf_op jit(solution)/shard_map/ppermute | solution.py:53
  29.3 0.0 collective-permute-done.8
  29.3 0.0 collective-permute-done.9
  29.3 0.0 collective-permute-done.6
  29.3 0.0 collective-permute-done.5
  29.3 4.2 %collective-permute-done.4 = bf16[64,1536]{1,0:T(8,128)(2,1)S(1)} collective-permute-done((bf16[64,1536]{1,0:T(8,128)(2,1)S(1)}, bf16[64,1536]{1,0:T(8,128)(2,1)S(1)}, u32[]{:S(2)}, u32[]{:S(2)}) %collective-permute-start.4) | collective-permute-done | bytes 196640 | tf_op jit(solution)/shard_map/ppermute | solution.py:53
  33.5 1.1 maximum_bitcast_fusion
  34.7 0.0 copy-start.6
  34.7 0.1 pad_maximum_fusion.refs_0_.refs_4_
  34.8 0.1 collective-permute-start.11
  34.9 2.0 %collective-permute-start.10 = (bf16[2,4,64,1536]{3,2,1,0:T(8,128)(2,1)S(1)}, bf16[2,4,64,1536]{3,2,1,0:T(8,128)(2,1)S(1)}, u32[]{:S(2)}, u32[]{:S(2)}) collective-permute-start(bf16[2,4,64,1536]{3,2,1,0:T(8,128)(2,1)S(1)} %pad_maximum_fusion.refs_0_.refs_4_), channel_id=1, source_target_pairs={{0,32},{1,5},{2,34},{3,7},{4,36},{5,9},{6,38},{7,11},{8,40},{9,13}... | collective-permute-start | bytes 4718600 | tf_op jit(solution)/shard_map/ppermute | solution.py:53
  37.0 0.1 pad_maximum_fusion.2
  37.1 0.1 collective-permute-start.12
  37.2 0.1 maximum_bitcast_fusion.2
  37.2 9.2 %collective-permute-done.12 = bf16[4,192,256]{2,1,0:T(8,128)(2,1)S(1)} collective-permute-done((bf16[4,192,256]{2,1,0:T(8,128)(2,1)S(1)}, bf16[4,192,256]{2,1,0:T(8,128)(2,1)S(1)}, u32[]{:S(2)}, u32[]{:S(2)}) %collective-permute-start.12) | collective-permute-done | bytes 393248 | tf_op jit(solution)/shard_map/ppermute | solution.py:21
  46.4 1.0 pad_maximum_fusion.1.refs_0_
  47.4 7.9 %collective-permute-done.11.refs_2_.refs_6_ = bf16[2,4,64,1536]{3,2,1,0:T(8,128)(2,1)S(1)} collective-permute-done((bf16[2,4,64,1536]{3,2,1,0:T(8,128)(2,1)S(1)}, bf16[2,4,64,1536]{3,2,1,0:T(8,128)(2,1)S(1)}, u32[]{:S(2)}, u32[]{:S(2)}) %collective-permute-start.11) | collective-permute-done | bytes 1572896 | tf_op jit(solution)/shard_map/ppermute | solution.py:53
  55.3 0.1 slice.41
  55.4 1.3 %collective-permute-start.14 = (bf16[1,4,64,1536]{3,2,1,0:T(8,128)(2,1)S(1)}, bf16[1,4,64,1536]{3,2,1,0:T(8,128)(2,1)}, u32[]{:S(2)}, u32[]{:S(2)}) collective-permute-start(bf16[1,4,64,1536]{3,2,1,0:T(8,128)(2,1)S(1)} %slice.41), channel_id=1, source_target_pairs={{0,96},{1,13},{2,98},{3,15},{4,100},{5,1},{6,102},{7,3},{8,104},{9... | collective-permute-start | bytes 2359304 | tf_op jit(solution)/shard_map/ppermute | solution.py:53
  56.7 0.2 collective-permute-done.10.refs_1_.refs_5_
  56.9 0.1 slice.40
  56.9 0.7 collective-permute-start.13
  57.6 0.4 copy-done.5
  58.0 9.2 %shard_map.51 = (bf16[6,2,192,256]{3,2,1,0:T(8,128)(2,1)}, bf16[6,2,192,256]{3,2,1,0:T(8,128)(2,1)}) custom-call(s32[5]{0:T(128)} %stack.77.at, bf16[768,1536]{1,0:T(8,128)(2,1)} %bitcast.35, bf16[2,4,64,1536]{3,2,1,0:T(8,128)(2,1)} %copy-done.1, bf16[2,4,64,1536]{3,2,1,0:T(8,128)(2,1)} %copy-done.5, bf16[2,4,64,1536]{3,2,1,0:T(8,128)(2,1)} %copy-done.4), custom_call_target="tpu_custom_call" | custom-call | flops 3623878656 | bytes 9437184 | tf_op jit(solution)/shard_map/pallas_call | solution.py:261
  67.2 0.1 collective-permute-start.15
  67.3 1.2 collective-permute-start.17
  68.5 0.0 collective-permute-done.14.refs_1_.refs_8_
  68.5 1.7 %collective-permute-done.13.refs_0_.refs_7_ = bf16[1,4,64,1536]{3,2,1,0:T(8,128)(2,1)S(1)} collective-permute-done((bf16[1,4,64,1536]{3,2,1,0:T(8,128)(2,1)S(1)}, bf16[1,4,64,1536]{3,2,1,0:T(8,128)(2,1)S(1)}, u32[]{:S(2)}, u32[]{:S(2)}) %collective-permute-start.13) | collective-permute-done | bytes 786464 | tf_op jit(solution)/shard_map/ppermute | solution.py:53
  70.2 0.9 copy-done.7
  71.1 5.0 %shard_map.52 = (bf16[2,2,192,256]{3,2,1,0:T(8,128)(2,1)}, bf16[2,2,192,256]{3,2,1,0:T(8,128)(2,1)}) custom-call(s32[5]{0:T(128)} %stack.77.at, bf16[768,1536]{1,0:T(8,128)(2,1)} %bitcast.36, bf16[1,4,64,1536]{3,2,1,0:T(8,128)(2,1)} %copy-done.7, bf16[1,4,64,1536]{3,2,1,0:T(8,128)(2,1)} %collective-permute-done.14.refs_1_.refs_8_), custom_call_target="tpu_custom_call" | custom-call | flops 1207959552 | bytes 4718592 | tf_op jit(solution)/shard_map/pallas_call | solution.py:261
  76.1 0.1 collective-permute-start.16
  76.2 1.9 %collective-permute-done.16.other2 = bf16[2,2,192,256]{3,2,1,0:T(8,128)(2,1)S(1)} collective-permute-done((bf16[2,2,192,256]{3,2,1,0:T(8,128)(2,1)}, bf16[2,2,192,256]{3,2,1,0:T(8,128)(2,1)S(1)}, u32[]{:S(2)}, u32[]{:S(2)}) %collective-permute-start.16) | collective-permute-done | bytes 393248 | tf_op jit(solution)/shard_map/ppermute | solution.py:21
  78.1 0.0 collective-permute-done.15.other
  78.1 0.8 copy-done.3
  78.9 0.4 copy-done.2
  79.3 3.4 %shard_map.53 = bf16[8,2,192,256]{3,2,1,0:T(8,128)(2,1)} custom-call(s32[5]{0:T(128)} %stack.77.at, bf16[6,2,192,256]{3,2,1,0:T(8,128)(2,1)} %get-tuple-element.50.mine, bf16[2,2,192,256]{3,2,1,0:T(8,128)(2,1)} %get-tuple-element.51.mine2, bf16[6,2,192,256]{3,2,1,0:T(8,128)(2,1)} %copy-done.2, bf16[2,2,192,256]{3,2,1,0:T(8,128)(2,1)} %copy-done.3), custom_call_target="tpu_custom_call" | custom-call | flops 1572864 | bytes 4718592 | tf_op jit(solution)/shard_map/pallas_call | solution.py:282
  82.7 3.7 %all-to-all-start = ((bf16[16,192,256]{2,1,0:T(8,128)(2,1)}), bf16[16,192,256]{2,1,0:T(8,128)(2,1)S(1)}, u32[]{:S(2)}, u32[]{:S(2)}) async-start(bf16[16,192,256]{2,1,0:T(8,128)(2,1)} %bitcast.24), calls=%async_computation | async-start | bytes 3145728 | tf_op jit(solution)/shard_map/all_to_all | solution.py:291
  86.4 1.1 collective-permute-done.17.refs_1_
  87.5 0.0 collective-permute-start.18
  87.5 0.5 collective-permute-start.19
  88.0 3.1 %collective-permute-done.18.refs_2_ = bf16[2,4,192,256]{3,2,1,0:T(8,128)(2,1)S(1)} collective-permute-done((bf16[2,4,192,256]{3,2,1,0:T(8,128)(2,1)}, bf16[2,4,192,256]{3,2,1,0:T(8,128)(2,1)S(1)}, u32[]{:S(2)}, u32[]{:S(2)}) %collective-permute-start.18) | collective-permute-done | bytes 786464 | tf_op jit(solution)/shard_map/ppermute | solution.py:21
  91.1 0.0 collective-permute-done.19.refs_3_
  91.1 0.9 copy-done.9
  92.0 0.9 copy-done.10
  92.8 12.2 %shard_map.54 = bf16[768,1536]{1,0:T(8,128)(2,1)} custom-call(s32[5]{0:T(128)} %stack.77.at, bf16[2,4,192,256]{3,2,1,0:T(8,128)(2,1)} %pad_maximum_fusion.1.refs_0_, bf16[2,4,192,256]{3,2,1,0:T(8,128)(2,1)} %copy-done.8, bf16[2,4,192,256]{3,2,1,0:T(8,128)(2,1)} %copy-done.9, bf16[2,4,192,256]{3,2,1,0:T(8,128)(2,1)} %copy-done.10, ...), custom_call_target="tpu_custom_call" | custom-call | flops 4831838208 | bytes 11010048 | tf_op jit(solution)/shard_map/pallas_call | solution.py:296
  105.0 6.3 %all-to-all-done = bf16[16,192,256]{2,1,0:T(8,128)(2,1)S(1)} async-done(((bf16[16,192,256]{2,1,0:T(8,128)(2,1)}), bf16[16,192,256]{2,1,0:T(8,128)(2,1)S(1)}, u32[]{:S(2)}, u32[]{:S(2)}) %all-to-all-start) | async-done | bytes 1572896 | tf_op jit(solution)/shard_map/all_to_all | solution.py:291
  111.3 1.1 copy-done
  112.5 5.3 %shard_map.55 = bf16[256,1536]{1,0:T(8,128)(2,1)} custom-call(s32[5]{0:T(128)} %stack.77.at, f32[256,1536]{1,0:T(8,128)} %get-tuple-element.30.slope, bf16[8,2,192,256]{3,2,1,0:T(8,128)(2,1)} %bitcast.25), custom_call_target="tpu_custom_call" | custom-call | flops 201326592 | bytes 3145728 | tf_op jit(solution)/shard_map/pallas_call | solution.py:304
  (16 shorter events, 0.1 us)
Async XLA Ops:
  0.6 14.5 %collective-permute-start.2 = (bf16[64,1536]{1,0:T(8,128)(2,1)}, bf16[64,1536]{1,0:T(8,128)(2,1)S(1)}, u32[]{:S(2)}, u32[]{:S(2)}) collective-permute-start(bf16[64,1536]{1,0:T(8,128)(2,1)} %param.4), channel_id=1, source_target_pairs={{0,12},{1,97},{2,14},{3,99},{4,0},{5,101},{6,2},{7,103},{8,4},{9,1... | collective-permute-start | bytes 589832 | tf_op jit(solution)/shard_map/ppermute | solution.py:53
  3.8 14.0 %collective-permute-start.1 = (bf16[64,1536]{1,0:T(8,128)(2,1)}, bf16[64,1536]{1,0:T(8,128)(2,1)S(1)}, u32[]{:S(2)}, u32[]{:S(2)}) collective-permute-start(bf16[64,1536]{1,0:T(8,128)(2,1)} %param.4), channel_id=1, source_target_pairs={{0,8},{1,65},{2,10},{3,67},{4,12},{5,69},{6,14},{7,71},{8,0},{9,73... | collective-permute-start | bytes 589832 | tf_op jit(solution)/shard_map/ppermute | solution.py:53
  4.4 17.1 %collective-permute-start = (bf16[64,1536]{1,0:T(8,128)(2,1)}, bf16[64,1536]{1,0:T(8,128)(2,1)S(1)}, u32[]{:S(2)}, u32[]{:S(2)}) collective-permute-start(bf16[64,1536]{1,0:T(8,128)(2,1)} %param.4), channel_id=1, source_target_pairs={{0,4},{1,33},{2,6},{3,35},{4,8},{5,37},{6,10},{7,39},{8,12},{9,41}... | collective-permute-start | bytes 589832 | tf_op jit(solution)/shard_map/ppermute | solution.py:53
  5.4 13.9 %collective-permute-start.3 = (bf16[64,1536]{1,0:T(8,128)(2,1)}, bf16[64,1536]{1,0:T(8,128)(2,1)S(1)}, u32[]{:S(2)}, u32[]{:S(2)}) collective-permute-start(bf16[64,1536]{1,0:T(8,128)(2,1)} %param.4), channel_id=1, source_target_pairs={{0,16},{16,0},{32,48},{48,32},{64,80},{80,64},{96,112},{112,96},{1... | collective-permute-start | bytes 589832 | tf_op jit(solution)/shard_map/ppermute | solution.py:21
  13.6 13.1 %collective-permute-start.7 = (bf16[2,192,256]{2,1,0:T(8,128)(2,1)}, bf16[2,192,256]{2,1,0:T(8,128)(2,1)S(1)}, u32[]{:S(2)}, u32[]{:S(2)}) collective-permute-start(bf16[2,192,256]{2,1,0:T(8,128)(2,1)} %get-tuple-element.32), channel_id=1, source_target_pairs={{0,32},{16,48},{32,64},{48,80},{64,96},{80,112},{96,0},{112,16},{1... | collective-permute-start | bytes 589832 | tf_op jit(solution)/shard_map/ppermute | solution.py:21
  15.1 14.2 %collective-permute-start.8 = (bf16[2,192,256]{2,1,0:T(8,128)(2,1)}, bf16[2,192,256]{2,1,0:T(8,128)(2,1)S(1)}, u32[]{:S(2)}, u32[]{:S(2)}) collective-permute-start(bf16[2,192,256]{2,1,0:T(8,128)(2,1)} %get-tuple-element.33), channel_id=1, source_target_pairs={{0,64},{16,80},{32,96},{48,112},{64,0},{80,16},{96,32},{112,48},{1... | collective-permute-start | bytes 589832 | tf_op jit(solution)/shard_map/ppermute | solution.py:21
  17.8 11.5 %collective-permute-start.9 = (bf16[2,192,256]{2,1,0:T(8,128)(2,1)}, bf16[2,192,256]{2,1,0:T(8,128)(2,1)S(1)}, u32[]{:S(2)}, u32[]{:S(2)}) collective-permute-start(bf16[2,192,256]{2,1,0:T(8,128)(2,1)} %get-tuple-element.34), channel_id=1, source_target_pairs={{0,96},{16,112},{32,0},{48,16},{64,32},{80,48},{96,64},{112,80},{1... | collective-permute-start | bytes 589832 | tf_op jit(solution)/shard_map/ppermute | solution.py:21
  19.3 10.0 %collective-permute-start.6 = (bf16[64,1536]{1,0:T(8,128)(2,1)S(1)}, bf16[64,1536]{1,0:T(8,128)(2,1)S(1)}, u32[]{:S(2)}, u32[]{:S(2)}) collective-permute-start(bf16[64,1536]{1,0:T(8,128)(2,1)S(1)} %collective-permute-done.3), channel_id=1, source_target_pairs={{0,12},{1,97},{2,14},{3,99},{4,0},{5,101},{6,2},{7,103},{8,4},{9,1... | collective-permute-start | bytes 589832 | tf_op jit(solution)/shard_map/ppermute | solution.py:53
  21.5 7.8 %collective-permute-start.5 = (bf16[64,1536]{1,0:T(8,128)(2,1)S(1)}, bf16[64,1536]{1,0:T(8,128)(2,1)S(1)}, u32[]{:S(2)}, u32[]{:S(2)}) collective-permute-start(bf16[64,1536]{1,0:T(8,128)(2,1)S(1)} %collective-permute-done.3), channel_id=1, source_target_pairs={{0,8},{1,65},{2,10},{3,67},{4,12},{5,69},{6,14},{7,71},{8,0},{9,73... | collective-permute-start | bytes 589832 | tf_op jit(solution)/shard_map/ppermute | solution.py:53
  26.7 6.9 %collective-permute-start.4 = (bf16[64,1536]{1,0:T(8,128)(2,1)S(1)}, bf16[64,1536]{1,0:T(8,128)(2,1)S(1)}, u32[]{:S(2)}, u32[]{:S(2)}) collective-permute-start(bf16[64,1536]{1,0:T(8,128)(2,1)S(1)} %collective-permute-done.3), channel_id=1, source_target_pairs={{0,4},{1,33},{2,6},{3,35},{4,8},{5,37},{6,10},{7,39},{8,12},{9,41}... | collective-permute-start | bytes 589832 | tf_op jit(solution)/shard_map/ppermute | solution.py:53
  34.7 2.3 %copy-start.6 = (bf16[2,192,256]{2,1,0:T(8,128)(2,1)S(1)}, bf16[2,192,256]{2,1,0:T(8,128)(2,1)}, u32[]{:S(2)}) copy-start(bf16[2,192,256]{2,1,0:T(8,128)(2,1)} %get-tuple-element.43) | copy-start | bytes 589828
  34.8 2.4 %copy-start.1 = (bf16[2,4,64,1536]{3,2,1,0:T(8,128)(2,1)}, bf16[2,4,64,1536]{3,2,1,0:T(8,128)(2,1)S(1)}, u32[]{:S(2)}) copy-start(bf16[2,4,64,1536]{3,2,1,0:T(8,128)(2,1)S(1)} %pad_maximum_fusion.refs_0_.refs_4_) | copy-start | bytes 4718596
  34.8 20.5 %collective-permute-start.11 = (bf16[2,4,64,1536]{3,2,1,0:T(8,128)(2,1)S(1)}, bf16[2,4,64,1536]{3,2,1,0:T(8,128)(2,1)S(1)}, u32[]{:S(2)}, u32[]{:S(2)}) collective-permute-start(bf16[2,4,64,1536]{3,2,1,0:T(8,128)(2,1)S(1)} %pad_maximum_fusion.refs_0_.refs_4_), channel_id=1, source_target_pairs={{0,96},{1,13},{2,98},{3,15},{4,100},{5,1},{6,102},{7,3},{8,104},{9... | collective-permute-start | bytes 4718600 | tf_op jit(solution)/shard_map/ppermute | solution.py:53
  34.9 21.9 %collective-permute-start.10 = (bf16[2,4,64,1536]{3,2,1,0:T(8,128)(2,1)S(1)}, bf16[2,4,64,1536]{3,2,1,0:T(8,128)(2,1)S(1)}, u32[]{:S(2)}, u32[]{:S(2)}) collective-permute-start(bf16[2,4,64,1536]{3,2,1,0:T(8,128)(2,1)S(1)} %pad_maximum_fusion.refs_0_.refs_4_), channel_id=1, source_target_pairs={{0,32},{1,5},{2,34},{3,7},{4,36},{5,9},{6,38},{7,11},{8,40},{9,13}... | collective-permute-start | bytes 4718600 | tf_op jit(solution)/shard_map/ppermute | solution.py:53
  37.1 9.4 %collective-permute-start.12 = (bf16[4,192,256]{2,1,0:T(8,128)(2,1)S(1)}, bf16[4,192,256]{2,1,0:T(8,128)(2,1)S(1)}, u32[]{:S(2)}, u32[]{:S(2)}) collective-permute-start(bf16[4,192,256]{2,1,0:T(8,128)(2,1)S(1)} %pad_maximum_fusion.2), channel_id=1, source_target_pairs={{0,16},{16,0},{32,48},{48,32},{64,80},{80,64},{96,112},{112,96},{1... | collective-permute-start | bytes 1179656 | tf_op jit(solution)/shard_map/ppermute | solution.py:21
  55.3 1.6 %copy-start.4 = (bf16[2,4,64,1536]{3,2,1,0:T(8,128)(2,1)}, bf16[2,4,64,1536]{3,2,1,0:T(8,128)(2,1)S(1)}, u32[]{:S(2)}) copy-start(bf16[2,4,64,1536]{3,2,1,0:T(8,128)(2,1)S(1)} %collective-permute-done.11.refs_2_.refs_6_) | copy-start | bytes 4718596
  55.4 13.1 %collective-permute-start.14 = (bf16[1,4,64,1536]{3,2,1,0:T(8,128)(2,1)S(1)}, bf16[1,4,64,1536]{3,2,1,0:T(8,128)(2,1)}, u32[]{:S(2)}, u32[]{:S(2)}) collective-permute-start(bf16[1,4,64,1536]{3,2,1,0:T(8,128)(2,1)S(1)} %slice.41), channel_id=1, source_target_pairs={{0,96},{1,13},{2,98},{3,15},{4,100},{5,1},{6,102},{7,3},{8,104},{9... | collective-permute-start | bytes 2359304 | tf_op jit(solution)/shard_map/ppermute | solution.py:53
  56.9 1.1 copy-start.5
  56.9 13.3 %collective-permute-start.13 = (bf16[1,4,64,1536]{3,2,1,0:T(8,128)(2,1)S(1)}, bf16[1,4,64,1536]{3,2,1,0:T(8,128)(2,1)S(1)}, u32[]{:S(2)}, u32[]{:S(2)}) collective-permute-start(bf16[1,4,64,1536]{3,2,1,0:T(8,128)(2,1)S(1)} %slice.40), channel_id=1, source_target_pairs={{0,32},{1,5},{2,34},{3,7},{4,36},{5,9},{6,38},{7,11},{8,40},{9,13}... | collective-permute-start | bytes 2359304 | tf_op jit(solution)/shard_map/ppermute | solution.py:53
  67.2 10.9 %collective-permute-start.15 = (bf16[6,2,192,256]{3,2,1,0:T(8,128)(2,1)}, bf16[6,2,192,256]{3,2,1,0:T(8,128)(2,1)S(1)}, u32[]{:S(2)}, u32[]{:S(2)}) collective-permute-start(bf16[6,2,192,256]{3,2,1,0:T(8,128)(2,1)} %get-tuple-element.52), channel_id=1, source_target_pairs={{0,1},{1,0},{2,3},{3,2},{4,5},{5,4},{6,7},{7,6},{8,9},{9,8},{10,11... | collective-permute-start | bytes 3538952 | tf_op jit(solution)/shard_map/ppermute | solution.py:21
  67.3 20.2 %collective-permute-start.17 = (bf16[2,4,192,256]{3,2,1,0:T(8,128)(2,1)}, bf16[2,4,192,256]{3,2,1,0:T(8,128)(2,1)S(1)}, u32[]{:S(2)}, u32[]{:S(2)}) collective-permute-start(bf16[2,4,192,256]{3,2,1,0:T(8,128)(2,1)} %pad_maximum_fusion.1.refs_0_), channel_id=1, source_target_pairs={{0,2},{1,3},{2,0},{3,1},{4,6},{5,7},{6,4},{7,5},{8,10},{9,11},{10,... | collective-permute-start | bytes 2359304 | tf_op jit(solution)/shard_map/ppermute | solution.py:21
  70.2 0.9 copy-start.7
  76.1 2.0 %collective-permute-start.16 = (bf16[2,2,192,256]{3,2,1,0:T(8,128)(2,1)}, bf16[2,2,192,256]{3,2,1,0:T(8,128)(2,1)S(1)}, u32[]{:S(2)}, u32[]{:S(2)}) collective-permute-start(bf16[2,2,192,256]{3,2,1,0:T(8,128)(2,1)} %get-tuple-element.53), channel_id=1, source_target_pairs={{0,1},{1,0},{2,3},{3,2},{4,5},{5,4},{6,7},{7,6},{8,9},{9,8},{10,11... | collective-permute-start | bytes 1179656 | tf_op jit(solution)/shard_map/ppermute | solution.py:21
  78.1 0.8 copy-start.3
  78.1 1.1 copy-start.2
  82.7 28.6 %all-to-all-start = ((bf16[16,192,256]{2,1,0:T(8,128)(2,1)}), bf16[16,192,256]{2,1,0:T(8,128)(2,1)S(1)}, u32[]{:S(2)}, u32[]{:S(2)}) async-start(bf16[16,192,256]{2,1,0:T(8,128)(2,1)} %bitcast.24), calls=%async_computation | async-start | bytes 3145728 | tf_op jit(solution)/shard_map/all_to_all | solution.py:291
  87.5 3.6 %copy-start.8 = (bf16[2,4,192,256]{3,2,1,0:T(8,128)(2,1)}, bf16[2,4,192,256]{3,2,1,0:T(8,128)(2,1)S(1)}, u32[]{:S(2)}) copy-start(bf16[2,4,192,256]{3,2,1,0:T(8,128)(2,1)S(1)} %collective-permute-done.17.refs_1_) | copy-start | bytes 2359300
  87.5 3.6 %collective-permute-start.18 = (bf16[2,4,192,256]{3,2,1,0:T(8,128)(2,1)}, bf16[2,4,192,256]{3,2,1,0:T(8,128)(2,1)S(1)}, u32[]{:S(2)}, u32[]{:S(2)}) collective-permute-start(bf16[2,4,192,256]{3,2,1,0:T(8,128)(2,1)} %pad_maximum_fusion.1.refs_0_), channel_id=1, source_target_pairs={{0,1},{1,0},{2,3},{3,2},{4,5},{5,4},{6,7},{7,6},{8,9},{9,8},{10,11... | collective-permute-start | bytes 2359304 | tf_op jit(solution)/shard_map/ppermute | solution.py:21
  87.5 3.6 %collective-permute-start.19 = (bf16[2,4,192,256]{3,2,1,0:T(8,128)(2,1)S(1)}, bf16[2,4,192,256]{3,2,1,0:T(8,128)(2,1)S(1)}, u32[]{:S(2)}, u32[]{:S(2)}) collective-permute-start(bf16[2,4,192,256]{3,2,1,0:T(8,128)(2,1)S(1)} %collective-permute-done.17.refs_1_), channel_id=1, source_target_pairs={{0,1},{1,0},{2,3},{3,2},{4,5},{5,4},{6,7},{7,6},{8,9},{9,8},{10,11... | collective-permute-start | bytes 2359304 | tf_op jit(solution)/shard_map/ppermute | solution.py:21
  91.1 0.9 copy-start.9
  92.0 0.9 copy-start.10
  111.3 1.1 copy-start

commit v7 on v6

--- a/solution.py
+++ b/solution.py
@@ -53,13 +53,12 @@
     return lax.ppermute(v, ("gx", "gy", "gz"), pairs)
 
 
-def call(body, out_shape, in_specs, cost, out_specs=None, scratch=(), grid=(), limit=56):
+def call(body, out_shape, in_specs, cost, out_specs=None, scratch=(), limit=56):
     if out_specs is None:
         out_specs = [VMEM] * len(out_shape)
     flops, moved = cost
     return pl.pallas_call(
         body,
-        grid=grid,
         out_shape=[jax.ShapeDtypeStruct(*s) for s in out_shape],
         in_specs=in_specs,
         out_specs=out_specs,
@@ -165,45 +164,51 @@
             c.wait()
 
 
-def core_sum_body(at, mine, mine2, other, other2, out, held, sems):
-    def leaving(k, z):
-        n = 2 * k + z
-        return pltpu.make_async_copy(held.at[n], out.at[group(at, k, z)], sems.at[n])
-
-    def block(early, late, k, z, lo, lanes=slice(None)):
-        if k == 2:
-            return late[z, lo, :, lanes]
-        return early[2 * (k - k // 3) + z, lo, :, lanes]
-
-    for core in range(2):
-
-        @pl.when(at[4] == core)
-        def _():
-            by_x, by_y = (mine, mine2), (other, other2)
-            if core:
-                by_x, by_y = by_y, by_x
-            for z in range(2):
-                for lo in range(2):
-                    for k in range(4):
-                        lanes = pl.ds(64 * k, 64)
-                        turned = jnp.concatenate([block(*by_y, n, z, lo, lanes) for n in range(4)], 1)
-                        total = block(*by_x, k, z, lo).astype(f32) + turned.astype(f32)
-                        held[2 * k + z, lo] = total.astype(bf16)
-                for k in range(4):
-                    leaving(k, z).start()
-
+def core_sum_body(at, mine, mine2, other, other2, out, given, held, in_sems, out_sems):
+    def coming(n, z, k):
+        early, late = ((mine, mine2), (other, other2))[n]
+        src = late.at[z] if k == 2 else early.at[2 * (k - k // 3) + z]
+        return pltpu.make_async_copy(src, given.at[n, z, k], in_sems.at[n, z, k])
+
+    def leaving(z, k):
+        return pltpu.make_async_copy(held.at[z, k], out.at[group(at, k, z)], out_sems.at[z, k])
+
+    every = [(n, k) for n in range(2) for k in range(4)]
+    for z in range(2):
+        for n, k in every:
+            coming(n, z, k).start()
+    by_x, by_y = at[4], 1 - at[4]
+    for z in range(2):
+        for n, k in every:
+            coming(n, z, k).wait()
+        for k in range(4):
+            lanes = pl.ds(64 * k, 64)
+            for lo in range(2):
+                turned = jnp.concatenate([given[by_y, z, n, lo, :, lanes] for n in range(4)], 1)
+                held[z, k, lo] = (given[by_x, z, k, lo].astype(f32) + turned.astype(f32)).astype(bf16)
+            leaving(z, k).start()
     for z in range(2):
         for k in range(4):
-            leaving(k, z).wait()
-
-
-def finish_body(at, slope, parts, out):
-    v = [parts[n, 0].astype(f32) + parts[n, 1].astype(f32) for n in range(8)]
-    v = jnp.concatenate(v, 0).astype(bf16)
-    total = lax.dot_general(v, one_hot(), (((0,), (0,)), ((), ())), preferred_element_type=f32)
-    result = (total * slope[...]).astype(bf16)
-    for k in range(4):
-        out[token_rows(at[2], k), :] = result[64 * k : 64 * k + 64, :]
+            leaving(z, k).wait()
+
+
+def finish_body(at, slope, parts, out, held, sems):
+    count = out.shape[1] // 256
+    copies = [
+        pltpu.make_async_copy(parts.at[:, :, pl.ds(32 * j, 32), :], held.at[j], sems.at[j]) for j in range(count)
+    ]
+    for c in copies:
+        c.start()
+    pick = one_hot()
+    for j in range(count):
+        cols = slice(256 * j, 256 * j + 256)
+        copies[j].wait()
+        v = [held[j, n, 0].astype(f32) + held[j, n, 1].astype(f32) for n in range(8)]
+        v = jnp.concatenate(v, 0).astype(bf16)
+        total = lax.dot_general(v, pick, (((0,), (0,)), ((), ())), preferred_element_type=f32)
+        result = (total * slope[:, cols]).astype(bf16)
+        for k in range(4):
+            out[token_rows(at[2], k), cols] = result[64 * k : 64 * k + 64, :]
 
 
 def weight_body(at, *refs):
@@ -282,10 +287,15 @@
     (sums,) = call(
         core_sum_body,
         [((8, 2) + block, bf16)],
-        [SMEM] + [VMEM] * 4,
+        [SMEM] + [HBM] * 4,
         (4 * size, 12 * size),
         out_specs=[HBM],
-        scratch=[pltpu.VMEM((8, 2) + block, bf16), pltpu.SemaphoreType.DMA((8,))],
+        scratch=[
+            pltpu.VMEM((2, 2, 4, 2) + block, bf16),
+            pltpu.VMEM((2, 4, 2) + block, bf16),
+            pltpu.SemaphoreType.DMA((2, 2, 4)),
+            pltpu.SemaphoreType.DMA((2, 4)),
+        ],
     )(at, mine, mine2, other, swap_core(theirs2))
     same_core = [[2 * (2 * i + k) + c for i in range(8) for k in range(2)] for c in range(2)]
     back = lax.all_to_all(
@@ -304,14 +314,9 @@
     (pre_grad,) = call(
         finish_body,
         [((tokens, columns), bf16)],
-        [
-            SMEM,
-            pl.BlockSpec((tokens, 256), lambda j: (0, j)),
-            pl.BlockSpec((8, 2, 32, tokens), lambda j: (0, 0, j, 0)),
-        ],
+        [SMEM, VMEM, HBM],
         (2 * tokens * 256 * columns, 8 * tokens * columns),
-        out_specs=[pl.BlockSpec((tokens, 256), lambda j: (0, j))],
-        grid=(columns // 256,),
+        scratch=[pltpu.VMEM((6, 8, 2, 32, tokens), bf16), pltpu.SemaphoreType.DMA((6,))],
     )(at, slope, back.reshape((8, 2) + block))
     return pre_grad, weight_grad.reshape(weight.shape)
 

time: 118 us -> 118 us (level)
  transfers between devices with their start and end apart: 21 -> 21, of which waited for: 10 -> 10; matrix products, arithmetic and copies ran while one was open for 2% -> 2% of each run, Pallas kernels for 28% -> 29%
where the time goes in v7:
time: 118 us
  waiting for transfers between devices  39 us (33%)
  Pallas kernels  38.8 us (33%)
  starting transfers between devices  30.6 us (26%)
  local copies, waits for them, and re-layouts  6.08 us (5%)
  other arithmetic  2.37 us (2%)
    ppermute x10, waiting for transfers between devices, send(): return lax.ppermute(v, axis, [(i, to(i)) for i in range(count)])  18.3 us
    ppermute x10, starting transfers between devices, send_by_core(): return lax.ppermute(v, ('gx', 'gy', 'gz'), pairs)  15.4 us
    pallas_call x2, Pallas kernels, input_part(): call(functools.partial(input_body, len(given)), [((count, 2) + block, bf1...  14.2 us
    ppermute x10, waiting for transfers between devices, send_by_core(): return lax.ppermute(v, ('gx', 'gy', 'gz'), pairs)  14.1 us
    pallas_call x1, Pallas kernels, per_device(): call(weight_body, [((4 * rows, features), bf16)], [SMEM] + [VMEM] * 4 + [...  12.2 us
    ppermute x10, starting transfers between devices, send(): return lax.ppermute(v, axis, [(i, to(i)) for i in range(count)])  11.4 us
    all_to_all x1, waiting for transfers between devices, per_device(): lax.all_to_all(sums.reshape((16,) + block), ('gx', 'gz'), 0, 0, tiled=Tru...  6.69 us
    unnamed x22, local copies, waits for them, and re-layouts  5.32 us
  transfers between devices with their start and end apart: 21, of which 10 were waited for; matrix products, arithmetic and copies ran while one was open for 2% of the time, Pallas kernels for 29%

profile of v7, /device:TPU:0, one launch (start us, length us, event | category | flops | bytes accessed | tf_op | source)
XLA Modules:
  0.0 117.7 jit_solution(4480733799252836347)
XLA Ops:
  0.6 3.2 %collective-permute-start.2 = (bf16[64,1536]{1,0:T(8,128)(2,1)}, bf16[64,1536]{1,0:T(8,128)(2,1)S(1)}, u32[]{:S(2)}, u32[]{:S(2)}) collective-permute-start(bf16[64,1536]{1,0:T(8,128)(2,1)} %param.4), channel_id=1, source_target_pairs={{0,12},{1,97},{2,14},{3,99},{4,0},{5,101},{6,2},{7,103},{8,4},{9,1... | collective-permute-start | bytes 589832 | tf_op jit(solution)/shard_map/ppermute | solution.py:53
  3.8 0.6 collective-permute-start.1
  4.4 1.0 collective-permute-start
  5.4 3.9 %collective-permute-start.3 = (bf16[64,1536]{1,0:T(8,128)(2,1)}, bf16[64,1536]{1,0:T(8,128)(2,1)S(1)}, u32[]{:S(2)}, u32[]{:S(2)}) collective-permute-start(bf16[64,1536]{1,0:T(8,128)(2,1)} %param.4), channel_id=1, source_target_pairs={{0,16},{16,0},{32,48},{48,32},{64,80},{80,64},{96,112},{112,96},{1... | collective-permute-start | bytes 589832 | tf_op jit(solution)/shard_map/ppermute | solution.py:21
  9.3 0.6 stack.77.at
  9.9 3.7 %shard_map.50 = (f32[256,1536]{1,0:T(8,128)}, bf16[2,192,256]{2,1,0:T(8,128)(2,1)}, bf16[2,192,256]{2,1,0:T(8,128)(2,1)}, bf16[2,192,256]{2,1,0:T(8,128)(2,1)}, bf16[2,192,256]{2,1,0:T(8,128)(2,1)}) custom-call(s32[5]{0:T(128)} %stack.77.at, bf16[256,1536]{1,0:T(8,128)(2,1)} %pre.1), custom_call_target="tpu_custom_call" | custom-call | flops 201326592 | bytes 3145728 | tf_op jit(solution)/shard_map/pallas_call | solution.py:243
  13.6 1.5 %collective-permute-start.7 = (bf16[2,192,256]{2,1,0:T(8,128)(2,1)}, bf16[2,192,256]{2,1,0:T(8,128)(2,1)S(1)}, u32[]{:S(2)}, u32[]{:S(2)}) collective-permute-start(bf16[2,192,256]{2,1,0:T(8,128)(2,1)} %get-tuple-element.32), channel_id=1, source_target_pairs={{0,32},{16,48},{32,64},{48,80},{64,96},{80,112},{96,0},{112,16},{1... | collective-permute-start | bytes 589832 | tf_op jit(solution)/shard_map/ppermute | solution.py:21
  15.1 0.0 collective-permute-done.2
  15.1 2.7 %collective-permute-start.8 = (bf16[2,192,256]{2,1,0:T(8,128)(2,1)}, bf16[2,192,256]{2,1,0:T(8,128)(2,1)S(1)}, u32[]{:S(2)}, u32[]{:S(2)}) collective-permute-start(bf16[2,192,256]{2,1,0:T(8,128)(2,1)} %get-tuple-element.33), channel_id=1, source_target_pairs={{0,64},{16,80},{32,96},{48,112},{64,0},{80,16},{96,32},{112,48},{1... | collective-permute-start | bytes 589832 | tf_op jit(solution)/shard_map/ppermute | solution.py:21
  17.8 0.0 collective-permute-done.1
  17.8 1.4 %collective-permute-start.9 = (bf16[2,192,256]{2,1,0:T(8,128)(2,1)}, bf16[2,192,256]{2,1,0:T(8,128)(2,1)S(1)}, u32[]{:S(2)}, u32[]{:S(2)}) collective-permute-start(bf16[2,192,256]{2,1,0:T(8,128)(2,1)} %get-tuple-element.34), channel_id=1, source_target_pairs={{0,96},{16,112},{32,0},{48,16},{64,32},{80,48},{96,64},{112,80},{1... | collective-permute-start | bytes 589832 | tf_op jit(solution)/shard_map/ppermute | solution.py:21
  19.2 0.0 collective-permute-done.3
  19.3 2.3 %collective-permute-start.6 = (bf16[64,1536]{1,0:T(8,128)(2,1)S(1)}, bf16[64,1536]{1,0:T(8,128)(2,1)S(1)}, u32[]{:S(2)}, u32[]{:S(2)}) collective-permute-start(bf16[64,1536]{1,0:T(8,128)(2,1)S(1)} %collective-permute-done.3), channel_id=1, source_target_pairs={{0,12},{1,97},{2,14},{3,99},{4,0},{5,101},{6,2},{7,103},{8,4},{9,1... | collective-permute-start | bytes 589832 | tf_op jit(solution)/shard_map/ppermute | solution.py:53
  21.5 0.0 collective-permute-done
  21.5 1.7 %collective-permute-start.5 = (bf16[64,1536]{1,0:T(8,128)(2,1)S(1)}, bf16[64,1536]{1,0:T(8,128)(2,1)S(1)}, u32[]{:S(2)}, u32[]{:S(2)}) collective-permute-start(bf16[64,1536]{1,0:T(8,128)(2,1)S(1)} %collective-permute-done.3), channel_id=1, source_target_pairs={{0,8},{1,65},{2,10},{3,67},{4,12},{5,69},{6,14},{7,71},{8,0},{9,73... | collective-permute-start | bytes 589832 | tf_op jit(solution)/shard_map/ppermute | solution.py:53
  23.2 3.4 %collective-permute-done.7 = bf16[2,192,256]{2,1,0:T(8,128)(2,1)S(1)} collective-permute-done((bf16[2,192,256]{2,1,0:T(8,128)(2,1)}, bf16[2,192,256]{2,1,0:T(8,128)(2,1)S(1)}, u32[]{:S(2)}, u32[]{:S(2)}) %collective-permute-start.7) | collective-permute-done | bytes 196640 | tf_op jit(solution)/shard_map/ppermute | solution.py:21
  26.7 2.6 %collective-permute-start.4 = (bf16[64,1536]{1,0:T(8,128)(2,1)S(1)}, bf16[64,1536]{1,0:T(8,128)(2,1)S(1)}, u32[]{:S(2)}, u32[]{:S(2)}) collective-permute-start(bf16[64,1536]{1,0:T(8,128)(2,1)S(1)} %collective-permute-done.3), channel_id=1, source_target_pairs={{0,4},{1,33},{2,6},{3,35},{4,8},{5,37},{6,10},{7,39},{8,12},{9,41}... | collective-permute-start | bytes 589832 | tf_op jit(solution)/shard_map/ppermute | solution.py:53
  29.3 0.0 collective-permute-done.8
  29.3 0.0 collective-permute-done.9
  29.3 0.0 collective-permute-done.6
  29.3 0.0 collective-permute-done.5
  29.3 4.2 %collective-permute-done.4 = bf16[64,1536]{1,0:T(8,128)(2,1)S(1)} collective-permute-done((bf16[64,1536]{1,0:T(8,128)(2,1)S(1)}, bf16[64,1536]{1,0:T(8,128)(2,1)S(1)}, u32[]{:S(2)}, u32[]{:S(2)}) %collective-permute-start.4) | collective-permute-done | bytes 196640 | tf_op jit(solution)/shard_map/ppermute | solution.py:53
  33.5 1.1 maximum_bitcast_fusion
  34.7 0.0 copy-start.6
  34.7 0.1 pad_maximum_fusion.refs_0_.refs_4_
  34.8 0.1 collective-permute-start.11
  34.9 2.0 %collective-permute-start.10 = (bf16[2,4,64,1536]{3,2,1,0:T(8,128)(2,1)S(1)}, bf16[2,4,64,1536]{3,2,1,0:T(8,128)(2,1)S(1)}, u32[]{:S(2)}, u32[]{:S(2)}) collective-permute-start(bf16[2,4,64,1536]{3,2,1,0:T(8,128)(2,1)S(1)} %pad_maximum_fusion.refs_0_.refs_4_), channel_id=1, source_target_pairs={{0,32},{1,5},{2,34},{3,7},{4,36},{5,9},{6,38},{7,11},{8,40},{9,13}... | collective-permute-start | bytes 4718600 | tf_op jit(solution)/shard_map/ppermute | solution.py:53
  37.0 0.1 pad_maximum_fusion.2
  37.1 0.1 collective-permute-start.12
  37.2 0.1 maximum_bitcast_fusion.2
  37.2 9.2 %collective-permute-done.12 = bf16[4,192,256]{2,1,0:T(8,128)(2,1)S(1)} collective-permute-done((bf16[4,192,256]{2,1,0:T(8,128)(2,1)S(1)}, bf16[4,192,256]{2,1,0:T(8,128)(2,1)S(1)}, u32[]{:S(2)}, u32[]{:S(2)}) %collective-permute-start.12) | collective-permute-done | bytes 393248 | tf_op jit(solution)/shard_map/ppermute | solution.py:21
  46.4 1.0 pad_maximum_fusion.1.refs_0_
  47.4 7.9 %collective-permute-done.11.refs_2_.refs_6_ = bf16[2,4,64,1536]{3,2,1,0:T(8,128)(2,1)S(1)} collective-permute-done((bf16[2,4,64,1536]{3,2,1,0:T(8,128)(2,1)S(1)}, bf16[2,4,64,1536]{3,2,1,0:T(8,128)(2,1)S(1)}, u32[]{:S(2)}, u32[]{:S(2)}) %collective-permute-start.11) | collective-permute-done | bytes 1572896 | tf_op jit(solution)/shard_map/ppermute | solution.py:53
  55.3 0.1 slice.41
  55.4 1.3 %collective-permute-start.14 = (bf16[1,4,64,1536]{3,2,1,0:T(8,128)(2,1)S(1)}, bf16[1,4,64,1536]{3,2,1,0:T(8,128)(2,1)}, u32[]{:S(2)}, u32[]{:S(2)}) collective-permute-start(bf16[1,4,64,1536]{3,2,1,0:T(8,128)(2,1)S(1)} %slice.41), channel_id=1, source_target_pairs={{0,96},{1,13},{2,98},{3,15},{4,100},{5,1},{6,102},{7,3},{8,104},{9... | collective-permute-start | bytes 2359304 | tf_op jit(solution)/shard_map/ppermute | solution.py:53
  56.7 0.2 collective-permute-done.10.refs_1_.refs_5_
  56.9 0.1 slice.40
  56.9 0.7 collective-permute-start.13
  57.6 0.4 copy-done.5
  58.0 9.2 %shard_map.51 = (bf16[6,2,192,256]{3,2,1,0:T(8,128)(2,1)}, bf16[6,2,192,256]{3,2,1,0:T(8,128)(2,1)}) custom-call(s32[5]{0:T(128)} %stack.77.at, bf16[768,1536]{1,0:T(8,128)(2,1)} %bitcast.35, bf16[2,4,64,1536]{3,2,1,0:T(8,128)(2,1)} %copy-done.1, bf16[2,4,64,1536]{3,2,1,0:T(8,128)(2,1)} %copy-done.5, bf16[2,4,64,1536]{3,2,1,0:T(8,128)(2,1)} %copy-done.4), custom_call_target="tpu_custom_call" | custom-call | flops 3623878656 | bytes 9437184 | tf_op jit(solution)/shard_map/pallas_call | solution.py:266
  67.2 0.1 collective-permute-start.15
  67.3 1.2 collective-permute-start.17
  68.5 0.0 collective-permute-done.14.refs_1_.refs_8_
  68.5 1.7 %collective-permute-done.13.refs_0_.refs_7_ = bf16[1,4,64,1536]{3,2,1,0:T(8,128)(2,1)S(1)} collective-permute-done((bf16[1,4,64,1536]{3,2,1,0:T(8,128)(2,1)S(1)}, bf16[1,4,64,1536]{3,2,1,0:T(8,128)(2,1)S(1)}, u32[]{:S(2)}, u32[]{:S(2)}) %collective-permute-start.13) | collective-permute-done | bytes 786464 | tf_op jit(solution)/shard_map/ppermute | solution.py:53
  70.2 0.9 copy-done.7
  71.1 5.0 %shard_map.52 = (bf16[2,2,192,256]{3,2,1,0:T(8,128)(2,1)}, bf16[2,2,192,256]{3,2,1,0:T(8,128)(2,1)}) custom-call(s32[5]{0:T(128)} %stack.77.at, bf16[768,1536]{1,0:T(8,128)(2,1)} %bitcast.36, bf16[1,4,64,1536]{3,2,1,0:T(8,128)(2,1)} %copy-done.7, bf16[1,4,64,1536]{3,2,1,0:T(8,128)(2,1)} %collective-permute-done.14.refs_1_.refs_8_), custom_call_target="tpu_custom_call" | custom-call | flops 1207959552 | bytes 4718592 | tf_op jit(solution)/shard_map/pallas_call | solution.py:266
  76.1 0.1 collective-permute-start.16
  76.2 1.9 %collective-permute-done.16.other2 = bf16[2,2,192,256]{3,2,1,0:T(8,128)(2,1)S(1)} collective-permute-done((bf16[2,2,192,256]{3,2,1,0:T(8,128)(2,1)}, bf16[2,2,192,256]{3,2,1,0:T(8,128)(2,1)S(1)}, u32[]{:S(2)}, u32[]{:S(2)}) %collective-permute-start.16) | collective-permute-done | bytes 393248 | tf_op jit(solution)/shard_map/ppermute | solution.py:21
  78.1 0.0 collective-permute-done.15.other
  78.1 0.8 copy-done.3
  78.9 0.4 copy-done.2
  79.3 3.8 %shard_map.53 = bf16[8,2,192,256]{3,2,1,0:T(8,128)(2,1)} custom-call(s32[5]{0:T(128)} %stack.77.at, bf16[6,2,192,256]{3,2,1,0:T(8,128)(2,1)} %get-tuple-element.50.mine, bf16[2,2,192,256]{3,2,1,0:T(8,128)(2,1)} %get-tuple-element.51.mine2, bf16[6,2,192,256]{3,2,1,0:T(8,128)(2,1)} %copy-done.2, bf16[2,2,192,256]{3,2,1,0:T(8,128)(2,1)} %copy-done.3), custom_call_target="tpu_custom_call" | custom-call | flops 1572864 | bytes 4718592 | tf_op jit(solution)/shard_map/pallas_call | solution.py:287
  83.1 3.7 %all-to-all-start = ((bf16[16,192,256]{2,1,0:T(8,128)(2,1)}), bf16[16,192,256]{2,1,0:T(8,128)(2,1)S(1)}, u32[]{:S(2)}, u32[]{:S(2)}) async-start(bf16[16,192,256]{2,1,0:T(8,128)(2,1)} %bitcast.24), calls=%async_computation | async-start | bytes 3145728 | tf_op jit(solution)/shard_map/all_to_all | solution.py:301
  86.8 0.6 collective-permute-done.17.refs_1_
  87.5 0.0 collective-permute-start.18
  87.5 0.5 collective-permute-start.19
  88.0 3.1 %collective-permute-done.18.refs_2_ = bf16[2,4,192,256]{3,2,1,0:T(8,128)(2,1)S(1)} collective-permute-done((bf16[2,4,192,256]{3,2,1,0:T(8,128)(2,1)}, bf16[2,4,192,256]{3,2,1,0:T(8,128)(2,1)S(1)}, u32[]{:S(2)}, u32[]{:S(2)}) %collective-permute-start.18) | collective-permute-done | bytes 786464 | tf_op jit(solution)/shard_map/ppermute | solution.py:21
  91.1 0.0 collective-permute-done.19.refs_3_
  91.1 0.9 copy-done.9
  92.0 0.9 copy-done.10
  92.8 12.2 %shard_map.54 = bf16[768,1536]{1,0:T(8,128)(2,1)} custom-call(s32[5]{0:T(128)} %stack.77.at, bf16[2,4,192,256]{3,2,1,0:T(8,128)(2,1)} %pad_maximum_fusion.1.refs_0_, bf16[2,4,192,256]{3,2,1,0:T(8,128)(2,1)} %copy-done.8, bf16[2,4,192,256]{3,2,1,0:T(8,128)(2,1)} %copy-done.9, bf16[2,4,192,256]{3,2,1,0:T(8,128)(2,1)} %copy-done.10, ...), custom_call_target="tpu_custom_call" | custom-call | flops 4831838208 | bytes 11010048 | tf_op jit(solution)/shard_map/pallas_call | solution.py:306
  105.0 6.7 %all-to-all-done = bf16[16,192,256]{2,1,0:T(8,128)(2,1)S(1)} async-done(((bf16[16,192,256]{2,1,0:T(8,128)(2,1)}), bf16[16,192,256]{2,1,0:T(8,128)(2,1)S(1)}, u32[]{:S(2)}, u32[]{:S(2)}) %all-to-all-start) | async-done | bytes 1572896 | tf_op jit(solution)/shard_map/all_to_all | solution.py:301
  111.7 1.1 copy-done
  112.9 4.8 %shard_map.55 = bf16[256,1536]{1,0:T(8,128)(2,1)} custom-call(s32[5]{0:T(128)} %stack.77.at, f32[256,1536]{1,0:T(8,128)} %get-tuple-element.30.slope, bf16[8,2,192,256]{3,2,1,0:T(8,128)(2,1)} %bitcast.25), custom_call_target="tpu_custom_call" | custom-call | flops 201326592 | bytes 3145728 | tf_op jit(solution)/shard_map/pallas_call | solution.py:314
  (16 shorter events, 0.1 us)
Async XLA Ops:
  0.6 14.5 %collective-permute-start.2 = (bf16[64,1536]{1,0:T(8,128)(2,1)}, bf16[64,1536]{1,0:T(8,128)(2,1)S(1)}, u32[]{:S(2)}, u32[]{:S(2)}) collective-permute-start(bf16[64,1536]{1,0:T(8,128)(2,1)} %param.4), channel_id=1, source_target_pairs={{0,12},{1,97},{2,14},{3,99},{4,0},{5,101},{6,2},{7,103},{8,4},{9,1... | collective-permute-start | bytes 589832 | tf_op jit(solution)/shard_map/ppermute | solution.py:53
  3.8 14.0 %collective-permute-start.1 = (bf16[64,1536]{1,0:T(8,128)(2,1)}, bf16[64,1536]{1,0:T(8,128)(2,1)S(1)}, u32[]{:S(2)}, u32[]{:S(2)}) collective-permute-start(bf16[64,1536]{1,0:T(8,128)(2,1)} %param.4), channel_id=1, source_target_pairs={{0,8},{1,65},{2,10},{3,67},{4,12},{5,69},{6,14},{7,71},{8,0},{9,73... | collective-permute-start | bytes 589832 | tf_op jit(solution)/shard_map/ppermute | solution.py:53
  4.4 17.1 %collective-permute-start = (bf16[64,1536]{1,0:T(8,128)(2,1)}, bf16[64,1536]{1,0:T(8,128)(2,1)S(1)}, u32[]{:S(2)}, u32[]{:S(2)}) collective-permute-start(bf16[64,1536]{1,0:T(8,128)(2,1)} %param.4), channel_id=1, source_target_pairs={{0,4},{1,33},{2,6},{3,35},{4,8},{5,37},{6,10},{7,39},{8,12},{9,41}... | collective-permute-start | bytes 589832 | tf_op jit(solution)/shard_map/ppermute | solution.py:53
  5.4 13.9 %collective-permute-start.3 = (bf16[64,1536]{1,0:T(8,128)(2,1)}, bf16[64,1536]{1,0:T(8,128)(2,1)S(1)}, u32[]{:S(2)}, u32[]{:S(2)}) collective-permute-start(bf16[64,1536]{1,0:T(8,128)(2,1)} %param.4), channel_id=1, source_target_pairs={{0,16},{16,0},{32,48},{48,32},{64,80},{80,64},{96,112},{112,96},{1... | collective-permute-start | bytes 589832 | tf_op jit(solution)/shard_map/ppermute | solution.py:21
  13.6 13.1 %collective-permute-start.7 = (bf16[2,192,256]{2,1,0:T(8,128)(2,1)}, bf16[2,192,256]{2,1,0:T(8,128)(2,1)S(1)}, u32[]{:S(2)}, u32[]{:S(2)}) collective-permute-start(bf16[2,192,256]{2,1,0:T(8,128)(2,1)} %get-tuple-element.32), channel_id=1, source_target_pairs={{0,32},{16,48},{32,64},{48,80},{64,96},{80,112},{96,0},{112,16},{1... | collective-permute-start | bytes 589832 | tf_op jit(solution)/shard_map/ppermute | solution.py:21
  15.1 14.2 %collective-permute-start.8 = (bf16[2,192,256]{2,1,0:T(8,128)(2,1)}, bf16[2,192,256]{2,1,0:T(8,128)(2,1)S(1)}, u32[]{:S(2)}, u32[]{:S(2)}) collective-permute-start(bf16[2,192,256]{2,1,0:T(8,128)(2,1)} %get-tuple-element.33), channel_id=1, source_target_pairs={{0,64},{16,80},{32,96},{48,112},{64,0},{80,16},{96,32},{112,48},{1... | collective-permute-start | bytes 589832 | tf_op jit(solution)/shard_map/ppermute | solution.py:21
  17.8 11.5 %collective-permute-start.9 = (bf16[2,192,256]{2,1,0:T(8,128)(2,1)}, bf16[2,192,256]{2,1,0:T(8,128)(2,1)S(1)}, u32[]{:S(2)}, u32[]{:S(2)}) collective-permute-start(bf16[2,192,256]{2,1,0:T(8,128)(2,1)} %get-tuple-element.34), channel_id=1, source_target_pairs={{0,96},{16,112},{32,0},{48,16},{64,32},{80,48},{96,64},{112,80},{1... | collective-permute-start | bytes 589832 | tf_op jit(solution)/shard_map/ppermute | solution.py:21
  19.3 10.0 %collective-permute-start.6 = (bf16[64,1536]{1,0:T(8,128)(2,1)S(1)}, bf16[64,1536]{1,0:T(8,128)(2,1)S(1)}, u32[]{:S(2)}, u32[]{:S(2)}) collective-permute-start(bf16[64,1536]{1,0:T(8,128)(2,1)S(1)} %collective-permute-done.3), channel_id=1, source_target_pairs={{0,12},{1,97},{2,14},{3,99},{4,0},{5,101},{6,2},{7,103},{8,4},{9,1... | collective-permute-start | bytes 589832 | tf_op jit(solution)/shard_map/ppermute | solution.py:53
  21.5 7.8 %collective-permute-start.5 = (bf16[64,1536]{1,0:T(8,128)(2,1)S(1)}, bf16[64,1536]{1,0:T(8,128)(2,1)S(1)}, u32[]{:S(2)}, u32[]{:S(2)}) collective-permute-start(bf16[64,1536]{1,0:T(8,128)(2,1)S(1)} %collective-permute-done.3), channel_id=1, source_target_pairs={{0,8},{1,65},{2,10},{3,67},{4,12},{5,69},{6,14},{7,71},{8,0},{9,73... | collective-permute-start | bytes 589832 | tf_op jit(solution)/shard_map/ppermute | solution.py:53
  26.7 6.9 %collective-permute-start.4 = (bf16[64,1536]{1,0:T(8,128)(2,1)S(1)}, bf16[64,1536]{1,0:T(8,128)(2,1)S(1)}, u32[]{:S(2)}, u32[]{:S(2)}) collective-permute-start(bf16[64,1536]{1,0:T(8,128)(2,1)S(1)} %collective-permute-done.3), channel_id=1, source_target_pairs={{0,4},{1,33},{2,6},{3,35},{4,8},{5,37},{6,10},{7,39},{8,12},{9,41}... | collective-permute-start | bytes 589832 | tf_op jit(solution)/shard_map/ppermute | solution.py:53
  34.7 2.3 %copy-start.6 = (bf16[2,192,256]{2,1,0:T(8,128)(2,1)S(1)}, bf16[2,192,256]{2,1,0:T(8,128)(2,1)}, u32[]{:S(2)}) copy-start(bf16[2,192,256]{2,1,0:T(8,128)(2,1)} %get-tuple-element.43) | copy-start | bytes 589828
  34.8 2.4 %copy-start.1 = (bf16[2,4,64,1536]{3,2,1,0:T(8,128)(2,1)}, bf16[2,4,64,1536]{3,2,1,0:T(8,128)(2,1)S(1)}, u32[]{:S(2)}) copy-start(bf16[2,4,64,1536]{3,2,1,0:T(8,128)(2,1)S(1)} %pad_maximum_fusion.refs_0_.refs_4_) | copy-start | bytes 4718596
  34.8 20.5 %collective-permute-start.11 = (bf16[2,4,64,1536]{3,2,1,0:T(8,128)(2,1)S(1)}, bf16[2,4,64,1536]{3,2,1,0:T(8,128)(2,1)S(1)}, u32[]{:S(2)}, u32[]{:S(2)}) collective-permute-start(bf16[2,4,64,1536]{3,2,1,0:T(8,128)(2,1)S(1)} %pad_maximum_fusion.refs_0_.refs_4_), channel_id=1, source_target_pairs={{0,96},{1,13},{2,98},{3,15},{4,100},{5,1},{6,102},{7,3},{8,104},{9... | collective-permute-start | bytes 4718600 | tf_op jit(solution)/shard_map/ppermute | solution.py:53
  34.9 21.9 %collective-permute-start.10 = (bf16[2,4,64,1536]{3,2,1,0:T(8,128)(2,1)S(1)}, bf16[2,4,64,1536]{3,2,1,0:T(8,128)(2,1)S(1)}, u32[]{:S(2)}, u32[]{:S(2)}) collective-permute-start(bf16[2,4,64,1536]{3,2,1,0:T(8,128)(2,1)S(1)} %pad_maximum_fusion.refs_0_.refs_4_), channel_id=1, source_target_pairs={{0,32},{1,5},{2,34},{3,7},{4,36},{5,9},{6,38},{7,11},{8,40},{9,13}... | collective-permute-start | bytes 4718600 | tf_op jit(solution)/shard_map/ppermute | solution.py:53
  37.1 9.4 %collective-permute-start.12 = (bf16[4,192,256]{2,1,0:T(8,128)(2,1)S(1)}, bf16[4,192,256]{2,1,0:T(8,128)(2,1)S(1)}, u32[]{:S(2)}, u32[]{:S(2)}) collective-permute-start(bf16[4,192,256]{2,1,0:T(8,128)(2,1)S(1)} %pad_maximum_fusion.2), channel_id=1, source_target_pairs={{0,16},{16,0},{32,48},{48,32},{64,80},{80,64},{96,112},{112,96},{1... | collective-permute-start | bytes 1179656 | tf_op jit(solution)/shard_map/ppermute | solution.py:21
  55.3 1.6 %copy-start.4 = (bf16[2,4,64,1536]{3,2,1,0:T(8,128)(2,1)}, bf16[2,4,64,1536]{3,2,1,0:T(8,128)(2,1)S(1)}, u32[]{:S(2)}) copy-start(bf16[2,4,64,1536]{3,2,1,0:T(8,128)(2,1)S(1)} %collective-permute-done.11.refs_2_.refs_6_) | copy-start | bytes 4718596
  55.4 13.1 %collective-permute-start.14 = (bf16[1,4,64,1536]{3,2,1,0:T(8,128)(2,1)S(1)}, bf16[1,4,64,1536]{3,2,1,0:T(8,128)(2,1)}, u32[]{:S(2)}, u32[]{:S(2)}) collective-permute-start(bf16[1,4,64,1536]{3,2,1,0:T(8,128)(2,1)S(1)} %slice.41), channel_id=1, source_target_pairs={{0,96},{1,13},{2,98},{3,15},{4,100},{5,1},{6,102},{7,3},{8,104},{9... | collective-permute-start | bytes 2359304 | tf_op jit(solution)/shard_map/ppermute | solution.py:53
  56.9 1.1 copy-start.5
  56.9 13.3 %collective-permute-start.13 = (bf16[1,4,64,1536]{3,2,1,0:T(8,128)(2,1)S(1)}, bf16[1,4,64,1536]{3,2,1,0:T(8,128)(2,1)S(1)}, u32[]{:S(2)}, u32[]{:S(2)}) collective-permute-start(bf16[1,4,64,1536]{3,2,1,0:T(8,128)(2,1)S(1)} %slice.40), channel_id=1, source_target_pairs={{0,32},{1,5},{2,34},{3,7},{4,36},{5,9},{6,38},{7,11},{8,40},{9,13}... | collective-permute-start | bytes 2359304 | tf_op jit(solution)/shard_map/ppermute | solution.py:53
  67.2 10.9 %collective-permute-start.15 = (bf16[6,2,192,256]{3,2,1,0:T(8,128)(2,1)}, bf16[6,2,192,256]{3,2,1,0:T(8,128)(2,1)S(1)}, u32[]{:S(2)}, u32[]{:S(2)}) collective-permute-start(bf16[6,2,192,256]{3,2,1,0:T(8,128)(2,1)} %get-tuple-element.52), channel_id=1, source_target_pairs={{0,1},{1,0},{2,3},{3,2},{4,5},{5,4},{6,7},{7,6},{8,9},{9,8},{10,11... | collective-permute-start | bytes 3538952 | tf_op jit(solution)/shard_map/ppermute | solution.py:21
  67.3 20.2 %collective-permute-start.17 = (bf16[2,4,192,256]{3,2,1,0:T(8,128)(2,1)}, bf16[2,4,192,256]{3,2,1,0:T(8,128)(2,1)S(1)}, u32[]{:S(2)}, u32[]{:S(2)}) collective-permute-start(bf16[2,4,192,256]{3,2,1,0:T(8,128)(2,1)} %pad_maximum_fusion.1.refs_0_), channel_id=1, source_target_pairs={{0,2},{1,3},{2,0},{3,1},{4,6},{5,7},{6,4},{7,5},{8,10},{9,11},{10,... | collective-permute-start | bytes 2359304 | tf_op jit(solution)/shard_map/ppermute | solution.py:21
  70.2 0.9 copy-start.7
  76.1 2.0 %collective-permute-start.16 = (bf16[2,2,192,256]{3,2,1,0:T(8,128)(2,1)}, bf16[2,2,192,256]{3,2,1,0:T(8,128)(2,1)S(1)}, u32[]{:S(2)}, u32[]{:S(2)}) collective-permute-start(bf16[2,2,192,256]{3,2,1,0:T(8,128)(2,1)} %get-tuple-element.53), channel_id=1, source_target_pairs={{0,1},{1,0},{2,3},{3,2},{4,5},{5,4},{6,7},{7,6},{8,9},{9,8},{10,11... | collective-permute-start | bytes 1179656 | tf_op jit(solution)/shard_map/ppermute | solution.py:21
  78.1 0.8 copy-start.3
  78.1 1.1 copy-start.2
  83.1 28.6 %all-to-all-start = ((bf16[16,192,256]{2,1,0:T(8,128)(2,1)}), bf16[16,192,256]{2,1,0:T(8,128)(2,1)S(1)}, u32[]{:S(2)}, u32[]{:S(2)}) async-start(bf16[16,192,256]{2,1,0:T(8,128)(2,1)} %bitcast.24), calls=%async_computation | async-start | bytes 3145728 | tf_op jit(solution)/shard_map/all_to_all | solution.py:301
  87.5 3.6 %copy-start.8 = (bf16[2,4,192,256]{3,2,1,0:T(8,128)(2,1)}, bf16[2,4,192,256]{3,2,1,0:T(8,128)(2,1)S(1)}, u32[]{:S(2)}) copy-start(bf16[2,4,192,256]{3,2,1,0:T(8,128)(2,1)S(1)} %collective-permute-done.17.refs_1_) | copy-start | bytes 2359300
  87.5 3.6 %collective-permute-start.18 = (bf16[2,4,192,256]{3,2,1,0:T(8,128)(2,1)}, bf16[2,4,192,256]{3,2,1,0:T(8,128)(2,1)S(1)}, u32[]{:S(2)}, u32[]{:S(2)}) collective-permute-start(bf16[2,4,192,256]{3,2,1,0:T(8,128)(2,1)} %pad_maximum_fusion.1.refs_0_), channel_id=1, source_target_pairs={{0,1},{1,0},{2,3},{3,2},{4,5},{5,4},{6,7},{7,6},{8,9},{9,8},{10,11... | collective-permute-start | bytes 2359304 | tf_op jit(solution)/shard_map/ppermute | solution.py:21
  87.5 3.6 %collective-permute-start.19 = (bf16[2,4,192,256]{3,2,1,0:T(8,128)(2,1)S(1)}, bf16[2,4,192,256]{3,2,1,0:T(8,128)(2,1)S(1)}, u32[]{:S(2)}, u32[]{:S(2)}) collective-permute-start(bf16[2,4,192,256]{3,2,1,0:T(8,128)(2,1)S(1)} %collective-permute-done.17.refs_1_), channel_id=1, source_target_pairs={{0,1},{1,0},{2,3},{3,2},{4,5},{5,4},{6,7},{7,6},{8,9},{9,8},{10,11... | collective-permute-start | bytes 2359304 | tf_op jit(solution)/shard_map/ppermute | solution.py:21
  91.1 0.9 copy-start.9
  92.0 0.9 copy-start.10
  111.7 1.1 copy-start

commit v8 on v6

--- a/solution.py
+++ b/solution.py
@@ -14,7 +14,7 @@
 MIB = 1024 * 1024
 VMEM = pl.BlockSpec(memory_space=pltpu.VMEM)
 SMEM = pl.BlockSpec(memory_space=pltpu.SMEM)
-HBM = pl.BlockSpec(memory_space=pltpu.HBM)
+ANY = pl.BlockSpec(memory_space=pl.ANY)
 
 
 def send(v, axis, count, to):
@@ -53,13 +53,12 @@
     return lax.ppermute(v, ("gx", "gy", "gz"), pairs)
 
 
-def call(body, out_shape, in_specs, cost, out_specs=None, scratch=(), grid=(), limit=56):
+def call(body, out_shape, in_specs, cost, out_specs=None, scratch=(), limit=12):
     if out_specs is None:
         out_specs = [VMEM] * len(out_shape)
     flops, moved = cost
     return pl.pallas_call(
         body,
-        grid=grid,
         out_shape=[jax.ShapeDtypeStruct(*s) for s in out_shape],
         in_specs=in_specs,
         out_specs=out_specs,
@@ -198,12 +197,15 @@
 
 
 def finish_body(at, slope, parts, out):
-    v = [parts[n, 0].astype(f32) + parts[n, 1].astype(f32) for n in range(8)]
-    v = jnp.concatenate(v, 0).astype(bf16)
-    total = lax.dot_general(v, one_hot(), (((0,), (0,)), ((), ())), preferred_element_type=f32)
-    result = (total * slope[...]).astype(bf16)
-    for k in range(4):
-        out[token_rows(at[2], k), :] = result[64 * k : 64 * k + 64, :]
+    pick = one_hot()
+    for j in range(out.shape[1] // 256):
+        cols, units = slice(256 * j, 256 * j + 256), slice(32 * j, 32 * j + 32)
+        v = [(parts[n, 0, units, :].astype(f32) + parts[n, 1, units, :].astype(f32)) for n in range(8)]
+        v = jnp.concatenate(v, 0).astype(bf16)
+        total = lax.dot_general(v, pick, (((0,), (0,)), ((), ())), preferred_element_type=f32)
+        result = (total * slope[:, cols]).astype(bf16)
+        for k in range(4):
+            out[token_rows(at[2], k), cols] = result[64 * k : 64 * k + 64, :]
 
 
 def weight_body(at, *refs):
@@ -261,9 +263,9 @@
         return call(
             functools.partial(input_body, len(given)),
             [((count, 2) + block, bf16)] * 2,
-            [SMEM, HBM] + [HBM] * len(given),
+            [SMEM, ANY] + [ANY] * len(given),
             (product * count // 8, 2 * (4 * rows * features + count * (4 * rows + features) * tokens)),
-            out_specs=[HBM] * 2,
+            out_specs=[ANY] * 2,
             scratch=[
                 pltpu.VMEM((4 * rows, features), bf16),
                 pltpu.VMEM((count, 4, tokens // 4, features), bf16),
@@ -272,6 +274,7 @@
                 pltpu.SemaphoreType.DMA((count,)),
                 pltpu.SemaphoreType.DMA((2, 2)),
             ],
+            limit=10 + 2 * count,
         )(at, w, *given)
 
     early = lax.optimization_barrier((p0, p1, p3, own))
@@ -284,8 +287,9 @@
         [((8, 2) + block, bf16)],
         [SMEM] + [VMEM] * 4,
         (4 * size, 12 * size),
-        out_specs=[HBM],
+        out_specs=[ANY],
         scratch=[pltpu.VMEM((8, 2) + block, bf16), pltpu.SemaphoreType.DMA((8,))],
+        limit=12,
     )(at, mine, mine2, other, swap_core(theirs2))
     same_core = [[2 * (2 * i + k) + c for i in range(8) for k in range(2)] for c in range(2)]
     back = lax.all_to_all(
@@ -296,22 +300,18 @@
     (weight_grad,) = call(
         weight_body,
         [((4 * rows, features), bf16)],
-        [SMEM] + [VMEM] * 4 + [HBM] * 5,
+        [SMEM] + [VMEM] * 4 + [ANY] * 5,
         (product, 2 * (8 * rows * features + 2048 * features)),
         scratch=grad_scratch,
+        limit=32,
     )(at, *hidden, *pieces)
     back, weight_grad = lax.optimization_barrier((back, weight_grad))
     (pre_grad,) = call(
         finish_body,
         [((tokens, columns), bf16)],
-        [
-            SMEM,
-            pl.BlockSpec((tokens, 256), lambda j: (0, j)),
-            pl.BlockSpec((8, 2, 32, tokens), lambda j: (0, 0, j, 0)),
-        ],
+        [SMEM] + [VMEM] * 2,
         (2 * tokens * 256 * columns, 8 * tokens * columns),
-        out_specs=[pl.BlockSpec((tokens, 256), lambda j: (0, j))],
-        grid=(columns // 256,),
+        limit=12,
     )(at, slope, back.reshape((8, 2) + block))
     return pre_grad, weight_grad.reshape(weight.shape)
 

time: 118 us -> 122 us (1.034)
  the two profiles are of different devices: /device:TPU:0 before, /device:TPU:7 now
where the time goes in v8:
time: 122 us; the launch traced here: 121 us
  waiting for transfers between devices  47.6 us (39%)
  starting transfers between devices  33.7 us (28%)
  Pallas kernels  27.8 us (23%)
  local copies, waits for them, and re-layouts  9.07 us (7%)
  other arithmetic  2.32 us (2%)
    ppermute x10, waiting for transfers between devices, send(): return lax.ppermute(v, axis, [(i, to(i)) for i in range(count)])  34.6 us
    ppermute x10, starting transfers between devices, send(): return lax.ppermute(v, axis, [(i, to(i)) for i in range(count)])  14.3 us
    ppermute x10, starting transfers between devices, send_by_core(): return lax.ppermute(v, ('gx', 'gy', 'gz'), pairs)  13.7 us
    ppermute x10, waiting for transfers between devices, send_by_core(): return lax.ppermute(v, ('gx', 'gy', 'gz'), pairs)  13 us
    pallas_call x2, Pallas kernels, input_part(): call(functools.partial(input_body, len(given)), [((count, 2) + block, bf1...  12.6 us
    pallas_call x1, Pallas kernels, per_device(): call(weight_body, [((4 * rows, features), bf16)], [SMEM] + [VMEM] * 4 + [...  9.39 us
    unnamed x24, local copies, waits for them, and re-layouts  8.82 us
    all_to_all x1, starting transfers between devices, per_device(): lax.all_to_all(sums.reshape((16,) + block), ('gx', 'gz'), 0, 0, tiled=Tru...  5.61 us
  transfers between devices with their start and end apart: 21, of which 9 were waited for; matrix products, arithmetic and copies ran while one was open for 1% of the time, Pallas kernels for 21%

profile of v8, /device:TPU:7, one launch (start us, length us, event | category | flops | bytes accessed | tf_op | source)
XLA Modules:
  0.0 121.3 jit_solution(8397750223222718027)
XLA Ops:
  0.6 0.6 collective-permute-start.2
  1.2 0.7 collective-permute-start.1
  1.9 2.0 %collective-permute-start = (bf16[64,1536]{1,0:T(8,128)(2,1)}, bf16[64,1536]{1,0:T(8,128)(2,1)S(1)}, u32[]{:S(2)}, u32[]{:S(2)}) collective-permute-start(bf16[64,1536]{1,0:T(8,128)(2,1)} %param.4), channel_id=1, source_target_pairs={{0,4},{1,33},{2,6},{3,35},{4,8},{5,37},{6,10},{7,39},{8,12},{9,41}... | collective-permute-start | bytes 589832 | tf_op jit(solution)/shard_map/ppermute | solution.py:53
  3.9 3.6 %collective-permute-start.3 = (bf16[64,1536]{1,0:T(8,128)(2,1)}, bf16[64,1536]{1,0:T(8,128)(2,1)S(1)}, u32[]{:S(2)}, u32[]{:S(2)}) collective-permute-start(bf16[64,1536]{1,0:T(8,128)(2,1)} %param.4), channel_id=1, source_target_pairs={{0,16},{16,0},{32,48},{48,32},{64,80},{80,64},{96,112},{112,96},{1... | collective-permute-start | bytes 589832 | tf_op jit(solution)/shard_map/ppermute | solution.py:21
  7.5 0.1 stack.77.at
  7.6 1.1 copy-done.2
  8.7 1.9 %shard_map.50 = (f32[256,1536]{1,0:T(8,128)S(1)}, bf16[2,192,256]{2,1,0:T(8,128)(2,1)S(1)}, bf16[2,192,256]{2,1,0:T(8,128)(2,1)S(1)}, bf16[2,192,256]{2,1,0:T(8,128)(2,1)S(1)}, bf16[2,192,256]{2,1,0:T(8,128)(2,1)S(1)}) custom-call(s32[5]{0:T(128)S(1)} %stack.77.at, bf16[256,1536]{1,0:T(8,128)(2,1)S(1)} %copy-done.2), custom_call_target="tpu_custom_call" | custom-call | flops 201326592 | bytes 3145728 | tf_op jit(solution)/shard_map/pallas_call | solution.py:240
  10.6 1.2 copy-done
  11.8 0.6 collective-permute-start.7
  12.4 0.0 collective-permute-done.2
  12.4 1.2 %collective-permute-start.8 = (bf16[2,192,256]{2,1,0:T(8,128)(2,1)S(1)}, bf16[2,192,256]{2,1,0:T(8,128)(2,1)S(1)}, u32[]{:S(2)}, u32[]{:S(2)}) collective-permute-start(bf16[2,192,256]{2,1,0:T(8,128)(2,1)S(1)} %get-tuple-element.33), channel_id=1, source_target_pairs={{0,64},{16,80},{32,96},{48,112},{64,0},{80,16},{96,32},{112,48},{1... | collective-permute-start | bytes 589832 | tf_op jit(solution)/shard_map/ppermute | solution.py:21
  13.7 0.0 collective-permute-done.1
  13.7 0.9 collective-permute-start.9
  14.5 0.0 collective-permute-done.3
  14.5 0.5 collective-permute-start.6
  15.1 0.0 collective-permute-done
  15.1 2.5 %collective-permute-start.5 = (bf16[64,1536]{1,0:T(8,128)(2,1)S(1)}, bf16[64,1536]{1,0:T(8,128)(2,1)S(1)}, u32[]{:S(2)}, u32[]{:S(2)}) collective-permute-start(bf16[64,1536]{1,0:T(8,128)(2,1)S(1)} %collective-permute-done.3), channel_id=1, source_target_pairs={{0,8},{1,65},{2,10},{3,67},{4,12},{5,69},{6,14},{7,71},{8,0},{9,73... | collective-permute-start | bytes 589832 | tf_op jit(solution)/shard_map/ppermute | solution.py:53
  17.6 0.0 collective-permute-done.7
  17.6 1.4 %collective-permute-start.4 = (bf16[64,1536]{1,0:T(8,128)(2,1)S(1)}, bf16[64,1536]{1,0:T(8,128)(2,1)S(1)}, u32[]{:S(2)}, u32[]{:S(2)}) collective-permute-start(bf16[64,1536]{1,0:T(8,128)(2,1)S(1)} %collective-permute-done.3), channel_id=1, source_target_pairs={{0,4},{1,33},{2,6},{3,35},{4,8},{5,37},{6,10},{7,39},{8,12},{9,41}... | collective-permute-start | bytes 589832 | tf_op jit(solution)/shard_map/ppermute | solution.py:53
  19.0 0.0 collective-permute-done.8
  19.0 4.0 %collective-permute-done.9 = bf16[2,192,256]{2,1,0:T(8,128)(2,1)S(1)} collective-permute-done((bf16[2,192,256]{2,1,0:T(8,128)(2,1)S(1)}, bf16[2,192,256]{2,1,0:T(8,128)(2,1)S(1)}, u32[]{:S(2)}, u32[]{:S(2)}) %collective-permute-start.9) | collective-permute-done | bytes 196640 | tf_op jit(solution)/shard_map/ppermute | solution.py:21
  23.0 4.9 %collective-permute-done.6 = bf16[64,1536]{1,0:T(8,128)(2,1)S(1)} collective-permute-done((bf16[64,1536]{1,0:T(8,128)(2,1)S(1)}, bf16[64,1536]{1,0:T(8,128)(2,1)S(1)}, u32[]{:S(2)}, u32[]{:S(2)}) %collective-permute-start.6) | collective-permute-done | bytes 196640 | tf_op jit(solution)/shard_map/ppermute | solution.py:53
  27.8 1.1 collective-permute-done.5
  29.0 0.0 collective-permute-done.4
  29.0 1.1 maximum_bitcast_fusion
  30.1 0.1 pad_maximum_fusion.refs_0_.refs_4_
  30.3 2.8 %collective-permute-start.11 = (bf16[2,4,64,1536]{3,2,1,0:T(8,128)(2,1)S(1)}, bf16[2,4,64,1536]{3,2,1,0:T(8,128)(2,1)S(1)}, u32[]{:S(2)}, u32[]{:S(2)}) collective-permute-start(bf16[2,4,64,1536]{3,2,1,0:T(8,128)(2,1)S(1)} %pad_maximum_fusion.refs_0_.refs_4_), channel_id=1, source_target_pairs={{0,96},{1,13},{2,98},{3,15},{4,100},{5,1},{6,102},{7,3},{8,104},{9... | collective-permute-start | bytes 4718600 | tf_op jit(solution)/shard_map/ppermute | solution.py:53
  33.1 0.0 collective-permute-start.10
  33.2 0.1 pad_maximum_fusion.2
  33.2 0.3 collective-permute-start.12
  33.5 0.1 maximum_bitcast_fusion.2
  33.5 9.0 %collective-permute-done.12 = bf16[4,192,256]{2,1,0:T(8,128)(2,1)S(1)} collective-permute-done((bf16[4,192,256]{2,1,0:T(8,128)(2,1)S(1)}, bf16[4,192,256]{2,1,0:T(8,128)(2,1)S(1)}, u32[]{:S(2)}, u32[]{:S(2)}) %collective-permute-start.12) | collective-permute-done | bytes 393248 | tf_op jit(solution)/shard_map/ppermute | solution.py:21
  42.5 0.9 pad_maximum_fusion.1.refs_0_
  43.5 7.0 %collective-permute-done.11.refs_2_.refs_6_ = bf16[2,4,64,1536]{3,2,1,0:T(8,128)(2,1)S(1)} collective-permute-done((bf16[2,4,64,1536]{3,2,1,0:T(8,128)(2,1)S(1)}, bf16[2,4,64,1536]{3,2,1,0:T(8,128)(2,1)S(1)}, u32[]{:S(2)}, u32[]{:S(2)}) %collective-permute-start.11) | collective-permute-done | bytes 1572896 | tf_op jit(solution)/shard_map/ppermute | solution.py:53
  50.4 0.1 slice.41
  50.5 3.2 %collective-permute-start.14 = (bf16[1,4,64,1536]{3,2,1,0:T(8,128)(2,1)S(1)}, bf16[1,4,64,1536]{3,2,1,0:T(8,128)(2,1)S(1)}, u32[]{:S(2)}, u32[]{:S(2)}) collective-permute-start(bf16[1,4,64,1536]{3,2,1,0:T(8,128)(2,1)S(1)} %slice.41), channel_id=1, source_target_pairs={{0,96},{1,13},{2,98},{3,15},{4,100},{5,1},{6,102},{7,3},{8,104},{9... | collective-permute-start | bytes 2359304 | tf_op jit(solution)/shard_map/ppermute | solution.py:53
  53.7 0.0 collective-permute-done.10.refs_1_.refs_5_
  53.7 0.1 slice.40
  53.8 0.1 collective-permute-start.13
  53.9 9.1 %shard_map.51 = (bf16[6,2,192,256]{3,2,1,0:T(8,128)(2,1)S(1)}, bf16[6,2,192,256]{3,2,1,0:T(8,128)(2,1)S(1)}) custom-call(s32[5]{0:T(128)S(1)} %stack.77.at, bf16[768,1536]{1,0:T(8,128)(2,1)S(1)} %bitcast.25, bf16[2,4,64,1536]{3,2,1,0:T(8,128)(2,1)S(1)} %pad_maximum_fusion.refs_0_.refs_4_, ...), custom_call_target="tpu_custom_call" | custom-call | flops 3623878656 | bytes 9437184 | tf_op jit(solution)/shard_map/pallas_call | solution.py:263
  62.9 3.9 %collective-permute-start.15 = (bf16[6,2,192,256]{3,2,1,0:T(8,128)(2,1)S(1)}, bf16[6,2,192,256]{3,2,1,0:T(8,128)(2,1)S(1)}, u32[]{:S(2)}, u32[]{:S(2)}) collective-permute-start(bf16[6,2,192,256]{3,2,1,0:T(8,128)(2,1)S(1)} %get-tuple-element.52), channel_id=1, source_target_pairs={{0,1},{1,0},{2,3},{3,2},{4,5},{5,4},{6,7},{7,6},{8,9},{9,8},{10,11... | collective-permute-start | bytes 3538952 | tf_op jit(solution)/shard_map/ppermute | solution.py:21
  66.9 0.8 collective-permute-start.17
  67.6 0.0 collective-permute-done.14.refs_1_.refs_8_
  67.7 0.0 collective-permute-done.13.refs_0_.refs_7_
  67.7 0.0 copy-start.10
  67.7 3.5 %shard_map.52 = (bf16[2,2,192,256]{3,2,1,0:T(8,128)(2,1)S(1)}, bf16[2,2,192,256]{3,2,1,0:T(8,128)(2,1)S(1)}) custom-call(s32[5]{0:T(128)S(1)} %stack.77.at, bf16[768,1536]{1,0:T(8,128)(2,1)S(1)} %bitcast.26, bf16[1,4,64,1536]{3,2,1,0:T(8,128)(2,1)S(1)} %collective-permute-done.13.refs_0_.refs_7_, ...), custom_call_target="tpu_custom_call" | custom-call | flops 1207959552 | bytes 4718592 | tf_op jit(solution)/shard_map/pallas_call | solution.py:263
  71.2 1.1 collective-permute-start.16
  72.3 1.3 %collective-permute-done.16.other2 = bf16[2,2,192,256]{3,2,1,0:T(8,128)(2,1)S(1)} collective-permute-done((bf16[2,2,192,256]{3,2,1,0:T(8,128)(2,1)S(1)}, bf16[2,2,192,256]{3,2,1,0:T(8,128)(2,1)S(1)}, u32[]{:S(2)}, u32[]{:S(2)}) %collective-permute-start.16) | collective-permute-done | bytes 393248 | tf_op jit(solution)/shard_map/ppermute | solution.py:21
  73.6 0.0 collective-permute-done.15.other
  73.6 2.1 %shard_map.53 = bf16[8,2,192,256]{3,2,1,0:T(8,128)(2,1)} custom-call(s32[5]{0:T(128)S(1)} %stack.77.at, bf16[6,2,192,256]{3,2,1,0:T(8,128)(2,1)S(1)} %get-tuple-element.50.mine, bf16[2,2,192,256]{3,2,1,0:T(8,128)(2,1)S(1)} %get-tuple-element.51.mine2, bf16[6,2,192,256]{3,2,1,0:T(8,128)(2,1)S(1)} %collective-permute-done.15.other, ...), custom_call_target="tpu_custom_call" | custom-call | flops 1572864 | bytes 4718592 | tf_op jit(solution)/shard_map/pallas_call | solution.py:285
  75.7 5.6 %all-to-all-start = ((bf16[16,192,256]{2,1,0:T(8,128)(2,1)}), bf16[16,192,256]{2,1,0:T(8,128)(2,1)S(1)}, u32[]{:S(2)}, u32[]{:S(2)}) async-start(bf16[16,192,256]{2,1,0:T(8,128)(2,1)} %bitcast.18), calls=%async_computation | async-start | bytes 3145728 | tf_op jit(solution)/shard_map/all_to_all | solution.py:295
  81.3 17.0 %collective-permute-done.17.refs_1_ = bf16[2,4,192,256]{3,2,1,0:T(8,128)(2,1)} collective-permute-done((bf16[2,4,192,256]{3,2,1,0:T(8,128)(2,1)}, bf16[2,4,192,256]{3,2,1,0:T(8,128)(2,1)}, u32[]{:S(2)}, u32[]{:S(2)}) %collective-permute-start.17) | collective-permute-done | bytes 786464 | tf_op jit(solution)/shard_map/ppermute | solution.py:21
  98.3 2.0 %collective-permute-start.18 = (bf16[2,4,192,256]{3,2,1,0:T(8,128)(2,1)}, bf16[2,4,192,256]{3,2,1,0:T(8,128)(2,1)S(1)}, u32[]{:S(2)}, u32[]{:S(2)}) collective-permute-start(bf16[2,4,192,256]{3,2,1,0:T(8,128)(2,1)} %pad_maximum_fusion.1.refs_0_), channel_id=1, source_target_pairs={{0,1},{1,0},{2,3},{3,2},{4,5},{5,4},{6,7},{7,6},{8,9},{9,8},{10,11... | collective-permute-start | bytes 2359304 | tf_op jit(solution)/shard_map/ppermute | solution.py:21
  100.3 0.0 collective-permute-start.19
  100.3 2.1 %collective-permute-done.18.refs_2_ = bf16[2,4,192,256]{3,2,1,0:T(8,128)(2,1)S(1)} collective-permute-done((bf16[2,4,192,256]{3,2,1,0:T(8,128)(2,1)}, bf16[2,4,192,256]{3,2,1,0:T(8,128)(2,1)S(1)}, u32[]{:S(2)}, u32[]{:S(2)}) %collective-permute-start.18) | collective-permute-done | bytes 786464 | tf_op jit(solution)/shard_map/ppermute | solution.py:21
  102.4 1.1 collective-permute-done.19.refs_3_
  103.5 1.4 %copy-done.4 = bf16[2,4,64,1536]{3,2,1,0:T(8,128)(2,1)S(1)} copy-done((bf16[2,4,64,1536]{3,2,1,0:T(8,128)(2,1)S(1)}, bf16[2,4,64,1536]{3,2,1,0:T(8,128)(2,1)}, u32[]{:S(2)}) %copy-start.4) | copy-done | bytes 1572888
  104.9 1.4 %copy-done.6 = bf16[2,4,64,1536]{3,2,1,0:T(8,128)(2,1)S(1)} copy-done((bf16[2,4,64,1536]{3,2,1,0:T(8,128)(2,1)S(1)}, bf16[2,4,64,1536]{3,2,1,0:T(8,128)(2,1)}, u32[]{:S(2)}) %copy-start.6) | copy-done | bytes 1572888
  106.4 1.1 copy-done.9
  107.5 1.1 copy-done.11
  108.6 9.4 %shard_map.54 = bf16[768,1536]{1,0:T(8,128)(2,1)} custom-call(s32[5]{0:T(128)S(1)} %stack.77.at, bf16[2,4,192,256]{3,2,1,0:T(8,128)(2,1)} %pad_maximum_fusion.1.refs_0_, bf16[2,4,192,256]{3,2,1,0:T(8,128)(2,1)} %collective-permute-done.17.refs_1_, bf16[2,4,192,256]{3,2,1,0:T(8,128)(2,1)S(1)} %collective-permute-done.18.refs_2_, ...), custom_call_target="tpu_custom_call" | custom-call | flops 4831838208 | bytes 11010048 | tf_op jit(solution)/shard_map/pallas_call | solution.py:300
  118.0 0.0 all-to-all-done
  118.0 1.4 %copy-done.1 = f32[256,1536]{1,0:T(8,128)S(1)} copy-done((f32[256,1536]{1,0:T(8,128)S(1)}, f32[256,1536]{1,0:T(8,128)}, u32[]{:S(2)}) %copy-start.1) | copy-done | bytes 1572888
  119.4 1.9 %shard_map.55 = bf16[256,1536]{1,0:T(8,128)(2,1)} custom-call(s32[5]{0:T(128)S(1)} %stack.77.at, f32[256,1536]{1,0:T(8,128)S(1)} %copy-done.1, bf16[8,2,192,256]{3,2,1,0:T(8,128)(2,1)S(1)} %bitcast.24), custom_call_target="tpu_custom_call" | custom-call | flops 201326592 | bytes 3145728 | tf_op jit(solution)/shard_map/pallas_call | solution.py:309
  (18 shorter events, 0.1 us)
Async XLA Ops:
  0.6 11.8 %collective-permute-start.2 = (bf16[64,1536]{1,0:T(8,128)(2,1)}, bf16[64,1536]{1,0:T(8,128)(2,1)S(1)}, u32[]{:S(2)}, u32[]{:S(2)}) collective-permute-start(bf16[64,1536]{1,0:T(8,128)(2,1)} %param.4), channel_id=1, source_target_pairs={{0,12},{1,97},{2,14},{3,99},{4,0},{5,101},{6,2},{7,103},{8,4},{9,1... | collective-permute-start | bytes 589832 | tf_op jit(solution)/shard_map/ppermute | solution.py:53
  1.2 12.4 %collective-permute-start.1 = (bf16[64,1536]{1,0:T(8,128)(2,1)}, bf16[64,1536]{1,0:T(8,128)(2,1)S(1)}, u32[]{:S(2)}, u32[]{:S(2)}) collective-permute-start(bf16[64,1536]{1,0:T(8,128)(2,1)} %param.4), channel_id=1, source_target_pairs={{0,8},{1,65},{2,10},{3,67},{4,12},{5,69},{6,14},{7,71},{8,0},{9,73... | collective-permute-start | bytes 589832 | tf_op jit(solution)/shard_map/ppermute | solution.py:53
  1.9 13.2 %collective-permute-start = (bf16[64,1536]{1,0:T(8,128)(2,1)}, bf16[64,1536]{1,0:T(8,128)(2,1)S(1)}, u32[]{:S(2)}, u32[]{:S(2)}) collective-permute-start(bf16[64,1536]{1,0:T(8,128)(2,1)} %param.4), channel_id=1, source_target_pairs={{0,4},{1,33},{2,6},{3,35},{4,8},{5,37},{6,10},{7,39},{8,12},{9,41}... | collective-permute-start | bytes 589832 | tf_op jit(solution)/shard_map/ppermute | solution.py:53
  3.9 10.6 %collective-permute-start.3 = (bf16[64,1536]{1,0:T(8,128)(2,1)}, bf16[64,1536]{1,0:T(8,128)(2,1)S(1)}, u32[]{:S(2)}, u32[]{:S(2)}) collective-permute-start(bf16[64,1536]{1,0:T(8,128)(2,1)} %param.4), channel_id=1, source_target_pairs={{0,16},{16,0},{32,48},{48,32},{64,80},{80,64},{96,112},{112,96},{1... | collective-permute-start | bytes 589832 | tf_op jit(solution)/shard_map/ppermute | solution.py:21
  7.6 1.1 copy-start.2
  10.6 1.2 copy-start
  11.8 5.7 %collective-permute-start.7 = (bf16[2,192,256]{2,1,0:T(8,128)(2,1)S(1)}, bf16[2,192,256]{2,1,0:T(8,128)(2,1)S(1)}, u32[]{:S(2)}, u32[]{:S(2)}) collective-permute-start(bf16[2,192,256]{2,1,0:T(8,128)(2,1)S(1)} %get-tuple-element.32), channel_id=1, source_target_pairs={{0,32},{16,48},{32,64},{48,80},{64,96},{80,112},{96,0},{112,16},{1... | collective-permute-start | bytes 589832 | tf_op jit(solution)/shard_map/ppermute | solution.py:21
  12.4 6.5 %collective-permute-start.8 = (bf16[2,192,256]{2,1,0:T(8,128)(2,1)S(1)}, bf16[2,192,256]{2,1,0:T(8,128)(2,1)S(1)}, u32[]{:S(2)}, u32[]{:S(2)}) collective-permute-start(bf16[2,192,256]{2,1,0:T(8,128)(2,1)S(1)} %get-tuple-element.33), channel_id=1, source_target_pairs={{0,64},{16,80},{32,96},{48,112},{64,0},{80,16},{96,32},{112,48},{1... | collective-permute-start | bytes 589832 | tf_op jit(solution)/shard_map/ppermute | solution.py:21
  13.7 9.3 %collective-permute-start.9 = (bf16[2,192,256]{2,1,0:T(8,128)(2,1)S(1)}, bf16[2,192,256]{2,1,0:T(8,128)(2,1)S(1)}, u32[]{:S(2)}, u32[]{:S(2)}) collective-permute-start(bf16[2,192,256]{2,1,0:T(8,128)(2,1)S(1)} %get-tuple-element.34), channel_id=1, source_target_pairs={{0,96},{16,112},{32,0},{48,16},{64,32},{80,48},{96,64},{112,80},{1... | collective-permute-start | bytes 589832 | tf_op jit(solution)/shard_map/ppermute | solution.py:21
  14.5 13.3 %collective-permute-start.6 = (bf16[64,1536]{1,0:T(8,128)(2,1)S(1)}, bf16[64,1536]{1,0:T(8,128)(2,1)S(1)}, u32[]{:S(2)}, u32[]{:S(2)}) collective-permute-start(bf16[64,1536]{1,0:T(8,128)(2,1)S(1)} %collective-permute-done.3), channel_id=1, source_target_pairs={{0,12},{1,97},{2,14},{3,99},{4,0},{5,101},{6,2},{7,103},{8,4},{9,1... | collective-permute-start | bytes 589832 | tf_op jit(solution)/shard_map/ppermute | solution.py:53
  15.1 13.9 %collective-permute-start.5 = (bf16[64,1536]{1,0:T(8,128)(2,1)S(1)}, bf16[64,1536]{1,0:T(8,128)(2,1)S(1)}, u32[]{:S(2)}, u32[]{:S(2)}) collective-permute-start(bf16[64,1536]{1,0:T(8,128)(2,1)S(1)} %collective-permute-done.3), channel_id=1, source_target_pairs={{0,8},{1,65},{2,10},{3,67},{4,12},{5,69},{6,14},{7,71},{8,0},{9,73... | collective-permute-start | bytes 589832 | tf_op jit(solution)/shard_map/ppermute | solution.py:53
  17.6 11.4 %collective-permute-start.4 = (bf16[64,1536]{1,0:T(8,128)(2,1)S(1)}, bf16[64,1536]{1,0:T(8,128)(2,1)S(1)}, u32[]{:S(2)}, u32[]{:S(2)}) collective-permute-start(bf16[64,1536]{1,0:T(8,128)(2,1)S(1)} %collective-permute-done.3), channel_id=1, source_target_pairs={{0,4},{1,33},{2,6},{3,35},{4,8},{5,37},{6,10},{7,39},{8,12},{9,41}... | collective-permute-start | bytes 589832 | tf_op jit(solution)/shard_map/ppermute | solution.py:53
  30.3 20.2 %collective-permute-start.11 = (bf16[2,4,64,1536]{3,2,1,0:T(8,128)(2,1)S(1)}, bf16[2,4,64,1536]{3,2,1,0:T(8,128)(2,1)S(1)}, u32[]{:S(2)}, u32[]{:S(2)}) collective-permute-start(bf16[2,4,64,1536]{3,2,1,0:T(8,128)(2,1)S(1)} %pad_maximum_fusion.refs_0_.refs_4_), channel_id=1, source_target_pairs={{0,96},{1,13},{2,98},{3,15},{4,100},{5,1},{6,102},{7,3},{8,104},{9... | collective-permute-start | bytes 4718600 | tf_op jit(solution)/shard_map/ppermute | solution.py:53
  33.1 20.6 %collective-permute-start.10 = (bf16[2,4,64,1536]{3,2,1,0:T(8,128)(2,1)S(1)}, bf16[2,4,64,1536]{3,2,1,0:T(8,128)(2,1)S(1)}, u32[]{:S(2)}, u32[]{:S(2)}) collective-permute-start(bf16[2,4,64,1536]{3,2,1,0:T(8,128)(2,1)S(1)} %pad_maximum_fusion.refs_0_.refs_4_), channel_id=1, source_target_pairs={{0,32},{1,5},{2,34},{3,7},{4,36},{5,9},{6,38},{7,11},{8,40},{9,13}... | collective-permute-start | bytes 4718600 | tf_op jit(solution)/shard_map/ppermute | solution.py:53
  33.2 9.3 %collective-permute-start.12 = (bf16[4,192,256]{2,1,0:T(8,128)(2,1)S(1)}, bf16[4,192,256]{2,1,0:T(8,128)(2,1)S(1)}, u32[]{:S(2)}, u32[]{:S(2)}) collective-permute-start(bf16[4,192,256]{2,1,0:T(8,128)(2,1)S(1)} %pad_maximum_fusion.2), channel_id=1, source_target_pairs={{0,16},{16,0},{32,48},{48,32},{64,80},{80,64},{96,112},{112,96},{1... | collective-permute-start | bytes 1179656 | tf_op jit(solution)/shard_map/ppermute | solution.py:21
  43.5 10.4 %copy-start.7 = (bf16[768,1,1536]{2,0,1:T(8,128)(2,1)S(1)}, bf16[768,1,1536]{2,0,1:T(8,128)(2,1)}, u32[]{:S(2)}) copy-start(bf16[768,1,1536]{2,0,1:T(8,128)(2,1)} %param.5) | copy-start | bytes 7077892
  50.4 3.4 %copy-start.3 = (bf16[2,4,64,1536]{3,2,1,0:T(8,128)(2,1)}, bf16[2,4,64,1536]{3,2,1,0:T(8,128)(2,1)S(1)}, u32[]{:S(2)}) copy-start(bf16[2,4,64,1536]{3,2,1,0:T(8,128)(2,1)S(1)} %collective-permute-done.11.refs_2_.refs_6_) | copy-start | bytes 4718596
  50.5 17.1 %collective-permute-start.14 = (bf16[1,4,64,1536]{3,2,1,0:T(8,128)(2,1)S(1)}, bf16[1,4,64,1536]{3,2,1,0:T(8,128)(2,1)S(1)}, u32[]{:S(2)}, u32[]{:S(2)}) collective-permute-start(bf16[1,4,64,1536]{3,2,1,0:T(8,128)(2,1)S(1)} %slice.41), channel_id=1, source_target_pairs={{0,96},{1,13},{2,98},{3,15},{4,100},{5,1},{6,102},{7,3},{8,104},{9... | collective-permute-start | bytes 2359304 | tf_op jit(solution)/shard_map/ppermute | solution.py:53
  53.7 9.2 %copy-start.5 = (bf16[2,4,64,1536]{3,2,1,0:T(8,128)(2,1)}, bf16[2,4,64,1536]{3,2,1,0:T(8,128)(2,1)S(1)}, u32[]{:S(2)}) copy-start(bf16[2,4,64,1536]{3,2,1,0:T(8,128)(2,1)S(1)} %collective-permute-done.10.refs_1_.refs_5_) | copy-start | bytes 4718596
  53.8 13.9 %collective-permute-start.13 = (bf16[1,4,64,1536]{3,2,1,0:T(8,128)(2,1)S(1)}, bf16[1,4,64,1536]{3,2,1,0:T(8,128)(2,1)S(1)}, u32[]{:S(2)}, u32[]{:S(2)}) collective-permute-start(bf16[1,4,64,1536]{3,2,1,0:T(8,128)(2,1)S(1)} %slice.40), channel_id=1, source_target_pairs={{0,32},{1,5},{2,34},{3,7},{4,36},{5,9},{6,38},{7,11},{8,40},{9,13}... | collective-permute-start | bytes 2359304 | tf_op jit(solution)/shard_map/ppermute | solution.py:53
  62.9 10.7 %collective-permute-start.15 = (bf16[6,2,192,256]{3,2,1,0:T(8,128)(2,1)S(1)}, bf16[6,2,192,256]{3,2,1,0:T(8,128)(2,1)S(1)}, u32[]{:S(2)}, u32[]{:S(2)}) collective-permute-start(bf16[6,2,192,256]{3,2,1,0:T(8,128)(2,1)S(1)} %get-tuple-element.52), channel_id=1, source_target_pairs={{0,1},{1,0},{2,3},{3,2},{4,5},{5,4},{6,7},{7,6},{8,9},{9,8},{10,11... | collective-permute-start | bytes 3538952 | tf_op jit(solution)/shard_map/ppermute | solution.py:21
  66.9 31.4 %collective-permute-start.17 = (bf16[2,4,192,256]{3,2,1,0:T(8,128)(2,1)}, bf16[2,4,192,256]{3,2,1,0:T(8,128)(2,1)}, u32[]{:S(2)}, u32[]{:S(2)}) collective-permute-start(bf16[2,4,192,256]{3,2,1,0:T(8,128)(2,1)} %pad_maximum_fusion.1.refs_0_), channel_id=1, source_target_pairs={{0,2},{1,3},{2,0},{3,1},{4,6},{5,7},{6,4},{7,5},{8,10},{9,11},{10,... | collective-permute-start | bytes 2359304 | tf_op jit(solution)/shard_map/ppermute | solution.py:21
  67.7 3.5 %copy-start.8 = (bf16[1,4,64,1536]{3,2,1,0:T(8,128)(2,1)}, bf16[1,4,64,1536]{3,2,1,0:T(8,128)(2,1)S(1)}, u32[]{:S(2)}) copy-start(bf16[1,4,64,1536]{3,2,1,0:T(8,128)(2,1)S(1)} %collective-permute-done.14.refs_1_.refs_8_) | copy-start | bytes 2359300
  67.7 3.5 %copy-start.10 = (bf16[1,4,64,1536]{3,2,1,0:T(8,128)(2,1)}, bf16[1,4,64,1536]{3,2,1,0:T(8,128)(2,1)S(1)}, u32[]{:S(2)}) copy-start(bf16[1,4,64,1536]{3,2,1,0:T(8,128)(2,1)S(1)} %collective-permute-done.13.refs_0_.refs_7_) | copy-start | bytes 2359300
  71.2 2.4 %collective-permute-start.16 = (bf16[2,2,192,256]{3,2,1,0:T(8,128)(2,1)S(1)}, bf16[2,2,192,256]{3,2,1,0:T(8,128)(2,1)S(1)}, u32[]{:S(2)}, u32[]{:S(2)}) collective-permute-start(bf16[2,2,192,256]{3,2,1,0:T(8,128)(2,1)S(1)} %get-tuple-element.53), channel_id=1, source_target_pairs={{0,1},{1,0},{2,3},{3,2},{4,5},{5,4},{6,7},{7,6},{8,9},{9,8},{10,11... | collective-permute-start | bytes 1179656 | tf_op jit(solution)/shard_map/ppermute | solution.py:21
  75.7 42.3 %all-to-all-start = ((bf16[16,192,256]{2,1,0:T(8,128)(2,1)}), bf16[16,192,256]{2,1,0:T(8,128)(2,1)S(1)}, u32[]{:S(2)}, u32[]{:S(2)}) async-start(bf16[16,192,256]{2,1,0:T(8,128)(2,1)} %bitcast.18), calls=%async_computation | async-start | bytes 3145728 | tf_op jit(solution)/shard_map/all_to_all | solution.py:295
  98.3 4.1 %collective-permute-start.18 = (bf16[2,4,192,256]{3,2,1,0:T(8,128)(2,1)}, bf16[2,4,192,256]{3,2,1,0:T(8,128)(2,1)S(1)}, u32[]{:S(2)}, u32[]{:S(2)}) collective-permute-start(bf16[2,4,192,256]{3,2,1,0:T(8,128)(2,1)} %pad_maximum_fusion.1.refs_0_), channel_id=1, source_target_pairs={{0,1},{1,0},{2,3},{3,2},{4,5},{5,4},{6,7},{7,6},{8,9},{9,8},{10,11... | collective-permute-start | bytes 2359304 | tf_op jit(solution)/shard_map/ppermute | solution.py:21
  100.3 3.2 %collective-permute-start.19 = (bf16[2,4,192,256]{3,2,1,0:T(8,128)(2,1)}, bf16[2,4,192,256]{3,2,1,0:T(8,128)(2,1)S(1)}, u32[]{:S(2)}, u32[]{:S(2)}) collective-permute-start(bf16[2,4,192,256]{3,2,1,0:T(8,128)(2,1)} %collective-permute-done.17.refs_1_), channel_id=1, source_target_pairs={{0,1},{1,0},{2,3},{3,2},{4,5},{5,4},{6,7},{7,6},{8,9},{9,8},{10,11... | collective-permute-start | bytes 2359304 | tf_op jit(solution)/shard_map/ppermute | solution.py:21
  103.5 1.4 %copy-start.4 = (bf16[2,4,64,1536]{3,2,1,0:T(8,128)(2,1)S(1)}, bf16[2,4,64,1536]{3,2,1,0:T(8,128)(2,1)}, u32[]{:S(2)}) copy-start(bf16[2,4,64,1536]{3,2,1,0:T(8,128)(2,1)} %copy-done.3) | copy-start | bytes 4718596
  104.9 1.4 %copy-start.6 = (bf16[2,4,64,1536]{3,2,1,0:T(8,128)(2,1)S(1)}, bf16[2,4,64,1536]{3,2,1,0:T(8,128)(2,1)}, u32[]{:S(2)}) copy-start(bf16[2,4,64,1536]{3,2,1,0:T(8,128)(2,1)} %copy-done.5) | copy-start | bytes 4718596
  106.4 1.1 copy-start.9
  107.5 1.1 copy-start.11
  118.0 1.4 %copy-start.1 = (f32[256,1536]{1,0:T(8,128)S(1)}, f32[256,1536]{1,0:T(8,128)}, u32[]{:S(2)}) copy-start(f32[256,1536]{1,0:T(8,128)} %copy-done) | copy-start | bytes 4718596

commit v9 on v8

--- a/solution.py
+++ b/solution.py
@@ -209,11 +209,16 @@
 
 
 def weight_body(at, *refs):
-    hidden, pieces, (out, held, sems) = refs[:4], refs[4:9], refs[9:]
+    hidden, pieces, (out, held, own, sems, own_sems) = refs[:8], refs[8:13], refs[13:]
+    copies = [pltpu.make_async_copy(h, own.at[n], own_sems.at[n]) for n, h in enumerate(hidden)]
+    for c in copies:
+        c.start()
     load_grads(at, pieces, held, sems)
+    for c in copies:
+        c.wait()
     rows = out.shape[0] // 4
     lhs = jnp.concatenate(
-        [jnp.concatenate([h[z, k] for k in range(4) for z in range(2)], 1) for h in hidden], 0
+        [jnp.concatenate([own[2 * n + z, k] for k in range(4) for z in range(2)], 1) for n in range(4)], 0
     )
 
     @pl.loop(0, out.shape[1] // 256)
@@ -234,7 +239,6 @@
     at = jnp.stack([gx // 2, gx % 2, y, gz // 2, gz % 2]).astype(jnp.int32)
     w = weight.reshape(4 * rows, features)
     block = (rows, tokens)
-    grad_scratch = [pltpu.VMEM((4, 2, 4, tokens // 4, features), bf16), pltpu.SemaphoreType.DMA((8,))]
     product = 2 * 4 * rows * 8 * tokens * features
 
     slope, *parts = call(
@@ -254,9 +258,8 @@
 
     p2p, p2m = send_by_core(p1[:1], 1, False), send_by_core(p3[1:], 3, False)
     pieces = p0, p1, p3, p2p, p2m
-    own = jnp.stack([p[0] for p in by_x])
-    own = jnp.stack([own, swap_z_hi(jnp.stack([p[1] for p in by_x]))])
-    far = swap_z_lo(own)
+    own = [jnp.stack([p[0] for p in by_x]), swap_z_hi(jnp.stack([p[1] for p in by_x]))]
+    far = [swap_z_lo(own[0])]
 
     def input_part(*given):
         count = sum(p.shape[0] for p in given)
@@ -277,7 +280,8 @@
             limit=10 + 2 * count,
         )(at, w, *given)
 
-    early = lax.optimization_barrier((p0, p1, p3, own))
+    early = lax.optimization_barrier((p0, p1, p3, far[0], own[1]))
+    far, own[1] = [early[3], swap_z_lo(early[4])], early[4]
     mine, theirs = input_part(*early[:3])
     other = swap_core(theirs)
     mine2, theirs2 = input_part(p2p, p2m)
@@ -295,15 +299,20 @@
     back = lax.all_to_all(
         sums.reshape((16,) + block), ("gx", "gz"), 0, 0, tiled=True, axis_index_groups=same_core
     )
-    own, far, _ = lax.optimization_barrier((own, far, sums))
-    hidden = [own, far, swap_core(own), swap_core(far)]
+    near, _ = lax.optimization_barrier((own + far, sums))
+    hidden = near + [swap_core(v) for v in near]
     (weight_grad,) = call(
         weight_body,
         [((4 * rows, features), bf16)],
-        [SMEM] + [VMEM] * 4 + [ANY] * 5,
+        [SMEM] + [ANY] * 13,
         (product, 2 * (8 * rows * features + 2048 * features)),
-        scratch=grad_scratch,
-        limit=32,
+        scratch=[
+            pltpu.VMEM((4, 2, 4, tokens // 4, features), bf16),
+            pltpu.VMEM((8, 4) + block, bf16),
+            pltpu.SemaphoreType.DMA((8,)),
+            pltpu.SemaphoreType.DMA((8,)),
+        ],
+        limit=24,
     )(at, *hidden, *pieces)
     back, weight_grad = lax.optimization_barrier((back, weight_grad))
     (pre_grad,) = call(

time: 122 us -> 134 us (1.098)
  the two profiles are of different devices: /device:TPU:7 before, /device:TPU:0 now
where the time goes in v9:
time: 134 us; the launch traced here: 133 us
  waiting for transfers between devices  53.8 us (40%)
  starting transfers between devices  37 us (28%)
  Pallas kernels  28.4 us (21%)
  local copies, waits for them, and re-layouts  11.5 us (9%)
  other arithmetic  1.38 us (1%)
    ppermute x13, waiting for transfers between devices, send(): return lax.ppermute(v, axis, [(i, to(i)) for i in range(count)])  30.9 us
    ppermute x10, waiting for transfers between devices, send_by_core(): return lax.ppermute(v, ('gx', 'gy', 'gz'), pairs)  22.9 us
    ppermute x10, starting transfers between devices, send_by_core(): return lax.ppermute(v, ('gx', 'gy', 'gz'), pairs)  18.4 us
    ppermute x13, starting transfers between devices, send(): return lax.ppermute(v, axis, [(i, to(i)) for i in range(count)])  14.9 us
    pallas_call x2, Pallas kernels, input_part(): call(functools.partial(input_body, len(given)), [((count, 2) + block, bf1...  12.6 us
    unnamed x32, local copies, waits for them, and re-layouts  11.2 us
    pallas_call x1, Pallas kernels, per_device(): call(weight_body, [((4 * rows, features), bf16)], [SMEM] + [ANY] * 13, (p...  9.92 us
    all_to_all x1, starting transfers between devices, per_device(): lax.all_to_all(sums.reshape((16,) + block), ('gx', 'gz'), 0, 0, tiled=Tru...  3.72 us
  transfers between devices with their start and end apart: 24, of which 10 were waited for; matrix products, arithmetic and copies ran while one was open for 0% of the time, Pallas kernels for 18%

profile of v9, /device:TPU:0, one launch (start us, length us, event | category | flops | bytes accessed | tf_op | source)
XLA Modules:
  0.0 133.0 jit_solution(17442990711234094518)
XLA Ops:
  0.6 3.2 %collective-permute-start.2 = (bf16[64,1536]{1,0:T(8,128)(2,1)}, bf16[64,1536]{1,0:T(8,128)(2,1)S(1)}, u32[]{:S(2)}, u32[]{:S(2)}) collective-permute-start(bf16[64,1536]{1,0:T(8,128)(2,1)} %param.4), channel_id=1, source_target_pairs={{0,12},{1,97},{2,14},{3,99},{4,0},{5,101},{6,2},{7,103},{8,4},{9,1... | collective-permute-start | bytes 589832 | tf_op jit(solution)/shard_map/ppermute | solution.py:53
  3.8 0.6 collective-permute-start.1
  4.4 1.0 collective-permute-start
  5.4 3.9 %collective-permute-start.3 = (bf16[64,1536]{1,0:T(8,128)(2,1)}, bf16[64,1536]{1,0:T(8,128)(2,1)S(1)}, u32[]{:S(2)}, u32[]{:S(2)}) collective-permute-start(bf16[64,1536]{1,0:T(8,128)(2,1)} %param.4), channel_id=1, source_target_pairs={{0,16},{16,0},{32,48},{48,32},{64,80},{80,64},{96,112},{112,96},{1... | collective-permute-start | bytes 589832 | tf_op jit(solution)/shard_map/ppermute | solution.py:21
  9.3 0.1 stack.68.at
  9.4 1.1 copy-done.2
  10.5 1.9 %shard_map.50 = (f32[256,1536]{1,0:T(8,128)S(1)}, bf16[2,192,256]{2,1,0:T(8,128)(2,1)S(1)}, bf16[2,192,256]{2,1,0:T(8,128)(2,1)S(1)}, bf16[2,192,256]{2,1,0:T(8,128)(2,1)S(1)}, bf16[2,192,256]{2,1,0:T(8,128)(2,1)S(1)}) custom-call(s32[5]{0:T(128)S(1)} %stack.68.at, bf16[256,1536]{1,0:T(8,128)(2,1)S(1)} %copy-done.2), custom_call_target="tpu_custom_call" | custom-call | flops 201326592 | bytes 3145728 | tf_op jit(solution)/shard_map/pallas_call | solution.py:244
  12.4 1.2 copy-done
  13.6 1.5 %collective-permute-start.7 = (bf16[2,192,256]{2,1,0:T(8,128)(2,1)S(1)}, bf16[2,192,256]{2,1,0:T(8,128)(2,1)S(1)}, u32[]{:S(2)}, u32[]{:S(2)}) collective-permute-start(bf16[2,192,256]{2,1,0:T(8,128)(2,1)S(1)} %get-tuple-element.36), channel_id=1, source_target_pairs={{0,32},{16,48},{32,64},{48,80},{64,96},{80,112},{96,0},{112,16},{1... | collective-permute-start | bytes 589832 | tf_op jit(solution)/shard_map/ppermute | solution.py:21
  15.1 2.7 %collective-permute-start.8 = (bf16[2,192,256]{2,1,0:T(8,128)(2,1)S(1)}, bf16[2,192,256]{2,1,0:T(8,128)(2,1)S(1)}, u32[]{:S(2)}, u32[]{:S(2)}) collective-permute-start(bf16[2,192,256]{2,1,0:T(8,128)(2,1)S(1)} %get-tuple-element.37), channel_id=1, source_target_pairs={{0,64},{16,80},{32,96},{48,112},{64,0},{80,16},{96,32},{112,48},{1... | collective-permute-start | bytes 589832 | tf_op jit(solution)/shard_map/ppermute | solution.py:21
  17.8 0.0 collective-permute-done.1
  17.8 1.4 %collective-permute-start.9 = (bf16[2,192,256]{2,1,0:T(8,128)(2,1)S(1)}, bf16[2,192,256]{2,1,0:T(8,128)(2,1)S(1)}, u32[]{:S(2)}, u32[]{:S(2)}) collective-permute-start(bf16[2,192,256]{2,1,0:T(8,128)(2,1)S(1)} %get-tuple-element.38), channel_id=1, source_target_pairs={{0,96},{16,112},{32,0},{48,16},{64,32},{80,48},{96,64},{112,80},{1... | collective-permute-start | bytes 589832 | tf_op jit(solution)/shard_map/ppermute | solution.py:21
  19.3 2.3 %collective-permute-start.6 = (bf16[64,1536]{1,0:T(8,128)(2,1)S(1)}, bf16[64,1536]{1,0:T(8,128)(2,1)S(1)}, u32[]{:S(2)}, u32[]{:S(2)}) collective-permute-start(bf16[64,1536]{1,0:T(8,128)(2,1)S(1)} %collective-permute-done.3), channel_id=1, source_target_pairs={{0,12},{1,97},{2,14},{3,99},{4,0},{5,101},{6,2},{7,103},{8,4},{9,1... | collective-permute-start | bytes 589832 | tf_op jit(solution)/shard_map/ppermute | solution.py:53
  21.5 0.0 collective-permute-done
  21.5 1.7 %collective-permute-start.5 = (bf16[64,1536]{1,0:T(8,128)(2,1)S(1)}, bf16[64,1536]{1,0:T(8,128)(2,1)S(1)}, u32[]{:S(2)}, u32[]{:S(2)}) collective-permute-start(bf16[64,1536]{1,0:T(8,128)(2,1)S(1)} %collective-permute-done.3), channel_id=1, source_target_pairs={{0,8},{1,65},{2,10},{3,67},{4,12},{5,69},{6,14},{7,71},{8,0},{9,73... | collective-permute-start | bytes 589832 | tf_op jit(solution)/shard_map/ppermute | solution.py:53
  23.2 0.4 collective-permute-done.7
  23.6 5.2 %collective-permute-start.4 = (bf16[64,1536]{1,0:T(8,128)(2,1)S(1)}, bf16[64,1536]{1,0:T(8,128)(2,1)S(1)}, u32[]{:S(2)}, u32[]{:S(2)}) collective-permute-start(bf16[64,1536]{1,0:T(8,128)(2,1)S(1)} %collective-permute-done.3), channel_id=1, source_target_pairs={{0,4},{1,33},{2,6},{3,35},{4,8},{5,37},{6,10},{7,39},{8,12},{9,41}... | collective-permute-start | bytes 589832 | tf_op jit(solution)/shard_map/ppermute | solution.py:53
  28.9 0.0 collective-permute-done.8
  28.9 0.0 collective-permute-done.9
  28.9 0.0 collective-permute-done.5
  28.9 3.2 %collective-permute-done.4 = bf16[64,1536]{1,0:T(8,128)(2,1)S(1)} collective-permute-done((bf16[64,1536]{1,0:T(8,128)(2,1)S(1)}, bf16[64,1536]{1,0:T(8,128)(2,1)S(1)}, u32[]{:S(2)}, u32[]{:S(2)}) %collective-permute-start.4) | collective-permute-done | bytes 196640 | tf_op jit(solution)/shard_map/ppermute | solution.py:53
  32.1 1.1 maximum_bitcast_fusion
  33.2 0.1 pad_maximum_fusion.refs_0_.refs_8_
  33.3 0.1 collective-permute-start.11
  33.4 2.0 %collective-permute-start.10 = (bf16[2,4,64,1536]{3,2,1,0:T(8,128)(2,1)S(1)}, bf16[2,4,64,1536]{3,2,1,0:T(8,128)(2,1)S(1)}, u32[]{:S(2)}, u32[]{:S(2)}) collective-permute-start(bf16[2,4,64,1536]{3,2,1,0:T(8,128)(2,1)S(1)} %pad_maximum_fusion.refs_0_.refs_8_), channel_id=1, source_target_pairs={{0,32},{1,5},{2,34},{3,7},{4,36},{5,9},{6,38},{7,11},{8,40},{9,13}... | collective-permute-start | bytes 4718600 | tf_op jit(solution)/shard_map/ppermute | solution.py:53
  35.5 0.1 pad_maximum_fusion.1.refs_0_
  35.6 1.1 collective-permute-start.12
  36.7 0.1 pad_maximum_fusion.2
  36.7 0.0 copy-start.7
  36.7 1.2 collective-permute-start.13
  38.0 15.9 %collective-permute-done.11.refs_2_.refs_10_ = bf16[2,4,64,1536]{3,2,1,0:T(8,128)(2,1)S(1)} collective-permute-done((bf16[2,4,64,1536]{3,2,1,0:T(8,128)(2,1)S(1)}, bf16[2,4,64,1536]{3,2,1,0:T(8,128)(2,1)S(1)}, u32[]{:S(2)}, u32[]{:S(2)}) %collective-permute-start.11) | collective-permute-done | bytes 1572896 | tf_op jit(solution)/shard_map/ppermute | solution.py:53
  53.8 0.1 slice.41
  53.9 2.3 %collective-permute-start.15 = (bf16[1,4,64,1536]{3,2,1,0:T(8,128)(2,1)S(1)}, bf16[1,4,64,1536]{3,2,1,0:T(8,128)(2,1)S(1)}, u32[]{:S(2)}, u32[]{:S(2)}) collective-permute-start(bf16[1,4,64,1536]{3,2,1,0:T(8,128)(2,1)S(1)} %slice.41), channel_id=1, source_target_pairs={{0,96},{1,13},{2,98},{3,15},{4,100},{5,1},{6,102},{7,3},{8,104},{9... | collective-permute-start | bytes 2359304 | tf_op jit(solution)/shard_map/ppermute | solution.py:53
  56.2 0.0 collective-permute-done.12.refs_2_
  56.2 0.3 collective-permute-done.10.refs_1_.refs_9_
  56.5 0.1 slice.40
  56.6 0.1 collective-permute-start.14
  56.7 0.3 copy-done.12
  57.0 0.1 copy-done.14
  57.1 9.1 %shard_map.51 = (bf16[6,2,192,256]{3,2,1,0:T(8,128)(2,1)S(1)}, bf16[6,2,192,256]{3,2,1,0:T(8,128)(2,1)S(1)}) custom-call(s32[5]{0:T(128)S(1)} %stack.68.at, bf16[768,1536]{1,0:T(8,128)(2,1)S(1)} %bitcast.22, bf16[2,4,64,1536]{3,2,1,0:T(8,128)(2,1)S(1)} %pad_maximum_fusion.refs_0_.refs_8_, ...), custom_call_target="tpu_custom_call" | custom-call | flops 3623878656 | bytes 9437184 | tf_op jit(solution)/shard_map/pallas_call | solution.py:266
  66.2 0.1 collective-permute-start.16
  66.3 3.6 %collective-permute-done.14.refs_0_.refs_11_ = bf16[1,4,64,1536]{3,2,1,0:T(8,128)(2,1)S(1)} collective-permute-done((bf16[1,4,64,1536]{3,2,1,0:T(8,128)(2,1)S(1)}, bf16[1,4,64,1536]{3,2,1,0:T(8,128)(2,1)S(1)}, u32[]{:S(2)}, u32[]{:S(2)}) %collective-permute-start.14) | collective-permute-done | bytes 786464 | tf_op jit(solution)/shard_map/ppermute | solution.py:53
  69.9 3.5 %shard_map.52 = (bf16[2,2,192,256]{3,2,1,0:T(8,128)(2,1)S(1)}, bf16[2,2,192,256]{3,2,1,0:T(8,128)(2,1)S(1)}) custom-call(s32[5]{0:T(128)S(1)} %stack.68.at, bf16[768,1536]{1,0:T(8,128)(2,1)S(1)} %bitcast.23, bf16[1,4,64,1536]{3,2,1,0:T(8,128)(2,1)S(1)} %collective-permute-done.14.refs_0_.refs_11_, ...), custom_call_target="tpu_custom_call" | custom-call | flops 1207959552 | bytes 4718592 | tf_op jit(solution)/shard_map/pallas_call | solution.py:266
  73.4 0.1 collective-permute-start.17
  73.5 1.7 %collective-permute-done.17.other2 = bf16[2,2,192,256]{3,2,1,0:T(8,128)(2,1)S(1)} collective-permute-done((bf16[2,2,192,256]{3,2,1,0:T(8,128)(2,1)S(1)}, bf16[2,2,192,256]{3,2,1,0:T(8,128)(2,1)S(1)}, u32[]{:S(2)}, u32[]{:S(2)}) %collective-permute-start.17) | collective-permute-done | bytes 393248 | tf_op jit(solution)/shard_map/ppermute | solution.py:21
  75.2 2.1 %shard_map.53 = bf16[8,2,192,256]{3,2,1,0:T(8,128)(2,1)} custom-call(s32[5]{0:T(128)S(1)} %stack.68.at, bf16[6,2,192,256]{3,2,1,0:T(8,128)(2,1)S(1)} %get-tuple-element.54.mine, bf16[2,2,192,256]{3,2,1,0:T(8,128)(2,1)S(1)} %get-tuple-element.55.mine2, bf16[6,2,192,256]{3,2,1,0:T(8,128)(2,1)S(1)} %collective-permute-done.16.other, ...), custom_call_target="tpu_custom_call" | custom-call | flops 1572864 | bytes 4718592 | tf_op jit(solution)/shard_map/pallas_call | solution.py:289
  77.3 3.7 %all-to-all-start = ((bf16[16,192,256]{2,1,0:T(8,128)(2,1)}), bf16[16,192,256]{2,1,0:T(8,128)(2,1)S(1)}, u32[]{:S(2)}, u32[]{:S(2)}) async-start(bf16[16,192,256]{2,1,0:T(8,128)(2,1)} %bitcast.16), calls=%async_computation | async-start | bytes 3145728 | tf_op jit(solution)/shard_map/all_to_all | solution.py:299
  81.0 1.8 %collective-permute-start.18 = (bf16[4,192,256]{2,1,0:T(8,128)(2,1)}, bf16[4,192,256]{2,1,0:T(8,128)(2,1)S(1)}, u32[]{:S(2)}, u32[]{:S(2)}) collective-permute-start(bf16[4,192,256]{2,1,0:T(8,128)(2,1)} %copy-done.14), channel_id=1, source_target_pairs={{0,2},{1,3},{2,0},{3,1},{4,6},{5,7},{6,4},{7,5},{8,10},{9,11},{10,... | collective-permute-start | bytes 1179656 | tf_op jit(solution)/shard_map/ppermute | solution.py:21
  82.8 26.2 %collective-permute-done.18.refs_3_ = bf16[4,192,256]{2,1,0:T(8,128)(2,1)S(1)} collective-permute-done((bf16[4,192,256]{2,1,0:T(8,128)(2,1)}, bf16[4,192,256]{2,1,0:T(8,128)(2,1)S(1)}, u32[]{:S(2)}, u32[]{:S(2)}) %collective-permute-start.18) | collective-permute-done | bytes 393248 | tf_op jit(solution)/shard_map/ppermute | solution.py:21
  109.0 0.5 collective-permute-start.20
  109.5 0.0 collective-permute-start.21
  109.5 0.5 collective-permute-start.22
  110.0 1.2 collective-permute-done.19.refs_4_
  111.3 0.3 collective-permute-done.20.refs_5_
  111.6 1.1 collective-permute-done.21.refs_6_
  112.6 1.4 %copy-done.4 = bf16[2,4,64,1536]{3,2,1,0:T(8,128)(2,1)S(1)} copy-done((bf16[2,4,64,1536]{3,2,1,0:T(8,128)(2,1)S(1)}, bf16[2,4,64,1536]{3,2,1,0:T(8,128)(2,1)}, u32[]{:S(2)}) %copy-start.4) | copy-done | bytes 1572888
  114.1 1.4 %copy-done.6 = bf16[2,4,64,1536]{3,2,1,0:T(8,128)(2,1)S(1)} copy-done((bf16[2,4,64,1536]{3,2,1,0:T(8,128)(2,1)S(1)}, bf16[2,4,64,1536]{3,2,1,0:T(8,128)(2,1)}, u32[]{:S(2)}) %copy-start.6) | copy-done | bytes 1572888
  115.5 1.1 copy-done.9
  116.6 1.1 copy-done.11
  117.7 1.0 copy-done.13
  118.7 1.0 copy-done.15
  119.7 9.9 %shard_map.54 = bf16[768,1536]{1,0:T(8,128)(2,1)} custom-call(s32[5]{0:T(128)S(1)} %stack.68.at, bf16[4,192,256]{2,1,0:T(8,128)(2,1)S(1)} %pad_maximum_fusion.1.refs_0_, bf16[4,192,256]{2,1,0:T(8,128)(2,1)S(1)} %copy-done.15, bf16[4,192,256]{2,1,0:T(8,128)(2,1)S(1)} %copy-done.13, bf16[4,192,256]{2,1,0:T(8,128)(2,1)S(1)} %collective-permute-done.18.refs_3_, ...), custom_call_target="tpu_custom_call" | custom-call | flops 4831838208 | bytes 11010048 | tf_op jit(solution)/shard_map/pallas_call | solution.py:304
  129.7 1.4 %copy-done.1 = f32[256,1536]{1,0:T(8,128)S(1)} copy-done((f32[256,1536]{1,0:T(8,128)S(1)}, f32[256,1536]{1,0:T(8,128)}, u32[]{:S(2)}) %copy-start.1) | copy-done | bytes 1572888
  131.1 1.9 %shard_map.55 = bf16[256,1536]{1,0:T(8,128)(2,1)} custom-call(s32[5]{0:T(128)S(1)} %stack.68.at, f32[256,1536]{1,0:T(8,128)S(1)} %copy-done.1, bf16[8,2,192,256]{3,2,1,0:T(8,128)(2,1)S(1)} %bitcast.21), custom_call_target="tpu_custom_call" | custom-call | flops 201326592 | bytes 3145728 | tf_op jit(solution)/shard_map/pallas_call | solution.py:318
  (31 shorter events, 0.1 us)
Async XLA Ops:
  0.6 14.5 %collective-permute-start.2 = (bf16[64,1536]{1,0:T(8,128)(2,1)}, bf16[64,1536]{1,0:T(8,128)(2,1)S(1)}, u32[]{:S(2)}, u32[]{:S(2)}) collective-permute-start(bf16[64,1536]{1,0:T(8,128)(2,1)} %param.4), channel_id=1, source_target_pairs={{0,12},{1,97},{2,14},{3,99},{4,0},{5,101},{6,2},{7,103},{8,4},{9,1... | collective-permute-start | bytes 589832 | tf_op jit(solution)/shard_map/ppermute | solution.py:53
  3.8 14.0 %collective-permute-start.1 = (bf16[64,1536]{1,0:T(8,128)(2,1)}, bf16[64,1536]{1,0:T(8,128)(2,1)S(1)}, u32[]{:S(2)}, u32[]{:S(2)}) collective-permute-start(bf16[64,1536]{1,0:T(8,128)(2,1)} %param.4), channel_id=1, source_target_pairs={{0,8},{1,65},{2,10},{3,67},{4,12},{5,69},{6,14},{7,71},{8,0},{9,73... | collective-permute-start | bytes 589832 | tf_op jit(solution)/shard_map/ppermute | solution.py:53
  4.4 17.1 %collective-permute-start = (bf16[64,1536]{1,0:T(8,128)(2,1)}, bf16[64,1536]{1,0:T(8,128)(2,1)S(1)}, u32[]{:S(2)}, u32[]{:S(2)}) collective-permute-start(bf16[64,1536]{1,0:T(8,128)(2,1)} %param.4), channel_id=1, source_target_pairs={{0,4},{1,33},{2,6},{3,35},{4,8},{5,37},{6,10},{7,39},{8,12},{9,41}... | collective-permute-start | bytes 589832 | tf_op jit(solution)/shard_map/ppermute | solution.py:53
  5.4 13.9 %collective-permute-start.3 = (bf16[64,1536]{1,0:T(8,128)(2,1)}, bf16[64,1536]{1,0:T(8,128)(2,1)S(1)}, u32[]{:S(2)}, u32[]{:S(2)}) collective-permute-start(bf16[64,1536]{1,0:T(8,128)(2,1)} %param.4), channel_id=1, source_target_pairs={{0,16},{16,0},{32,48},{48,32},{64,80},{80,64},{96,112},{112,96},{1... | collective-permute-start | bytes 589832 | tf_op jit(solution)/shard_map/ppermute | solution.py:21
  9.4 1.1 copy-start.2
  12.4 1.2 copy-start
  13.6 10.0 %collective-permute-start.7 = (bf16[2,192,256]{2,1,0:T(8,128)(2,1)S(1)}, bf16[2,192,256]{2,1,0:T(8,128)(2,1)S(1)}, u32[]{:S(2)}, u32[]{:S(2)}) collective-permute-start(bf16[2,192,256]{2,1,0:T(8,128)(2,1)S(1)} %get-tuple-element.36), channel_id=1, source_target_pairs={{0,32},{16,48},{32,64},{48,80},{64,96},{80,112},{96,0},{112,16},{1... | collective-permute-start | bytes 589832 | tf_op jit(solution)/shard_map/ppermute | solution.py:21
  15.1 13.8 %collective-permute-start.8 = (bf16[2,192,256]{2,1,0:T(8,128)(2,1)S(1)}, bf16[2,192,256]{2,1,0:T(8,128)(2,1)S(1)}, u32[]{:S(2)}, u32[]{:S(2)}) collective-permute-start(bf16[2,192,256]{2,1,0:T(8,128)(2,1)S(1)} %get-tuple-element.37), channel_id=1, source_target_pairs={{0,64},{16,80},{32,96},{48,112},{64,0},{80,16},{96,32},{112,48},{1... | collective-permute-start | bytes 589832 | tf_op jit(solution)/shard_map/ppermute | solution.py:21
  17.8 11.0 %collective-permute-start.9 = (bf16[2,192,256]{2,1,0:T(8,128)(2,1)S(1)}, bf16[2,192,256]{2,1,0:T(8,128)(2,1)S(1)}, u32[]{:S(2)}, u32[]{:S(2)}) collective-permute-start(bf16[2,192,256]{2,1,0:T(8,128)(2,1)S(1)} %get-tuple-element.38), channel_id=1, source_target_pairs={{0,96},{16,112},{32,0},{48,16},{64,32},{80,48},{96,64},{112,80},{1... | collective-permute-start | bytes 589832 | tf_op jit(solution)/shard_map/ppermute | solution.py:21
  19.3 9.6 %collective-permute-start.6 = (bf16[64,1536]{1,0:T(8,128)(2,1)S(1)}, bf16[64,1536]{1,0:T(8,128)(2,1)S(1)}, u32[]{:S(2)}, u32[]{:S(2)}) collective-permute-start(bf16[64,1536]{1,0:T(8,128)(2,1)S(1)} %collective-permute-done.3), channel_id=1, source_target_pairs={{0,12},{1,97},{2,14},{3,99},{4,0},{5,101},{6,2},{7,103},{8,4},{9,1... | collective-permute-start | bytes 589832 | tf_op jit(solution)/shard_map/ppermute | solution.py:53
  21.5 7.3 %collective-permute-start.5 = (bf16[64,1536]{1,0:T(8,128)(2,1)S(1)}, bf16[64,1536]{1,0:T(8,128)(2,1)S(1)}, u32[]{:S(2)}, u32[]{:S(2)}) collective-permute-start(bf16[64,1536]{1,0:T(8,128)(2,1)S(1)} %collective-permute-done.3), channel_id=1, source_target_pairs={{0,8},{1,65},{2,10},{3,67},{4,12},{5,69},{6,14},{7,71},{8,0},{9,73... | collective-permute-start | bytes 589832 | tf_op jit(solution)/shard_map/ppermute | solution.py:53
  23.6 8.4 %collective-permute-start.4 = (bf16[64,1536]{1,0:T(8,128)(2,1)S(1)}, bf16[64,1536]{1,0:T(8,128)(2,1)S(1)}, u32[]{:S(2)}, u32[]{:S(2)}) collective-permute-start(bf16[64,1536]{1,0:T(8,128)(2,1)S(1)} %collective-permute-done.3), channel_id=1, source_target_pairs={{0,4},{1,33},{2,6},{3,35},{4,8},{5,37},{6,10},{7,39},{8,12},{9,41}... | collective-permute-start | bytes 589832 | tf_op jit(solution)/shard_map/ppermute | solution.py:53
  33.3 20.5 %collective-permute-start.11 = (bf16[2,4,64,1536]{3,2,1,0:T(8,128)(2,1)S(1)}, bf16[2,4,64,1536]{3,2,1,0:T(8,128)(2,1)S(1)}, u32[]{:S(2)}, u32[]{:S(2)}) collective-permute-start(bf16[2,4,64,1536]{3,2,1,0:T(8,128)(2,1)S(1)} %pad_maximum_fusion.refs_0_.refs_8_), channel_id=1, source_target_pairs={{0,96},{1,13},{2,98},{3,15},{4,100},{5,1},{6,102},{7,3},{8,104},{9... | collective-permute-start | bytes 4718600 | tf_op jit(solution)/shard_map/ppermute | solution.py:53
  33.4 23.1 %collective-permute-start.10 = (bf16[2,4,64,1536]{3,2,1,0:T(8,128)(2,1)S(1)}, bf16[2,4,64,1536]{3,2,1,0:T(8,128)(2,1)S(1)}, u32[]{:S(2)}, u32[]{:S(2)}) collective-permute-start(bf16[2,4,64,1536]{3,2,1,0:T(8,128)(2,1)S(1)} %pad_maximum_fusion.refs_0_.refs_8_), channel_id=1, source_target_pairs={{0,32},{1,5},{2,34},{3,7},{4,36},{5,9},{6,38},{7,11},{8,40},{9,13}... | collective-permute-start | bytes 4718600 | tf_op jit(solution)/shard_map/ppermute | solution.py:53
  35.6 20.6 %collective-permute-start.12 = (bf16[4,192,256]{2,1,0:T(8,128)(2,1)S(1)}, bf16[4,192,256]{2,1,0:T(8,128)(2,1)S(1)}, u32[]{:S(2)}, u32[]{:S(2)}) collective-permute-start(bf16[4,192,256]{2,1,0:T(8,128)(2,1)S(1)} %pad_maximum_fusion.1.refs_0_), channel_id=1, source_target_pairs={{0,2},{1,3},{2,0},{3,1},{4,6},{5,7},{6,4},{7,5},{8,10},{9,11},{10,... | collective-permute-start | bytes 1179656 | tf_op jit(solution)/shard_map/ppermute | solution.py:21
  36.7 20.4 %copy-start.7 = (bf16[768,1,1536]{2,0,1:T(8,128)(2,1)S(1)}, bf16[768,1,1536]{2,0,1:T(8,128)(2,1)}, u32[]{:S(2)}) copy-start(bf16[768,1,1536]{2,0,1:T(8,128)(2,1)} %param.5) | copy-start | bytes 7077892
  36.7 19.5 %collective-permute-start.13 = (bf16[4,192,256]{2,1,0:T(8,128)(2,1)S(1)}, bf16[4,192,256]{2,1,0:T(8,128)(2,1)S(1)}, u32[]{:S(2)}, u32[]{:S(2)}) collective-permute-start(bf16[4,192,256]{2,1,0:T(8,128)(2,1)S(1)} %pad_maximum_fusion.2), channel_id=1, source_target_pairs={{0,16},{16,0},{32,48},{48,32},{64,80},{80,64},{96,112},{112,96},{1... | collective-permute-start | bytes 1179656 | tf_op jit(solution)/shard_map/ppermute | solution.py:21
  53.8 3.3 %copy-start.3 = (bf16[2,4,64,1536]{3,2,1,0:T(8,128)(2,1)}, bf16[2,4,64,1536]{3,2,1,0:T(8,128)(2,1)S(1)}, u32[]{:S(2)}) copy-start(bf16[2,4,64,1536]{3,2,1,0:T(8,128)(2,1)S(1)} %collective-permute-done.11.refs_2_.refs_10_) | copy-start | bytes 4718596
  53.9 12.4 %collective-permute-start.15 = (bf16[1,4,64,1536]{3,2,1,0:T(8,128)(2,1)S(1)}, bf16[1,4,64,1536]{3,2,1,0:T(8,128)(2,1)S(1)}, u32[]{:S(2)}, u32[]{:S(2)}) collective-permute-start(bf16[1,4,64,1536]{3,2,1,0:T(8,128)(2,1)S(1)} %slice.41), channel_id=1, source_target_pairs={{0,96},{1,13},{2,98},{3,15},{4,100},{5,1},{6,102},{7,3},{8,104},{9... | collective-permute-start | bytes 2359304 | tf_op jit(solution)/shard_map/ppermute | solution.py:53
  56.2 0.7 copy-start.12
  56.2 0.9 copy-start.14
  56.5 9.6 %copy-start.5 = (bf16[2,4,64,1536]{3,2,1,0:T(8,128)(2,1)}, bf16[2,4,64,1536]{3,2,1,0:T(8,128)(2,1)S(1)}, u32[]{:S(2)}) copy-start(bf16[2,4,64,1536]{3,2,1,0:T(8,128)(2,1)S(1)} %collective-permute-done.10.refs_1_.refs_9_) | copy-start | bytes 4718596
  56.6 13.3 %collective-permute-start.14 = (bf16[1,4,64,1536]{3,2,1,0:T(8,128)(2,1)S(1)}, bf16[1,4,64,1536]{3,2,1,0:T(8,128)(2,1)S(1)}, u32[]{:S(2)}, u32[]{:S(2)}) collective-permute-start(bf16[1,4,64,1536]{3,2,1,0:T(8,128)(2,1)S(1)} %slice.40), channel_id=1, source_target_pairs={{0,32},{1,5},{2,34},{3,7},{4,36},{5,9},{6,38},{7,11},{8,40},{9,13}... | collective-permute-start | bytes 2359304 | tf_op jit(solution)/shard_map/ppermute | solution.py:53
  66.2 9.0 %collective-permute-start.16 = (bf16[6,2,192,256]{3,2,1,0:T(8,128)(2,1)S(1)}, bf16[6,2,192,256]{3,2,1,0:T(8,128)(2,1)S(1)}, u32[]{:S(2)}, u32[]{:S(2)}) collective-permute-start(bf16[6,2,192,256]{3,2,1,0:T(8,128)(2,1)S(1)} %get-tuple-element.56), channel_id=1, source_target_pairs={{0,1},{1,0},{2,3},{3,2},{4,5},{5,4},{6,7},{7,6},{8,9},{9,8},{10,11... | collective-permute-start | bytes 3538952 | tf_op jit(solution)/shard_map/ppermute | solution.py:21
  66.3 7.1 %copy-start.8 = (bf16[1,4,64,1536]{3,2,1,0:T(8,128)(2,1)}, bf16[1,4,64,1536]{3,2,1,0:T(8,128)(2,1)S(1)}, u32[]{:S(2)}) copy-start(bf16[1,4,64,1536]{3,2,1,0:T(8,128)(2,1)S(1)} %collective-permute-done.15.refs_1_.refs_12_) | copy-start | bytes 2359300
  69.9 3.5 %copy-start.10 = (bf16[1,4,64,1536]{3,2,1,0:T(8,128)(2,1)}, bf16[1,4,64,1536]{3,2,1,0:T(8,128)(2,1)S(1)}, u32[]{:S(2)}) copy-start(bf16[1,4,64,1536]{3,2,1,0:T(8,128)(2,1)S(1)} %collective-permute-done.14.refs_0_.refs_11_) | copy-start | bytes 2359300
  73.4 1.8 %collective-permute-start.17 = (bf16[2,2,192,256]{3,2,1,0:T(8,128)(2,1)S(1)}, bf16[2,2,192,256]{3,2,1,0:T(8,128)(2,1)S(1)}, u32[]{:S(2)}, u32[]{:S(2)}) collective-permute-start(bf16[2,2,192,256]{3,2,1,0:T(8,128)(2,1)S(1)} %get-tuple-element.57), channel_id=1, source_target_pairs={{0,1},{1,0},{2,3},{3,2},{4,5},{5,4},{6,7},{7,6},{8,9},{9,8},{10,11... | collective-permute-start | bytes 1179656 | tf_op jit(solution)/shard_map/ppermute | solution.py:21
  77.3 52.4 %all-to-all-start = ((bf16[16,192,256]{2,1,0:T(8,128)(2,1)}), bf16[16,192,256]{2,1,0:T(8,128)(2,1)S(1)}, u32[]{:S(2)}, u32[]{:S(2)}) async-start(bf16[16,192,256]{2,1,0:T(8,128)(2,1)} %bitcast.16), calls=%async_computation | async-start | bytes 3145728 | tf_op jit(solution)/shard_map/all_to_all | solution.py:299
  81.0 28.0 %collective-permute-start.18 = (bf16[4,192,256]{2,1,0:T(8,128)(2,1)}, bf16[4,192,256]{2,1,0:T(8,128)(2,1)S(1)}, u32[]{:S(2)}, u32[]{:S(2)}) collective-permute-start(bf16[4,192,256]{2,1,0:T(8,128)(2,1)} %copy-done.14), channel_id=1, source_target_pairs={{0,2},{1,3},{2,0},{3,1},{4,6},{5,7},{6,4},{7,5},{8,10},{9,11},{10,... | collective-permute-start | bytes 1179656 | tf_op jit(solution)/shard_map/ppermute | solution.py:21
  109.0 2.2 %collective-permute-start.19 = (bf16[4,192,256]{2,1,0:T(8,128)(2,1)S(1)}, bf16[4,192,256]{2,1,0:T(8,128)(2,1)S(1)}, u32[]{:S(2)}, u32[]{:S(2)}) collective-permute-start(bf16[4,192,256]{2,1,0:T(8,128)(2,1)S(1)} %pad_maximum_fusion.1.refs_0_), channel_id=1, source_target_pairs={{0,1},{1,0},{2,3},{3,2},{4,5},{5,4},{6,7},{7,6},{8,9},{9,8},{10,11... | collective-permute-start | bytes 1179656 | tf_op jit(solution)/shard_map/ppermute | solution.py:21
  109.0 2.5 %collective-permute-start.20 = (bf16[4,192,256]{2,1,0:T(8,128)(2,1)}, bf16[4,192,256]{2,1,0:T(8,128)(2,1)S(1)}, u32[]{:S(2)}, u32[]{:S(2)}) collective-permute-start(bf16[4,192,256]{2,1,0:T(8,128)(2,1)} %copy-done.14), channel_id=1, source_target_pairs={{0,1},{1,0},{2,3},{3,2},{4,5},{5,4},{6,7},{7,6},{8,9},{9,8},{10,11... | collective-permute-start | bytes 1179656 | tf_op jit(solution)/shard_map/ppermute | solution.py:21
  109.5 3.1 %collective-permute-start.21 = (bf16[4,192,256]{2,1,0:T(8,128)(2,1)}, bf16[4,192,256]{2,1,0:T(8,128)(2,1)S(1)}, u32[]{:S(2)}, u32[]{:S(2)}) collective-permute-start(bf16[4,192,256]{2,1,0:T(8,128)(2,1)} %copy-done.12), channel_id=1, source_target_pairs={{0,1},{1,0},{2,3},{3,2},{4,5},{5,4},{6,7},{7,6},{8,9},{9,8},{10,11... | collective-permute-start | bytes 1179656 | tf_op jit(solution)/shard_map/ppermute | solution.py:21
  109.5 3.1 %collective-permute-start.22 = (bf16[4,192,256]{2,1,0:T(8,128)(2,1)S(1)}, bf16[4,192,256]{2,1,0:T(8,128)(2,1)S(1)}, u32[]{:S(2)}, u32[]{:S(2)}) collective-permute-start(bf16[4,192,256]{2,1,0:T(8,128)(2,1)S(1)} %collective-permute-done.18.refs_3_), channel_id=1, source_target_pairs={{0,1},{1,0},{2,3},{3,2},{4,5},{5,4},{6,7},{7,6},{8,9},{9,8},{10,11... | collective-permute-start | bytes 1179656 | tf_op jit(solution)/shard_map/ppermute | solution.py:21
  112.6 1.4 %copy-start.4 = (bf16[2,4,64,1536]{3,2,1,0:T(8,128)(2,1)S(1)}, bf16[2,4,64,1536]{3,2,1,0:T(8,128)(2,1)}, u32[]{:S(2)}) copy-start(bf16[2,4,64,1536]{3,2,1,0:T(8,128)(2,1)} %copy-done.3) | copy-start | bytes 4718596
  114.1 1.4 %copy-start.6 = (bf16[2,4,64,1536]{3,2,1,0:T(8,128)(2,1)S(1)}, bf16[2,4,64,1536]{3,2,1,0:T(8,128)(2,1)}, u32[]{:S(2)}) copy-start(bf16[2,4,64,1536]{3,2,1,0:T(8,128)(2,1)} %copy-done.5) | copy-start | bytes 4718596
  115.5 1.1 copy-start.9
  116.6 1.1 copy-start.11
  117.7 1.0 copy-start.13
  118.7 1.0 copy-start.15
  129.7 1.4 %copy-start.1 = (f32[256,1536]{1,0:T(8,128)S(1)}, f32[256,1536]{1,0:T(8,128)}, u32[]{:S(2)}) copy-start(f32[256,1536]{1,0:T(8,128)} %copy-done) | copy-start | bytes 4718596

commit v10 on v9

--- a/solution.py
+++ b/solution.py
@@ -15,6 +15,7 @@
 VMEM = pl.BlockSpec(memory_space=pltpu.VMEM)
 SMEM = pl.BlockSpec(memory_space=pltpu.SMEM)
 ANY = pl.BlockSpec(memory_space=pl.ANY)
+HBM = pl.BlockSpec(memory_space=pltpu.HBM)
 
 
 def send(v, axis, count, to):
@@ -196,14 +197,21 @@
             leaving(k, z).wait()
 
 
-def finish_body(at, slope, parts, out):
+def finish_body(at, slope, parts, out, held, sems):
+    count = out.shape[1] // 256
+    copies = [
+        pltpu.make_async_copy(slope.at[:, pl.ds(256 * j, 256)], held.at[j], sems.at[j]) for j in range(count)
+    ]
+    for c in copies:
+        c.start()
     pick = one_hot()
-    for j in range(out.shape[1] // 256):
+    for j in range(count):
         cols, units = slice(256 * j, 256 * j + 256), slice(32 * j, 32 * j + 32)
         v = [(parts[n, 0, units, :].astype(f32) + parts[n, 1, units, :].astype(f32)) for n in range(8)]
         v = jnp.concatenate(v, 0).astype(bf16)
         total = lax.dot_general(v, pick, (((0,), (0,)), ((), ())), preferred_element_type=f32)
-        result = (total * slope[:, cols]).astype(bf16)
+        copies[j].wait()
+        result = (total * held[j]).astype(bf16)
         for k in range(4):
             out[token_rows(at[2], k), cols] = result[64 * k : 64 * k + 64, :]
 
@@ -258,8 +266,8 @@
 
     p2p, p2m = send_by_core(p1[:1], 1, False), send_by_core(p3[1:], 3, False)
     pieces = p0, p1, p3, p2p, p2m
-    own = [jnp.stack([p[0] for p in by_x]), swap_z_hi(jnp.stack([p[1] for p in by_x]))]
-    far = [swap_z_lo(own[0])]
+    keep, away = [jnp.stack([p[z] for p in by_x]) for z in range(2)]
+    near = [keep, swap_z_hi(away), swap_z_lo(keep), send(away, ("gx", "gz"), 32, lambda i: i ^ 6)]
 
     def input_part(*given):
         count = sum(p.shape[0] for p in given)
@@ -280,9 +288,8 @@
             limit=10 + 2 * count,
         )(at, w, *given)
 
-    early = lax.optimization_barrier((p0, p1, p3, far[0], own[1]))
-    far, own[1] = [early[3], swap_z_lo(early[4])], early[4]
-    mine, theirs = input_part(*early[:3])
+    early, near = lax.optimization_barrier(((p0, p1, p3), near))
+    mine, theirs = input_part(*early)
     other = swap_core(theirs)
     mine2, theirs2 = input_part(p2p, p2m)
     size = 2 * 4 * rows * tokens
@@ -299,12 +306,12 @@
     back = lax.all_to_all(
         sums.reshape((16,) + block), ("gx", "gz"), 0, 0, tiled=True, axis_index_groups=same_core
     )
-    near, _ = lax.optimization_barrier((own + far, sums))
+    near, _ = lax.optimization_barrier((near, sums))
     hidden = near + [swap_core(v) for v in near]
     (weight_grad,) = call(
         weight_body,
         [((4 * rows, features), bf16)],
-        [SMEM] + [ANY] * 13,
+        [SMEM] + [HBM] * 13,
         (product, 2 * (8 * rows * features + 2048 * features)),
         scratch=[
             pltpu.VMEM((4, 2, 4, tokens // 4, features), bf16),
@@ -312,14 +319,15 @@
             pltpu.SemaphoreType.DMA((8,)),
             pltpu.SemaphoreType.DMA((8,)),
         ],
-        limit=24,
+        limit=56,
     )(at, *hidden, *pieces)
     back, weight_grad = lax.optimization_barrier((back, weight_grad))
     (pre_grad,) = call(
         finish_body,
         [((tokens, columns), bf16)],
-        [SMEM] + [VMEM] * 2,
+        [SMEM, HBM, VMEM],
         (2 * tokens * 256 * columns, 8 * tokens * columns),
+        scratch=[pltpu.VMEM((columns // 256, tokens, 256), f32), pltpu.SemaphoreType.DMA((columns // 256,))],
         limit=12,
     )(at, slope, back.reshape((8, 2) + block))
     return pre_grad, weight_grad.reshape(weight.shape)

time: 134 us -> 109 us (0.81)
  waiting for transfers between devices: 53.8 us -> 34.6 us
  local copies, waits for them, and re-layouts: 11.5 us -> 3.55 us
  Pallas kernels: 28.4 us -> 31.5 us
    ppermute x13, waiting for transfers between devices: 30.9 us -> 4.73 us  [send(): return lax.ppermute(v, axis, [(i, to(i)) for i in range(count)])]
    all_to_all x1, waiting for transfers between devices: 0.01 us -> 8.43 us  [per_device(): lax.all_to_all(sums.reshape((16,) + block), ('gx', 'gz'), 0, 0, tiled=Tru...]
    unnamed x32, local copies, waits for them, and re-layouts: 11.2 us -> 3.3 us
    pallas_call x2, Pallas kernels: 11.8 us -> 15 us  [the longest x1 11.8 us: per_device(): call(weight_body, [((4 * rows, features), bf16)], [SMEM] + [HBM] * 13, (p...]
    ppermute x10, waiting for transfers between devices: 22.9 us -> 21.4 us  [send_by_core(): return lax.ppermute(v, ('gx', 'gy', 'gz'), pairs)]
  transfers between devices with their start and end apart: 24 -> 24, of which waited for: 10 -> 12; matrix products, arithmetic and copies ran while one was open for 0% -> 0% of each run, Pallas kernels for 18% -> 24%
where the time goes in v10:
time: 109 us
  starting transfers between devices  37.2 us (34%)
  waiting for transfers between devices  34.6 us (32%)
  Pallas kernels  31.5 us (29%)
  local copies, waits for them, and re-layouts  3.55 us (3%)
  other arithmetic  1.37 us (1%)
    ppermute x10, waiting for transfers between devices, send_by_core(): return lax.ppermute(v, ('gx', 'gy', 'gz'), pairs)  21.4 us
    ppermute x10, starting transfers between devices, send_by_core(): return lax.ppermute(v, ('gx', 'gy', 'gz'), pairs)  18.4 us
    ppermute x13, starting transfers between devices, send(): return lax.ppermute(v, axis, [(i, to(i)) for i in range(count)])  15 us
    pallas_call x2, Pallas kernels, input_part(): call(functools.partial(input_body, len(given)), [((count, 2) + block, bf1...  12.6 us
    pallas_call x1, Pallas kernels, per_device(): call(weight_body, [((4 * rows, features), bf16)], [SMEM] + [HBM] * 13, (p...  11.8 us
    all_to_all x1, waiting for transfers between devices, per_device(): lax.all_to_all(sums.reshape((16,) + block), ('gx', 'gz'), 0, 0, tiled=Tru...  8.43 us
    ppermute x13, waiting for transfers between devices, send(): return lax.ppermute(v, axis, [(i, to(i)) for i in range(count)])  4.73 us
    all_to_all x1, starting transfers between devices, per_device(): lax.all_to_all(sums.reshape((16,) + block), ('gx', 'gz'), 0, 0, tiled=Tru...  3.72 us
  transfers between devices with their start and end apart: 24, of which 12 were waited for; matrix products, arithmetic and copies ran while one was open for 0% of the time, Pallas kernels for 24%

profile of v10, /device:TPU:0, one launch (start us, length us, event | category | flops | bytes accessed | tf_op | source)
XLA Modules:
  0.0 109.1 jit_solution(14613262178694557873)
XLA Ops:
  0.6 3.2 %collective-permute-start.2 = (bf16[64,1536]{1,0:T(8,128)(2,1)}, bf16[64,1536]{1,0:T(8,128)(2,1)S(1)}, u32[]{:S(2)}, u32[]{:S(2)}) collective-permute-start(bf16[64,1536]{1,0:T(8,128)(2,1)} %param.4), channel_id=1, source_target_pairs={{0,12},{1,97},{2,14},{3,99},{4,0},{5,101},{6,2},{7,103},{8,4},{9,1... | collective-permute-start | bytes 589832 | tf_op jit(solution)/shard_map/ppermute | solution.py:54
  3.8 0.6 collective-permute-start.1
  4.4 1.0 collective-permute-start
  5.4 3.9 %collective-permute-start.3 = (bf16[64,1536]{1,0:T(8,128)(2,1)}, bf16[64,1536]{1,0:T(8,128)(2,1)S(1)}, u32[]{:S(2)}, u32[]{:S(2)}) collective-permute-start(bf16[64,1536]{1,0:T(8,128)(2,1)} %param.4), channel_id=1, source_target_pairs={{0,16},{16,0},{32,48},{48,32},{64,80},{80,64},{96,112},{112,96},{1... | collective-permute-start | bytes 589832 | tf_op jit(solution)/shard_map/ppermute | solution.py:22
  9.3 0.1 stack.68.at
  9.4 1.1 %copy-done.3 = bf16[256,1536]{1,0:T(8,128)(2,1)S(1)} copy-done((bf16[256,1536]{1,0:T(8,128)(2,1)S(1)}, bf16[256,1536]{1,0:T(8,128)(2,1)}, u32[]{:S(2)}) %copy-start.3) | copy-done | bytes 786456
  10.5 1.9 %shard_map.50 = (f32[256,1536]{1,0:T(8,128)S(1)}, bf16[2,192,256]{2,1,0:T(8,128)(2,1)S(1)}, bf16[2,192,256]{2,1,0:T(8,128)(2,1)S(1)}, bf16[2,192,256]{2,1,0:T(8,128)(2,1)S(1)}, bf16[2,192,256]{2,1,0:T(8,128)(2,1)S(1)}) custom-call(s32[5]{0:T(128)S(1)} %stack.68.at, bf16[256,1536]{1,0:T(8,128)(2,1)S(1)} %copy-done.3), custom_call_target="tpu_custom_call" | custom-call | flops 201326592 | bytes 3145728 | tf_op jit(solution)/shard_map/pallas_call | solution.py:252
  12.4 1.2 %copy-done.1 = f32[256,1536]{1,0:T(8,128)} copy-done((f32[256,1536]{1,0:T(8,128)}, f32[256,1536]{1,0:T(8,128)S(1)}, u32[]{:S(2)}) %copy-start.1) | copy-done | bytes 1572888
  13.6 1.5 %collective-permute-start.7 = (bf16[2,192,256]{2,1,0:T(8,128)(2,1)S(1)}, bf16[2,192,256]{2,1,0:T(8,128)(2,1)S(1)}, u32[]{:S(2)}, u32[]{:S(2)}) collective-permute-start(bf16[2,192,256]{2,1,0:T(8,128)(2,1)S(1)} %get-tuple-element.38), channel_id=1, source_target_pairs={{0,32},{16,48},{32,64},{48,80},{64,96},{80,112},{96,0},{112,16},{1... | collective-permute-start | bytes 589832 | tf_op jit(solution)/shard_map/ppermute | solution.py:22
  15.1 0.0 collective-permute-done.2
  15.1 2.7 %collective-permute-start.8 = (bf16[2,192,256]{2,1,0:T(8,128)(2,1)S(1)}, bf16[2,192,256]{2,1,0:T(8,128)(2,1)S(1)}, u32[]{:S(2)}, u32[]{:S(2)}) collective-permute-start(bf16[2,192,256]{2,1,0:T(8,128)(2,1)S(1)} %get-tuple-element.39), channel_id=1, source_target_pairs={{0,64},{16,80},{32,96},{48,112},{64,0},{80,16},{96,32},{112,48},{1... | collective-permute-start | bytes 589832 | tf_op jit(solution)/shard_map/ppermute | solution.py:22
  17.8 0.0 collective-permute-done.1
  17.8 1.4 %collective-permute-start.9 = (bf16[2,192,256]{2,1,0:T(8,128)(2,1)S(1)}, bf16[2,192,256]{2,1,0:T(8,128)(2,1)S(1)}, u32[]{:S(2)}, u32[]{:S(2)}) collective-permute-start(bf16[2,192,256]{2,1,0:T(8,128)(2,1)S(1)} %get-tuple-element.40), channel_id=1, source_target_pairs={{0,96},{16,112},{32,0},{48,16},{64,32},{80,48},{96,64},{112,80},{1... | collective-permute-start | bytes 589832 | tf_op jit(solution)/shard_map/ppermute | solution.py:22
  19.3 0.0 collective-permute-done.3
  19.3 2.3 %collective-permute-start.6 = (bf16[64,1536]{1,0:T(8,128)(2,1)S(1)}, bf16[64,1536]{1,0:T(8,128)(2,1)S(1)}, u32[]{:S(2)}, u32[]{:S(2)}) collective-permute-start(bf16[64,1536]{1,0:T(8,128)(2,1)S(1)} %collective-permute-done.3), channel_id=1, source_target_pairs={{0,12},{1,97},{2,14},{3,99},{4,0},{5,101},{6,2},{7,103},{8,4},{9,1... | collective-permute-start | bytes 589832 | tf_op jit(solution)/shard_map/ppermute | solution.py:54
  21.5 0.0 collective-permute-done
  21.5 1.7 %collective-permute-start.5 = (bf16[64,1536]{1,0:T(8,128)(2,1)S(1)}, bf16[64,1536]{1,0:T(8,128)(2,1)S(1)}, u32[]{:S(2)}, u32[]{:S(2)}) collective-permute-start(bf16[64,1536]{1,0:T(8,128)(2,1)S(1)} %collective-permute-done.3), channel_id=1, source_target_pairs={{0,8},{1,65},{2,10},{3,67},{4,12},{5,69},{6,14},{7,71},{8,0},{9,73... | collective-permute-start | bytes 589832 | tf_op jit(solution)/shard_map/ppermute | solution.py:54
  23.2 0.4 collective-permute-done.7
  23.6 5.2 %collective-permute-start.4 = (bf16[64,1536]{1,0:T(8,128)(2,1)S(1)}, bf16[64,1536]{1,0:T(8,128)(2,1)S(1)}, u32[]{:S(2)}, u32[]{:S(2)}) collective-permute-start(bf16[64,1536]{1,0:T(8,128)(2,1)S(1)} %collective-permute-done.3), channel_id=1, source_target_pairs={{0,4},{1,33},{2,6},{3,35},{4,8},{5,37},{6,10},{7,39},{8,12},{9,41}... | collective-permute-start | bytes 589832 | tf_op jit(solution)/shard_map/ppermute | solution.py:54
  28.9 0.0 collective-permute-done.8
  28.9 0.0 collective-permute-done.9
  28.9 0.0 collective-permute-done.6
  28.9 0.0 collective-permute-done.5
  28.9 3.2 %collective-permute-done.4 = bf16[64,1536]{1,0:T(8,128)(2,1)S(1)} collective-permute-done((bf16[64,1536]{1,0:T(8,128)(2,1)S(1)}, bf16[64,1536]{1,0:T(8,128)(2,1)S(1)}, u32[]{:S(2)}, u32[]{:S(2)}) %collective-permute-start.4) | collective-permute-done | bytes 196640 | tf_op jit(solution)/shard_map/ppermute | solution.py:54
  32.1 1.1 %maximum_bitcast_fusion = (bf16[1,4,64,1536]{3,2,1,0:T(8,128)(2,1)S(1)}, bf16[1,4,64,1536]{3,2,1,0:T(8,128)(2,1)S(1)}) fusion(bf16[1,64,1536]{2,1,0:T(8,128)(2,1)S(1)} %bitcast.25, bf16[1,64,1536]{2,1,0:T(8,128)(2,1)S(1)} %bitcast.26, bf16[1,64,1536]{2,1,0:T(8,128)(2,1)S(1)} %bitcast.27, bf16[1,64,1536]{2,1,0:T(8,128)(2,1)} %bitcast.24, ...), kind=kLoop, calls=%fused_computation.1 | loop fusion | flops 2359296 | bytes 3145728 | tf_op jit(solution)/shard_map/stack | solution.py:264
  33.2 0.1 pad_maximum_fusion.refs_0_.refs_8_
  33.3 0.1 collective-permute-start.11
  33.4 2.0 %collective-permute-start.10 = (bf16[2,4,64,1536]{3,2,1,0:T(8,128)(2,1)S(1)}, bf16[2,4,64,1536]{3,2,1,0:T(8,128)(2,1)S(1)}, u32[]{:S(2)}, u32[]{:S(2)}) collective-permute-start(bf16[2,4,64,1536]{3,2,1,0:T(8,128)(2,1)S(1)} %pad_maximum_fusion.refs_0_.refs_8_), channel_id=1, source_target_pairs={{0,32},{1,5},{2,34},{3,7},{4,36},{5,9},{6,38},{7,11},{8,40},{9,13}... | collective-permute-start | bytes 4718600 | tf_op jit(solution)/shard_map/ppermute | solution.py:54
  35.5 0.1 pad_maximum_fusion.1.refs_0_
  35.6 1.1 %collective-permute-start.13 = (bf16[4,192,256]{2,1,0:T(8,128)(2,1)S(1)}, bf16[4,192,256]{2,1,0:T(8,128)(2,1)}, u32[]{:S(2)}, u32[]{:S(2)}) collective-permute-start(bf16[4,192,256]{2,1,0:T(8,128)(2,1)S(1)} %pad_maximum_fusion.1.refs_0_), channel_id=1, source_target_pairs={{0,2},{1,3},{2,0},{3,1},{4,6},{5,7},{6,4},{7,5},{8,10},{9,11},{10,... | collective-permute-start | bytes 1179656 | tf_op jit(solution)/shard_map/ppermute | solution.py:22
  36.7 0.1 pad_maximum_fusion.2
  36.7 0.0 copy-start.8
  36.7 0.1 collective-permute-start.14
  36.8 3.1 %collective-permute-start.12 = (bf16[4,192,256]{2,1,0:T(8,128)(2,1)S(1)}, bf16[4,192,256]{2,1,0:T(8,128)(2,1)}, u32[]{:S(2)}, u32[]{:S(2)}) collective-permute-start(bf16[4,192,256]{2,1,0:T(8,128)(2,1)S(1)} %pad_maximum_fusion.2), channel_id=1, source_target_pairs={{0,16},{16,0},{32,48},{48,32},{64,80},{80,64},{96,112},{112,96},{1... | collective-permute-start | bytes 1179656 | tf_op jit(solution)/shard_map/ppermute | solution.py:22
  39.9 13.9 %collective-permute-done.11.refs_2_.refs_10_ = bf16[2,4,64,1536]{3,2,1,0:T(8,128)(2,1)S(1)} collective-permute-done((bf16[2,4,64,1536]{3,2,1,0:T(8,128)(2,1)S(1)}, bf16[2,4,64,1536]{3,2,1,0:T(8,128)(2,1)S(1)}, u32[]{:S(2)}, u32[]{:S(2)}) %collective-permute-start.11) | collective-permute-done | bytes 1572896 | tf_op jit(solution)/shard_map/ppermute | solution.py:54
  53.8 0.1 slice.41
  53.9 2.3 %collective-permute-start.16 = (bf16[1,4,64,1536]{3,2,1,0:T(8,128)(2,1)S(1)}, bf16[1,4,64,1536]{3,2,1,0:T(8,128)(2,1)S(1)}, u32[]{:S(2)}, u32[]{:S(2)}) collective-permute-start(bf16[1,4,64,1536]{3,2,1,0:T(8,128)(2,1)S(1)} %slice.41), channel_id=1, source_target_pairs={{0,96},{1,13},{2,98},{3,15},{4,100},{5,1},{6,102},{7,3},{8,104},{9... | collective-permute-start | bytes 2359304 | tf_op jit(solution)/shard_map/ppermute | solution.py:54
  56.2 0.0 collective-permute-done.13.refs_2_
  56.2 0.3 collective-permute-done.10.refs_1_.refs_9_
  56.5 0.1 slice.40
  56.6 0.1 collective-permute-start.15
  56.7 9.1 %shard_map.51 = (bf16[6,2,192,256]{3,2,1,0:T(8,128)(2,1)S(1)}, bf16[6,2,192,256]{3,2,1,0:T(8,128)(2,1)S(1)}) custom-call(s32[5]{0:T(128)S(1)} %stack.68.at, bf16[768,1536]{1,0:T(8,128)(2,1)S(1)} %bitcast.22, bf16[2,4,64,1536]{3,2,1,0:T(8,128)(2,1)S(1)} %pad_maximum_fusion.refs_0_.refs_8_, ...), custom_call_target="tpu_custom_call" | custom-call | flops 3623878656 | bytes 9437184 | tf_op jit(solution)/shard_map/pallas_call | solution.py:274
  65.8 0.1 collective-permute-start.17
  65.9 0.2 collective-permute-done.16.refs_1_.refs_12_
  66.0 3.8 %collective-permute-done.15.refs_0_.refs_11_ = bf16[1,4,64,1536]{3,2,1,0:T(8,128)(2,1)S(1)} collective-permute-done((bf16[1,4,64,1536]{3,2,1,0:T(8,128)(2,1)S(1)}, bf16[1,4,64,1536]{3,2,1,0:T(8,128)(2,1)S(1)}, u32[]{:S(2)}, u32[]{:S(2)}) %collective-permute-start.15) | collective-permute-done | bytes 786464 | tf_op jit(solution)/shard_map/ppermute | solution.py:54
  69.9 3.5 %shard_map.52 = (bf16[2,2,192,256]{3,2,1,0:T(8,128)(2,1)S(1)}, bf16[2,2,192,256]{3,2,1,0:T(8,128)(2,1)S(1)}) custom-call(s32[5]{0:T(128)S(1)} %stack.68.at, bf16[768,1536]{1,0:T(8,128)(2,1)S(1)} %bitcast.23, bf16[1,4,64,1536]{3,2,1,0:T(8,128)(2,1)S(1)} %collective-permute-done.15.refs_0_.refs_11_, ...), custom_call_target="tpu_custom_call" | custom-call | flops 1207959552 | bytes 4718592 | tf_op jit(solution)/shard_map/pallas_call | solution.py:274
  73.4 0.1 collective-permute-start.18
  73.5 1.7 %collective-permute-done.18.other2 = bf16[2,2,192,256]{3,2,1,0:T(8,128)(2,1)S(1)} collective-permute-done((bf16[2,2,192,256]{3,2,1,0:T(8,128)(2,1)S(1)}, bf16[2,2,192,256]{3,2,1,0:T(8,128)(2,1)S(1)}, u32[]{:S(2)}, u32[]{:S(2)}) %collective-permute-start.18) | collective-permute-done | bytes 393248 | tf_op jit(solution)/shard_map/ppermute | solution.py:22
  75.2 0.0 collective-permute-done.17.other
  75.2 2.1 %shard_map.53 = bf16[8,2,192,256]{3,2,1,0:T(8,128)(2,1)} custom-call(s32[5]{0:T(128)S(1)} %stack.68.at, bf16[6,2,192,256]{3,2,1,0:T(8,128)(2,1)S(1)} %get-tuple-element.56.mine, bf16[2,2,192,256]{3,2,1,0:T(8,128)(2,1)S(1)} %get-tuple-element.57.mine2, bf16[6,2,192,256]{3,2,1,0:T(8,128)(2,1)S(1)} %collective-permute-done.17.other, ...), custom_call_target="tpu_custom_call" | custom-call | flops 1572864 | bytes 4718592 | tf_op jit(solution)/shard_map/pallas_call | solution.py:296
  77.3 3.7 %all-to-all-start = ((bf16[16,192,256]{2,1,0:T(8,128)(2,1)}), bf16[16,192,256]{2,1,0:T(8,128)(2,1)S(1)}, u32[]{:S(2)}, u32[]{:S(2)}) async-start(bf16[16,192,256]{2,1,0:T(8,128)(2,1)} %bitcast.16), calls=%async_computation | async-start | bytes 3145728 | tf_op jit(solution)/shard_map/all_to_all | solution.py:306
  81.1 0.2 collective-permute-start.19
  81.3 0.4 collective-permute-start.20
  81.6 0.1 collective-permute-start.21
  81.8 0.4 collective-permute-start.22
  82.2 0.7 collective-permute-done.19.refs_4_
  82.9 0.8 collective-permute-done.20.refs_5_
  83.6 0.6 collective-permute-done.21.refs_6_
  84.2 0.6 collective-permute-done.22.refs_7_
  84.8 0.2 copy-done.14
  84.9 0.8 copy-done.15
  85.7 11.8 %shard_map.54 = bf16[768,1536]{1,0:T(8,128)(2,1)} custom-call(s32[5]{0:T(128)} %copy-done.6, bf16[4,192,256]{2,1,0:T(8,128)(2,1)} %copy-done.11, bf16[4,192,256]{2,1,0:T(8,128)(2,1)} %collective-permute-done.12.refs_1_, bf16[4,192,256]{2,1,0:T(8,128)(2,1)} %collective-permute-done.13.refs_2_, bf16[4,192,256]{2,1,0:T(8,128)(2,1)} %collective-permute-done.14.refs_3_, ...), custom_call_target="tpu_custom_call" | custom-call | flops 4831838208 | bytes 11010048 | tf_op jit(solution)/shard_map/pallas_call | solution.py:311
  97.5 8.4 %all-to-all-done = bf16[16,192,256]{2,1,0:T(8,128)(2,1)S(1)} async-done(((bf16[16,192,256]{2,1,0:T(8,128)(2,1)}), bf16[16,192,256]{2,1,0:T(8,128)(2,1)S(1)}, u32[]{:S(2)}, u32[]{:S(2)}) %all-to-all-start) | async-done | bytes 1572896 | tf_op jit(solution)/shard_map/all_to_all | solution.py:306
  105.9 3.2 %shard_map.55 = bf16[256,1536]{1,0:T(8,128)(2,1)} custom-call(s32[5]{0:T(128)S(1)} %copy-done.7, f32[256,1536]{1,0:T(8,128)S(1)} %copy-done.2, bf16[8,2,192,256]{3,2,1,0:T(8,128)(2,1)S(1)} %bitcast.21), custom_call_target="tpu_custom_call" | custom-call | flops 201326592 | bytes 3145728 | tf_op jit(solution)/shard_map/pallas_call | solution.py:325
  (31 shorter events, 0.1 us)
Async XLA Ops:
  0.6 14.5 %collective-permute-start.2 = (bf16[64,1536]{1,0:T(8,128)(2,1)}, bf16[64,1536]{1,0:T(8,128)(2,1)S(1)}, u32[]{:S(2)}, u32[]{:S(2)}) collective-permute-start(bf16[64,1536]{1,0:T(8,128)(2,1)} %param.4), channel_id=1, source_target_pairs={{0,12},{1,97},{2,14},{3,99},{4,0},{5,101},{6,2},{7,103},{8,4},{9,1... | collective-permute-start | bytes 589832 | tf_op jit(solution)/shard_map/ppermute | solution.py:54
  3.8 14.0 %collective-permute-start.1 = (bf16[64,1536]{1,0:T(8,128)(2,1)}, bf16[64,1536]{1,0:T(8,128)(2,1)S(1)}, u32[]{:S(2)}, u32[]{:S(2)}) collective-permute-start(bf16[64,1536]{1,0:T(8,128)(2,1)} %param.4), channel_id=1, source_target_pairs={{0,8},{1,65},{2,10},{3,67},{4,12},{5,69},{6,14},{7,71},{8,0},{9,73... | collective-permute-start | bytes 589832 | tf_op jit(solution)/shard_map/ppermute | solution.py:54
  4.4 17.1 %collective-permute-start = (bf16[64,1536]{1,0:T(8,128)(2,1)}, bf16[64,1536]{1,0:T(8,128)(2,1)S(1)}, u32[]{:S(2)}, u32[]{:S(2)}) collective-permute-start(bf16[64,1536]{1,0:T(8,128)(2,1)} %param.4), channel_id=1, source_target_pairs={{0,4},{1,33},{2,6},{3,35},{4,8},{5,37},{6,10},{7,39},{8,12},{9,41}... | collective-permute-start | bytes 589832 | tf_op jit(solution)/shard_map/ppermute | solution.py:54
  5.4 13.9 %collective-permute-start.3 = (bf16[64,1536]{1,0:T(8,128)(2,1)}, bf16[64,1536]{1,0:T(8,128)(2,1)S(1)}, u32[]{:S(2)}, u32[]{:S(2)}) collective-permute-start(bf16[64,1536]{1,0:T(8,128)(2,1)} %param.4), channel_id=1, source_target_pairs={{0,16},{16,0},{32,48},{48,32},{64,80},{80,64},{96,112},{112,96},{1... | collective-permute-start | bytes 589832 | tf_op jit(solution)/shard_map/ppermute | solution.py:22
  9.4 1.1 %copy-start.3 = (bf16[256,1536]{1,0:T(8,128)(2,1)S(1)}, bf16[256,1536]{1,0:T(8,128)(2,1)}, u32[]{:S(2)}) copy-start(bf16[256,1536]{1,0:T(8,128)(2,1)} %pre.1) | copy-start | bytes 2359300
  10.5 64.7 %copy-start.6 = (s32[5]{0:T(128)}, s32[5]{0:T(128)S(1)}, u32[]{:S(2)}) copy-start(s32[5]{0:T(128)S(1)} %stack.68.at) | copy-start | bytes 64
  12.4 1.2 %copy-start.1 = (f32[256,1536]{1,0:T(8,128)}, f32[256,1536]{1,0:T(8,128)S(1)}, u32[]{:S(2)}) copy-start(f32[256,1536]{1,0:T(8,128)S(1)} %get-tuple-element.36.slope) | copy-start | bytes 4718596
  13.6 10.0 %collective-permute-start.7 = (bf16[2,192,256]{2,1,0:T(8,128)(2,1)S(1)}, bf16[2,192,256]{2,1,0:T(8,128)(2,1)S(1)}, u32[]{:S(2)}, u32[]{:S(2)}) collective-permute-start(bf16[2,192,256]{2,1,0:T(8,128)(2,1)S(1)} %get-tuple-element.38), channel_id=1, source_target_pairs={{0,32},{16,48},{32,64},{48,80},{64,96},{80,112},{96,0},{112,16},{1... | collective-permute-start | bytes 589832 | tf_op jit(solution)/shard_map/ppermute | solution.py:22
  15.1 13.8 %collective-permute-start.8 = (bf16[2,192,256]{2,1,0:T(8,128)(2,1)S(1)}, bf16[2,192,256]{2,1,0:T(8,128)(2,1)S(1)}, u32[]{:S(2)}, u32[]{:S(2)}) collective-permute-start(bf16[2,192,256]{2,1,0:T(8,128)(2,1)S(1)} %get-tuple-element.39), channel_id=1, source_target_pairs={{0,64},{16,80},{32,96},{48,112},{64,0},{80,16},{96,32},{112,48},{1... | collective-permute-start | bytes 589832 | tf_op jit(solution)/shard_map/ppermute | solution.py:22
  17.8 11.0 %collective-permute-start.9 = (bf16[2,192,256]{2,1,0:T(8,128)(2,1)S(1)}, bf16[2,192,256]{2,1,0:T(8,128)(2,1)S(1)}, u32[]{:S(2)}, u32[]{:S(2)}) collective-permute-start(bf16[2,192,256]{2,1,0:T(8,128)(2,1)S(1)} %get-tuple-element.40), channel_id=1, source_target_pairs={{0,96},{16,112},{32,0},{48,16},{64,32},{80,48},{96,64},{112,80},{1... | collective-permute-start | bytes 589832 | tf_op jit(solution)/shard_map/ppermute | solution.py:22
  19.3 9.6 %collective-permute-start.6 = (bf16[64,1536]{1,0:T(8,128)(2,1)S(1)}, bf16[64,1536]{1,0:T(8,128)(2,1)S(1)}, u32[]{:S(2)}, u32[]{:S(2)}) collective-permute-start(bf16[64,1536]{1,0:T(8,128)(2,1)S(1)} %collective-permute-done.3), channel_id=1, source_target_pairs={{0,12},{1,97},{2,14},{3,99},{4,0},{5,101},{6,2},{7,103},{8,4},{9,1... | collective-permute-start | bytes 589832 | tf_op jit(solution)/shard_map/ppermute | solution.py:54
  21.5 7.3 %collective-permute-start.5 = (bf16[64,1536]{1,0:T(8,128)(2,1)S(1)}, bf16[64,1536]{1,0:T(8,128)(2,1)S(1)}, u32[]{:S(2)}, u32[]{:S(2)}) collective-permute-start(bf16[64,1536]{1,0:T(8,128)(2,1)S(1)} %collective-permute-done.3), channel_id=1, source_target_pairs={{0,8},{1,65},{2,10},{3,67},{4,12},{5,69},{6,14},{7,71},{8,0},{9,73... | collective-permute-start | bytes 589832 | tf_op jit(solution)/shard_map/ppermute | solution.py:54
  23.6 8.4 %collective-permute-start.4 = (bf16[64,1536]{1,0:T(8,128)(2,1)S(1)}, bf16[64,1536]{1,0:T(8,128)(2,1)S(1)}, u32[]{:S(2)}, u32[]{:S(2)}) collective-permute-start(bf16[64,1536]{1,0:T(8,128)(2,1)S(1)} %collective-permute-done.3), channel_id=1, source_target_pairs={{0,4},{1,33},{2,6},{3,35},{4,8},{5,37},{6,10},{7,39},{8,12},{9,41}... | collective-permute-start | bytes 589832 | tf_op jit(solution)/shard_map/ppermute | solution.py:54
  33.3 23.3 %copy-start = (bf16[2,4,64,1536]{3,2,1,0:T(8,128)(2,1)}, bf16[2,4,64,1536]{3,2,1,0:T(8,128)(2,1)S(1)}, u32[]{:S(2)}) copy-start(bf16[2,4,64,1536]{3,2,1,0:T(8,128)(2,1)S(1)} %pad_maximum_fusion.refs_0_.refs_8_) | copy-start | bytes 4718596
  33.3 20.5 %collective-permute-start.11 = (bf16[2,4,64,1536]{3,2,1,0:T(8,128)(2,1)S(1)}, bf16[2,4,64,1536]{3,2,1,0:T(8,128)(2,1)S(1)}, u32[]{:S(2)}, u32[]{:S(2)}) collective-permute-start(bf16[2,4,64,1536]{3,2,1,0:T(8,128)(2,1)S(1)} %pad_maximum_fusion.refs_0_.refs_8_), channel_id=1, source_target_pairs={{0,96},{1,13},{2,98},{3,15},{4,100},{5,1},{6,102},{7,3},{8,104},{9... | collective-permute-start | bytes 4718600 | tf_op jit(solution)/shard_map/ppermute | solution.py:54
  33.4 23.1 %collective-permute-start.10 = (bf16[2,4,64,1536]{3,2,1,0:T(8,128)(2,1)S(1)}, bf16[2,4,64,1536]{3,2,1,0:T(8,128)(2,1)S(1)}, u32[]{:S(2)}, u32[]{:S(2)}) collective-permute-start(bf16[2,4,64,1536]{3,2,1,0:T(8,128)(2,1)S(1)} %pad_maximum_fusion.refs_0_.refs_8_), channel_id=1, source_target_pairs={{0,32},{1,5},{2,34},{3,7},{4,36},{5,9},{6,38},{7,11},{8,40},{9,13}... | collective-permute-start | bytes 4718600 | tf_op jit(solution)/shard_map/ppermute | solution.py:54
  35.6 45.5 %copy-start.11 = (bf16[4,192,256]{2,1,0:T(8,128)(2,1)}, bf16[4,192,256]{2,1,0:T(8,128)(2,1)S(1)}, u32[]{:S(2)}) copy-start(bf16[4,192,256]{2,1,0:T(8,128)(2,1)S(1)} %pad_maximum_fusion.1.refs_0_) | copy-start | bytes 1179652
  35.6 20.6 %collective-permute-start.13 = (bf16[4,192,256]{2,1,0:T(8,128)(2,1)S(1)}, bf16[4,192,256]{2,1,0:T(8,128)(2,1)}, u32[]{:S(2)}, u32[]{:S(2)}) collective-permute-start(bf16[4,192,256]{2,1,0:T(8,128)(2,1)S(1)} %pad_maximum_fusion.1.refs_0_), channel_id=1, source_target_pairs={{0,2},{1,3},{2,0},{3,1},{4,6},{5,7},{6,4},{7,5},{8,10},{9,11},{10,... | collective-permute-start | bytes 1179656 | tf_op jit(solution)/shard_map/ppermute | solution.py:22
  36.7 20.0 %copy-start.8 = (bf16[768,1,1536]{2,0,1:T(8,128)(2,1)S(1)}, bf16[768,1,1536]{2,0,1:T(8,128)(2,1)}, u32[]{:S(2)}) copy-start(bf16[768,1,1536]{2,0,1:T(8,128)(2,1)} %param.5) | copy-start | bytes 7077892
  36.7 19.5 %collective-permute-start.14 = (bf16[4,192,256]{2,1,0:T(8,128)(2,1)S(1)}, bf16[4,192,256]{2,1,0:T(8,128)(2,1)}, u32[]{:S(2)}, u32[]{:S(2)}) collective-permute-start(bf16[4,192,256]{2,1,0:T(8,128)(2,1)S(1)} %pad_maximum_fusion.2), channel_id=1, source_target_pairs={{0,18},{1,19},{2,16},{3,17},{16,2},{17,3},{18,0},{19,1},{32,50},{3... | collective-permute-start | bytes 1179656 | tf_op jit(solution)/shard_map/ppermute | solution.py:22
  36.8 19.4 %collective-permute-start.12 = (bf16[4,192,256]{2,1,0:T(8,128)(2,1)S(1)}, bf16[4,192,256]{2,1,0:T(8,128)(2,1)}, u32[]{:S(2)}, u32[]{:S(2)}) collective-permute-start(bf16[4,192,256]{2,1,0:T(8,128)(2,1)S(1)} %pad_maximum_fusion.2), channel_id=1, source_target_pairs={{0,16},{16,0},{32,48},{48,32},{64,80},{80,64},{96,112},{112,96},{1... | collective-permute-start | bytes 1179656 | tf_op jit(solution)/shard_map/ppermute | solution.py:22
  53.8 2.9 %copy-start.4 = (bf16[2,4,64,1536]{3,2,1,0:T(8,128)(2,1)}, bf16[2,4,64,1536]{3,2,1,0:T(8,128)(2,1)S(1)}, u32[]{:S(2)}) copy-start(bf16[2,4,64,1536]{3,2,1,0:T(8,128)(2,1)S(1)} %collective-permute-done.11.refs_2_.refs_10_) | copy-start | bytes 4718596
  53.9 12.1 %collective-permute-start.16 = (bf16[1,4,64,1536]{3,2,1,0:T(8,128)(2,1)S(1)}, bf16[1,4,64,1536]{3,2,1,0:T(8,128)(2,1)S(1)}, u32[]{:S(2)}, u32[]{:S(2)}) collective-permute-start(bf16[1,4,64,1536]{3,2,1,0:T(8,128)(2,1)S(1)} %slice.41), channel_id=1, source_target_pairs={{0,96},{1,13},{2,98},{3,15},{4,100},{5,1},{6,102},{7,3},{8,104},{9... | collective-permute-start | bytes 2359304 | tf_op jit(solution)/shard_map/ppermute | solution.py:54
  56.5 9.2 %copy-start.5 = (bf16[2,4,64,1536]{3,2,1,0:T(8,128)(2,1)}, bf16[2,4,64,1536]{3,2,1,0:T(8,128)(2,1)S(1)}, u32[]{:S(2)}) copy-start(bf16[2,4,64,1536]{3,2,1,0:T(8,128)(2,1)S(1)} %collective-permute-done.10.refs_1_.refs_9_) | copy-start | bytes 4718596
  56.6 13.3 %collective-permute-start.15 = (bf16[1,4,64,1536]{3,2,1,0:T(8,128)(2,1)S(1)}, bf16[1,4,64,1536]{3,2,1,0:T(8,128)(2,1)S(1)}, u32[]{:S(2)}, u32[]{:S(2)}) collective-permute-start(bf16[1,4,64,1536]{3,2,1,0:T(8,128)(2,1)S(1)} %slice.40), channel_id=1, source_target_pairs={{0,32},{1,5},{2,34},{3,7},{4,36},{5,9},{6,38},{7,11},{8,40},{9,13}... | collective-permute-start | bytes 2359304 | tf_op jit(solution)/shard_map/ppermute | solution.py:54
  65.8 9.4 %collective-permute-start.17 = (bf16[6,2,192,256]{3,2,1,0:T(8,128)(2,1)S(1)}, bf16[6,2,192,256]{3,2,1,0:T(8,128)(2,1)S(1)}, u32[]{:S(2)}, u32[]{:S(2)}) collective-permute-start(bf16[6,2,192,256]{3,2,1,0:T(8,128)(2,1)S(1)} %get-tuple-element.58), channel_id=1, source_target_pairs={{0,1},{1,0},{2,3},{3,2},{4,5},{5,4},{6,7},{7,6},{8,9},{9,8},{10,11... | collective-permute-start | bytes 3538952 | tf_op jit(solution)/shard_map/ppermute | solution.py:22
  66.0 7.4 %copy-start.9 = (bf16[1,4,64,1536]{3,2,1,0:T(8,128)(2,1)}, bf16[1,4,64,1536]{3,2,1,0:T(8,128)(2,1)S(1)}, u32[]{:S(2)}) copy-start(bf16[1,4,64,1536]{3,2,1,0:T(8,128)(2,1)S(1)} %collective-permute-done.16.refs_1_.refs_12_) | copy-start | bytes 2359300
  69.9 3.5 %copy-start.10 = (bf16[1,4,64,1536]{3,2,1,0:T(8,128)(2,1)}, bf16[1,4,64,1536]{3,2,1,0:T(8,128)(2,1)S(1)}, u32[]{:S(2)}) copy-start(bf16[1,4,64,1536]{3,2,1,0:T(8,128)(2,1)S(1)} %collective-permute-done.15.refs_0_.refs_11_) | copy-start | bytes 2359300
  73.4 1.8 %collective-permute-start.18 = (bf16[2,2,192,256]{3,2,1,0:T(8,128)(2,1)S(1)}, bf16[2,2,192,256]{3,2,1,0:T(8,128)(2,1)S(1)}, u32[]{:S(2)}, u32[]{:S(2)}) collective-permute-start(bf16[2,2,192,256]{3,2,1,0:T(8,128)(2,1)S(1)} %get-tuple-element.59), channel_id=1, source_target_pairs={{0,1},{1,0},{2,3},{3,2},{4,5},{5,4},{6,7},{7,6},{8,9},{9,8},{10,11... | collective-permute-start | bytes 1179656 | tf_op jit(solution)/shard_map/ppermute | solution.py:22
  77.3 28.6 %all-to-all-start = ((bf16[16,192,256]{2,1,0:T(8,128)(2,1)}), bf16[16,192,256]{2,1,0:T(8,128)(2,1)S(1)}, u32[]{:S(2)}, u32[]{:S(2)}) async-start(bf16[16,192,256]{2,1,0:T(8,128)(2,1)} %bitcast.16), calls=%async_computation | async-start | bytes 3145728 | tf_op jit(solution)/shard_map/all_to_all | solution.py:306
  81.0 24.9 %copy-start.2 = (f32[256,1536]{1,0:T(8,128)S(1)}, f32[256,1536]{1,0:T(8,128)}, u32[]{:S(2)}) copy-start(f32[256,1536]{1,0:T(8,128)} %copy-done.1) | copy-start | bytes 4718596
  81.0 24.9 %copy-start.7 = (s32[5]{0:T(128)S(1)}, s32[5]{0:T(128)}, u32[]{:S(2)}) copy-start(s32[5]{0:T(128)} %copy-done.6) | copy-start | bytes 64
  81.1 1.8 %collective-permute-start.19 = (bf16[4,192,256]{2,1,0:T(8,128)(2,1)S(1)}, bf16[4,192,256]{2,1,0:T(8,128)(2,1)S(1)}, u32[]{:S(2)}, u32[]{:S(2)}) collective-permute-start(bf16[4,192,256]{2,1,0:T(8,128)(2,1)S(1)} %pad_maximum_fusion.1.refs_0_), channel_id=1, source_target_pairs={{0,1},{1,0},{2,3},{3,2},{4,5},{5,4},{6,7},{7,6},{8,9},{9,8},{10,11... | collective-permute-start | bytes 1179656 | tf_op jit(solution)/shard_map/ppermute | solution.py:22
  81.3 2.4 %collective-permute-start.20 = (bf16[4,192,256]{2,1,0:T(8,128)(2,1)}, bf16[4,192,256]{2,1,0:T(8,128)(2,1)S(1)}, u32[]{:S(2)}, u32[]{:S(2)}) collective-permute-start(bf16[4,192,256]{2,1,0:T(8,128)(2,1)} %collective-permute-done.12.refs_1_), channel_id=1, source_target_pairs={{0,1},{1,0},{2,3},{3,2},{4,5},{5,4},{6,7},{7,6},{8,9},{9,8},{10,11... | collective-permute-start | bytes 1179656 | tf_op jit(solution)/shard_map/ppermute | solution.py:22
  81.6 2.5 %collective-permute-start.21 = (bf16[4,192,256]{2,1,0:T(8,128)(2,1)}, bf16[4,192,256]{2,1,0:T(8,128)(2,1)S(1)}, u32[]{:S(2)}, u32[]{:S(2)}) collective-permute-start(bf16[4,192,256]{2,1,0:T(8,128)(2,1)} %collective-permute-done.13.refs_2_), channel_id=1, source_target_pairs={{0,1},{1,0},{2,3},{3,2},{4,5},{5,4},{6,7},{7,6},{8,9},{9,8},{10,11... | collective-permute-start | bytes 1179656 | tf_op jit(solution)/shard_map/ppermute | solution.py:22
  81.8 3.0 %collective-permute-start.22 = (bf16[4,192,256]{2,1,0:T(8,128)(2,1)}, bf16[4,192,256]{2,1,0:T(8,128)(2,1)S(1)}, u32[]{:S(2)}, u32[]{:S(2)}) collective-permute-start(bf16[4,192,256]{2,1,0:T(8,128)(2,1)} %collective-permute-done.14.refs_3_), channel_id=1, source_target_pairs={{0,1},{1,0},{2,3},{3,2},{4,5},{5,4},{6,7},{7,6},{8,9},{9,8},{10,11... | collective-permute-start | bytes 1179656 | tf_op jit(solution)/shard_map/ppermute | solution.py:22
  82.9 1.9 %copy-start.12 = (bf16[4,192,256]{2,1,0:T(8,128)(2,1)}, bf16[4,192,256]{2,1,0:T(8,128)(2,1)S(1)}, u32[]{:S(2)}) copy-start(bf16[4,192,256]{2,1,0:T(8,128)(2,1)S(1)} %collective-permute-done.19.refs_4_) | copy-start | bytes 1179652
  83.6 1.1 %copy-start.13 = (bf16[4,192,256]{2,1,0:T(8,128)(2,1)}, bf16[4,192,256]{2,1,0:T(8,128)(2,1)S(1)}, u32[]{:S(2)}) copy-start(bf16[4,192,256]{2,1,0:T(8,128)(2,1)S(1)} %collective-permute-done.20.refs_5_) | copy-start | bytes 1179652
  84.2 0.7 copy-start.14
  84.9 0.8 copy-start.15

commit v11 on v10

--- a/solution.py
+++ b/solution.py
@@ -256,6 +256,7 @@
         (2 * tokens * 256 * columns, 8 * tokens * columns),
     )(at, pre_act)
 
+    grad_out, parts = lax.optimization_barrier((grad_out, parts))
     other = swap_z_hi(grad_out)
     first = [[v] + [send_by_core(v, k, True) for k in (1, 2, 3)] for v in (grad_out, other)]
 

time: 109 us -> 110 us (level)
    ppermute x10, starting transfers between devices: 18.4 us -> 16.2 us  [send_by_core(): return lax.ppermute(v, ('gx', 'gy', 'gz'), pairs)]
    ppermute x13, starting transfers between devices: 15 us -> 16.7 us  [send(): return lax.ppermute(v, axis, [(i, to(i)) for i in range(count)])]
    unnamed x32 -> x38, local copies, waits for them, and re-layouts: 3.3 us -> 4.19 us
  transfers between devices with their start and end apart: 24 -> 24, of which waited for: 12 -> 13; matrix products, arithmetic and copies ran while one was open for 0% -> 0% of each run, Pallas kernels for 24% -> 22%
where the time goes in v11:
time: 110 us
  starting transfers between devices  36.7 us (33%)
  waiting for transfers between devices  34.5 us (31%)
  Pallas kernels  31.5 us (29%)
  local copies, waits for them, and re-layouts  4.44 us (4%)
  other arithmetic  1.37 us (1%)
    ppermute x10, waiting for transfers between devices, send_by_core(): return lax.ppermute(v, ('gx', 'gy', 'gz'), pairs)  21.5 us
    ppermute x13, starting transfers between devices, send(): return lax.ppermute(v, axis, [(i, to(i)) for i in range(count)])  16.7 us
    ppermute x10, starting transfers between devices, send_by_core(): return lax.ppermute(v, ('gx', 'gy', 'gz'), pairs)  16.2 us
    pallas_call x2, Pallas kernels, input_part(): call(functools.partial(input_body, len(given)), [((count, 2) + block, bf1...  12.6 us
    pallas_call x1, Pallas kernels, per_device(): call(weight_body, [((4 * rows, features), bf16)], [SMEM] + [HBM] * 13, (p...  11.8 us
    all_to_all x1, waiting for transfers between devices, per_device(): lax.all_to_all(sums.reshape((16,) + block), ('gx', 'gz'), 0, 0, tiled=Tru...  8.43 us
    ppermute x13, waiting for transfers between devices, send(): return lax.ppermute(v, axis, [(i, to(i)) for i in range(count)])  4.57 us
    unnamed x38, local copies, waits for them, and re-layouts  4.19 us
  transfers between devices with their start and end apart: 24, of which 13 were waited for; matrix products, arithmetic and copies ran while one was open for 0% of the time, Pallas kernels for 22%

profile of v11, /device:TPU:0, one launch (start us, length us, event | category | flops | bytes accessed | tf_op | source)
XLA Modules:
  0.0 109.5 jit_solution(1157201614012031046)
XLA Ops:
  0.7 0.1 stack.68.at
  0.8 1.1 %copy-done.3 = bf16[256,1536]{1,0:T(8,128)(2,1)S(1)} copy-done((bf16[256,1536]{1,0:T(8,128)(2,1)S(1)}, bf16[256,1536]{1,0:T(8,128)(2,1)}, u32[]{:S(2)}) %copy-start.3) | copy-done | bytes 786456
  1.9 1.9 %shard_map.50 = (f32[256,1536]{1,0:T(8,128)S(1)}, bf16[2,192,256]{2,1,0:T(8,128)(2,1)S(1)}, bf16[2,192,256]{2,1,0:T(8,128)(2,1)S(1)}, bf16[2,192,256]{2,1,0:T(8,128)(2,1)S(1)}, bf16[2,192,256]{2,1,0:T(8,128)(2,1)S(1)}) custom-call(s32[5]{0:T(128)S(1)} %stack.68.at, bf16[256,1536]{1,0:T(8,128)(2,1)S(1)} %copy-done.3), custom_call_target="tpu_custom_call" | custom-call | flops 201326592 | bytes 3145728 | tf_op jit(solution)/shard_map/pallas_call | solution.py:252
  3.8 1.2 %copy-done.1 = f32[256,1536]{1,0:T(8,128)} copy-done((f32[256,1536]{1,0:T(8,128)}, f32[256,1536]{1,0:T(8,128)S(1)}, u32[]{:S(2)}) %copy-start.1) | copy-done | bytes 1572888
  5.0 1.6 %collective-permute-start.7 = (bf16[2,192,256]{2,1,0:T(8,128)(2,1)S(1)}, bf16[2,192,256]{2,1,0:T(8,128)(2,1)S(1)}, u32[]{:S(2)}, u32[]{:S(2)}) collective-permute-start(bf16[2,192,256]{2,1,0:T(8,128)(2,1)S(1)} %get-tuple-element.48), channel_id=1, source_target_pairs={{0,32},{16,48},{32,64},{48,80},{64,96},{80,112},{96,0},{112,16},{1... | collective-permute-start | bytes 589832 | tf_op jit(solution)/shard_map/ppermute | solution.py:22
  6.6 2.7 %collective-permute-start.8 = (bf16[2,192,256]{2,1,0:T(8,128)(2,1)S(1)}, bf16[2,192,256]{2,1,0:T(8,128)(2,1)S(1)}, u32[]{:S(2)}, u32[]{:S(2)}) collective-permute-start(bf16[2,192,256]{2,1,0:T(8,128)(2,1)S(1)} %get-tuple-element.49), channel_id=1, source_target_pairs={{0,64},{16,80},{32,96},{48,112},{64,0},{80,16},{96,32},{112,48},{1... | collective-permute-start | bytes 589832 | tf_op jit(solution)/shard_map/ppermute | solution.py:22
  9.3 3.9 %collective-permute-start.3 = (bf16[64,1536]{1,0:T(8,128)(2,1)}, bf16[64,1536]{1,0:T(8,128)(2,1)S(1)}, u32[]{:S(2)}, u32[]{:S(2)}) collective-permute-start(bf16[64,1536]{1,0:T(8,128)(2,1)} %param.4), channel_id=1, source_target_pairs={{0,16},{16,0},{32,48},{48,32},{64,80},{80,64},{96,112},{112,96},{1... | collective-permute-start | bytes 589832 | tf_op jit(solution)/shard_map/ppermute | solution.py:22
  13.2 1.4 %collective-permute-start.9 = (bf16[2,192,256]{2,1,0:T(8,128)(2,1)S(1)}, bf16[2,192,256]{2,1,0:T(8,128)(2,1)S(1)}, u32[]{:S(2)}, u32[]{:S(2)}) collective-permute-start(bf16[2,192,256]{2,1,0:T(8,128)(2,1)S(1)} %get-tuple-element.50), channel_id=1, source_target_pairs={{0,96},{16,112},{32,0},{48,16},{64,32},{80,48},{96,64},{112,80},{1... | collective-permute-start | bytes 589832 | tf_op jit(solution)/shard_map/ppermute | solution.py:22
  14.6 3.0 %collective-permute-start.2 = (bf16[64,1536]{1,0:T(8,128)(2,1)}, bf16[64,1536]{1,0:T(8,128)(2,1)S(1)}, u32[]{:S(2)}, u32[]{:S(2)}) collective-permute-start(bf16[64,1536]{1,0:T(8,128)(2,1)} %param.4), channel_id=1, source_target_pairs={{0,12},{1,97},{2,14},{3,99},{4,0},{5,101},{6,2},{7,103},{8,4},{9,1... | collective-permute-start | bytes 589832 | tf_op jit(solution)/shard_map/ppermute | solution.py:54
  17.6 0.0 collective-permute-done.7
  17.6 0.6 collective-permute-start.1
  18.3 0.3 collective-permute-done.8
  18.5 1.6 %collective-permute-start = (bf16[64,1536]{1,0:T(8,128)(2,1)}, bf16[64,1536]{1,0:T(8,128)(2,1)S(1)}, u32[]{:S(2)}, u32[]{:S(2)}) collective-permute-start(bf16[64,1536]{1,0:T(8,128)(2,1)} %param.4), channel_id=1, source_target_pairs={{0,4},{1,33},{2,6},{3,35},{4,8},{5,37},{6,10},{7,39},{8,12},{9,41}... | collective-permute-start | bytes 589832 | tf_op jit(solution)/shard_map/ppermute | solution.py:54
  20.1 0.0 collective-permute-done.3
  20.1 1.7 %collective-permute-start.6 = (bf16[64,1536]{1,0:T(8,128)(2,1)S(1)}, bf16[64,1536]{1,0:T(8,128)(2,1)S(1)}, u32[]{:S(2)}, u32[]{:S(2)}) collective-permute-start(bf16[64,1536]{1,0:T(8,128)(2,1)S(1)} %collective-permute-done.3), channel_id=1, source_target_pairs={{0,12},{1,97},{2,14},{3,99},{4,0},{5,101},{6,2},{7,103},{8,4},{9,1... | collective-permute-start | bytes 589832 | tf_op jit(solution)/shard_map/ppermute | solution.py:54
  21.8 0.0 collective-permute-done.9
  21.8 2.4 %collective-permute-start.5 = (bf16[64,1536]{1,0:T(8,128)(2,1)S(1)}, bf16[64,1536]{1,0:T(8,128)(2,1)S(1)}, u32[]{:S(2)}, u32[]{:S(2)}) collective-permute-start(bf16[64,1536]{1,0:T(8,128)(2,1)S(1)} %collective-permute-done.3), channel_id=1, source_target_pairs={{0,8},{1,65},{2,10},{3,67},{4,12},{5,69},{6,14},{7,71},{8,0},{9,73... | collective-permute-start | bytes 589832 | tf_op jit(solution)/shard_map/ppermute | solution.py:54
  24.2 0.0 collective-permute-done.2
  24.2 0.7 collective-permute-start.4
  24.9 0.2 collective-permute-done.1
  25.1 2.0 %collective-permute-done = bf16[64,1536]{1,0:T(8,128)(2,1)S(1)} collective-permute-done((bf16[64,1536]{1,0:T(8,128)(2,1)}, bf16[64,1536]{1,0:T(8,128)(2,1)S(1)}, u32[]{:S(2)}, u32[]{:S(2)}) %collective-permute-start) | collective-permute-done | bytes 196640 | tf_op jit(solution)/shard_map/ppermute | solution.py:54
  27.1 2.1 %collective-permute-done.5 = bf16[64,1536]{1,0:T(8,128)(2,1)S(1)} collective-permute-done((bf16[64,1536]{1,0:T(8,128)(2,1)S(1)}, bf16[64,1536]{1,0:T(8,128)(2,1)S(1)}, u32[]{:S(2)}, u32[]{:S(2)}) %collective-permute-start.5) | collective-permute-done | bytes 196640 | tf_op jit(solution)/shard_map/ppermute | solution.py:54
  29.3 2.1 %collective-permute-done.4 = bf16[64,1536]{1,0:T(8,128)(2,1)S(1)} collective-permute-done((bf16[64,1536]{1,0:T(8,128)(2,1)S(1)}, bf16[64,1536]{1,0:T(8,128)(2,1)S(1)}, u32[]{:S(2)}, u32[]{:S(2)}) %collective-permute-start.4) | collective-permute-done | bytes 196640 | tf_op jit(solution)/shard_map/ppermute | solution.py:54
  31.3 1.1 %maximum_bitcast_fusion = (bf16[1,4,64,1536]{3,2,1,0:T(8,128)(2,1)S(1)}, bf16[1,4,64,1536]{3,2,1,0:T(8,128)(2,1)S(1)}) fusion(bf16[1,64,1536]{2,1,0:T(8,128)(2,1)S(1)} %bitcast.26, bf16[1,64,1536]{2,1,0:T(8,128)(2,1)S(1)} %bitcast.27, bf16[1,64,1536]{2,1,0:T(8,128)(2,1)S(1)} %bitcast.28, bf16[1,64,1536]{2,1,0:T(8,128)(2,1)} %bitcast.24, ...), kind=kLoop, calls=%fused_computation.1 | loop fusion | flops 2359296 | bytes 3145728 | tf_op jit(solution)/shard_map/stack | solution.py:265
  32.5 0.1 pad_maximum_fusion.refs_0_.refs_8_
  32.6 2.5 %collective-permute-start.11 = (bf16[2,4,64,1536]{3,2,1,0:T(8,128)(2,1)S(1)}, bf16[2,4,64,1536]{3,2,1,0:T(8,128)(2,1)S(1)}, u32[]{:S(2)}, u32[]{:S(2)}) collective-permute-start(bf16[2,4,64,1536]{3,2,1,0:T(8,128)(2,1)S(1)} %pad_maximum_fusion.refs_0_.refs_8_), channel_id=1, source_target_pairs={{0,96},{1,13},{2,98},{3,15},{4,100},{5,1},{6,102},{7,3},{8,104},{9... | collective-permute-start | bytes 4718600 | tf_op jit(solution)/shard_map/ppermute | solution.py:54
  35.2 0.1 pad_maximum_fusion.1.refs_0_
  35.2 2.1 %collective-permute-start.13 = (bf16[4,192,256]{2,1,0:T(8,128)(2,1)S(1)}, bf16[4,192,256]{2,1,0:T(8,128)(2,1)S(1)}, u32[]{:S(2)}, u32[]{:S(2)}) collective-permute-start(bf16[4,192,256]{2,1,0:T(8,128)(2,1)S(1)} %pad_maximum_fusion.1.refs_0_), channel_id=1, source_target_pairs={{0,2},{1,3},{2,0},{3,1},{4,6},{5,7},{6,4},{7,5},{8,10},{9,11},{10,... | collective-permute-start | bytes 1179656 | tf_op jit(solution)/shard_map/ppermute | solution.py:22
  37.3 0.1 pad_maximum_fusion.2
  37.4 0.0 copy-start.8
  37.4 2.6 %collective-permute-start.14 = (bf16[4,192,256]{2,1,0:T(8,128)(2,1)S(1)}, bf16[4,192,256]{2,1,0:T(8,128)(2,1)S(1)}, u32[]{:S(2)}, u32[]{:S(2)}) collective-permute-start(bf16[4,192,256]{2,1,0:T(8,128)(2,1)S(1)} %pad_maximum_fusion.2), channel_id=1, source_target_pairs={{0,18},{1,19},{2,16},{3,17},{16,2},{17,3},{18,0},{19,1},{32,50},{3... | collective-permute-start | bytes 1179656 | tf_op jit(solution)/shard_map/ppermute | solution.py:22
  40.0 1.1 %collective-permute-start.12 = (bf16[4,192,256]{2,1,0:T(8,128)(2,1)S(1)}, bf16[4,192,256]{2,1,0:T(8,128)(2,1)S(1)}, u32[]{:S(2)}, u32[]{:S(2)}) collective-permute-start(bf16[4,192,256]{2,1,0:T(8,128)(2,1)S(1)} %pad_maximum_fusion.2), channel_id=1, source_target_pairs={{0,16},{16,0},{32,48},{48,32},{64,80},{80,64},{96,112},{112,96},{1... | collective-permute-start | bytes 1179656 | tf_op jit(solution)/shard_map/ppermute | solution.py:22
  41.2 12.0 %collective-permute-done.11.refs_2_.refs_10_ = bf16[2,4,64,1536]{3,2,1,0:T(8,128)(2,1)S(1)} collective-permute-done((bf16[2,4,64,1536]{3,2,1,0:T(8,128)(2,1)S(1)}, bf16[2,4,64,1536]{3,2,1,0:T(8,128)(2,1)S(1)}, u32[]{:S(2)}, u32[]{:S(2)}) %collective-permute-start.11) | collective-permute-done | bytes 1572896 | tf_op jit(solution)/shard_map/ppermute | solution.py:54
  53.1 0.1 slice.41
  53.2 3.7 %collective-permute-start.16 = (bf16[1,4,64,1536]{3,2,1,0:T(8,128)(2,1)S(1)}, bf16[1,4,64,1536]{3,2,1,0:T(8,128)(2,1)S(1)}, u32[]{:S(2)}, u32[]{:S(2)}) collective-permute-start(bf16[1,4,64,1536]{3,2,1,0:T(8,128)(2,1)S(1)} %slice.41), channel_id=1, source_target_pairs={{0,96},{1,13},{2,98},{3,15},{4,100},{5,1},{6,102},{7,3},{8,104},{9... | collective-permute-start | bytes 2359304 | tf_op jit(solution)/shard_map/ppermute | solution.py:54
  56.9 0.0 collective-permute-done.14.refs_3_
  56.9 0.0 collective-permute-done.12.refs_1_
  56.9 0.1 slice.40
  57.0 0.1 collective-permute-start.15
  57.1 0.5 copy-done.12
  57.6 0.2 copy-done.13
  57.8 0.2 copy-done.14
  58.0 9.1 %shard_map.51 = (bf16[6,2,192,256]{3,2,1,0:T(8,128)(2,1)S(1)}, bf16[6,2,192,256]{3,2,1,0:T(8,128)(2,1)S(1)}) custom-call(s32[5]{0:T(128)S(1)} %stack.68.at, bf16[768,1536]{1,0:T(8,128)(2,1)S(1)} %bitcast.22, bf16[2,4,64,1536]{3,2,1,0:T(8,128)(2,1)S(1)} %pad_maximum_fusion.refs_0_.refs_8_, ...), custom_call_target="tpu_custom_call" | custom-call | flops 3623878656 | bytes 9437184 | tf_op jit(solution)/shard_map/pallas_call | solution.py:275
  67.0 0.1 collective-permute-start.17
  67.1 3.1 %collective-permute-done.15.refs_0_.refs_11_ = bf16[1,4,64,1536]{3,2,1,0:T(8,128)(2,1)S(1)} collective-permute-done((bf16[1,4,64,1536]{3,2,1,0:T(8,128)(2,1)S(1)}, bf16[1,4,64,1536]{3,2,1,0:T(8,128)(2,1)S(1)}, u32[]{:S(2)}, u32[]{:S(2)}) %collective-permute-start.15) | collective-permute-done | bytes 786464 | tf_op jit(solution)/shard_map/ppermute | solution.py:54
  70.3 3.5 %shard_map.52 = (bf16[2,2,192,256]{3,2,1,0:T(8,128)(2,1)S(1)}, bf16[2,2,192,256]{3,2,1,0:T(8,128)(2,1)S(1)}) custom-call(s32[5]{0:T(128)S(1)} %stack.68.at, bf16[768,1536]{1,0:T(8,128)(2,1)S(1)} %bitcast.23, bf16[1,4,64,1536]{3,2,1,0:T(8,128)(2,1)S(1)} %collective-permute-done.15.refs_0_.refs_11_, ...), custom_call_target="tpu_custom_call" | custom-call | flops 1207959552 | bytes 4718592 | tf_op jit(solution)/shard_map/pallas_call | solution.py:275
  73.8 0.1 collective-permute-start.18
  73.9 1.7 %collective-permute-done.18.other2 = bf16[2,2,192,256]{3,2,1,0:T(8,128)(2,1)S(1)} collective-permute-done((bf16[2,2,192,256]{3,2,1,0:T(8,128)(2,1)S(1)}, bf16[2,2,192,256]{3,2,1,0:T(8,128)(2,1)S(1)}, u32[]{:S(2)}, u32[]{:S(2)}) %collective-permute-start.18) | collective-permute-done | bytes 393248 | tf_op jit(solution)/shard_map/ppermute | solution.py:22
  75.6 0.0 collective-permute-done.17.other
  75.6 2.1 %shard_map.53 = bf16[8,2,192,256]{3,2,1,0:T(8,128)(2,1)} custom-call(s32[5]{0:T(128)S(1)} %stack.68.at, bf16[6,2,192,256]{3,2,1,0:T(8,128)(2,1)S(1)} %get-tuple-element.66.mine, bf16[2,2,192,256]{3,2,1,0:T(8,128)(2,1)S(1)} %get-tuple-element.67.mine2, bf16[6,2,192,256]{3,2,1,0:T(8,128)(2,1)S(1)} %collective-permute-done.17.other, ...), custom_call_target="tpu_custom_call" | custom-call | flops 1572864 | bytes 4718592 | tf_op jit(solution)/shard_map/pallas_call | solution.py:297
  77.7 3.7 %all-to-all-start = ((bf16[16,192,256]{2,1,0:T(8,128)(2,1)}), bf16[16,192,256]{2,1,0:T(8,128)(2,1)S(1)}, u32[]{:S(2)}, u32[]{:S(2)}) async-start(bf16[16,192,256]{2,1,0:T(8,128)(2,1)} %bitcast.16), calls=%async_computation | async-start | bytes 3145728 | tf_op jit(solution)/shard_map/all_to_all | solution.py:307
  81.4 0.2 collective-permute-start.19
  81.7 0.4 collective-permute-start.20
  82.0 0.1 collective-permute-start.21
  82.2 0.4 collective-permute-start.22
  82.5 0.7 collective-permute-done.19.refs_4_
  83.2 0.8 collective-permute-done.20.refs_5_
  84.0 0.6 collective-permute-done.21.refs_6_
  84.6 0.6 collective-permute-done.22.refs_7_
  85.1 0.2 copy-done.17
  85.3 0.8 copy-done.18
  86.1 11.8 %shard_map.54 = bf16[768,1536]{1,0:T(8,128)(2,1)} custom-call(s32[5]{0:T(128)} %copy-done.6, bf16[4,192,256]{2,1,0:T(8,128)(2,1)} %copy-done.11, bf16[4,192,256]{2,1,0:T(8,128)(2,1)} %copy-done.14, bf16[4,192,256]{2,1,0:T(8,128)(2,1)} %copy-done.12, bf16[4,192,256]{2,1,0:T(8,128)(2,1)} %copy-done.13, bf16[4,192,256]{2,1,0:T(8,128)(2,1)} %copy-done.15, ...), custom_call_target="tpu_custom_call" | custom-call | flops 4831838208 | bytes 11010048 | tf_op jit(solution)/shard_map/pallas_call | solution.py:312
  97.9 8.4 %all-to-all-done = bf16[16,192,256]{2,1,0:T(8,128)(2,1)S(1)} async-done(((bf16[16,192,256]{2,1,0:T(8,128)(2,1)}), bf16[16,192,256]{2,1,0:T(8,128)(2,1)S(1)}, u32[]{:S(2)}, u32[]{:S(2)}) %all-to-all-start) | async-done | bytes 1572896 | tf_op jit(solution)/shard_map/all_to_all | solution.py:307
  106.3 3.2 %shard_map.55 = bf16[256,1536]{1,0:T(8,128)(2,1)} custom-call(s32[5]{0:T(128)S(1)} %copy-done.7, f32[256,1536]{1,0:T(8,128)S(1)} %copy-done.2, bf16[8,2,192,256]{3,2,1,0:T(8,128)(2,1)S(1)} %bitcast.21), custom_call_target="tpu_custom_call" | custom-call | flops 201326592 | bytes 3145728 | tf_op jit(solution)/shard_map/pallas_call | solution.py:326
  (37 shorter events, 0.1 us)
Async XLA Ops:
  0.7 1.1 %copy-start.3 = (bf16[256,1536]{1,0:T(8,128)(2,1)S(1)}, bf16[256,1536]{1,0:T(8,128)(2,1)}, u32[]{:S(2)}) copy-start(bf16[256,1536]{1,0:T(8,128)(2,1)} %pre.1) | copy-start | bytes 2359300
  1.9 73.7 %copy-start.6 = (s32[5]{0:T(128)}, s32[5]{0:T(128)S(1)}, u32[]{:S(2)}) copy-start(s32[5]{0:T(128)S(1)} %stack.68.at) | copy-start | bytes 64
  3.8 1.2 %copy-start.1 = (f32[256,1536]{1,0:T(8,128)}, f32[256,1536]{1,0:T(8,128)S(1)}, u32[]{:S(2)}) copy-start(f32[256,1536]{1,0:T(8,128)S(1)} %get-tuple-element.41.slope) | copy-start | bytes 4718596
  5.0 12.6 %collective-permute-start.7 = (bf16[2,192,256]{2,1,0:T(8,128)(2,1)S(1)}, bf16[2,192,256]{2,1,0:T(8,128)(2,1)S(1)}, u32[]{:S(2)}, u32[]{:S(2)}) collective-permute-start(bf16[2,192,256]{2,1,0:T(8,128)(2,1)S(1)} %get-tuple-element.48), channel_id=1, source_target_pairs={{0,32},{16,48},{32,64},{48,80},{64,96},{80,112},{96,0},{112,16},{1... | collective-permute-start | bytes 589832 | tf_op jit(solution)/shard_map/ppermute | solution.py:22
  6.6 11.9 %collective-permute-start.8 = (bf16[2,192,256]{2,1,0:T(8,128)(2,1)S(1)}, bf16[2,192,256]{2,1,0:T(8,128)(2,1)S(1)}, u32[]{:S(2)}, u32[]{:S(2)}) collective-permute-start(bf16[2,192,256]{2,1,0:T(8,128)(2,1)S(1)} %get-tuple-element.49), channel_id=1, source_target_pairs={{0,64},{16,80},{32,96},{48,112},{64,0},{80,16},{96,32},{112,48},{1... | collective-permute-start | bytes 589832 | tf_op jit(solution)/shard_map/ppermute | solution.py:22
  9.3 10.8 %collective-permute-start.3 = (bf16[64,1536]{1,0:T(8,128)(2,1)}, bf16[64,1536]{1,0:T(8,128)(2,1)S(1)}, u32[]{:S(2)}, u32[]{:S(2)}) collective-permute-start(bf16[64,1536]{1,0:T(8,128)(2,1)} %param.4), channel_id=1, source_target_pairs={{0,16},{16,0},{32,48},{48,32},{64,80},{80,64},{96,112},{112,96},{1... | collective-permute-start | bytes 589832 | tf_op jit(solution)/shard_map/ppermute | solution.py:22
  13.2 8.6 %collective-permute-start.9 = (bf16[2,192,256]{2,1,0:T(8,128)(2,1)S(1)}, bf16[2,192,256]{2,1,0:T(8,128)(2,1)S(1)}, u32[]{:S(2)}, u32[]{:S(2)}) collective-permute-start(bf16[2,192,256]{2,1,0:T(8,128)(2,1)S(1)} %get-tuple-element.50), channel_id=1, source_target_pairs={{0,96},{16,112},{32,0},{48,16},{64,32},{80,48},{96,64},{112,80},{1... | collective-permute-start | bytes 589832 | tf_op jit(solution)/shard_map/ppermute | solution.py:22
  14.6 9.6 %collective-permute-start.2 = (bf16[64,1536]{1,0:T(8,128)(2,1)}, bf16[64,1536]{1,0:T(8,128)(2,1)S(1)}, u32[]{:S(2)}, u32[]{:S(2)}) collective-permute-start(bf16[64,1536]{1,0:T(8,128)(2,1)} %param.4), channel_id=1, source_target_pairs={{0,12},{1,97},{2,14},{3,99},{4,0},{5,101},{6,2},{7,103},{8,4},{9,1... | collective-permute-start | bytes 589832 | tf_op jit(solution)/shard_map/ppermute | solution.py:54
  17.6 7.5 %collective-permute-start.1 = (bf16[64,1536]{1,0:T(8,128)(2,1)}, bf16[64,1536]{1,0:T(8,128)(2,1)S(1)}, u32[]{:S(2)}, u32[]{:S(2)}) collective-permute-start(bf16[64,1536]{1,0:T(8,128)(2,1)} %param.4), channel_id=1, source_target_pairs={{0,8},{1,65},{2,10},{3,67},{4,12},{5,69},{6,14},{7,71},{8,0},{9,73... | collective-permute-start | bytes 589832 | tf_op jit(solution)/shard_map/ppermute | solution.py:54
  18.5 8.6 %collective-permute-start = (bf16[64,1536]{1,0:T(8,128)(2,1)}, bf16[64,1536]{1,0:T(8,128)(2,1)S(1)}, u32[]{:S(2)}, u32[]{:S(2)}) collective-permute-start(bf16[64,1536]{1,0:T(8,128)(2,1)} %param.4), channel_id=1, source_target_pairs={{0,4},{1,33},{2,6},{3,35},{4,8},{5,37},{6,10},{7,39},{8,12},{9,41}... | collective-permute-start | bytes 589832 | tf_op jit(solution)/shard_map/ppermute | solution.py:54
  20.1 7.0 %collective-permute-start.6 = (bf16[64,1536]{1,0:T(8,128)(2,1)S(1)}, bf16[64,1536]{1,0:T(8,128)(2,1)S(1)}, u32[]{:S(2)}, u32[]{:S(2)}) collective-permute-start(bf16[64,1536]{1,0:T(8,128)(2,1)S(1)} %collective-permute-done.3), channel_id=1, source_target_pairs={{0,12},{1,97},{2,14},{3,99},{4,0},{5,101},{6,2},{7,103},{8,4},{9,1... | collective-permute-start | bytes 589832 | tf_op jit(solution)/shard_map/ppermute | solution.py:54
  21.8 7.5 %collective-permute-start.5 = (bf16[64,1536]{1,0:T(8,128)(2,1)S(1)}, bf16[64,1536]{1,0:T(8,128)(2,1)S(1)}, u32[]{:S(2)}, u32[]{:S(2)}) collective-permute-start(bf16[64,1536]{1,0:T(8,128)(2,1)S(1)} %collective-permute-done.3), channel_id=1, source_target_pairs={{0,8},{1,65},{2,10},{3,67},{4,12},{5,69},{6,14},{7,71},{8,0},{9,73... | collective-permute-start | bytes 589832 | tf_op jit(solution)/shard_map/ppermute | solution.py:54
  24.2 7.1 %collective-permute-start.4 = (bf16[64,1536]{1,0:T(8,128)(2,1)S(1)}, bf16[64,1536]{1,0:T(8,128)(2,1)S(1)}, u32[]{:S(2)}, u32[]{:S(2)}) collective-permute-start(bf16[64,1536]{1,0:T(8,128)(2,1)S(1)} %collective-permute-done.3), channel_id=1, source_target_pairs={{0,4},{1,33},{2,6},{3,35},{4,8},{5,37},{6,10},{7,39},{8,12},{9,41}... | collective-permute-start | bytes 589832 | tf_op jit(solution)/shard_map/ppermute | solution.py:54
  32.6 25.3 %copy-start = (bf16[2,4,64,1536]{3,2,1,0:T(8,128)(2,1)}, bf16[2,4,64,1536]{3,2,1,0:T(8,128)(2,1)S(1)}, u32[]{:S(2)}) copy-start(bf16[2,4,64,1536]{3,2,1,0:T(8,128)(2,1)S(1)} %pad_maximum_fusion.refs_0_.refs_8_) | copy-start | bytes 4718596
  32.6 20.5 %collective-permute-start.11 = (bf16[2,4,64,1536]{3,2,1,0:T(8,128)(2,1)S(1)}, bf16[2,4,64,1536]{3,2,1,0:T(8,128)(2,1)S(1)}, u32[]{:S(2)}, u32[]{:S(2)}) collective-permute-start(bf16[2,4,64,1536]{3,2,1,0:T(8,128)(2,1)S(1)} %pad_maximum_fusion.refs_0_.refs_8_), channel_id=1, source_target_pairs={{0,96},{1,13},{2,98},{3,15},{4,100},{5,1},{6,102},{7,3},{8,104},{9... | collective-permute-start | bytes 4718600 | tf_op jit(solution)/shard_map/ppermute | solution.py:54
  35.1 21.8 %collective-permute-start.10 = (bf16[2,4,64,1536]{3,2,1,0:T(8,128)(2,1)S(1)}, bf16[2,4,64,1536]{3,2,1,0:T(8,128)(2,1)S(1)}, u32[]{:S(2)}, u32[]{:S(2)}) collective-permute-start(bf16[2,4,64,1536]{3,2,1,0:T(8,128)(2,1)S(1)} %pad_maximum_fusion.refs_0_.refs_8_), channel_id=1, source_target_pairs={{0,32},{1,5},{2,34},{3,7},{4,36},{5,9},{6,38},{7,11},{8,40},{9,13}... | collective-permute-start | bytes 4718600 | tf_op jit(solution)/shard_map/ppermute | solution.py:54
  35.2 46.2 %copy-start.11 = (bf16[4,192,256]{2,1,0:T(8,128)(2,1)}, bf16[4,192,256]{2,1,0:T(8,128)(2,1)S(1)}, u32[]{:S(2)}) copy-start(bf16[4,192,256]{2,1,0:T(8,128)(2,1)S(1)} %pad_maximum_fusion.1.refs_0_) | copy-start | bytes 1179652
  35.2 21.6 %collective-permute-start.13 = (bf16[4,192,256]{2,1,0:T(8,128)(2,1)S(1)}, bf16[4,192,256]{2,1,0:T(8,128)(2,1)S(1)}, u32[]{:S(2)}, u32[]{:S(2)}) collective-permute-start(bf16[4,192,256]{2,1,0:T(8,128)(2,1)S(1)} %pad_maximum_fusion.1.refs_0_), channel_id=1, source_target_pairs={{0,2},{1,3},{2,0},{3,1},{4,6},{5,7},{6,4},{7,5},{8,10},{9,11},{10,... | collective-permute-start | bytes 1179656 | tf_op jit(solution)/shard_map/ppermute | solution.py:22
  37.4 20.6 %copy-start.8 = (bf16[768,1,1536]{2,0,1:T(8,128)(2,1)S(1)}, bf16[768,1,1536]{2,0,1:T(8,128)(2,1)}, u32[]{:S(2)}) copy-start(bf16[768,1,1536]{2,0,1:T(8,128)(2,1)} %param.5) | copy-start | bytes 7077892
  37.4 19.5 %collective-permute-start.14 = (bf16[4,192,256]{2,1,0:T(8,128)(2,1)S(1)}, bf16[4,192,256]{2,1,0:T(8,128)(2,1)S(1)}, u32[]{:S(2)}, u32[]{:S(2)}) collective-permute-start(bf16[4,192,256]{2,1,0:T(8,128)(2,1)S(1)} %pad_maximum_fusion.2), channel_id=1, source_target_pairs={{0,18},{1,19},{2,16},{3,17},{16,2},{17,3},{18,0},{19,1},{32,50},{3... | collective-permute-start | bytes 1179656 | tf_op jit(solution)/shard_map/ppermute | solution.py:22
  40.0 16.9 %collective-permute-start.12 = (bf16[4,192,256]{2,1,0:T(8,128)(2,1)S(1)}, bf16[4,192,256]{2,1,0:T(8,128)(2,1)S(1)}, u32[]{:S(2)}, u32[]{:S(2)}) collective-permute-start(bf16[4,192,256]{2,1,0:T(8,128)(2,1)S(1)} %pad_maximum_fusion.2), channel_id=1, source_target_pairs={{0,16},{16,0},{32,48},{48,32},{64,80},{80,64},{96,112},{112,96},{1... | collective-permute-start | bytes 1179656 | tf_op jit(solution)/shard_map/ppermute | solution.py:22
  53.1 4.8 %copy-start.4 = (bf16[2,4,64,1536]{3,2,1,0:T(8,128)(2,1)}, bf16[2,4,64,1536]{3,2,1,0:T(8,128)(2,1)S(1)}, u32[]{:S(2)}) copy-start(bf16[2,4,64,1536]{3,2,1,0:T(8,128)(2,1)S(1)} %collective-permute-done.11.refs_2_.refs_10_) | copy-start | bytes 4718596
  53.2 13.9 %collective-permute-start.16 = (bf16[1,4,64,1536]{3,2,1,0:T(8,128)(2,1)S(1)}, bf16[1,4,64,1536]{3,2,1,0:T(8,128)(2,1)S(1)}, u32[]{:S(2)}, u32[]{:S(2)}) collective-permute-start(bf16[1,4,64,1536]{3,2,1,0:T(8,128)(2,1)S(1)} %slice.41), channel_id=1, source_target_pairs={{0,96},{1,13},{2,98},{3,15},{4,100},{5,1},{6,102},{7,3},{8,104},{9... | collective-permute-start | bytes 2359304 | tf_op jit(solution)/shard_map/ppermute | solution.py:54
  56.9 0.7 copy-start.12
  56.9 0.9 copy-start.13
  56.9 1.1 copy-start.14
  56.9 10.1 %copy-start.5 = (bf16[2,4,64,1536]{3,2,1,0:T(8,128)(2,1)}, bf16[2,4,64,1536]{3,2,1,0:T(8,128)(2,1)S(1)}, u32[]{:S(2)}) copy-start(bf16[2,4,64,1536]{3,2,1,0:T(8,128)(2,1)S(1)} %collective-permute-done.10.refs_1_.refs_9_) | copy-start | bytes 4718596
  57.0 13.3 %collective-permute-start.15 = (bf16[1,4,64,1536]{3,2,1,0:T(8,128)(2,1)S(1)}, bf16[1,4,64,1536]{3,2,1,0:T(8,128)(2,1)S(1)}, u32[]{:S(2)}, u32[]{:S(2)}) collective-permute-start(bf16[1,4,64,1536]{3,2,1,0:T(8,128)(2,1)S(1)} %slice.40), channel_id=1, source_target_pairs={{0,32},{1,5},{2,34},{3,7},{4,36},{5,9},{6,38},{7,11},{8,40},{9,13}... | collective-permute-start | bytes 2359304 | tf_op jit(solution)/shard_map/ppermute | solution.py:54
  67.0 8.6 %collective-permute-start.17 = (bf16[6,2,192,256]{3,2,1,0:T(8,128)(2,1)S(1)}, bf16[6,2,192,256]{3,2,1,0:T(8,128)(2,1)S(1)}, u32[]{:S(2)}, u32[]{:S(2)}) collective-permute-start(bf16[6,2,192,256]{3,2,1,0:T(8,128)(2,1)S(1)} %get-tuple-element.68), channel_id=1, source_target_pairs={{0,1},{1,0},{2,3},{3,2},{4,5},{5,4},{6,7},{7,6},{8,9},{9,8},{10,11... | collective-permute-start | bytes 3538952 | tf_op jit(solution)/shard_map/ppermute | solution.py:22
  67.1 6.6 %copy-start.9 = (bf16[1,4,64,1536]{3,2,1,0:T(8,128)(2,1)}, bf16[1,4,64,1536]{3,2,1,0:T(8,128)(2,1)S(1)}, u32[]{:S(2)}) copy-start(bf16[1,4,64,1536]{3,2,1,0:T(8,128)(2,1)S(1)} %collective-permute-done.16.refs_1_.refs_12_) | copy-start | bytes 2359300
  70.3 3.5 %copy-start.10 = (bf16[1,4,64,1536]{3,2,1,0:T(8,128)(2,1)}, bf16[1,4,64,1536]{3,2,1,0:T(8,128)(2,1)S(1)}, u32[]{:S(2)}) copy-start(bf16[1,4,64,1536]{3,2,1,0:T(8,128)(2,1)S(1)} %collective-permute-done.15.refs_0_.refs_11_) | copy-start | bytes 2359300
  73.8 1.8 %collective-permute-start.18 = (bf16[2,2,192,256]{3,2,1,0:T(8,128)(2,1)S(1)}, bf16[2,2,192,256]{3,2,1,0:T(8,128)(2,1)S(1)}, u32[]{:S(2)}, u32[]{:S(2)}) collective-permute-start(bf16[2,2,192,256]{3,2,1,0:T(8,128)(2,1)S(1)} %get-tuple-element.69), channel_id=1, source_target_pairs={{0,1},{1,0},{2,3},{3,2},{4,5},{5,4},{6,7},{7,6},{8,9},{9,8},{10,11... | collective-permute-start | bytes 1179656 | tf_op jit(solution)/shard_map/ppermute | solution.py:22
  77.7 28.6 %all-to-all-start = ((bf16[16,192,256]{2,1,0:T(8,128)(2,1)}), bf16[16,192,256]{2,1,0:T(8,128)(2,1)S(1)}, u32[]{:S(2)}, u32[]{:S(2)}) async-start(bf16[16,192,256]{2,1,0:T(8,128)(2,1)} %bitcast.16), calls=%async_computation | async-start | bytes 3145728 | tf_op jit(solution)/shard_map/all_to_all | solution.py:307
  81.4 24.9 %copy-start.2 = (f32[256,1536]{1,0:T(8,128)S(1)}, f32[256,1536]{1,0:T(8,128)}, u32[]{:S(2)}) copy-start(f32[256,1536]{1,0:T(8,128)} %copy-done.1) | copy-start | bytes 4718596
  81.4 24.9 %copy-start.7 = (s32[5]{0:T(128)S(1)}, s32[5]{0:T(128)}, u32[]{:S(2)}) copy-start(s32[5]{0:T(128)} %copy-done.6) | copy-start | bytes 64
  81.4 1.8 %collective-permute-start.19 = (bf16[4,192,256]{2,1,0:T(8,128)(2,1)S(1)}, bf16[4,192,256]{2,1,0:T(8,128)(2,1)S(1)}, u32[]{:S(2)}, u32[]{:S(2)}) collective-permute-start(bf16[4,192,256]{2,1,0:T(8,128)(2,1)S(1)} %pad_maximum_fusion.1.refs_0_), channel_id=1, source_target_pairs={{0,1},{1,0},{2,3},{3,2},{4,5},{5,4},{6,7},{7,6},{8,9},{9,8},{10,11... | collective-permute-start | bytes 1179656 | tf_op jit(solution)/shard_map/ppermute | solution.py:22
  81.7 2.4 %collective-permute-start.20 = (bf16[4,192,256]{2,1,0:T(8,128)(2,1)}, bf16[4,192,256]{2,1,0:T(8,128)(2,1)S(1)}, u32[]{:S(2)}, u32[]{:S(2)}) collective-permute-start(bf16[4,192,256]{2,1,0:T(8,128)(2,1)} %copy-done.14), channel_id=1, source_target_pairs={{0,1},{1,0},{2,3},{3,2},{4,5},{5,4},{6,7},{7,6},{8,9},{9,8},{10,11... | collective-permute-start | bytes 1179656 | tf_op jit(solution)/shard_map/ppermute | solution.py:22
  82.0 2.5 %collective-permute-start.21 = (bf16[4,192,256]{2,1,0:T(8,128)(2,1)}, bf16[4,192,256]{2,1,0:T(8,128)(2,1)S(1)}, u32[]{:S(2)}, u32[]{:S(2)}) collective-permute-start(bf16[4,192,256]{2,1,0:T(8,128)(2,1)} %copy-done.12), channel_id=1, source_target_pairs={{0,1},{1,0},{2,3},{3,2},{4,5},{5,4},{6,7},{7,6},{8,9},{9,8},{10,11... | collective-permute-start | bytes 1179656 | tf_op jit(solution)/shard_map/ppermute | solution.py:22
  82.2 3.0 %collective-permute-start.22 = (bf16[4,192,256]{2,1,0:T(8,128)(2,1)}, bf16[4,192,256]{2,1,0:T(8,128)(2,1)S(1)}, u32[]{:S(2)}, u32[]{:S(2)}) collective-permute-start(bf16[4,192,256]{2,1,0:T(8,128)(2,1)} %copy-done.13), channel_id=1, source_target_pairs={{0,1},{1,0},{2,3},{3,2},{4,5},{5,4},{6,7},{7,6},{8,9},{9,8},{10,11... | collective-permute-start | bytes 1179656 | tf_op jit(solution)/shard_map/ppermute | solution.py:22
  83.2 1.9 %copy-start.15 = (bf16[4,192,256]{2,1,0:T(8,128)(2,1)}, bf16[4,192,256]{2,1,0:T(8,128)(2,1)S(1)}, u32[]{:S(2)}) copy-start(bf16[4,192,256]{2,1,0:T(8,128)(2,1)S(1)} %collective-permute-done.19.refs_4_) | copy-start | bytes 1179652
  84.0 1.1 %copy-start.16 = (bf16[4,192,256]{2,1,0:T(8,128)(2,1)}, bf16[4,192,256]{2,1,0:T(8,128)(2,1)S(1)}, u32[]{:S(2)}) copy-start(bf16[4,192,256]{2,1,0:T(8,128)(2,1)S(1)} %collective-permute-done.20.refs_5_) | copy-start | bytes 1179652
  84.6 0.8 copy-start.17
  85.3 0.8 copy-start.18
